TPU v7x, 32 devices: a whole 2x2x4 slice. The times are simulated.
32 devices in a mesh: mp: 2 (over x), dp: 8 (over z, core), tensor: 2 (over y).
Axes of the slice: x: 2, y: 2, z: 4, core: 2. Of those that a mesh axis runs over, the one named last changes fastest.
Arguments:
- acts: bfloat16 [2, 256, 8192], P('mp', 'dp', 'tensor'), may hold values from -6 to 6
- gate_w: bfloat16 [2, 8192, 28672], P('mp', 'tensor', 'dp'), may hold values from -0.0625 to 0.0625
- up_w: bfloat16 [2, 8192, 28672], P('mp', 'tensor', 'dp'), may hold values from -0.0625 to 0.0625
- panel_units: int32 [8192], replicated, may hold values from 0 to 28671, as said below
Outputs:
- score: bfloat16 [8192, 28672], P(('mp', 'tensor'), 'dp')
Inputs may be any that keep to these rules, and one draw needn't show every extreme that they name: `panel_units`: write an entry's position as ((r * 8) + b) * 256 + k with 0 <= k < 256; the entry lies in [b * 3584, (b + 1) * 3584), all entries are distinct, and the first and the last unit of every block are among them.
All inputs are finite; a program needn't handle non-finite values.
Results may differ from a plain program's by a relative error of at most 0.03.
Values may be sent and summed in bfloat16 or wider, within the bound.
No kernel may reach another device: no remote copies, remote signals or barrier semaphores. Data moves between devices by JAX's collectives and lax.ppermute only.
A program may use at most 128 MiB of HBM per device.

v0:
```python
import math

import jax
import jax.numpy as jnp
from jax import lax
from jax.sharding import PartitionSpec as P

epsilon = 1e-05


def from_partner(block, axis, distance):
    count = lax.axis_size(axis)
    route = []
    for low in range(count):
        high = low | 1 << distance
        if high != low and high < count:
            route += [(low, high), (high, low)]
    return lax.ppermute(block, axis, route)


def cross_models(full_units, panel_own, panel_next, model_index):
    other_units, other_panel = from_partner((full_units, panel_next), "mp", 0)
    is_first = model_index == 0
    return (
        jnp.where(is_first, panel_own, other_panel),
        jnp.where(is_first, other_units, full_units),
    )


def body(acts, gate_w, up_w, panel_units):
    model_index = lax.axis_index("mp")
    unit_block = lax.axis_index("dp")
    n_model = lax.axis_size("mp")
    n_data = lax.axis_size("dp")
    n_width = lax.axis_size("tensor")
    weight_gate = gate_w[0]
    weight_up = up_w[0]
    units = weight_gate.shape[1]
    gathered = lax.all_gather(acts[0], "dp", axis=0, tiled=True)
    tokens = gathered.shape[0]
    token_share = tokens // n_width
    score_scale = 1.0 / math.sqrt(tokens)
    panel_picks = panel_units.reshape(n_model, n_width, n_data, -1)
    panel_picks = (
        lax.dynamic_index_in_dim(panel_picks, unit_block, axis=2, keepdims=False)
        - unit_block * units
    )
    gate_part = jnp.dot(gathered, weight_gate, preferred_element_type=jnp.float32)
    up_part = jnp.dot(gathered, weight_up, preferred_element_type=jnp.float32)
    summed = lax.psum_scatter(
        jnp.concatenate([gate_part, up_part], axis=1).astype(jnp.bfloat16),
        "tensor",
        scatter_dimension=0,
        tiled=True,
    ).astype(jnp.float32)
    hidden = (jax.nn.silu(summed[:, :units]) * summed[:, units:]).astype(jnp.bfloat16)
    wide_hidden = hidden.astype(jnp.float32)
    totals = lax.psum(
        (jnp.sum(wide_hidden, axis=0), jnp.sum(wide_hidden * wide_hidden, axis=0)), "tensor"
    )
    unit_mean = totals[0] / tokens
    unit_var = totals[1] / tokens - unit_mean * unit_mean
    scored = ((wide_hidden - unit_mean) * lax.rsqrt(unit_var + epsilon)).astype(jnp.bfloat16)
    full_units = lax.all_gather(scored, "tensor", axis=0, tiled=True)
    order_list = panel_picks.transpose(1, 0, 2).reshape(-1)
    chosen = jnp.take(scored, order_list, axis=1).reshape(token_share, n_width, -1)
    moved_rows = lax.all_to_all(chosen, "tensor", split_axis=1, concat_axis=0, tiled=True)
    moved_rows = moved_rows.reshape(tokens, n_model, -1)
    panel_cols = lax.all_gather(moved_rows, "dp", axis=2, tiled=True)
    mine_a, mine_b = cross_models(full_units, panel_cols[:, 0], panel_cols[:, 1], model_index)
    result = lax.dot_general(
        mine_a, mine_b, (((0,), (0,)), ((), ())), preferred_element_type=jnp.float32
    )
    return (result * score_scale).astype(jnp.bfloat16)


def solution(mesh):
    in_specs = (P("mp", "dp", "tensor"), P("mp", "tensor", "dp"), P("mp", "tensor", "dp"), P())
    out_specs = P(("mp", "tensor"), "dp")
    return jax.shard_map(body, mesh=mesh, in_specs=in_specs, out_specs=out_specs, check_vma=False)
```

profile of v0, /device:TPU:0, one launch (start us, length us, event | category | flops | bytes accessed | tf_op | source)
XLA Modules:
  0.0 249.9 jit_solution(1860375420980347319)
XLA Ops:
  6.5 0.0 all-gather.9.cloned.1.call-start
  6.5 0.7 all-gather.9.cloned.1.call-update
  7.3 0.0 reduce-scatter.2.cloned.1.call-start
  7.3 33.5 %all-gather.9.cloned.1.call-done = bf16[1,256,4096]{2,1,0:T(8,128)(2,1)} async-done(((bf16[1,32,4096]{2,1,0:T(8,128)(2,1)}), bf16[1,256,4096]{2,1,0:T(8,128)(2,1)}) %all-gather.9.cloned.1.call-update) | async-done | bytes 2097168 | tf_op jit(solution)/shard_map/all_gather | solution.py:39
  40.8 0.0 copy-start.1
  40.8 17.8 %fusion.7 = bf16[256,3584]{1,0:T(8,128)(2,1)S(1)} fusion(bf16[1,4096,3584]{2,1,0:T(8,128)(2,1)} %param.6, bf16[1,256,4096]{2,1,0:T(8,128)(2,1)} %all-gather.9.cloned.1.call-done), kind=kOutput, calls=%fused_computation.7 | convolution fusion | flops 7517110272 | bytes 33292288 | tf_op jit(solution)/shard_map/dot_general | solution.py:49
  58.6 0.0 copy-done.1
  58.7 13.5 %fusion.4 = bf16[256,3584]{1,0:T(8,128)(2,1)S(1)} fusion(bf16[1,4096,3584]{2,1,0:T(8,128)(2,1)} %param.5, bf16[1,256,4096]{2,1,0:T(8,128)(2,1)S(1)} %copy-done.1), kind=kOutput, calls=%fused_computation.6 | convolution fusion | flops 7517110272 | bytes 33292288 | tf_op jit(solution)/shard_map/dot_general | solution.py:48
  72.2 2.3 pad_maximum_fusion
  74.5 0.0 reduce-scatter.2.cloned.1.call-update
  74.5 0.0 all-gather.7.cloned.1.call-start
  74.5 48.7 %reduce-scatter.2.cloned.1.call-done = bf16[128,7168]{1,0:T(8,128)(2,1)} async-done(((bf16[256,7168]{1,0:T(8,128)(2,1)}), bf16[128,7168]{1,0:T(8,128)(2,1)}) %reduce-scatter.2.cloned.1.call-update) | async-done | bytes 1835024 | tf_op jit(solution)/shard_map/reduce_scatter | solution.py:50
  123.2 1.9 convert_element_type.16
  125.1 0.7 convert_reduce_fusion
  125.8 0.0 copy-start
  125.8 7.2 %all-reduce = (f32[3584]{0:T(1024)S(1)}, f32[3584]{0:T(1024)S(1)}) all-reduce(f32[3584]{0:T(1024)S(1)} %get-tuple-element.6, f32[3584]{0:T(1024)S(1)} %get-tuple-element.5), channel_id=1, replica_groups=mesh['mp'=2,'dp'=8,'tensor'=2] {'tensor'}, use_global_device_ids=true, to_apply=%region_4.5 | all-reduce | flops 7168 | bytes 57344 | tf_op jit(solution)/shard_map/psum | solution.py:58
  133.0 1.1 fusion.13
  134.2 0.0 all-gather.7.cloned.1.call-update
  134.2 0.0 all-gather.5.cloned.1.call-start
  134.3 0.0 copy-done
  134.4 1.6 copy.13
  135.9 3.2 %gather_fusion = bf16[1024,128]{1,0:T(8,128)(2,1)S(1)} fusion(bf16[128,3584]{0,1:T(8,128)(2,1)S(1)} %copy.13, s32[1024]{0:T(1024)S(1)} %broadcast_clamp_fusion), kind=kCustom, calls=%fused_computation | custom fusion | bytes 528384 | tf_op jit(solution)/shard_map/jit(_take)/gather | solution.py:66
  139.2 0.1 copy.14
  139.4 10.6 %all_to_all.15 = bf16[128,2,512]{2,0,1:T(8,128)(2,1)S(1)} all-to-all(bf16[128,2,512]{2,0,1:T(8,128)(2,1)S(1)} %broadcast_select_fusion), channel_id=1, replica_groups=mesh['mp'=2,'dp'=8,'tensor'=2] {'tensor'}, dimensions={1} | all-to-all | bytes 524288 | tf_op jit(solution)/shard_map/all_to_all | solution.py:67
  150.0 0.8 reshape.60
  150.7 0.0 all-gather.5.cloned.1.call-update
  150.7 16.3 %all-gather.7.cloned.1.call-done = bf16[256,3584]{1,0:T(8,128)(2,1)} async-done(((bf16[128,3584]{1,0:T(8,128)(2,1)}), bf16[256,3584]{1,0:T(8,128)(2,1)}) %all-gather.7.cloned.1.call-update) | async-done | bytes 1835024 | tf_op jit(solution)/shard_map/all_gather | solution.py:64
  167.1 1.5 collective-permute-start.1
  168.5 30.9 %all-gather.5.cloned.1.call-done = bf16[256,2,2048]{2,1,0:T(2,128)(2,1)} async-done(((bf16[256,2,256]{2,1,0:T(2,128)(2,1)}), bf16[256,2,2048]{2,1,0:T(2,128)(2,1)}) %all-gather.5.cloned.1.call-update) | async-done | bytes 2097168 | tf_op jit(solution)/shard_map/all_gather | solution.py:69
  199.5 5.6 %fusion.21 = (bf16[256,1,2048]{2,1,0:T(2,128)(2,1)S(1)}, bf16[256,1,2048]{2,1,0:T(2,128)(2,1)S(1)}) fusion(bf16[256,2,2048]{2,1,0:T(2,128)(2,1)} %all-gather.5.cloned.1.call-done), kind=kLoop, calls=%fused_computation.34 | loop fusion | bytes 4194304 | tf_op jit(solution)/shard_map/slice | solution.py:70
  205.1 0.6 copy.25
  205.7 1.3 collective-permute-start
  207.0 2.9 %collective-permute-done.1 = bf16[256,3584]{1,0:T(8,128)(2,1)} collective-permute-done((bf16[256,3584]{1,0:T(8,128)(2,1)}, bf16[256,3584]{1,0:T(8,128)(2,1)}, u32[]{:S(2)}, u32[]{:S(2)}) %collective-permute-start.1) | collective-permute-done | bytes 1835040 | tf_op jit(solution)/shard_map/ppermute | solution.py:18
  209.9 21.9 %collective-permute-done = bf16[256,2048]{1,0:T(8,128)(2,1)} collective-permute-done((bf16[256,2048]{1,0:T(8,128)(2,1)S(1)}, bf16[256,2048]{1,0:T(8,128)(2,1)}, u32[]{:S(2)}, u32[]{:S(2)}) %collective-permute-start) | collective-permute-done | bytes 1048608 | tf_op jit(solution)/shard_map/ppermute | solution.py:18
  231.8 11.5 %multiply_convert_fusion = bf16[2048,3584]{1,0:T(8,128)(2,1)} fusion(bf16[256,3584]{1,0:T(8,128)(2,1)} %collective-permute-done.1, bf16[256,3584]{1,0:T(8,128)(2,1)} %all-gather.7.cloned.1.call-done, pred[]{:T(512)S(6)} %eq.3, bf16[256,2048]{1,0:T(8,128)(2,1)} %collective-permute-done, bf16[256,1,2048]{2,1,0:T(2,128)(2,1)S(1)} %get-tuple-element.10), kind=kOutput, calls=%fused_computation.5 | convolution fusion | flops 3774218240 | bytes 20447232 | tf_op jit(solution)/shard_map/dot_general | solution.py:71
  (10 shorter events, 0.1 us)
Async XLA Ops:
  6.5 34.3 %all-gather.9.cloned.1.call-start = ((), (), s32[]{:S(2)}) async-start(), calls=%async_computation.5 | async-start | bytes 2359296 | tf_op jit(solution)/shard_map/all_gather | solution.py:39
  7.3 116.0 %reduce-scatter.2.cloned.1.call-start = ((), (), s32[]{:S(2)}) async-start(), calls=%async_computation.2 | async-start | bytes 5505024 | tf_op jit(solution)/shard_map/reduce_scatter | solution.py:50
  40.8 17.9 %copy-start.1 = (bf16[1,256,4096]{2,1,0:T(8,128)(2,1)S(1)}, bf16[1,256,4096]{2,1,0:T(8,128)(2,1)}, u32[]{:S(2)}) copy-start(bf16[1,256,4096]{2,1,0:T(8,128)(2,1)} %all-gather.9.cloned.1.call-done) | copy-start | bytes 6291460
  74.5 92.6 %all-gather.7.cloned.1.call-start = ((), (), s32[]{:S(2)}) async-start(), calls=%async_computation.4 | async-start | bytes 2752512 | tf_op jit(solution)/shard_map/all_gather | solution.py:64
  125.8 8.4 %copy-start = (s32[8192]{0:T(1024)S(1)}, s32[8192]{0:T(1024)}, u32[]{:S(2)}) copy-start(s32[8192]{0:T(1024)} %param.7) | copy-start | bytes 98308
  134.2 65.3 %all-gather.5.cloned.1.call-start = ((), (), s32[]{:S(2)}) async-start(), calls=%async_computation.3 | async-start | bytes 2359296 | tf_op jit(solution)/shard_map/all_gather | solution.py:69
  167.1 42.8 %collective-permute-start.1 = (bf16[256,3584]{1,0:T(8,128)(2,1)}, bf16[256,3584]{1,0:T(8,128)(2,1)}, u32[]{:S(2)}, u32[]{:S(2)}) collective-permute-start(bf16[256,3584]{1,0:T(8,128)(2,1)} %all-gather.7.cloned.1.call-done), channel_id=1, source_target_pairs={{0,16},{16,0},{1,17},{17,1},{2,18},{18,2},{3,19},{19,3},{4,20},{20... | collective-permute-start | bytes 5505032 | tf_op jit(solution)/shard_map/ppermute | solution.py:18
  205.7 26.1 %collective-permute-start = (bf16[256,2048]{1,0:T(8,128)(2,1)S(1)}, bf16[256,2048]{1,0:T(8,128)(2,1)}, u32[]{:S(2)}, u32[]{:S(2)}) collective-permute-start(bf16[256,2048]{1,0:T(8,128)(2,1)S(1)} %bitcast.41), channel_id=1, source_target_pairs={{0,16},{16,0},{1,17},{17,1},{2,18},{18,2},{3,19},{19,3},{4,20},{20... | collective-permute-start | bytes 3145736 | tf_op jit(solution)/shard_map/ppermute | solution.py:18
Sparse Core Ops, SparseCore 0:
  9.0 31.7 all-gather.8
  74.6 48.5 reduce-scatter.1
  134.3 32.7 all-gather.6
  168.6 30.8 all-gather.4
where the time goes:
time: 250 us
  waiting for transfers between devices  155 us (62%)
  matrix products  42.9 us (17%)
  blocking collectives  17.8 us (7%)
  between operations  13.3 us (5%)
  local copies, waits for them, and re-layouts  12 us (5%)
  other arithmetic  6.05 us (2%)
  starting transfers between devices  2.86 us (1%)
    reduce_scatter x1, waiting for transfers between devices, body(): lax.psum_scatter(jnp.concatenate([gate_part, up_part], axis=1).astype(jnp...  48.7 us
    all_gather x1, waiting for transfers between devices, body(): gathered = lax.all_gather(acts[0], 'dp', axis=0, tiled=True)  33.5 us
    all_gather x1, waiting for transfers between devices, body(): panel_cols = lax.all_gather(moved_rows, 'dp', axis=2, tiled=True)  30.9 us
    ppermute x2, waiting for transfers between devices, from_partner(): return lax.ppermute(block, axis, route)  24.8 us
    dot_general x1, matrix products, body(): up_part = jnp.dot(gathered, weight_up, preferred_element_type=jnp.float32)  17.8 us
    all_gather x1, waiting for transfers between devices, body(): full_units = lax.all_gather(scored, 'tensor', axis=0, tiled=True)  16.3 us
    dot_general x1, matrix products, body(): jnp.dot(gathered, weight_gate, preferred_element_type=jnp.float32)  13.5 us
    dot_general x1, matrix products, body(): lax.dot_general(mine_a, mine_b, (((0,), (0,)), ((), ())), preferred_eleme...  11.5 us
  transfers between devices with their start and end apart: 6, of which 6 were waited for; matrix products, arithmetic and copies ran while one was open for 5% of the time, Pallas kernels for 0%

commit v1 on v0

--- a/solution.py
+++ b/solution.py
@@ -1,11 +1,16 @@
+import functools
 import math
 
 import jax
 import jax.numpy as jnp
 from jax import lax
+from jax.experimental import pallas as pl
+from jax.experimental.pallas import tpu as pltpu
 from jax.sharding import PartitionSpec as P
 
 epsilon = 1e-05
+AXES = ("mp", "dp", "tensor")
+MIB = 1 << 20
 
 
 def from_partner(block, axis, distance):
@@ -27,7 +32,7 @@
     )
 
 
-def body(acts, gate_w, up_w, panel_units):
+def general_body(acts, gate_w, up_w, panel_units):
     model_index = lax.axis_index("mp")
     unit_block = lax.axis_index("dp")
     n_model = lax.axis_size("mp")
@@ -74,7 +79,303 @@
     return (result * score_scale).astype(jnp.bfloat16)
 
 
+def routes(sizes, move):
+    n_model, n_data, n_width = sizes
+    pairs = []
+    for m in range(n_model):
+        for d in range(n_data):
+            for t in range(n_width):
+                to = move(m, d, t)
+                if to is not None:
+                    source = (m * n_data + d) * n_width + t
+                    pairs.append((source, (to[0] * n_data + to[1]) * n_width + to[2]))
+    return pairs
+
+
+def send(block, sizes, move):
+    return lax.ppermute(block, AXES, routes(sizes, move))
+
+
+def along_chips(step, sources):
+    def move(m, d, t):
+        return (m, d + 2 * step, t) if d // 2 in sources else None
+
+    return move
+
+
+def gather_chips(block, sizes, chip, core):
+    up = send(block, sizes, along_chips(1, (0, 1, 2)))
+    down = send(block, sizes, along_chips(-1, (1, 2, 3)))
+    far = jnp.where(chip == 2, down, up)
+
+    def across(m, d, t):
+        return {2: (m, d - 4, t), 1: (m, d + 4, t)}.get(d // 2)
+
+    further_down = send(down, sizes, along_chips(-1, (1, 2)))
+    further_up = send(up, sizes, along_chips(1, (1, 2)))
+    ends = send(far, sizes, across)
+    line = jnp.stack([ends, further_up, up, block, down, further_down, ends])
+    same = lax.dynamic_slice_in_dim(line, 3 - chip, 4, axis=0)
+    other = send(same, sizes, lambda m, d, t: (m, d ^ 1, t))
+    first = core == 0
+    pairs = jnp.stack([jnp.where(first, same, other), jnp.where(first, other, same)], axis=1)
+    return pairs.reshape((-1,) + block.shape[1:])
+
+
+def partial_kernel(place_ref, x_ref, gate_ref, up_ref, out_ref):
+    x = x_ref[...]
+    out_ref[0] = jnp.dot(x, gate_ref[...], preferred_element_type=jnp.float32).astype(jnp.bfloat16)
+    out_ref[1] = jnp.dot(x, up_ref[...], preferred_element_type=jnp.float32).astype(jnp.bfloat16)
+
+
+def partials(place, x, gate, up, tile, first, count):
+    tokens, width = x.shape
+    weights = pl.BlockSpec((width, tile), lambda i, place_ref: (0, place_ref[0] + first + i))
+    return pl.pallas_call(
+        partial_kernel,
+        out_shape=jax.ShapeDtypeStruct((2, tokens, tile * count), jnp.bfloat16),
+        grid_spec=pltpu.PrefetchScalarGridSpec(
+            num_scalar_prefetch=1,
+            grid=(count,),
+            in_specs=[
+                pl.BlockSpec((tokens, width), lambda i, place_ref: (0, 0)),
+                weights,
+                weights,
+            ],
+            out_specs=pl.BlockSpec((2, tokens, tile), lambda i, place_ref: (0, 0, i)),
+        ),
+        compiler_params=pltpu.CompilerParams(vmem_limit_bytes=32 * MIB),
+        cost_estimate=pl.CostEstimate(
+            flops=4 * tokens * width * tile * count,
+            bytes_accessed=4 * width * tile * count,
+            transcendentals=0,
+        ),
+    )(place, x, gate, up)
+
+
+def pick_kernel(counts, tile, bases_ref, picks_ref, *refs):
+    out_ref = refs[-1]
+    tokens, picked = out_ref.shape[1:]
+    total = jnp.zeros((2 * tokens, picked), jnp.float32)
+    for part, (ref, count) in enumerate(zip(refs[:-1], counts)):
+        for i in range(count):
+            base = bases_ref[part] + i * tile
+            unit = lax.broadcasted_iota(jnp.int32, (tile, picked), 0) + base
+            chosen = jnp.where(unit == picks_ref[...], 1.0, 0.0).astype(jnp.bfloat16)
+            block = ref[:, :, i * tile : (i + 1) * tile].reshape(2 * tokens, tile)
+            total += jnp.dot(block, chosen, preferred_element_type=jnp.float32)
+    out_ref[...] = total.astype(jnp.bfloat16).reshape(2, tokens, picked)
+
+
+def pick(bases, picks, parts, tile):
+    tokens = parts[0].shape[1]
+    picked = picks.shape[1]
+    counts = [part.shape[2] // tile for part in parts]
+    vmem = pl.BlockSpec(memory_space=pltpu.VMEM)
+    return pl.pallas_call(
+        functools.partial(pick_kernel, counts, tile),
+        out_shape=jax.ShapeDtypeStruct((2, tokens, picked), jnp.bfloat16),
+        in_specs=[pl.BlockSpec(memory_space=pltpu.SMEM), vmem] + [vmem] * len(parts),
+        out_specs=vmem,
+        compiler_params=pltpu.CompilerParams(vmem_limit_bytes=32 * MIB),
+        cost_estimate=pl.CostEstimate(
+            flops=4 * tokens * picked * tile * sum(counts),
+            bytes_accessed=4 * tokens * tile * sum(counts),
+            transcendentals=0,
+        ),
+    )(bases, picks, *parts)
+
+
+def zscore(mine, theirs):
+    tokens = mine.shape[1]
+    gate = mine[0].astype(jnp.float32) + theirs[0].astype(jnp.float32)
+    up = mine[1].astype(jnp.float32) + theirs[1].astype(jnp.float32)
+    hidden = (gate / (1.0 + jnp.exp(-gate)) * up).astype(jnp.bfloat16).astype(jnp.float32)
+    mean = jnp.sum(hidden, axis=0, keepdims=True) / tokens
+    var = jnp.sum(hidden * hidden, axis=0, keepdims=True) / tokens - mean * mean
+    return (hidden - mean) * lax.rsqrt(var + epsilon)
+
+
+def unit_kernel(mine_ref, theirs_ref, out_ref):
+    out_ref[...] = zscore(mine_ref[...], theirs_ref[...]).astype(jnp.bfloat16)
+
+
+def unit_scores(mine, theirs, tile, first):
+    _, tokens, count = theirs.shape
+    return pl.pallas_call(
+        unit_kernel,
+        out_shape=jax.ShapeDtypeStruct((tokens, count), jnp.bfloat16),
+        grid=(count // tile,),
+        in_specs=[
+            pl.BlockSpec((2, tokens, tile), lambda i: (0, 0, first + i)),
+            pl.BlockSpec((2, tokens, tile), lambda i: (0, 0, i)),
+        ],
+        out_specs=pl.BlockSpec((tokens, tile), lambda i: (0, i)),
+        compiler_params=pltpu.CompilerParams(vmem_limit_bytes=16 * MIB),
+        cost_estimate=pl.CostEstimate(
+            flops=20 * tokens * count, bytes_accessed=10 * tokens * count, transcendentals=tokens * count
+        ),
+    )(mine, theirs)
+
+
+def panel_kernel(mine_ref, theirs_ref, out_ref):
+    out_ref[...] = zscore(mine_ref[...], theirs_ref[...]).T.astype(jnp.bfloat16)
+
+
+def panel_scores(mine, theirs, tile):
+    _, tokens, count = theirs.shape
+    block = pl.BlockSpec((2, tokens, tile), lambda i: (0, 0, i))
+    return pl.pallas_call(
+        panel_kernel,
+        out_shape=jax.ShapeDtypeStruct((count, tokens), jnp.bfloat16),
+        grid=(count // tile,),
+        in_specs=[block, block],
+        out_specs=pl.BlockSpec((tile, tokens), lambda i: (i, 0)),
+        compiler_params=pltpu.CompilerParams(vmem_limit_bytes=16 * MIB),
+        cost_estimate=pl.CostEstimate(
+            flops=20 * tokens * count, bytes_accessed=10 * tokens * count, transcendentals=tokens * count
+        ),
+    )(mine, theirs)
+
+
+def score_kernel(scale, count, where_ref, panel_ref, b_mine, a_mine, b_far, a_far, *refs):
+    out_ref = refs[-1]
+    is_b = where_ref[0] == 1
+    step = pl.program_id(0)
+
+    def write(units):
+        total = jnp.dot(panel_ref[...], units, preferred_element_type=jnp.float32)
+        out_ref[...] = (total * scale).astype(jnp.bfloat16)
+
+    @pl.when(step < count)
+    def _():
+        write(jnp.where(is_b, b_mine[...], a_mine[...]))
+
+    @pl.when(step >= count)
+    def _():
+        write(jnp.where(is_b, b_far[...], a_far[...]))
+
+
+def scores(where, panel, pieces, tile, first, half, so_far):
+    rows, tokens = panel.shape
+    count = pieces[0].shape[1] // tile
+    near = pl.BlockSpec((tokens, tile), lambda i, where_ref: (0, jnp.minimum(i, count - 1)))
+    far = pl.BlockSpec((tokens, tile), lambda i, where_ref: (0, jnp.maximum(i - count, 0)))
+
+    def place(i, where_ref):
+        side = jnp.where(i < count, where_ref[1], 1 - where_ref[1])
+        return 0, side * half + first + lax.rem(i, count)
+
+    carried = [] if so_far is None else [so_far]
+    return pl.pallas_call(
+        functools.partial(score_kernel, 1.0 / math.sqrt(tokens), count),
+        out_shape=jax.ShapeDtypeStruct((rows, 2 * half * tile), jnp.bfloat16),
+        grid_spec=pltpu.PrefetchScalarGridSpec(
+            num_scalar_prefetch=1,
+            grid=(2 * count,),
+            in_specs=[pl.BlockSpec((rows, tokens), lambda i, where_ref: (0, 0)), near, near, far, far]
+            + [pl.BlockSpec(memory_space=pl.ANY)] * len(carried),
+            out_specs=pl.BlockSpec((rows, tile), place),
+        ),
+        input_output_aliases={6: 0} if carried else {},
+        compiler_params=pltpu.CompilerParams(vmem_limit_bytes=32 * MIB),
+        cost_estimate=pl.CostEstimate(
+            flops=4 * rows * tokens * tile * count,
+            bytes_accessed=4 * rows * tile * count,
+            transcendentals=0,
+        ),
+    )(where, panel, *pieces, *carried)
+
+
+def split_tiles(count):
+    sizes = []
+    while count > 0:
+        sizes.append(min(2, count))
+        count -= sizes[-1]
+    return sizes
+
+
+def paired_body(acts, gate_w, up_w, panel_units):
+    model = lax.axis_index("mp")
+    block = lax.axis_index("dp")
+    side = lax.axis_index("tensor")
+    sizes = tuple(lax.axis_size(name) for name in AXES)
+    gate, up = gate_w[0], up_w[0]
+    units = gate.shape[1]
+    tile = 256
+    half = units // 2 // tile
+    chunks = split_tiles(half)
+
+    x = gather_chips(acts[0], sizes, block // 2, block % 2)
+
+    to_side = jnp.reshape((1 - side) * half, (1,)).astype(jnp.int32)
+    own_side = jnp.reshape(side * half, (1,)).astype(jnp.int32)
+
+    def b_sides(m, d, t):
+        return (m, d, 1 - t) if m == 1 else None
+
+    def a_sides(m, d, t):
+        return (m, d, 1 - t) if m == 0 else None
+
+    def b_to_a(m, d, t):
+        return (0, d, t) if m == 1 else None
+
+    def a_to_b(m, d, t):
+        return (1, d, t) if m == 0 else None
+
+    sent, came, first = [], [], 0
+    for count in chunks:
+        sent.append(partials(to_side, x, gate, up, tile, first, count))
+        came.append(send(sent[-1], sizes, b_sides))
+        first += count
+    kept = partials(own_side, x, gate, up, tile, 0, half)
+
+    picks = panel_units.reshape(2, 2, sizes[1], -1)
+    picks = lax.dynamic_index_in_dim(picks, block, axis=2, keepdims=False) - block * units
+    picks_far = lax.dynamic_index_in_dim(picks, 1 - side, axis=1, keepdims=False).reshape(1, -1)
+    picks_own = lax.dynamic_index_in_dim(picks, side, axis=1, keepdims=False).reshape(1, -1)
+    bases, first = [], 0
+    for count in chunks:
+        bases.append((to_side[0] + first) * tile)
+        first += count
+    bases = jnp.stack(bases + [own_side[0] * tile]).astype(jnp.int32)
+    parts = sent + [kept]
+    panel_came = send(pick(bases, picks_far, parts, tile), sizes, a_sides)
+    panel_kept = pick(bases, picks_own, parts, tile)
+    rows = panel_scores(panel_kept, panel_came, tile)
+    share = rows.shape[0] // 2
+    rows_b = send(rows[share:], sizes, a_to_b)
+    rows = jnp.where(model == 0, rows[:share], rows_b)
+    panel = gather_chips(rows, sizes, block // 2, block % 2)
+
+    pieces, first = [], 0
+    for index, count in enumerate(chunks):
+        z = unit_scores(kept, came[index], tile, first)
+        first += count
+        a_mine = send(z, sizes, b_to_a)
+        a_far = send(a_mine, sizes, a_sides)
+        if index == 0:
+            b_far = send(a_far, sizes, a_to_b)
+        else:
+            b_far = send(z, sizes, b_sides)
+        pieces.append((z, a_mine, b_far, a_far))
+
+    where = jnp.stack([model, side]).astype(jnp.int32)
+    result, first = None, 0
+    for count, piece in zip(chunks, pieces):
+        result = scores(where, panel, piece, tile, first, half, result)
+        first += count
+    return result
+
+
 def solution(mesh):
     in_specs = (P("mp", "dp", "tensor"), P("mp", "tensor", "dp"), P("mp", "tensor", "dp"), P())
     out_specs = P(("mp", "tensor"), "dp")
+    paired = mesh.shape["mp"] == 2 and mesh.shape["tensor"] == 2 and mesh.shape["dp"] == 8
+
+    def body(acts, gate_w, up_w, panel_units):
+        if paired and gate_w.shape[2] % 512 == 0:
+            return paired_body(acts, gate_w, up_w, panel_units)
+        return general_body(acts, gate_w, up_w, panel_units)
+
     return jax.shard_map(body, mesh=mesh, in_specs=in_specs, out_specs=out_specs, check_vma=False)

time: 250 us -> 171 us (0.68)
  waiting for transfers between devices: 155 us -> 63.7 us
  Pallas kernels: 0 us -> 54.8 us
  starting transfers between devices: 2.86 us -> 47.8 us
  matrix products: 42.9 us -> 0 us
  blocking collectives: 17.8 us -> 0 us
  between operations: 13.3 us -> 0.66 us
  local copies, waits for them, and re-layouts: 12 us -> 2.28 us
  other arithmetic: 6.05 us -> 0.66 us
    all_gather x3 -> x0, waiting for transfers between devices: 80.8 us -> none  [the longest x1 33.5 us: body(): gathered = lax.all_gather(acts[0], 'dp', axis=0, tiled=True)]
    pallas_call x0 -> x16, Pallas kernels: none -> 54.8 us  [the longest x5 32.4 us: partials(): pl.pallas_call(partial_kernel, out_shape=jax.ShapeDtypeStruct((2, tokens,...]
    reduce_scatter x1 -> x0, waiting for transfers between devices: 48.7 us -> none  [body(): lax.psum_scatter(jnp.concatenate([gate_part, up_part], axis=1).astype(jnp...]
    ppermute x2 -> x30, starting transfers between devices: 2.74 us -> 47.8 us  [send(): return lax.ppermute(block, AXES, routes(sizes, move))]
    dot_general x3 -> x0, matrix products: 42.9 us -> none  [the longest x1 17.8 us: body(): up_part = jnp.dot(gathered, weight_up, preferred_element_type=jnp.float32)]
    ppermute x2 -> x30, waiting for transfers between devices: 24.8 us -> 63.7 us  [send(): return lax.ppermute(block, AXES, routes(sizes, move))]
    all_to_all x1 -> x0, blocking collectives: 10.6 us -> none  [body(): lax.all_to_all(chosen, 'tensor', split_axis=1, concat_axis=0, tiled=True)]
    psum x1 -> x0, blocking collectives: 7.16 us -> none  [body(): lax.psum((jnp.sum(wide_hidden, axis=0), jnp.sum(wide_hidden * wide_hidden...]
  transfers between devices with their start and end apart: 6 -> 30, of which waited for: 6 -> 14; matrix products, arithmetic and copies ran while one was open for 5% -> 0% of each run, Pallas kernels for 0% -> 10%
where the time goes in v1:
time: 171 us; the launch traced here: 170 us
  waiting for transfers between devices  63.7 us (37%)
  Pallas kernels  54.8 us (32%)
  starting transfers between devices  47.8 us (28%)
  local copies, waits for them, and re-layouts  2.28 us (1%)
    ppermute x30, waiting for transfers between devices, send(): return lax.ppermute(block, AXES, routes(sizes, move))  63.7 us
    ppermute x30, starting transfers between devices, send(): return lax.ppermute(block, AXES, routes(sizes, move))  47.8 us
    pallas_call x5, Pallas kernels, partials(): pl.pallas_call(partial_kernel, out_shape=jax.ShapeDtypeStruct((2, tokens,...  32.4 us
    pallas_call x4, Pallas kernels, scores(): pl.pallas_call(functools.partial(score_kernel, 1.0 / math.sqrt(tokens), c...  14.5 us
    pallas_call x2, Pallas kernels, pick(): pl.pallas_call(functools.partial(pick_kernel, counts, tile), out_shape=ja...  5.2 us
  transfers between devices with their start and end apart: 30, of which 14 were waited for; matrix products, arithmetic and copies ran while one was open for 0% of the time, Pallas kernels for 10%

profile of v1, /device:TPU:0, one launch (start us, length us, event | category | flops | bytes accessed | tf_op | source)
XLA Modules:
  0.0 170.0 jit_solution(6429042303620212141)
XLA Ops:
  0.0 5.1 %collective-permute-start.1 = (bf16[32,4096]{1,0:T(8,128)(2,1)}, bf16[32,4096]{1,0:T(8,128)(2,1)S(1)}, u32[]{:S(2)}, u32[]{:S(2)}) collective-permute-start(bf16[32,4096]{1,0:T(8,128)(2,1)} %bitcast.69), channel_id=1, source_target_pairs={{0,4},{1,5},{2,6},{3,7},{4,8},{5,9},{6,10},{7,11},{8,12},{9,13},{1... | collective-permute-start | bytes 786440 | tf_op jit(solution)/shard_map/ppermute | solution.py:96
  5.1 1.3 collective-permute-start
  6.4 4.5 %collective-permute-done.1 = bf16[32,4096]{1,0:T(8,128)(2,1)S(1)} collective-permute-done((bf16[32,4096]{1,0:T(8,128)(2,1)}, bf16[32,4096]{1,0:T(8,128)(2,1)S(1)}, u32[]{:S(2)}, u32[]{:S(2)}) %collective-permute-start.1) | collective-permute-done | bytes 262176 | tf_op jit(solution)/shard_map/ppermute | solution.py:96
  10.9 4.0 %collective-permute-done = bf16[32,4096]{1,0:T(8,128)(2,1)S(1)} collective-permute-done((bf16[32,4096]{1,0:T(8,128)(2,1)}, bf16[32,4096]{1,0:T(8,128)(2,1)S(1)}, u32[]{:S(2)}, u32[]{:S(2)}) %collective-permute-start) | collective-permute-done | bytes 262176 | tf_op jit(solution)/shard_map/ppermute | solution.py:96
  15.0 1.3 collective-permute-start.2
  17.0 1.3 collective-permute-start.4
  18.3 6.6 %collective-permute-done.2 = bf16[32,4096]{1,0:T(8,128)(2,1)S(1)} collective-permute-done((bf16[32,4096]{1,0:T(8,128)(2,1)S(1)}, bf16[32,4096]{1,0:T(8,128)(2,1)S(1)}, u32[]{:S(2)}, u32[]{:S(2)}) %collective-permute-start.2) | collective-permute-done | bytes 262176 | tf_op jit(solution)/shard_map/ppermute | solution.py:96
  25.0 5.2 %collective-permute-done.4 = bf16[32,4096]{1,0:T(8,128)(2,1)S(1)} collective-permute-done((bf16[32,4096]{1,0:T(8,128)(2,1)S(1)}, bf16[32,4096]{1,0:T(8,128)(2,1)S(1)}, u32[]{:S(2)}, u32[]{:S(2)}) %collective-permute-start.4) | collective-permute-done | bytes 262176 | tf_op jit(solution)/shard_map/ppermute | solution.py:96
  30.3 1.0 constant_dynamic-slice_fusion.2
  31.5 2.7 %collective-permute-done.5 = bf16[4,32,4096]{2,1,0:T(8,128)(2,1)S(1)} collective-permute-done((bf16[4,32,4096]{2,1,0:T(8,128)(2,1)}, bf16[4,32,4096]{2,1,0:T(8,128)(2,1)S(1)}, u32[]{:S(2)}, u32[]{:S(2)}) %collective-permute-start.5) | collective-permute-done | bytes 1048608 | tf_op jit(solution)/shard_map/ppermute | solution.py:96
  34.7 3.5 %shard_map.49.refs_3_ = bf16[2,256,256]{2,1,0:T(8,128)(2,1)S(1)} custom-call(s32[1]{0:T(128)} %bitcast.8.place_ref, bf16[256,4096]{1,0:T(8,128)(2,1)S(1)} %bitcast.48, bf16[4096,3584]{1,0:T(8,128)(2,1)} %bitcast.59, bf16[4096,3584]{1,0:T(8,128)(2,1)} %bitcast.64), custom_call_target="tpu_custom_call" | custom-call | flops 1073741824 | bytes 4194304 | tf_op jit(solution)/shard_map/pallas_call | solution.py:134
  38.2 4.8 %shard_map.48.refs_2_ = bf16[2,256,512]{2,1,0:T(8,128)(2,1)S(1)} custom-call(s32[1]{0:T(128)} %bitcast.8.place_ref, bf16[256,4096]{1,0:T(8,128)(2,1)S(1)} %bitcast.49, bf16[4096,3584]{1,0:T(8,128)(2,1)} %bitcast.60, bf16[4096,3584]{1,0:T(8,128)(2,1)} %bitcast.65), custom_call_target="tpu_custom_call" | custom-call | flops 2147483648 | bytes 8388608 | tf_op jit(solution)/shard_map/pallas_call | solution.py:134
  43.0 4.8 %shard_map.47.refs_1_ = bf16[2,256,512]{2,1,0:T(8,128)(2,1)S(1)} custom-call(s32[1]{0:T(128)} %bitcast.8.place_ref, bf16[256,4096]{1,0:T(8,128)(2,1)S(1)} %bitcast.50, bf16[4096,3584]{1,0:T(8,128)(2,1)} %bitcast.61, bf16[4096,3584]{1,0:T(8,128)(2,1)} %bitcast.66), custom_call_target="tpu_custom_call" | custom-call | flops 2147483648 | bytes 8388608 | tf_op jit(solution)/shard_map/pallas_call | solution.py:134
  47.9 4.9 %shard_map.46.refs_0_ = bf16[2,256,512]{2,1,0:T(8,128)(2,1)S(1)} custom-call(s32[1]{0:T(128)} %bitcast.8.place_ref, bf16[256,4096]{1,0:T(8,128)(2,1)S(1)} %bitcast.51, bf16[4096,3584]{1,0:T(8,128)(2,1)} %bitcast.62, bf16[4096,3584]{1,0:T(8,128)(2,1)} %bitcast.67), custom_call_target="tpu_custom_call" | custom-call | flops 2147483648 | bytes 8388608 | tf_op jit(solution)/shard_map/pallas_call | solution.py:134
  52.8 14.4 %shard_map.50.refs_4_.mine_ref = bf16[2,256,1792]{2,1,0:T(8,128)(2,1)S(1)} custom-call(s32[1]{0:T(128)} %bitcast.20.place_ref, bf16[256,4096]{1,0:T(8,128)(2,1)S(1)} %bitcast.52, bf16[4096,3584]{1,0:T(8,128)(2,1)} %bitcast.63, bf16[4096,3584]{1,0:T(8,128)(2,1)} %bitcast.68), custom_call_target="tpu_custom_call" | custom-call | flops 7516192768 | bytes 29360128 | tf_op jit(solution)/shard_map/pallas_call | solution.py:134
  67.2 2.6 %shard_map.52 = bf16[2,256,512]{2,1,0:T(8,128)(2,1)S(1)} custom-call(s32[5]{0:T(128)S(1)} %stack.94.bases_ref, s32[1,512]{1,0:T(1,128)S(1)} %bitcast.58, bf16[2,256,512]{2,1,0:T(8,128)(2,1)S(1)} %shard_map.46.refs_0_, bf16[2,256,512]{2,1,0:T(8,128)(2,1)S(1)} %shard_map.47.refs_1_, bf16[2,256,512]{2,1,0:T(8,128)(2,1)S(1)} %shard_map.48.refs_2_, ...), custom_call_target="tpu_custom_call" | custom-call | flops 1879048192 | bytes 3670016 | tf_op jit(solution)/shard_map/pallas_call | solution.py:175
  69.8 3.4 %collective-permute-start.6 = (bf16[2,256,512]{2,1,0:T(8,128)(2,1)S(1)}, bf16[2,256,512]{2,1,0:T(8,128)(2,1)S(1)}, u32[]{:S(2)}, u32[]{:S(2)}) collective-permute-start(bf16[2,256,512]{2,1,0:T(8,128)(2,1)S(1)} %shard_map.52), channel_id=1, source_target_pairs={{0,1},{1,0},{2,3},{3,2},{4,5},{5,4},{6,7},{7,6},{8,9},{9,8},{10,11... | collective-permute-start | bytes 1572872 | tf_op jit(solution)/shard_map/ppermute | solution.py:96
  73.3 2.6 %shard_map.51.mine_ref = bf16[2,256,512]{2,1,0:T(8,128)(2,1)S(1)} custom-call(s32[5]{0:T(128)S(1)} %stack.94.bases_ref, s32[1,512]{1,0:T(1,128)S(1)} %bitcast.57, bf16[2,256,512]{2,1,0:T(8,128)(2,1)S(1)} %shard_map.46.refs_0_, bf16[2,256,512]{2,1,0:T(8,128)(2,1)S(1)} %shard_map.47.refs_1_, bf16[2,256,512]{2,1,0:T(8,128)(2,1)S(1)} %shard_map.48.refs_2_, ...), custom_call_target="tpu_custom_call" | custom-call | flops 1879048192 | bytes 3670016 | tf_op jit(solution)/shard_map/pallas_call | solution.py:175
  75.9 9.8 %collective-permute-done.6.theirs_ref = bf16[2,256,512]{2,1,0:T(8,128)(2,1)S(1)} collective-permute-done((bf16[2,256,512]{2,1,0:T(8,128)(2,1)S(1)}, bf16[2,256,512]{2,1,0:T(8,128)(2,1)S(1)}, u32[]{:S(2)}, u32[]{:S(2)}) %collective-permute-start.6) | collective-permute-done | bytes 524320 | tf_op jit(solution)/shard_map/ppermute | solution.py:96
  85.7 0.7 shard_map.53
  87.0 1.3 collective-permute-start.7
  88.3 0.7 collective-permute-start.26
  89.0 2.1 %collective-permute-done.7 = bf16[256,256]{1,0:T(8,128)(2,1)S(1)} collective-permute-done((bf16[256,256]{1,0:T(8,128)(2,1)}, bf16[256,256]{1,0:T(8,128)(2,1)S(1)}, u32[]{:S(2)}, u32[]{:S(2)}) %collective-permute-start.7) | collective-permute-done | bytes 131104 | tf_op jit(solution)/shard_map/ppermute | solution.py:96
  91.2 2.5 %collective-permute-start.9 = (bf16[256,256]{1,0:T(8,128)(2,1)S(1)}, bf16[256,256]{1,0:T(8,128)(2,1)S(1)}, u32[]{:S(2)}, u32[]{:S(2)}) collective-permute-start(bf16[256,256]{1,0:T(8,128)(2,1)S(1)} %slice_select_fusion), channel_id=1, source_target_pairs={{0,4},{1,5},{2,6},{3,7},{4,8},{5,9},{6,10},{7,11},{8,12},{9,13},{1... | collective-permute-start | bytes 393224 | tf_op jit(solution)/shard_map/ppermute | solution.py:96
  93.6 1.3 collective-permute-start.8
  94.9 1.2 collective-permute-done.9
  96.1 4.4 %collective-permute-done.8 = bf16[256,256]{1,0:T(8,128)(2,1)S(1)} collective-permute-done((bf16[256,256]{1,0:T(8,128)(2,1)S(1)}, bf16[256,256]{1,0:T(8,128)(2,1)S(1)}, u32[]{:S(2)}, u32[]{:S(2)}) %collective-permute-start.8) | collective-permute-done | bytes 131104 | tf_op jit(solution)/shard_map/ppermute | solution.py:96
  100.5 1.3 collective-permute-start.10
  101.8 0.7 collective-permute-start.22
  103.8 1.3 collective-permute-start.27
  105.8 2.5 %collective-permute-done.10 = bf16[256,256]{1,0:T(8,128)(2,1)S(1)} collective-permute-done((bf16[256,256]{1,0:T(8,128)(2,1)S(1)}, bf16[256,256]{1,0:T(8,128)(2,1)S(1)}, u32[]{:S(2)}, u32[]{:S(2)}) %collective-permute-start.10) | collective-permute-done | bytes 131104 | tf_op jit(solution)/shard_map/ppermute | solution.py:96
  108.3 1.3 collective-permute-start.12
  109.7 6.3 %collective-permute-done.12 = bf16[256,256]{1,0:T(8,128)(2,1)S(1)} collective-permute-done((bf16[256,256]{1,0:T(8,128)(2,1)S(1)}, bf16[256,256]{1,0:T(8,128)(2,1)S(1)}, u32[]{:S(2)}, u32[]{:S(2)}) %collective-permute-start.12) | collective-permute-done | bytes 131104 | tf_op jit(solution)/shard_map/ppermute | solution.py:96
  117.5 1.3 collective-permute-start.23
  118.8 3.4 %collective-permute-start.28 = (bf16[256,512]{1,0:T(8,128)(2,1)S(1)}, bf16[256,512]{1,0:T(8,128)(2,1)S(1)}, u32[]{:S(2)}, u32[]{:S(2)}) collective-permute-start(bf16[256,512]{1,0:T(8,128)(2,1)S(1)} %collective-permute-done.27.a_mine), channel_id=1, source_target_pairs={{0,1},{1,0},{2,3},{3,2},{4,5},{5,4},{6,7},{7,6},{8,9},{9,8},{10,11... | collective-permute-start | bytes 786440 | tf_op jit(solution)/shard_map/ppermute | solution.py:96
  122.5 1.3 collective-permute-start.15
  125.1 9.9 %collective-permute-done.23.a_mine = bf16[256,512]{1,0:T(8,128)(2,1)S(1)} collective-permute-done((bf16[256,512]{1,0:T(8,128)(2,1)S(1)}, bf16[256,512]{1,0:T(8,128)(2,1)S(1)}, u32[]{:S(2)}, u32[]{:S(2)}) %collective-permute-start.23) | collective-permute-done | bytes 262176 | tf_op jit(solution)/shard_map/ppermute | solution.py:96
  135.0 1.3 collective-permute-start.19
  136.3 2.4 %collective-permute-start.25 = (bf16[256,512]{1,0:T(8,128)(2,1)S(1)}, bf16[256,512]{1,0:T(8,128)(2,1)S(1)}, u32[]{:S(2)}, u32[]{:S(2)}) collective-permute-start(bf16[256,512]{1,0:T(8,128)(2,1)S(1)} %collective-permute-done.23.a_mine), channel_id=1, source_target_pairs={{0,1},{1,0},{2,3},{3,2},{4,5},{5,4},{6,7},{7,6},{8,9},{9,8},{10,11... | collective-permute-start | bytes 786440 | tf_op jit(solution)/shard_map/ppermute | solution.py:96
  138.7 4.8 %collective-permute-start.29 = (bf16[256,512]{1,0:T(8,128)(2,1)S(1)}, bf16[256,512]{1,0:T(8,128)(2,1)S(1)}, u32[]{:S(2)}, u32[]{:S(2)}) collective-permute-start(bf16[256,512]{1,0:T(8,128)(2,1)S(1)} %collective-permute-done.28.a_far), channel_id=1, source_target_pairs={{0,16},{1,17},{2,18},{3,19},{4,20},{5,21},{6,22},{7,23},{8,24},{9,... | collective-permute-start | bytes 786440 | tf_op jit(solution)/shard_map/ppermute | solution.py:96
  143.7 3.2 %collective-permute-done.19.a_mine = bf16[256,512]{1,0:T(8,128)(2,1)S(1)} collective-permute-done((bf16[256,512]{1,0:T(8,128)(2,1)S(1)}, bf16[256,512]{1,0:T(8,128)(2,1)S(1)}, u32[]{:S(2)}, u32[]{:S(2)}) %collective-permute-start.19) | collective-permute-done | bytes 262176 | tf_op jit(solution)/shard_map/ppermute | solution.py:96
  147.5 1.2 collective-permute-done.29.b_far
  148.7 2.4 %collective-permute-start.21 = (bf16[256,512]{1,0:T(8,128)(2,1)S(1)}, bf16[256,512]{1,0:T(8,128)(2,1)S(1)}, u32[]{:S(2)}, u32[]{:S(2)}) collective-permute-start(bf16[256,512]{1,0:T(8,128)(2,1)S(1)} %collective-permute-done.19.a_mine), channel_id=1, source_target_pairs={{0,1},{1,0},{2,3},{3,2},{4,5},{5,4},{6,7},{7,6},{8,9},{9,8},{10,11... | collective-permute-start | bytes 786440 | tf_op jit(solution)/shard_map/ppermute | solution.py:96
  151.3 4.0 %shard_map.58.refs_0_ = bf16[2048,3584]{1,0:T(8,128)(2,1)} custom-call(s32[2]{0:T(128)S(1)} %pad_add_fusion.where_ref, bf16[2048,256]{1,0:T(8,128)(2,1)S(1)} %bitcast.53, bf16[256,512]{1,0:T(8,128)(2,1)S(1)} %shard_map.57.b_mine, bf16[256,512]{1,0:T(8,128)(2,1)S(1)} %collective-permute-done.27.a_mine, bf16[256,512]{1,0:T(8,128)(2,1)S(1)} %collective-permute-done.29.b_far, ...), custom_call_target="tpu_custom_call" | custom-call | flops 1073741824 | bytes 4194304 | tf_op jit(solution)/shard_map/pallas_call | solution.py:270
  156.0 3.4 %collective-permute-start.17 = (bf16[256,256]{1,0:T(8,128)(2,1)S(1)}, bf16[256,256]{1,0:T(8,128)(2,1)S(1)}, u32[]{:S(2)}, u32[]{:S(2)}) collective-permute-start(bf16[256,256]{1,0:T(8,128)(2,1)S(1)} %collective-permute-done.15.a_mine), channel_id=1, source_target_pairs={{0,1},{1,0},{2,3},{3,2},{4,5},{5,4},{6,7},{7,6},{8,9},{9,8},{10,11... | collective-permute-start | bytes 393224 | tf_op jit(solution)/shard_map/ppermute | solution.py:96
  159.5 4.0 %shard_map.59.refs_0_ = bf16[2048,3584]{1,0:T(8,128)(2,1)} custom-call(s32[2]{0:T(128)S(1)} %pad_add_fusion.where_ref, bf16[2048,256]{1,0:T(8,128)(2,1)S(1)} %bitcast.54, bf16[256,512]{1,0:T(8,128)(2,1)S(1)} %shard_map.56.b_mine, bf16[256,512]{1,0:T(8,128)(2,1)S(1)} %collective-permute-done.23.a_mine, ...), custom_call_target="tpu_custom_call", output_to_operand_aliasing={{}: (6, {})} | custom-call | flops 1073741824 | bytes 4194304 | tf_op jit(solution)/shard_map/pallas_call | solution.py:270
  163.5 4.0 %shard_map.60.refs_0_ = bf16[2048,3584]{1,0:T(8,128)(2,1)} custom-call(s32[2]{0:T(128)S(1)} %pad_add_fusion.where_ref, bf16[2048,256]{1,0:T(8,128)(2,1)S(1)} %bitcast.55, bf16[256,512]{1,0:T(8,128)(2,1)S(1)} %shard_map.55.b_mine, bf16[256,512]{1,0:T(8,128)(2,1)S(1)} %collective-permute-done.19.a_mine, ...), custom_call_target="tpu_custom_call", output_to_operand_aliasing={{}: (6, {})} | custom-call | flops 1073741824 | bytes 4194304 | tf_op jit(solution)/shard_map/pallas_call | solution.py:270
  167.5 2.5 %shard_map.61 = bf16[2048,3584]{1,0:T(8,128)(2,1)} custom-call(s32[2]{0:T(128)S(1)} %pad_add_fusion.where_ref, bf16[2048,256]{1,0:T(8,128)(2,1)S(1)} %bitcast.56, bf16[256,256]{1,0:T(8,128)(2,1)S(1)} %shard_map.54.b_mine, bf16[256,256]{1,0:T(8,128)(2,1)S(1)} %collective-permute-done.15.a_mine, ...), custom_call_target="tpu_custom_call", output_to_operand_aliasing={{}: (6, {})} | custom-call | flops 536870912 | bytes 2097152 | tf_op jit(solution)/shard_map/pallas_call | solution.py:270
  (65 shorter events, 8.7 us)
Async XLA Ops:
  0.0 24.9 %copy-start.1 = (bf16[1,32,4096]{2,1,0:T(8,128)(2,1)S(1)}, bf16[1,32,4096]{2,1,0:T(8,128)(2,1)}, u32[]{:S(2)}) copy-start(bf16[1,32,4096]{2,1,0:T(8,128)(2,1)} %param.4) | copy-start | bytes 786436
  0.0 10.9 %collective-permute-start.1 = (bf16[32,4096]{1,0:T(8,128)(2,1)}, bf16[32,4096]{1,0:T(8,128)(2,1)S(1)}, u32[]{:S(2)}, u32[]{:S(2)}) collective-permute-start(bf16[32,4096]{1,0:T(8,128)(2,1)} %bitcast.69), channel_id=1, source_target_pairs={{0,4},{1,5},{2,6},{3,7},{4,8},{5,9},{6,10},{7,11},{8,12},{9,13},{1... | collective-permute-start | bytes 786440 | tf_op jit(solution)/shard_map/ppermute | solution.py:96
  5.1 9.9 %collective-permute-start = (bf16[32,4096]{1,0:T(8,128)(2,1)}, bf16[32,4096]{1,0:T(8,128)(2,1)S(1)}, u32[]{:S(2)}, u32[]{:S(2)}) collective-permute-start(bf16[32,4096]{1,0:T(8,128)(2,1)} %bitcast.70), channel_id=1, source_target_pairs={{4,0},{5,1},{6,2},{7,3},{8,4},{9,5},{10,6},{11,7},{12,8},{13,9},{1... | collective-permute-start | bytes 786440 | tf_op jit(solution)/shard_map/ppermute | solution.py:96
  15.0 9.9 %collective-permute-start.2 = (bf16[32,4096]{1,0:T(8,128)(2,1)S(1)}, bf16[32,4096]{1,0:T(8,128)(2,1)S(1)}, u32[]{:S(2)}, u32[]{:S(2)}) collective-permute-start(bf16[32,4096]{1,0:T(8,128)(2,1)S(1)} %broadcast_select_fusion), channel_id=1, source_target_pairs={{4,12},{5,13},{6,14},{7,15},{8,0},{9,1},{10,2},{11,3},{20,28},{21,... | collective-permute-start | bytes 786440 | tf_op jit(solution)/shard_map/ppermute | solution.py:96
  16.3 8.6 %collective-permute-start.3 = (bf16[32,4096]{1,0:T(8,128)(2,1)S(1)}, bf16[32,4096]{1,0:T(8,128)(2,1)S(1)}, u32[]{:S(2)}, u32[]{:S(2)}) collective-permute-start(bf16[32,4096]{1,0:T(8,128)(2,1)S(1)} %collective-permute-done.1), channel_id=1, source_target_pairs={{4,8},{5,9},{6,10},{7,11},{8,12},{9,13},{10,14},{11,15},{20,24},{2... | collective-permute-start | bytes 786440 | tf_op jit(solution)/shard_map/ppermute | solution.py:96
  17.0 13.3 %collective-permute-start.4 = (bf16[32,4096]{1,0:T(8,128)(2,1)S(1)}, bf16[32,4096]{1,0:T(8,128)(2,1)S(1)}, u32[]{:S(2)}, u32[]{:S(2)}) collective-permute-start(bf16[32,4096]{1,0:T(8,128)(2,1)S(1)} %collective-permute-done), channel_id=1, source_target_pairs={{4,0},{5,1},{6,2},{7,3},{8,4},{9,5},{10,6},{11,7},{20,16},{21,17},... | collective-permute-start | bytes 786440 | tf_op jit(solution)/shard_map/ppermute | solution.py:96
  25.0 6.4 %copy-start.2 = (s32[8192]{0:T(1024)S(1)}, s32[8192]{0:T(1024)}, u32[]{:S(2)}) copy-start(s32[8192]{0:T(1024)} %param.7) | copy-start | bytes 98308
  31.3 2.9 %collective-permute-start.5 = (bf16[4,32,4096]{2,1,0:T(8,128)(2,1)}, bf16[4,32,4096]{2,1,0:T(8,128)(2,1)S(1)}, u32[]{:S(2)}, u32[]{:S(2)}) collective-permute-start(bf16[4,32,4096]{2,1,0:T(8,128)(2,1)} %constant_dynamic-slice_fusion.2), channel_id=1, source_target_pairs={{0,2},{1,3},{2,0},{3,1},{4,6},{5,7},{6,4},{7,5},{8,10},{9,11},{10,... | collective-permute-start | bytes 3145736 | tf_op jit(solution)/shard_map/ppermute | solution.py:96
  52.8 20.5 %copy-start = (bf16[2,256,512]{2,1,0:T(8,128)(2,1)}, bf16[2,256,512]{2,1,0:T(8,128)(2,1)S(1)}, u32[]{:S(2)}) copy-start(bf16[2,256,512]{2,1,0:T(8,128)(2,1)S(1)} %shard_map.46.refs_0_) | copy-start | bytes 1572868
  69.8 15.9 %collective-permute-start.6 = (bf16[2,256,512]{2,1,0:T(8,128)(2,1)S(1)}, bf16[2,256,512]{2,1,0:T(8,128)(2,1)S(1)}, u32[]{:S(2)}, u32[]{:S(2)}) collective-permute-start(bf16[2,256,512]{2,1,0:T(8,128)(2,1)S(1)} %shard_map.52), channel_id=1, source_target_pairs={{0,1},{1,0},{2,3},{3,2},{4,5},{5,4},{6,7},{7,6},{8,9},{9,8},{10,11... | collective-permute-start | bytes 1572872 | tf_op jit(solution)/shard_map/ppermute | solution.py:96
  87.0 4.1 %collective-permute-start.7 = (bf16[256,256]{1,0:T(8,128)(2,1)}, bf16[256,256]{1,0:T(8,128)(2,1)S(1)}, u32[]{:S(2)}, u32[]{:S(2)}) collective-permute-start(bf16[256,256]{1,0:T(8,128)(2,1)} %slice.9), channel_id=1, source_target_pairs={{0,16},{1,17},{2,18},{3,19},{4,20},{5,21},{6,22},{7,23},{8,24},{9,... | collective-permute-start | bytes 393224 | tf_op jit(solution)/shard_map/ppermute | solution.py:96
  88.3 14.9 %collective-permute-start.26 = (bf16[2,256,512]{2,1,0:T(8,128)(2,1)}, bf16[2,256,512]{2,1,0:T(8,128)(2,1)S(1)}, u32[]{:S(2)}, u32[]{:S(2)}) collective-permute-start(bf16[2,256,512]{2,1,0:T(8,128)(2,1)} %copy-done), channel_id=1, source_target_pairs={{16,17},{17,16},{18,19},{19,18},{20,21},{21,20},{22,23},{23,22},{2... | collective-permute-start | bytes 1572872 | tf_op jit(solution)/shard_map/ppermute | solution.py:96
  91.2 5.0 %collective-permute-start.9 = (bf16[256,256]{1,0:T(8,128)(2,1)S(1)}, bf16[256,256]{1,0:T(8,128)(2,1)S(1)}, u32[]{:S(2)}, u32[]{:S(2)}) collective-permute-start(bf16[256,256]{1,0:T(8,128)(2,1)S(1)} %slice_select_fusion), channel_id=1, source_target_pairs={{0,4},{1,5},{2,6},{3,7},{4,8},{5,9},{6,10},{7,11},{8,12},{9,13},{1... | collective-permute-start | bytes 393224 | tf_op jit(solution)/shard_map/ppermute | solution.py:96
  93.6 6.9 %collective-permute-start.8 = (bf16[256,256]{1,0:T(8,128)(2,1)S(1)}, bf16[256,256]{1,0:T(8,128)(2,1)S(1)}, u32[]{:S(2)}, u32[]{:S(2)}) collective-permute-start(bf16[256,256]{1,0:T(8,128)(2,1)S(1)} %slice_select_fusion), channel_id=1, source_target_pairs={{4,0},{5,1},{6,2},{7,3},{8,4},{9,5},{10,6},{11,7},{12,8},{13,9},{1... | collective-permute-start | bytes 393224 | tf_op jit(solution)/shard_map/ppermute | solution.py:96
  100.5 7.8 %collective-permute-start.10 = (bf16[256,256]{1,0:T(8,128)(2,1)S(1)}, bf16[256,256]{1,0:T(8,128)(2,1)S(1)}, u32[]{:S(2)}, u32[]{:S(2)}) collective-permute-start(bf16[256,256]{1,0:T(8,128)(2,1)S(1)} %broadcast_select_fusion.1), channel_id=1, source_target_pairs={{4,12},{5,13},{6,14},{7,15},{8,0},{9,1},{10,2},{11,3},{20,28},{21,... | collective-permute-start | bytes 393224 | tf_op jit(solution)/shard_map/ppermute | solution.py:96
  101.8 15.0 %collective-permute-start.22 = (bf16[2,256,512]{2,1,0:T(8,128)(2,1)S(1)}, bf16[2,256,512]{2,1,0:T(8,128)(2,1)S(1)}, u32[]{:S(2)}, u32[]{:S(2)}) collective-permute-start(bf16[2,256,512]{2,1,0:T(8,128)(2,1)S(1)} %shard_map.47.refs_1_), channel_id=1, source_target_pairs={{16,17},{17,16},{18,19},{19,18},{20,21},{21,20},{22,23},{23,22},{2... | collective-permute-start | bytes 1572872 | tf_op jit(solution)/shard_map/ppermute | solution.py:96
  102.5 21.3 %collective-permute-start.18 = (bf16[2,256,512]{2,1,0:T(8,128)(2,1)S(1)}, bf16[2,256,512]{2,1,0:T(8,128)(2,1)S(1)}, u32[]{:S(2)}, u32[]{:S(2)}) collective-permute-start(bf16[2,256,512]{2,1,0:T(8,128)(2,1)S(1)} %shard_map.48.refs_2_), channel_id=1, source_target_pairs={{16,17},{17,16},{18,19},{19,18},{20,21},{21,20},{22,23},{23,22},{2... | collective-permute-start | bytes 1572872 | tf_op jit(solution)/shard_map/ppermute | solution.py:96
  103.8 14.9 %collective-permute-start.27 = (bf16[256,512]{1,0:T(8,128)(2,1)S(1)}, bf16[256,512]{1,0:T(8,128)(2,1)S(1)}, u32[]{:S(2)}, u32[]{:S(2)}) collective-permute-start(bf16[256,512]{1,0:T(8,128)(2,1)S(1)} %shard_map.57.b_mine), channel_id=1, source_target_pairs={{16,0},{17,1},{18,2},{19,3},{20,4},{21,5},{22,6},{23,7},{24,8},{25... | collective-permute-start | bytes 786440 | tf_op jit(solution)/shard_map/ppermute | solution.py:96
  105.1 4.5 %collective-permute-start.11 = (bf16[256,256]{1,0:T(8,128)(2,1)S(1)}, bf16[256,256]{1,0:T(8,128)(2,1)S(1)}, u32[]{:S(2)}, u32[]{:S(2)}) collective-permute-start(bf16[256,256]{1,0:T(8,128)(2,1)S(1)} %collective-permute-done.9), channel_id=1, source_target_pairs={{4,8},{5,9},{6,10},{7,11},{8,12},{9,13},{10,14},{11,15},{20,24},{2... | collective-permute-start | bytes 393224 | tf_op jit(solution)/shard_map/ppermute | solution.py:96
  108.3 7.7 %collective-permute-start.12 = (bf16[256,256]{1,0:T(8,128)(2,1)S(1)}, bf16[256,256]{1,0:T(8,128)(2,1)S(1)}, u32[]{:S(2)}, u32[]{:S(2)}) collective-permute-start(bf16[256,256]{1,0:T(8,128)(2,1)S(1)} %collective-permute-done.8), channel_id=1, source_target_pairs={{4,0},{5,1},{6,2},{7,3},{8,4},{9,5},{10,6},{11,7},{20,16},{21,17},... | collective-permute-start | bytes 393224 | tf_op jit(solution)/shard_map/ppermute | solution.py:96
  116.1 22.6 %collective-permute-start.13 = (bf16[4,256,256]{2,1,0:T(8,128)(2,1)S(1)}, bf16[4,256,256]{2,1,0:T(8,128)(2,1)S(1)}, u32[]{:S(2)}, u32[]{:S(2)}) collective-permute-start(bf16[4,256,256]{2,1,0:T(8,128)(2,1)S(1)} %constant_dynamic-slice_fusion), channel_id=1, source_target_pairs={{0,2},{1,3},{2,0},{3,1},{4,6},{5,7},{6,4},{7,5},{8,10},{9,11},{10,... | collective-permute-start | bytes 1572872 | tf_op jit(solution)/shard_map/ppermute | solution.py:96
  116.2 6.1 %collective-permute-start.14 = (bf16[2,256,256]{2,1,0:T(8,128)(2,1)S(1)}, bf16[2,256,256]{2,1,0:T(8,128)(2,1)S(1)}, u32[]{:S(2)}, u32[]{:S(2)}) collective-permute-start(bf16[2,256,256]{2,1,0:T(8,128)(2,1)S(1)} %shard_map.49.refs_3_), channel_id=1, source_target_pairs={{16,17},{17,16},{18,19},{19,18},{20,21},{21,20},{22,23},{23,22},{2... | collective-permute-start | bytes 786440 | tf_op jit(solution)/shard_map/ppermute | solution.py:96
  117.5 17.5 %collective-permute-start.23 = (bf16[256,512]{1,0:T(8,128)(2,1)S(1)}, bf16[256,512]{1,0:T(8,128)(2,1)S(1)}, u32[]{:S(2)}, u32[]{:S(2)}) collective-permute-start(bf16[256,512]{1,0:T(8,128)(2,1)S(1)} %shard_map.56.b_mine), channel_id=1, source_target_pairs={{16,0},{17,1},{18,2},{19,3},{20,4},{21,5},{22,6},{23,7},{24,8},{25... | collective-permute-start | bytes 786440 | tf_op jit(solution)/shard_map/ppermute | solution.py:96
  118.8 17.5 %collective-permute-start.28 = (bf16[256,512]{1,0:T(8,128)(2,1)S(1)}, bf16[256,512]{1,0:T(8,128)(2,1)S(1)}, u32[]{:S(2)}, u32[]{:S(2)}) collective-permute-start(bf16[256,512]{1,0:T(8,128)(2,1)S(1)} %collective-permute-done.27.a_mine), channel_id=1, source_target_pairs={{0,1},{1,0},{2,3},{3,2},{4,5},{5,4},{6,7},{7,6},{8,9},{9,8},{10,11... | collective-permute-start | bytes 786440 | tf_op jit(solution)/shard_map/ppermute | solution.py:96
  122.5 32.8 %collective-permute-start.15 = (bf16[256,256]{1,0:T(8,128)(2,1)S(1)}, bf16[256,256]{1,0:T(8,128)(2,1)S(1)}, u32[]{:S(2)}, u32[]{:S(2)}) collective-permute-start(bf16[256,256]{1,0:T(8,128)(2,1)S(1)} %shard_map.54.b_mine), channel_id=1, source_target_pairs={{16,0},{17,1},{18,2},{19,3},{20,4},{21,5},{22,6},{23,7},{24,8},{25... | collective-permute-start | bytes 393224 | tf_op jit(solution)/shard_map/ppermute | solution.py:96
  123.8 32.2 %collective-permute-start.24 = (bf16[256,512]{1,0:T(8,128)(2,1)S(1)}, bf16[256,512]{1,0:T(8,128)(2,1)S(1)}, u32[]{:S(2)}, u32[]{:S(2)}) collective-permute-start(bf16[256,512]{1,0:T(8,128)(2,1)S(1)} %shard_map.56.b_mine), channel_id=1, source_target_pairs={{16,17},{17,16},{18,19},{19,18},{20,21},{21,20},{22,23},{23,22},{2... | collective-permute-start | bytes 786440 | tf_op jit(solution)/shard_map/ppermute | solution.py:96
  135.0 11.8 %collective-permute-start.19 = (bf16[256,512]{1,0:T(8,128)(2,1)S(1)}, bf16[256,512]{1,0:T(8,128)(2,1)S(1)}, u32[]{:S(2)}, u32[]{:S(2)}) collective-permute-start(bf16[256,512]{1,0:T(8,128)(2,1)S(1)} %shard_map.55.b_mine), channel_id=1, source_target_pairs={{16,0},{17,1},{18,2},{19,3},{20,4},{21,5},{22,6},{23,7},{24,8},{25... | collective-permute-start | bytes 786440 | tf_op jit(solution)/shard_map/ppermute | solution.py:96
  136.3 23.2 %collective-permute-start.25 = (bf16[256,512]{1,0:T(8,128)(2,1)S(1)}, bf16[256,512]{1,0:T(8,128)(2,1)S(1)}, u32[]{:S(2)}, u32[]{:S(2)}) collective-permute-start(bf16[256,512]{1,0:T(8,128)(2,1)S(1)} %collective-permute-done.23.a_mine), channel_id=1, source_target_pairs={{0,1},{1,0},{2,3},{3,2},{4,5},{5,4},{6,7},{7,6},{8,9},{9,8},{10,11... | collective-permute-start | bytes 786440 | tf_op jit(solution)/shard_map/ppermute | solution.py:96
  138.7 10.0 %collective-permute-start.29 = (bf16[256,512]{1,0:T(8,128)(2,1)S(1)}, bf16[256,512]{1,0:T(8,128)(2,1)S(1)}, u32[]{:S(2)}, u32[]{:S(2)}) collective-permute-start(bf16[256,512]{1,0:T(8,128)(2,1)S(1)} %collective-permute-done.28.a_far), channel_id=1, source_target_pairs={{0,16},{1,17},{2,18},{3,19},{4,20},{5,21},{6,22},{7,23},{8,24},{9,... | collective-permute-start | bytes 786440 | tf_op jit(solution)/shard_map/ppermute | solution.py:96
  146.8 16.7 %collective-permute-start.20 = (bf16[256,512]{1,0:T(8,128)(2,1)S(1)}, bf16[256,512]{1,0:T(8,128)(2,1)S(1)}, u32[]{:S(2)}, u32[]{:S(2)}) collective-permute-start(bf16[256,512]{1,0:T(8,128)(2,1)S(1)} %shard_map.55.b_mine), channel_id=1, source_target_pairs={{16,17},{17,16},{18,19},{19,18},{20,21},{21,20},{22,23},{23,22},{2... | collective-permute-start | bytes 786440 | tf_op jit(solution)/shard_map/ppermute | solution.py:96
  148.7 14.8 %collective-permute-start.21 = (bf16[256,512]{1,0:T(8,128)(2,1)S(1)}, bf16[256,512]{1,0:T(8,128)(2,1)S(1)}, u32[]{:S(2)}, u32[]{:S(2)}) collective-permute-start(bf16[256,512]{1,0:T(8,128)(2,1)S(1)} %collective-permute-done.19.a_mine), channel_id=1, source_target_pairs={{0,1},{1,0},{2,3},{3,2},{4,5},{5,4},{6,7},{7,6},{8,9},{9,8},{10,11... | collective-permute-start | bytes 786440 | tf_op jit(solution)/shard_map/ppermute | solution.py:96
  155.3 12.2 %collective-permute-start.16 = (bf16[256,256]{1,0:T(8,128)(2,1)S(1)}, bf16[256,256]{1,0:T(8,128)(2,1)S(1)}, u32[]{:S(2)}, u32[]{:S(2)}) collective-permute-start(bf16[256,256]{1,0:T(8,128)(2,1)S(1)} %shard_map.54.b_mine), channel_id=1, source_target_pairs={{16,17},{17,16},{18,19},{19,18},{20,21},{21,20},{22,23},{23,22},{2... | collective-permute-start | bytes 393224 | tf_op jit(solution)/shard_map/ppermute | solution.py:96
  156.0 11.5 %collective-permute-start.17 = (bf16[256,256]{1,0:T(8,128)(2,1)S(1)}, bf16[256,256]{1,0:T(8,128)(2,1)S(1)}, u32[]{:S(2)}, u32[]{:S(2)}) collective-permute-start(bf16[256,256]{1,0:T(8,128)(2,1)S(1)} %collective-permute-done.15.a_mine), channel_id=1, source_target_pairs={{0,1},{1,0},{2,3},{3,2},{4,5},{5,4},{6,7},{7,6},{8,9},{9,8},{10,11... | collective-permute-start | bytes 393224 | tf_op jit(solution)/shard_map/ppermute | solution.py:96

commit v2 on v0

--- a/solution.py
+++ b/solution.py
@@ -1,11 +1,16 @@
+import functools
 import math
 
 import jax
 import jax.numpy as jnp
 from jax import lax
+from jax.experimental import pallas as pl
+from jax.experimental.pallas import tpu as pltpu
 from jax.sharding import PartitionSpec as P
 
 epsilon = 1e-05
+AXES = ("mp", "dp", "tensor")
+MIB = 1 << 20
 
 
 def from_partner(block, axis, distance):
@@ -27,7 +32,7 @@
     )
 
 
-def body(acts, gate_w, up_w, panel_units):
+def general_body(acts, gate_w, up_w, panel_units):
     model_index = lax.axis_index("mp")
     unit_block = lax.axis_index("dp")
     n_model = lax.axis_size("mp")
@@ -74,7 +79,479 @@
     return (result * score_scale).astype(jnp.bfloat16)
 
 
+CHIPS = 4
+
+
+def routes(sizes, move):
+    n_model, n_data, n_width = sizes
+    pairs = []
+    for m in range(n_model):
+        for d in range(n_data):
+            for t in range(n_width):
+                to = move(m, d, t)
+                if to is not None:
+                    source = (m * n_data + d) * n_width + t
+                    pairs.append((source, (to[0] * n_data + to[1]) * n_width + to[2]))
+    return pairs
+
+
+def send(block, sizes, move):
+    return lax.ppermute(block, AXES, routes(sizes, move))
+
+
+def other_core(m, d, t):
+    return m, d ^ 1, t
+
+
+def shifted(step):
+    def move(m, d, t):
+        return m, (d + 2 * step) % (2 * CHIPS), t
+
+    return move
+
+
+def shifts(block, sizes):
+    came = [send(block, sizes, shifted(step)) for step in (1, CHIPS - 1, 2)]
+    return [block, came[0], came[2], came[1]]
+
+
+def gather_line(block, sizes):
+    return jnp.concatenate(shifts(block, sizes), axis=0)
+
+
+def join_kernel(*refs):
+    rows = refs[0].shape[0]
+    for i in range(CHIPS):
+        refs[-1][i * rows : (i + 1) * rows, :] = refs[i][...]
+
+
+def join(blocks, after):
+    rows, width = blocks[0].shape
+    vmem = pl.BlockSpec(memory_space=pltpu.VMEM)
+    return call(
+        join_kernel,
+        out_shape=jax.ShapeDtypeStruct((CHIPS * rows, width), blocks[0].dtype),
+        in_specs=[vmem] * CHIPS + [pl.BlockSpec(memory_space=pl.ANY)] * len(after),
+        out_specs=vmem,
+        flops=0,
+        moved=4 * CHIPS * rows * width,
+        vmem=16,
+    )(*blocks, *after)
+
+
+def canonical(index, chip, core):
+    line = lax.rem(chip + CHIPS - index % CHIPS, CHIPS)
+    return line * 2 + (core if index < CHIPS else 1 - core)
+
+
+def call(kernel, *, flops, moved, vmem, **rest):
+    return pl.pallas_call(
+        kernel,
+        compiler_params=pltpu.CompilerParams(vmem_limit_bytes=vmem * MIB),
+        cost_estimate=pl.CostEstimate(flops=flops, bytes_accessed=moved, transcendentals=0),
+        **rest,
+    )
+
+
+def early_kernel(place_ref, same_ref, other_ref, gate_ref, up_ref, out_ref):
+    x = jnp.concatenate([same_ref[...], other_ref[...]], axis=0)
+    out_ref[0] = jnp.dot(x, gate_ref[...], preferred_element_type=jnp.float32)
+    out_ref[1] = jnp.dot(x, up_ref[...], preferred_element_type=jnp.float32)
+
+
+def early_products(place, same, other, gate, up, tile, count):
+    tokens, width = 2 * same.shape[0], same.shape[1]
+    weights = pl.BlockSpec((width, tile), lambda i, place_ref: (0, place_ref[0] + i))
+    whole = pl.BlockSpec(same.shape, lambda i, place_ref: (0, 0))
+    return call(
+        early_kernel,
+        out_shape=jax.ShapeDtypeStruct((2, tokens, tile * count), jnp.float32),
+        grid_spec=pltpu.PrefetchScalarGridSpec(
+            num_scalar_prefetch=1,
+            grid=(count,),
+            in_specs=[whole, whole, weights, weights],
+            out_specs=pl.BlockSpec((2, tokens, tile), lambda i, place_ref: (0, 0, i)),
+        ),
+        flops=4 * tokens * width * tile * count,
+        moved=4 * width * tile * count,
+        vmem=32,
+    )(place, same, other, gate, up)
+
+
+def store_sorted(place_ref, out_ref, which, total):
+    rows = total.shape[0] // (2 * CHIPS)
+    total = total.astype(jnp.bfloat16)
+    for i in range(2 * CHIPS):
+        start = pl.multiple_of(canonical(i, place_ref[1], place_ref[2]) * rows, rows)
+        out_ref[which, pl.ds(start, rows), :] = total[i * rows : (i + 1) * rows]
+
+
+def late_kernel(place_ref, early_ref, same_ref, other_ref, gate_ref, up_ref, *refs):
+    x = jnp.concatenate([same_ref[...], other_ref[...]], axis=0)
+    for which, weight_ref in enumerate((gate_ref, up_ref)):
+        total = jnp.dot(x, weight_ref[...], preferred_element_type=jnp.float32)
+        store_sorted(place_ref, refs[-1], which, early_ref[which] + total)
+
+
+def late_products(place, early, same, other, gate, up, tile, first, count, after):
+    tokens, width = 2 * same.shape[0], same.shape[1]
+    weights = pl.BlockSpec((width, tile), lambda i, place_ref: (1, place_ref[0] + first + i))
+    whole = pl.BlockSpec(same.shape, lambda i, place_ref: (0, 0))
+    return call(
+        late_kernel,
+        out_shape=jax.ShapeDtypeStruct((2, tokens, tile * count), jnp.bfloat16),
+        grid_spec=pltpu.PrefetchScalarGridSpec(
+            num_scalar_prefetch=1,
+            grid=(count,),
+            in_specs=[
+                pl.BlockSpec((2, tokens, tile), lambda i, place_ref: (0, 0, first + i)),
+                whole,
+                whole,
+                weights,
+                weights,
+            ]
+            + [pl.BlockSpec(memory_space=pl.ANY)] * len(after),
+            out_specs=pl.BlockSpec((2, tokens, tile), lambda i, place_ref: (0, 0, i)),
+        ),
+        flops=4 * tokens * width * tile * count,
+        moved=4 * width * tile * count,
+        vmem=32,
+    )(place, early, same, other, gate, up, *after)
+
+
+KEPT_PARTS = 2
+KEPT_STEPS = 2
+
+
+def kept_kernel(place_ref, same_a, other_a, same_b, other_b, gate_ref, up_ref, *refs):
+    out_ref, total_ref = refs[-2:]
+    step = pl.program_id(1)
+    depth = gate_ref.shape[0]
+    for at in range(2 * KEPT_STEPS):
+        same_ref, other_ref = ((same_a, other_a), (same_b, other_b))[at // KEPT_STEPS]
+        start = at % KEPT_STEPS * depth
+
+        @pl.when(step == at)
+        def _():
+            x = jnp.concatenate(
+                [same_ref[:, start : start + depth], other_ref[:, start : start + depth]], axis=0
+            )
+            for which, weight_ref in enumerate((gate_ref, up_ref)):
+                total = jnp.dot(x, weight_ref[...], preferred_element_type=jnp.float32)
+                if at:
+                    total += total_ref[which]
+                if at < 2 * KEPT_STEPS - 1:
+                    total_ref[which] = total
+                else:
+                    store_sorted(place_ref, out_ref, which, total)
+
+
+def kept_products(place, same, other, gate, up, after):
+    tokens, width = 2 * same[0].shape[0], same[0].shape[1]
+    units = gate.shape[1] // 2
+    part, depth = units // KEPT_PARTS, width // KEPT_STEPS
+    weights = pl.BlockSpec((depth, part), lambda i, k, place_ref: (k, place_ref[3] * KEPT_PARTS + i))
+    whole = pl.BlockSpec(same[0].shape, lambda i, k, place_ref: (0, 0))
+    return call(
+        kept_kernel,
+        out_shape=jax.ShapeDtypeStruct((2, tokens, units), jnp.bfloat16),
+        grid_spec=pltpu.PrefetchScalarGridSpec(
+            num_scalar_prefetch=1,
+            grid=(KEPT_PARTS, 2 * KEPT_STEPS),
+            in_specs=[whole] * 4
+            + [weights, weights]
+            + [pl.BlockSpec(memory_space=pl.ANY)] * len(after),
+            out_specs=pl.BlockSpec((2, tokens, part), lambda i, k, place_ref: (0, 0, i)),
+            scratch_shapes=[pltpu.VMEM((2, tokens, part), jnp.float32)],
+        ),
+        flops=8 * tokens * width * units,
+        moved=8 * width * units,
+        vmem=40,
+    )(place, same[0], other[0], same[1], other[1], gate, up, *after)
+
+
+def pick_kernel(counts, tile, has_instead, bases_ref, picks_ref, *refs):
+    out_ref = refs[-1]
+    tokens, picked = out_ref.shape[1:]
+
+    @pl.when(bases_ref[len(counts)] == 0)
+    def _():
+        total = jnp.zeros((2 * tokens, picked), jnp.float32)
+        for part, (ref, count) in enumerate(zip(refs[: len(counts)], counts)):
+            for i in range(count):
+                base = bases_ref[part] + i * tile
+                unit = lax.broadcasted_iota(jnp.int32, (tile, picked), 0) + base
+                chosen = jnp.where(unit == picks_ref[...], 1.0, 0.0).astype(jnp.bfloat16)
+                block = ref[:, :, i * tile : (i + 1) * tile].reshape(2 * tokens, tile)
+                total += jnp.dot(block, chosen, preferred_element_type=jnp.float32)
+        out_ref[...] = total.astype(jnp.bfloat16).reshape(2, tokens, picked)
+
+    @pl.when(bases_ref[len(counts)] == 1)
+    def _():
+        out_ref[...] = refs[len(counts)][...] if has_instead else jnp.zeros_like(out_ref)
+
+
+def pick(bases, picks, parts, instead, tile, after):
+    tokens = parts[0].shape[1]
+    picked = picks.shape[1]
+    counts = [part.shape[2] // tile for part in parts]
+    vmem = pl.BlockSpec(memory_space=pltpu.VMEM)
+    return call(
+        functools.partial(pick_kernel, counts, tile, len(instead)),
+        out_shape=jax.ShapeDtypeStruct((2, tokens, picked), jnp.bfloat16),
+        in_specs=[pl.BlockSpec(memory_space=pltpu.SMEM), vmem]
+        + [vmem] * len(parts + instead)
+        + [pl.BlockSpec(memory_space=pl.ANY)] * len(after),
+        out_specs=vmem,
+        flops=4 * tokens * picked * tile * sum(counts),
+        moved=4 * tokens * tile * sum(counts),
+        vmem=32,
+    )(bases, picks, *parts, *instead, *after)
+
+
+def zscore(mine, theirs):
+    tokens = mine.shape[1]
+    gate = mine[0].astype(jnp.float32) + theirs[0].astype(jnp.float32)
+    up = mine[1].astype(jnp.float32) + theirs[1].astype(jnp.float32)
+    hidden = (gate / (1.0 + jnp.exp(-gate)) * up).astype(jnp.bfloat16).astype(jnp.float32)
+    mean = jnp.sum(hidden, axis=0, keepdims=True) / tokens
+    var = jnp.sum(hidden * hidden, axis=0, keepdims=True) / tokens - mean * mean
+    return (hidden - mean) * lax.rsqrt(var + epsilon)
+
+
+def unit_kernel(bounds, mine_ref, *refs):
+    out_ref = refs[-1]
+    for (start, stop), theirs_ref in zip(bounds, refs):
+        out_ref[:, start - bounds[0][0] : stop - bounds[0][0]] = zscore(
+            mine_ref[:, :, start:stop], theirs_ref[...]
+        ).astype(jnp.bfloat16)
+
+
+def unit_scores(mine, theirs, start):
+    tokens = mine.shape[1]
+    bounds = []
+    for part in theirs:
+        bounds.append((start, start + part.shape[2]))
+        start = bounds[-1][1]
+    count = start - bounds[0][0]
+    vmem = pl.BlockSpec(memory_space=pltpu.VMEM)
+    return call(
+        functools.partial(unit_kernel, bounds),
+        out_shape=jax.ShapeDtypeStruct((tokens, count), jnp.bfloat16),
+        in_specs=[vmem] * (1 + len(theirs)),
+        out_specs=vmem,
+        flops=20 * tokens * count,
+        moved=10 * tokens * count,
+        vmem=32,
+    )(mine, *theirs)
+
+
+def panel_kernel(mine_ref, theirs_ref, out_ref):
+    out_ref[...] = zscore(mine_ref[...], theirs_ref[...]).T.astype(jnp.bfloat16)
+
+
+def panel_scores(mine, theirs, first):
+    _, tokens, count = theirs.shape
+    return call(
+        panel_kernel,
+        out_shape=jax.ShapeDtypeStruct((count, tokens), jnp.bfloat16),
+        grid=(1,),
+        in_specs=[
+            pl.BlockSpec((2, tokens, count), lambda i: (0, 0, first)),
+            pl.BlockSpec((2, tokens, count), lambda i: (0, 0, 0)),
+        ],
+        out_specs=pl.BlockSpec((count, tokens), lambda i: (0, 0)),
+        flops=20 * tokens * count,
+        moved=10 * tokens * count,
+        vmem=16,
+    )(mine, theirs)
+
+
+def score_kernel(scale, n_pieces, has_before, where_ref, same_ref, other_ref, *refs):
+    pieces = refs[: 4 * n_pieces]
+    out_ref, near_ref, far_ref, block_ref, sems = refs[4 * n_pieces + has_before :]
+    model, chip, core, near_column, far_column = (where_ref[i] for i in range(5))
+    rows = same_ref.shape[0] // CHIPS
+    columns = near_ref.shape[1]
+
+    def assemble(at, into):
+        start = 0
+        for piece in range(n_pieces):
+            ref = pieces[4 * piece + at]
+            into[:, start : start + ref.shape[1]] = ref[...]
+            start += ref.shape[1]
+
+    for holder in range(2):
+
+        @pl.when(model == holder)
+        def _():
+            assemble(2 * holder, near_ref)
+            assemble(2 * holder + 1, far_ref)
+
+    def copy(slot, row, column):
+        return pltpu.make_async_copy(
+            block_ref.at[slot],
+            out_ref.at[
+                pl.ds(pl.multiple_of(row, rows), rows), pl.ds(pl.multiple_of(column, 128), columns)
+            ],
+            sems.at[slot],
+        )
+
+    def step(index, carry):
+        line = lax.rem(chip + CHIPS - index, CHIPS)
+        for which, panel_ref in enumerate((same_ref, other_ref)):
+            panel = panel_ref[pl.ds(pl.multiple_of(index * rows, rows), rows), :]
+            row = (line * 2 + (1 - core if which else core)) * rows
+            for far, units_ref in enumerate((near_ref, far_ref)):
+                slot = 2 * which + far
+                column = far_column if far else near_column
+
+                @pl.when(index > 0)
+                def _():
+                    copy(slot, row, column).wait()
+
+                total = jnp.dot(panel, units_ref[...], preferred_element_type=jnp.float32)
+                block_ref[slot] = (total * scale).astype(jnp.bfloat16)
+                copy(slot, row, column).start()
+        return carry
+
+    lax.fori_loop(0, CHIPS, step, 0)
+    for slot in range(4):
+        copy(slot, 0, 0).wait()
+
+
+def scores(where, same, other, pieces, tile, first, half, before):
+    tokens = same.shape[1]
+    rows = same.shape[0] // CHIPS
+    columns = sum(piece[0].shape[1] for piece in pieces)
+    model, chip, core, side = where
+    near = (side * half + first) * tile
+    far = ((1 - side) * half + first) * tile
+    where = jnp.stack([model, chip, core, near, far]).astype(jnp.int32)
+    vmem = pl.BlockSpec(memory_space=pltpu.VMEM)
+    anywhere = pl.BlockSpec(memory_space=pl.ANY)
+    flat = [array for piece in pieces for array in piece]
+    return call(
+        functools.partial(score_kernel, 1.0 / math.sqrt(tokens), len(pieces), len(before)),
+        out_shape=jax.ShapeDtypeStruct((2 * CHIPS * rows, 2 * half * tile), jnp.bfloat16),
+        in_specs=[pl.BlockSpec(memory_space=pltpu.SMEM), vmem, vmem]
+        + [vmem] * len(flat)
+        + [anywhere] * len(before),
+        out_specs=anywhere,
+        scratch_shapes=[
+            pltpu.VMEM((tokens, columns), jnp.bfloat16),
+            pltpu.VMEM((tokens, columns), jnp.bfloat16),
+            pltpu.VMEM((4, rows, columns), jnp.bfloat16),
+            pltpu.SemaphoreType.DMA((4,)),
+        ],
+        input_output_aliases={3 + len(flat): 0} if before else {},
+        flops=8 * CHIPS * rows * tokens * columns,
+        moved=8 * CHIPS * rows * columns,
+        vmem=32,
+    )(where, same, other, *flat, *before)
+
+
+def paired_body(acts, gate_w, up_w, panel_units):
+    model = lax.axis_index("mp")
+    block = lax.axis_index("dp")
+    side = lax.axis_index("tensor")
+    sizes = tuple(lax.axis_size(name) for name in AXES)
+    chip, core = block // 2, block % 2
+    gate, up = gate_w[0], up_w[0]
+    units = gate.shape[1]
+    picks = panel_units.reshape(2, 2, sizes[1], -1)
+    tile = picks.shape[3]
+    half = units // 2 // tile
+    large = (half - 1) // 2
+    chunks = [large, half - 2 - large, 1, 1]
+    starts = [0, large, half - 2, half - 1]
+
+    def b_sides(m, d, t):
+        return (m, d, 1 - t) if m == 1 else None
+
+    def both_sides(m, d, t):
+        return m, d, 1 - t
+
+    def a_sides(m, d, t):
+        return (m, d, 1 - t) if m == 0 else None
+
+    def b_to_a(m, d, t):
+        return (0, d, t) if m == 1 else None
+
+    def b_to_far_a(m, d, t):
+        return (0, d, 1 - t) if m == 1 else None
+
+    def a_to_b(m, d, t):
+        return (1, d, t) if m == 0 else None
+
+    middle = acts.shape[2] // 2
+    same = [gather_line(acts[0][:, :middle], sizes)]
+    other = [send(same[0], sizes, other_core)]
+    last = shifts(acts[0][:, middle:], sizes)
+
+    to_side = jnp.stack([(1 - side) * half, chip, core]).astype(jnp.int32)
+    own_side = jnp.stack([side * half, chip, core, side]).astype(jnp.int32)
+    early = early_products(to_side, same[0], other[0], gate, up, tile, half)
+    same.append(join(last, [early]))
+    other.append(send(same[1], sizes, other_core))
+    sent = []
+    for first, count in zip(starts, chunks):
+        sent.append(
+            late_products(
+                to_side, early, same[1], other[1], gate, up, tile, first, count, sent[-1:]
+            )
+        )
+    kept = kept_products(own_side, same, other, gate, up, sent[-1:])
+
+    picks = lax.dynamic_index_in_dim(picks, block, axis=2, keepdims=False) - block * units
+    picks_far = lax.dynamic_index_in_dim(picks, 1 - side, axis=1, keepdims=False)
+    picks_own = lax.dynamic_index_in_dim(picks, side, axis=1, keepdims=False).reshape(1, -1)
+    bases = [(to_side[0] + first) * tile for first in starts] + [own_side[0] * tile, model]
+    bases = jnp.stack(bases).astype(jnp.int32)
+    parts = sent + [kept]
+    shared_b = pick(bases, picks_far[1:], parts, sent[2:3], tile, [])
+    shared_a = pick(bases, picks_far[:1], parts, sent[3:], tile, [shared_b])
+    picked_own = pick(bases, picks_own, parts, [], tile, [shared_a])
+    came = [send(part, sizes, b_sides) for part in sent[:2]]
+    came += [send(part, sizes, both_sides) for part in (shared_b, shared_a)]
+
+    rows_b = send(panel_scores(picked_own, came[2], 1), sizes, a_to_b)
+    rows_a = panel_scores(picked_own, came[3], 0)
+    panel = gather_line(jnp.where(model == 0, rows_a, rows_b), sizes)
+    panel_other = send(panel, sizes, other_core)
+
+    z = unit_scores(kept, came[:1], 0)
+    a_mine = send(z, sizes, b_to_a)
+    a_far = send(a_mine, sizes, a_sides)
+    pieces = [(a_mine, a_far, z, send(a_far, sizes, a_to_b))]
+
+    z = unit_scores(kept, came[1:3], starts[1] * tile)
+    a_mine = send(z, sizes, b_to_a)
+    far = send(jnp.where(model == 0, a_mine, z), sizes, both_sides)
+    pieces.append((a_mine, far, z, far))
+
+    z = unit_scores(kept, came[3:], starts[3] * tile)
+    pieces.append(
+        (send(z, sizes, b_to_a), send(z, sizes, b_to_far_a), z, send(z, sizes, b_sides))
+    )
+
+    where = (model, chip, core, side)
+    result = scores(where, panel, panel_other, pieces[:1], tile, 0, half, [])
+    return scores(where, panel, panel_other, pieces[1:], tile, starts[1], half, [result])
+
+
 def solution(mesh):
     in_specs = (P("mp", "dp", "tensor"), P("mp", "tensor", "dp"), P("mp", "tensor", "dp"), P())
     out_specs = P(("mp", "tensor"), "dp")
+    paired = mesh.shape["mp"] == 2 and mesh.shape["tensor"] == 2 and mesh.shape["dp"] == 2 * CHIPS
+
+    def body(acts, gate_w, up_w, panel_units):
+        picked = panel_units.shape[0] // (4 * 2 * CHIPS)
+        units = gate_w.shape[2]
+        fits = picked % 128 == 0 and units % (2 * picked) == 0 and units % 512 == 0
+        fits = fits and units >= 8 * picked and acts.shape[2] % 512 == 0
+        if paired and fits and acts.shape[1] % 16 == 0:
+            return paired_body(acts, gate_w, up_w, panel_units)
+        return general_body(acts, gate_w, up_w, panel_units)
+
     return jax.shard_map(body, mesh=mesh, in_specs=in_specs, out_specs=out_specs, check_vma=False)

time: 250 us -> 138 us (0.55)
  waiting for transfers between devices: 155 us -> 22.3 us
  Pallas kernels: 0 us -> 65.3 us
  matrix products: 42.9 us -> 0 us
  starting transfers between devices: 2.86 us -> 39.5 us
  blocking collectives: 17.8 us -> 0 us
  between operations: 13.3 us -> 0.57 us
  other arithmetic: 6.05 us -> 1.05 us
  local copies, waits for them, and re-layouts: 12 us -> 8.2 us
    all_gather x3 -> x0, waiting for transfers between devices: 80.8 us -> none  [the longest x1 33.5 us: body(): gathered = lax.all_gather(acts[0], 'dp', axis=0, tiled=True)]
    pallas_call x0 -> x17, Pallas kernels: none -> 65.3 us  [the longest x1 15.8 us: kept_products(): call(kept_kernel, out_shape=jax.ShapeDtypeStruct((2, tokens, units), jnp....]
    reduce_scatter x1 -> x0, waiting for transfers between devices: 48.7 us -> none  [body(): lax.psum_scatter(jnp.concatenate([gate_part, up_part], axis=1).astype(jnp...]
    dot_general x3 -> x0, matrix products: 42.9 us -> none  [the longest x1 17.8 us: body(): up_part = jnp.dot(gathered, weight_up, preferred_element_type=jnp.float32)]
    ppermute x2 -> x25, starting transfers between devices: 2.74 us -> 39.5 us  [send(): return lax.ppermute(block, AXES, routes(sizes, move))]
    all_to_all x1 -> x0, blocking collectives: 10.6 us -> none  [body(): lax.all_to_all(chosen, 'tensor', split_axis=1, concat_axis=0, tiled=True)]
    psum x1 -> x0, blocking collectives: 7.16 us -> none  [body(): lax.psum((jnp.sum(wide_hidden, axis=0), jnp.sum(wide_hidden * wide_hidden...]
    unnamed x6 -> x26, local copies, waits for them, and re-layouts: 0.62 us -> 6.93 us
  transfers between devices with their start and end apart: 6 -> 25, of which waited for: 6 -> 9; matrix products, arithmetic and copies ran while one was open for 5% -> 1% of each run, Pallas kernels for 0% -> 39%
where the time goes in v2:
time: 138 us; the launch traced here: 137 us
  Pallas kernels  65.3 us (47%)
  starting transfers between devices  39.5 us (29%)
  waiting for transfers between devices  22.3 us (16%)
  local copies, waits for them, and re-layouts  8.2 us (6%)
    ppermute x25, starting transfers between devices, send(): return lax.ppermute(block, AXES, routes(sizes, move))  39.5 us
    ppermute x25, waiting for transfers between devices, send(): return lax.ppermute(block, AXES, routes(sizes, move))  22.3 us
    pallas_call x1, Pallas kernels, kept_products(): call(kept_kernel, out_shape=jax.ShapeDtypeStruct((2, tokens, units), jnp....  15.8 us
    pallas_call x4, Pallas kernels, late_products(): call(late_kernel, out_shape=jax.ShapeDtypeStruct((2, tokens, tile * count...  14.7 us
    pallas_call x2, Pallas kernels, scores(): call(functools.partial(score_kernel, 1.0 / math.sqrt(tokens), len(pieces)...  14.2 us
    pallas_call x1, Pallas kernels, early_products(): call(early_kernel, out_shape=jax.ShapeDtypeStruct((2, tokens, tile * coun...  9.88 us
    unnamed x26, local copies, waits for them, and re-layouts  6.93 us
    pallas_call x3, Pallas kernels, pick(): call(functools.partial(pick_kernel, counts, tile, len(instead)), out_shap...  6.83 us
  transfers between devices with their start and end apart: 25, of which 9 were waited for; matrix products, arithmetic and copies ran while one was open for 1% of the time, Pallas kernels for 39%

profile of v2, /device:TPU:0, one launch (start us, length us, event | category | flops | bytes accessed | tf_op | source)
XLA Modules:
  0.0 136.9 jit_solution(12103385651797637790)
XLA Ops:
  0.0 1.0 fusion
  1.0 5.1 %collective-permute-start.2 = (bf16[32,2048]{1,0:T(8,128)(2,1)S(1)}, bf16[32,2048]{1,0:T(8,128)(2,1)S(1)}, u32[]{:S(2)}, u32[]{:S(2)}) collective-permute-start(bf16[32,2048]{1,0:T(8,128)(2,1)S(1)} %get-tuple-element.6), channel_id=1, source_target_pairs={{0,12},{1,13},{2,14},{3,15},{4,0},{5,1},{6,2},{7,3},{8,4},{9,5},{1... | collective-permute-start | bytes 393224 | tf_op jit(solution)/shard_map/ppermute | solution.py:99
  6.1 1.0 collective-permute-start
  7.1 2.9 %collective-permute-done.2 = bf16[32,2048]{1,0:T(8,128)(2,1)S(1)} collective-permute-done((bf16[32,2048]{1,0:T(8,128)(2,1)S(1)}, bf16[32,2048]{1,0:T(8,128)(2,1)S(1)}, u32[]{:S(2)}, u32[]{:S(2)}) %collective-permute-start.2) | collective-permute-done | bytes 131104 | tf_op jit(solution)/shard_map/ppermute | solution.py:99
  10.0 7.3 %collective-permute-done.1 = bf16[32,2048]{1,0:T(8,128)(2,1)S(1)} collective-permute-done((bf16[32,2048]{1,0:T(8,128)(2,1)S(1)}, bf16[32,2048]{1,0:T(8,128)(2,1)S(1)}, u32[]{:S(2)}, u32[]{:S(2)}) %collective-permute-start.1) | collective-permute-done | bytes 131104 | tf_op jit(solution)/shard_map/ppermute | solution.py:99
  17.4 1.7 %collective-permute-start.6 = (bf16[32,2048]{1,0:T(8,128)(2,1)S(1)}, bf16[32,2048]{1,0:T(8,128)(2,1)S(1)}, u32[]{:S(2)}, u32[]{:S(2)}) collective-permute-start(bf16[32,2048]{1,0:T(8,128)(2,1)S(1)} %get-tuple-element.5.refs_0_), channel_id=1, source_target_pairs={{0,12},{1,13},{2,14},{3,15},{4,0},{5,1},{6,2},{7,3},{8,4},{9,5},{1... | collective-permute-start | bytes 393224 | tf_op jit(solution)/shard_map/ppermute | solution.py:99
  19.1 1.1 collective-permute-start.5
  20.2 1.9 %collective-permute-start.4 = (bf16[32,2048]{1,0:T(8,128)(2,1)S(1)}, bf16[32,2048]{1,0:T(8,128)(2,1)S(1)}, u32[]{:S(2)}, u32[]{:S(2)}) collective-permute-start(bf16[32,2048]{1,0:T(8,128)(2,1)S(1)} %get-tuple-element.5.refs_0_), channel_id=1, source_target_pairs={{0,4},{1,5},{2,6},{3,7},{4,8},{5,9},{6,10},{7,11},{8,12},{9,13},{1... | collective-permute-start | bytes 393224 | tf_op jit(solution)/shard_map/ppermute | solution.py:99
  22.2 9.9 %shard_map.46.refs_4_.early_ref = f32[2,256,1792]{2,1,0:T(8,128)S(1)} custom-call(s32[3]{0:T(128)S(1)} %pad_add_fusion.place_ref, bf16[128,2048]{1,0:T(8,128)(2,1)S(1)} %pad_maximum_fusion.same_ref.same_a, bf16[128,2048]{1,0:T(8,128)(2,1)S(1)} %collective-permute-done.3.other_ref.other_a, bf16[4096,3584]{1,0:T(8,128)(2,1)} %bitcast.21, ...), custom_call_target="tpu_custom_call" | custom-call | flops 3758096384 | bytes 14680064 | tf_op jit(solution)/shard_map/pallas_call | solution.py:166
  32.2 0.5 collective-permute-done.5.refs_2_
  32.7 1.8 %copy-done = f32[2,256,1792]{2,1,0:T(8,128)} copy-done((f32[2,256,1792]{2,1,0:T(8,128)}, f32[2,256,1792]{2,1,0:T(8,128)S(1)}, u32[]{:S(2)}) %copy-start) | copy-done | bytes 3670040
  34.8 1.7 %collective-permute-done.7.other_ref.other_b = bf16[128,2048]{1,0:T(8,128)(2,1)S(1)} collective-permute-done((bf16[128,2048]{1,0:T(8,128)(2,1)S(1)}, bf16[128,2048]{1,0:T(8,128)(2,1)S(1)}, u32[]{:S(2)}, u32[]{:S(2)}) %collective-permute-start.7) | collective-permute-done | bytes 524320 | tf_op jit(solution)/shard_map/ppermute | solution.py:99
  36.4 2.0 %copy-done.1 = f32[2,256,1792]{2,1,0:T(8,128)S(1)} copy-done((f32[2,256,1792]{2,1,0:T(8,128)S(1)}, f32[2,256,1792]{2,1,0:T(8,128)}, u32[]{:S(2)}) %copy-start.1) | copy-done | bytes 3670040
  38.5 5.3 %shard_map.48.refs_0_ = bf16[2,256,768]{2,1,0:T(8,128)(2,1)S(1)} custom-call(s32[3]{0:T(128)S(1)} %pad_add_fusion.place_ref, f32[2,256,1792]{2,1,0:T(8,128)S(1)} %copy-done.1, bf16[128,2048]{1,0:T(8,128)(2,1)S(1)} %shard_map.47.same_ref.same_b, bf16[128,2048]{1,0:T(8,128)(2,1)S(1)} %collective-permute-done.7.other_ref.other_b, bf16[4096,3584]{1,0:T(8,128)(2,1)} %bitcast.22, ...), custom_call_target="tpu_custom_call" | custom-call | flops 1610612736 | bytes 6291456 | tf_op jit(solution)/shard_map/pallas_call | solution.py:200
  43.8 0.7 collective-permute-start.21
  44.5 3.7 %shard_map.49.refs_0_.refs_1_ = bf16[2,256,512]{2,1,0:T(8,128)(2,1)S(1)} custom-call(s32[3]{0:T(128)S(1)} %pad_add_fusion.place_ref, f32[2,256,1792]{2,1,0:T(8,128)S(1)} %copy-done.1, bf16[128,2048]{1,0:T(8,128)(2,1)S(1)} %shard_map.47.same_ref.same_b, bf16[128,2048]{1,0:T(8,128)(2,1)S(1)} %collective-permute-done.7.other_ref.other_b, ...), custom_call_target="tpu_custom_call" | custom-call | flops 1073741824 | bytes 4194304 | tf_op jit(solution)/shard_map/pallas_call | solution.py:200
  48.2 1.5 %collective-permute-start.15 = (bf16[2,256,512]{2,1,0:T(8,128)(2,1)S(1)}, bf16[2,256,512]{2,1,0:T(8,128)(2,1)}, u32[]{:S(2)}, u32[]{:S(2)}) collective-permute-start(bf16[2,256,512]{2,1,0:T(8,128)(2,1)S(1)} %shard_map.49.refs_0_.refs_1_), channel_id=1, source_target_pairs={{16,17},{17,16},{18,19},{19,18},{20,21},{21,20},{22,23},{23,22},{2... | collective-permute-start | bytes 1572872 | tf_op jit(solution)/shard_map/ppermute | solution.py:99
  49.7 2.8 %shard_map.50.refs_0_.refs_2_.refs_5_ = bf16[2,256,256]{2,1,0:T(8,128)(2,1)S(1)} custom-call(s32[3]{0:T(128)S(1)} %pad_add_fusion.place_ref, f32[2,256,1792]{2,1,0:T(8,128)S(1)} %copy-done.1, bf16[128,2048]{1,0:T(8,128)(2,1)S(1)} %shard_map.47.same_ref.same_b, bf16[128,2048]{1,0:T(8,128)(2,1)S(1)} %collective-permute-done.7.other_ref.other_b, ...), custom_call_target="tpu_custom_call" | custom-call | flops 536870912 | bytes 2097152 | tf_op jit(solution)/shard_map/pallas_call | solution.py:200
  52.5 2.8 %shard_map.51.refs_0_.refs_3_.refs_5_ = bf16[2,256,256]{2,1,0:T(8,128)(2,1)S(1)} custom-call(s32[3]{0:T(128)S(1)} %pad_add_fusion.place_ref, f32[2,256,1792]{2,1,0:T(8,128)S(1)} %copy-done.1, bf16[128,2048]{1,0:T(8,128)(2,1)S(1)} %shard_map.47.same_ref.same_b, bf16[128,2048]{1,0:T(8,128)(2,1)S(1)} %collective-permute-done.7.other_ref.other_b, ...), custom_call_target="tpu_custom_call" | custom-call | flops 536870912 | bytes 2097152 | tf_op jit(solution)/shard_map/pallas_call | solution.py:200
  55.4 15.8 %shard_map.52.refs_4_.mine_ref = bf16[2,256,1792]{2,1,0:T(8,128)(2,1)S(1)} custom-call(s32[4]{0:T(128)S(1)} %pad_add_fusion.1.place_ref, bf16[128,2048]{1,0:T(8,128)(2,1)S(1)} %copy-done.3, bf16[128,2048]{1,0:T(8,128)(2,1)S(1)} %copy-done.5, bf16[128,2048]{1,0:T(8,128)(2,1)S(1)} %shard_map.47.same_ref.same_b, ...), custom_call_target="tpu_custom_call" | custom-call | flops 7516192768 | bytes 29360128 | tf_op jit(solution)/shard_map/pallas_call | solution.py:255
  71.2 1.7 %shard_map.53.refs_6_ = bf16[2,256,256]{2,1,0:T(8,128)(2,1)S(1)} custom-call(s32[6]{0:T(128)S(1)} %stack.72.bases_ref, s32[1,256]{1,0:T(1,128)S(1)} %get-tuple-element.7.picks_ref, bf16[2,256,768]{2,1,0:T(8,128)(2,1)S(1)} %shard_map.48.refs_0_, bf16[2,256,512]{2,1,0:T(8,128)(2,1)S(1)} %shard_map.49.refs_0_.refs_1_, ...), custom_call_target="tpu_custom_call" | custom-call | flops 939524096 | bytes 3670016 | tf_op jit(solution)/shard_map/pallas_call | solution.py:299
  72.9 1.6 %collective-permute-start.9 = (bf16[2,256,256]{2,1,0:T(8,128)(2,1)S(1)}, bf16[2,256,256]{2,1,0:T(8,128)(2,1)S(1)}, u32[]{:S(2)}, u32[]{:S(2)}) collective-permute-start(bf16[2,256,256]{2,1,0:T(8,128)(2,1)S(1)} %shard_map.53.refs_6_), channel_id=1, source_target_pairs={{0,1},{1,0},{2,3},{3,2},{4,5},{5,4},{6,7},{7,6},{8,9},{9,8},{10,11... | collective-permute-start | bytes 786440 | tf_op jit(solution)/shard_map/ppermute | solution.py:99
  74.5 1.4 %shard_map.60.refs_2_ = bf16[256,768]{1,0:T(8,128)(2,1)} custom-call(bf16[2,256,1792]{2,1,0:T(8,128)(2,1)S(1)} %shard_map.52.refs_4_.mine_ref, bf16[2,256,768]{2,1,0:T(8,128)(2,1)S(1)} %collective-permute-done.21.refs_0_), custom_call_target="tpu_custom_call" | custom-call | flops 3932160 | bytes 1966080 | tf_op jit(solution)/shard_map/pallas_call | solution.py:338
  75.9 1.3 collective-permute-start.22
  77.2 2.4 %shard_map.54.refs_5_ = bf16[2,256,256]{2,1,0:T(8,128)(2,1)} custom-call(s32[6]{0:T(128)S(1)} %stack.72.bases_ref, s32[1,256]{1,0:T(1,128)S(1)} %get-tuple-element.8.picks_ref, bf16[2,256,768]{2,1,0:T(8,128)(2,1)S(1)} %shard_map.48.refs_0_, bf16[2,256,512]{2,1,0:T(8,128)(2,1)S(1)} %shard_map.49.refs_0_.refs_1_, ...), custom_call_target="tpu_custom_call" | custom-call | flops 939524096 | bytes 3670016 | tf_op jit(solution)/shard_map/pallas_call | solution.py:299
  79.6 0.5 collective-permute-start.8
  80.1 2.8 %shard_map.55.mine_ref = bf16[2,256,512]{2,1,0:T(8,128)(2,1)S(1)} custom-call(s32[6]{0:T(128)S(1)} %stack.72.bases_ref, s32[1,512]{1,0:T(1,128)S(1)} %bitcast.20, bf16[2,256,768]{2,1,0:T(8,128)(2,1)S(1)} %shard_map.48.refs_0_, bf16[2,256,512]{2,1,0:T(8,128)(2,1)S(1)} %shard_map.49.refs_0_.refs_1_, ...), custom_call_target="tpu_custom_call" | custom-call | flops 1879048192 | bytes 3670016 | tf_op jit(solution)/shard_map/pallas_call | solution.py:299
  83.2 4.5 %collective-permute-start.10 = (bf16[256,256]{1,0:T(8,128)(2,1)S(1)}, bf16[256,256]{1,0:T(8,128)(2,1)}, u32[]{:S(2)}, u32[]{:S(2)}) collective-permute-start(bf16[256,256]{1,0:T(8,128)(2,1)S(1)} %shard_map.57), channel_id=1, source_target_pairs={{0,16},{1,17},{2,18},{3,19},{4,20},{5,21},{6,22},{7,23},{8,24},{9,... | collective-permute-start | bytes 393224 | tf_op jit(solution)/shard_map/ppermute | solution.py:99
  88.2 0.4 copy-done.8
  88.6 0.9 copy-done.11
  89.5 1.7 %shard_map.58.refs_2_ = bf16[256,768]{1,0:T(8,128)(2,1)S(1)} custom-call(bf16[2,256,1792]{2,1,0:T(8,128)(2,1)S(1)} %shard_map.52.refs_4_.mine_ref, bf16[2,256,512]{2,1,0:T(8,128)(2,1)} %collective-permute-done.15.refs_0_, bf16[2,256,256]{2,1,0:T(8,128)(2,1)S(1)} %copy-done.11), custom_call_target="tpu_custom_call" | custom-call | flops 3932160 | bytes 1966080 | tf_op jit(solution)/shard_map/pallas_call | solution.py:338
  91.2 1.3 collective-permute-start.16
  92.5 3.7 %collective-permute-start.23 = (bf16[256,768]{1,0:T(8,128)(2,1)}, bf16[256,768]{1,0:T(8,128)(2,1)}, u32[]{:S(2)}, u32[]{:S(2)}) collective-permute-start(bf16[256,768]{1,0:T(8,128)(2,1)} %collective-permute-done.22.refs_0_), channel_id=1, source_target_pairs={{0,1},{1,0},{2,3},{3,2},{4,5},{5,4},{6,7},{7,6},{8,9},{9,8},{10,11... | collective-permute-start | bytes 1179656 | tf_op jit(solution)/shard_map/ppermute | solution.py:99
  96.3 1.5 %collective-permute-start.13 = (bf16[256,256]{1,0:T(8,128)(2,1)S(1)}, bf16[256,256]{1,0:T(8,128)(2,1)S(1)}, u32[]{:S(2)}, u32[]{:S(2)}) collective-permute-start(bf16[256,256]{1,0:T(8,128)(2,1)S(1)} %broadcast_select_fusion.1), channel_id=1, source_target_pairs={{0,12},{1,13},{2,14},{3,15},{4,0},{5,1},{6,2},{7,3},{8,4},{9,5},{1... | collective-permute-start | bytes 393224 | tf_op jit(solution)/shard_map/ppermute | solution.py:99
  98.0 1.9 %collective-permute-start.11 = (bf16[256,256]{1,0:T(8,128)(2,1)S(1)}, bf16[256,256]{1,0:T(8,128)(2,1)S(1)}, u32[]{:S(2)}, u32[]{:S(2)}) collective-permute-start(bf16[256,256]{1,0:T(8,128)(2,1)S(1)} %broadcast_select_fusion.1), channel_id=1, source_target_pairs={{0,4},{1,5},{2,6},{3,7},{4,8},{5,9},{6,10},{7,11},{8,12},{9,13},{1... | collective-permute-start | bytes 393224 | tf_op jit(solution)/shard_map/ppermute | solution.py:99
  100.0 3.2 %collective-permute-done.13 = bf16[256,256]{1,0:T(8,128)(2,1)S(1)} collective-permute-done((bf16[256,256]{1,0:T(8,128)(2,1)S(1)}, bf16[256,256]{1,0:T(8,128)(2,1)S(1)}, u32[]{:S(2)}, u32[]{:S(2)}) %collective-permute-start.13) | collective-permute-done | bytes 131104 | tf_op jit(solution)/shard_map/ppermute | solution.py:99
  103.2 5.4 %collective-permute-done.12 = bf16[256,256]{1,0:T(8,128)(2,1)S(1)} collective-permute-done((bf16[256,256]{1,0:T(8,128)(2,1)S(1)}, bf16[256,256]{1,0:T(8,128)(2,1)S(1)}, u32[]{:S(2)}, u32[]{:S(2)}) %collective-permute-start.12) | collective-permute-done | bytes 131104 | tf_op jit(solution)/shard_map/ppermute | solution.py:99
  108.7 5.1 %collective-permute-start.24 = (bf16[256,768]{1,0:T(8,128)(2,1)}, bf16[256,768]{1,0:T(8,128)(2,1)}, u32[]{:S(2)}, u32[]{:S(2)}) collective-permute-start(bf16[256,768]{1,0:T(8,128)(2,1)} %collective-permute-done.23.refs_1_), channel_id=1, source_target_pairs={{0,16},{1,17},{2,18},{3,19},{4,20},{5,21},{6,22},{7,23},{8,24},{9,... | collective-permute-start | bytes 1179656 | tf_op jit(solution)/shard_map/ppermute | solution.py:99
  113.8 0.8 broadcast_select_fusion
  114.6 0.7 copy-done.6
  115.3 1.4 %collective-permute-start.17 = (bf16[256,768]{1,0:T(8,128)(2,1)}, bf16[256,768]{1,0:T(8,128)(2,1)}, u32[]{:S(2)}, u32[]{:S(2)}) collective-permute-start(bf16[256,768]{1,0:T(8,128)(2,1)} %broadcast_select_fusion), channel_id=1, source_target_pairs={{0,1},{1,0},{2,3},{3,2},{4,5},{5,4},{6,7},{7,6},{8,9},{9,8},{10,11... | collective-permute-start | bytes 1179656 | tf_op jit(solution)/shard_map/ppermute | solution.py:99
  116.9 0.9 copy-done.9
  118.1 0.7 collective-permute-start.20
  118.7 1.3 collective-permute-start.19
  120.0 1.3 collective-permute-start.18
  121.3 1.0 collective-permute-done.24.refs_3_
  122.3 7.1 %shard_map.61.refs_8_ = bf16[2048,3584]{1,0:T(8,128)(2,1)} custom-call(s32[5]{0:T(128)S(1)} %stack.78.where_ref, bf16[1024,256]{1,0:T(8,128)(2,1)S(1)} %pad_maximum_fusion.1.same_ref, bf16[1024,256]{1,0:T(8,128)(2,1)S(1)} %collective-permute-done.14.other_ref, bf16[256,768]{1,0:T(8,128)(2,1)} %collective-permute-done.22.refs_0_, ...), custom_call_target="tpu_custom_call" | custom-call | flops 1610612736 | bytes 6291456 | tf_op jit(solution)/shard_map/pallas_call | solution.py:434
  129.6 7.1 %shard_map.62 = bf16[2048,3584]{1,0:T(8,128)(2,1)} custom-call(s32[5]{0:T(128)S(1)} %stack.67.where_ref, bf16[1024,256]{1,0:T(8,128)(2,1)S(1)} %pad_maximum_fusion.1.same_ref, bf16[1024,256]{1,0:T(8,128)(2,1)S(1)} %collective-permute-done.14.other_ref, bf16[256,768]{1,0:T(8,128)(2,1)S(1)} %copy-done.7, ...), custom_call_target="tpu_custom_call", output_to_operand_aliasing={{}: (11, {})} | custom-call | flops 2147483648 | bytes 8388608 | tf_op jit(solution)/shard_map/pallas_call | solution.py:434
  (59 shorter events, 2.3 us)
Async XLA Ops:
  1.0 9.0 %collective-permute-start.2 = (bf16[32,2048]{1,0:T(8,128)(2,1)S(1)}, bf16[32,2048]{1,0:T(8,128)(2,1)S(1)}, u32[]{:S(2)}, u32[]{:S(2)}) collective-permute-start(bf16[32,2048]{1,0:T(8,128)(2,1)S(1)} %get-tuple-element.6), channel_id=1, source_target_pairs={{0,12},{1,13},{2,14},{3,15},{4,0},{5,1},{6,2},{7,3},{8,4},{9,5},{1... | collective-permute-start | bytes 393224 | tf_op jit(solution)/shard_map/ppermute | solution.py:99
  6.1 11.2 %collective-permute-start.1 = (bf16[32,2048]{1,0:T(8,128)(2,1)S(1)}, bf16[32,2048]{1,0:T(8,128)(2,1)S(1)}, u32[]{:S(2)}, u32[]{:S(2)}) collective-permute-start(bf16[32,2048]{1,0:T(8,128)(2,1)S(1)} %get-tuple-element.6), channel_id=1, source_target_pairs={{0,8},{1,9},{2,10},{3,11},{4,12},{5,13},{6,14},{7,15},{8,0},{9,1},... | collective-permute-start | bytes 393224 | tf_op jit(solution)/shard_map/ppermute | solution.py:99
  6.1 11.2 %collective-permute-start = (bf16[32,2048]{1,0:T(8,128)(2,1)S(1)}, bf16[32,2048]{1,0:T(8,128)(2,1)S(1)}, u32[]{:S(2)}, u32[]{:S(2)}) collective-permute-start(bf16[32,2048]{1,0:T(8,128)(2,1)S(1)} %get-tuple-element.6), channel_id=1, source_target_pairs={{0,4},{1,5},{2,6},{3,7},{4,8},{5,9},{6,10},{7,11},{8,12},{9,13},{1... | collective-permute-start | bytes 393224 | tf_op jit(solution)/shard_map/ppermute | solution.py:99
  17.3 14.8 %copy-start.2 = (bf16[128,2048]{1,0:T(8,128)(2,1)}, bf16[128,2048]{1,0:T(8,128)(2,1)S(1)}, u32[]{:S(2)}) copy-start(bf16[128,2048]{1,0:T(8,128)(2,1)S(1)} %pad_maximum_fusion.same_ref.same_a) | copy-start | bytes 1572868
  17.4 4.9 %collective-permute-start.3 = (bf16[128,2048]{1,0:T(8,128)(2,1)S(1)}, bf16[128,2048]{1,0:T(8,128)(2,1)S(1)}, u32[]{:S(2)}, u32[]{:S(2)}) collective-permute-start(bf16[128,2048]{1,0:T(8,128)(2,1)S(1)} %pad_maximum_fusion.same_ref.same_a), channel_id=1, source_target_pairs={{0,2},{1,3},{2,0},{3,1},{4,6},{5,7},{6,4},{7,5},{8,10},{9,11},{10,... | collective-permute-start | bytes 1572872 | tf_op jit(solution)/shard_map/ppermute | solution.py:99
  17.4 14.7 %collective-permute-start.6 = (bf16[32,2048]{1,0:T(8,128)(2,1)S(1)}, bf16[32,2048]{1,0:T(8,128)(2,1)S(1)}, u32[]{:S(2)}, u32[]{:S(2)}) collective-permute-start(bf16[32,2048]{1,0:T(8,128)(2,1)S(1)} %get-tuple-element.5.refs_0_), channel_id=1, source_target_pairs={{0,12},{1,13},{2,14},{3,15},{4,0},{5,1},{6,2},{7,3},{8,4},{9,5},{1... | collective-permute-start | bytes 393224 | tf_op jit(solution)/shard_map/ppermute | solution.py:99
  19.1 13.6 %collective-permute-start.5 = (bf16[32,2048]{1,0:T(8,128)(2,1)S(1)}, bf16[32,2048]{1,0:T(8,128)(2,1)S(1)}, u32[]{:S(2)}, u32[]{:S(2)}) collective-permute-start(bf16[32,2048]{1,0:T(8,128)(2,1)S(1)} %get-tuple-element.5.refs_0_), channel_id=1, source_target_pairs={{0,8},{1,9},{2,10},{3,11},{4,12},{5,13},{6,14},{7,15},{8,0},{9,1},... | collective-permute-start | bytes 393224 | tf_op jit(solution)/shard_map/ppermute | solution.py:99
  20.2 12.4 %collective-permute-start.4 = (bf16[32,2048]{1,0:T(8,128)(2,1)S(1)}, bf16[32,2048]{1,0:T(8,128)(2,1)S(1)}, u32[]{:S(2)}, u32[]{:S(2)}) collective-permute-start(bf16[32,2048]{1,0:T(8,128)(2,1)S(1)} %get-tuple-element.5.refs_0_), channel_id=1, source_target_pairs={{0,4},{1,5},{2,6},{3,7},{4,8},{5,9},{6,10},{7,11},{8,12},{9,13},{1... | collective-permute-start | bytes 393224 | tf_op jit(solution)/shard_map/ppermute | solution.py:99
  22.2 9.9 %copy-start.4 = (bf16[128,2048]{1,0:T(8,128)(2,1)}, bf16[128,2048]{1,0:T(8,128)(2,1)S(1)}, u32[]{:S(2)}) copy-start(bf16[128,2048]{1,0:T(8,128)(2,1)S(1)} %collective-permute-done.3.other_ref.other_a) | copy-start | bytes 1572868
  22.2 12.3 %copy-start.12 = (s32[8192]{0:T(1024)S(1)}, s32[8192]{0:T(1024)}, u32[]{:S(2)}) copy-start(s32[8192]{0:T(1024)} %param.7) | copy-start | bytes 98308
  32.7 1.8 %copy-start = (f32[2,256,1792]{2,1,0:T(8,128)}, f32[2,256,1792]{2,1,0:T(8,128)S(1)}, u32[]{:S(2)}) copy-start(f32[2,256,1792]{2,1,0:T(8,128)S(1)} %shard_map.46.refs_4_.early_ref) | copy-start | bytes 11010052
  34.5 1.9 %collective-permute-start.7 = (bf16[128,2048]{1,0:T(8,128)(2,1)S(1)}, bf16[128,2048]{1,0:T(8,128)(2,1)S(1)}, u32[]{:S(2)}, u32[]{:S(2)}) collective-permute-start(bf16[128,2048]{1,0:T(8,128)(2,1)S(1)} %shard_map.47.same_ref.same_b), channel_id=1, source_target_pairs={{0,2},{1,3},{2,0},{3,1},{4,6},{5,7},{6,4},{7,5},{8,10},{9,11},{10,... | collective-permute-start | bytes 1572872 | tf_op jit(solution)/shard_map/ppermute | solution.py:99
  36.4 2.0 %copy-start.1 = (f32[2,256,1792]{2,1,0:T(8,128)S(1)}, f32[2,256,1792]{2,1,0:T(8,128)}, u32[]{:S(2)}) copy-start(f32[2,256,1792]{2,1,0:T(8,128)} %copy-done) | copy-start | bytes 11010052
  43.8 30.7 %collective-permute-start.21 = (bf16[2,256,768]{2,1,0:T(8,128)(2,1)S(1)}, bf16[2,256,768]{2,1,0:T(8,128)(2,1)S(1)}, u32[]{:S(2)}, u32[]{:S(2)}) collective-permute-start(bf16[2,256,768]{2,1,0:T(8,128)(2,1)S(1)} %shard_map.48.refs_0_), channel_id=1, source_target_pairs={{16,17},{17,16},{18,19},{19,18},{20,21},{21,20},{22,23},{23,22},{2... | collective-permute-start | bytes 2359304 | tf_op jit(solution)/shard_map/ppermute | solution.py:99
  48.2 40.4 %collective-permute-start.15 = (bf16[2,256,512]{2,1,0:T(8,128)(2,1)S(1)}, bf16[2,256,512]{2,1,0:T(8,128)(2,1)}, u32[]{:S(2)}, u32[]{:S(2)}) collective-permute-start(bf16[2,256,512]{2,1,0:T(8,128)(2,1)S(1)} %shard_map.49.refs_0_.refs_1_), channel_id=1, source_target_pairs={{16,17},{17,16},{18,19},{19,18},{20,21},{21,20},{22,23},{23,22},{2... | collective-permute-start | bytes 1572872 | tf_op jit(solution)/shard_map/ppermute | solution.py:99
  52.5 2.9 %copy-start.3 = (bf16[128,2048]{1,0:T(8,128)(2,1)S(1)}, bf16[128,2048]{1,0:T(8,128)(2,1)}, u32[]{:S(2)}) copy-start(bf16[128,2048]{1,0:T(8,128)(2,1)} %copy-done.2) | copy-start | bytes 1572868
  52.5 2.9 %copy-start.5 = (bf16[128,2048]{1,0:T(8,128)(2,1)S(1)}, bf16[128,2048]{1,0:T(8,128)(2,1)}, u32[]{:S(2)}) copy-start(bf16[128,2048]{1,0:T(8,128)(2,1)} %copy-done.4) | copy-start | bytes 1572868
  72.9 10.0 %collective-permute-start.9 = (bf16[2,256,256]{2,1,0:T(8,128)(2,1)S(1)}, bf16[2,256,256]{2,1,0:T(8,128)(2,1)S(1)}, u32[]{:S(2)}, u32[]{:S(2)}) collective-permute-start(bf16[2,256,256]{2,1,0:T(8,128)(2,1)S(1)} %shard_map.53.refs_6_), channel_id=1, source_target_pairs={{0,1},{1,0},{2,3},{3,2},{4,5},{5,4},{6,7},{7,6},{8,9},{9,8},{10,11... | collective-permute-start | bytes 786440 | tf_op jit(solution)/shard_map/ppermute | solution.py:99
  75.9 16.6 %collective-permute-start.22 = (bf16[256,768]{1,0:T(8,128)(2,1)}, bf16[256,768]{1,0:T(8,128)(2,1)}, u32[]{:S(2)}, u32[]{:S(2)}) collective-permute-start(bf16[256,768]{1,0:T(8,128)(2,1)} %shard_map.60.refs_2_), channel_id=1, source_target_pairs={{16,0},{17,1},{18,2},{19,3},{20,4},{21,5},{22,6},{23,7},{24,8},{25... | collective-permute-start | bytes 1179656 | tf_op jit(solution)/shard_map/ppermute | solution.py:99
  79.6 8.3 %collective-permute-start.8 = (bf16[2,256,256]{2,1,0:T(8,128)(2,1)}, bf16[2,256,256]{2,1,0:T(8,128)(2,1)S(1)}, u32[]{:S(2)}, u32[]{:S(2)}) collective-permute-start(bf16[2,256,256]{2,1,0:T(8,128)(2,1)} %shard_map.54.refs_5_), channel_id=1, source_target_pairs={{0,1},{1,0},{2,3},{3,2},{4,5},{5,4},{6,7},{7,6},{8,9},{9,8},{10,11... | collective-permute-start | bytes 786440 | tf_op jit(solution)/shard_map/ppermute | solution.py:99
  82.9 5.3 %copy-start.10 = (bf16[2,256,256]{2,1,0:T(8,128)(2,1)}, bf16[2,256,256]{2,1,0:T(8,128)(2,1)S(1)}, u32[]{:S(2)}) copy-start(bf16[2,256,256]{2,1,0:T(8,128)(2,1)S(1)} %collective-permute-done.9.theirs_ref.refs_1_) | copy-start | bytes 786436
  83.2 13.0 %collective-permute-start.10 = (bf16[256,256]{1,0:T(8,128)(2,1)S(1)}, bf16[256,256]{1,0:T(8,128)(2,1)}, u32[]{:S(2)}, u32[]{:S(2)}) collective-permute-start(bf16[256,256]{1,0:T(8,128)(2,1)S(1)} %shard_map.57), channel_id=1, source_target_pairs={{0,16},{1,17},{2,18},{3,19},{4,20},{5,21},{6,22},{7,23},{8,24},{9,... | collective-permute-start | bytes 393224 | tf_op jit(solution)/shard_map/ppermute | solution.py:99
  87.9 0.7 copy-start.8
  88.6 1.0 copy-start.11
  91.2 22.6 %collective-permute-start.16 = (bf16[256,768]{1,0:T(8,128)(2,1)S(1)}, bf16[256,768]{1,0:T(8,128)(2,1)S(1)}, u32[]{:S(2)}, u32[]{:S(2)}) collective-permute-start(bf16[256,768]{1,0:T(8,128)(2,1)S(1)} %shard_map.58.refs_2_), channel_id=1, source_target_pairs={{16,0},{17,1},{18,2},{19,3},{20,4},{21,5},{22,6},{23,7},{24,8},{25... | collective-permute-start | bytes 1179656 | tf_op jit(solution)/shard_map/ppermute | solution.py:99
  92.5 16.2 %collective-permute-start.23 = (bf16[256,768]{1,0:T(8,128)(2,1)}, bf16[256,768]{1,0:T(8,128)(2,1)}, u32[]{:S(2)}, u32[]{:S(2)}) collective-permute-start(bf16[256,768]{1,0:T(8,128)(2,1)} %collective-permute-done.22.refs_0_), channel_id=1, source_target_pairs={{0,1},{1,0},{2,3},{3,2},{4,5},{5,4},{6,7},{7,6},{8,9},{9,8},{10,11... | collective-permute-start | bytes 1179656 | tf_op jit(solution)/shard_map/ppermute | solution.py:99
  96.3 6.9 %collective-permute-start.13 = (bf16[256,256]{1,0:T(8,128)(2,1)S(1)}, bf16[256,256]{1,0:T(8,128)(2,1)S(1)}, u32[]{:S(2)}, u32[]{:S(2)}) collective-permute-start(bf16[256,256]{1,0:T(8,128)(2,1)S(1)} %broadcast_select_fusion.1), channel_id=1, source_target_pairs={{0,12},{1,13},{2,14},{3,15},{4,0},{5,1},{6,2},{7,3},{8,4},{9,5},{1... | collective-permute-start | bytes 393224 | tf_op jit(solution)/shard_map/ppermute | solution.py:99
  97.7 10.9 %collective-permute-start.12 = (bf16[256,256]{1,0:T(8,128)(2,1)S(1)}, bf16[256,256]{1,0:T(8,128)(2,1)S(1)}, u32[]{:S(2)}, u32[]{:S(2)}) collective-permute-start(bf16[256,256]{1,0:T(8,128)(2,1)S(1)} %broadcast_select_fusion.1), channel_id=1, source_target_pairs={{0,8},{1,9},{2,10},{3,11},{4,12},{5,13},{6,14},{7,15},{8,0},{9,1},... | collective-permute-start | bytes 393224 | tf_op jit(solution)/shard_map/ppermute | solution.py:99
  98.0 10.5 %collective-permute-start.11 = (bf16[256,256]{1,0:T(8,128)(2,1)S(1)}, bf16[256,256]{1,0:T(8,128)(2,1)S(1)}, u32[]{:S(2)}, u32[]{:S(2)}) collective-permute-start(bf16[256,256]{1,0:T(8,128)(2,1)S(1)} %broadcast_select_fusion.1), channel_id=1, source_target_pairs={{0,4},{1,5},{2,6},{3,7},{4,8},{5,9},{6,10},{7,11},{8,12},{9,13},{1... | collective-permute-start | bytes 393224 | tf_op jit(solution)/shard_map/ppermute | solution.py:99
  108.6 11.4 %collective-permute-start.14 = (bf16[1024,256]{1,0:T(8,128)(2,1)S(1)}, bf16[1024,256]{1,0:T(8,128)(2,1)S(1)}, u32[]{:S(2)}, u32[]{:S(2)}) collective-permute-start(bf16[1024,256]{1,0:T(8,128)(2,1)S(1)} %pad_maximum_fusion.1.same_ref), channel_id=1, source_target_pairs={{0,2},{1,3},{2,0},{3,1},{4,6},{5,7},{6,4},{7,5},{8,10},{9,11},{10,... | collective-permute-start | bytes 1572872 | tf_op jit(solution)/shard_map/ppermute | solution.py:99
  108.7 13.6 %collective-permute-start.24 = (bf16[256,768]{1,0:T(8,128)(2,1)}, bf16[256,768]{1,0:T(8,128)(2,1)}, u32[]{:S(2)}, u32[]{:S(2)}) collective-permute-start(bf16[256,768]{1,0:T(8,128)(2,1)} %collective-permute-done.23.refs_1_), channel_id=1, source_target_pairs={{0,16},{1,17},{2,18},{3,19},{4,20},{5,21},{6,22},{7,23},{8,24},{9,... | collective-permute-start | bytes 1179656 | tf_op jit(solution)/shard_map/ppermute | solution.py:99
  114.6 0.7 copy-start.6
  115.3 14.3 %collective-permute-start.17 = (bf16[256,768]{1,0:T(8,128)(2,1)}, bf16[256,768]{1,0:T(8,128)(2,1)}, u32[]{:S(2)}, u32[]{:S(2)}) collective-permute-start(bf16[256,768]{1,0:T(8,128)(2,1)} %broadcast_select_fusion), channel_id=1, source_target_pairs={{0,1},{1,0},{2,3},{3,2},{4,5},{5,4},{6,7},{7,6},{8,9},{9,8},{10,11... | collective-permute-start | bytes 1179656 | tf_op jit(solution)/shard_map/ppermute | solution.py:99
  116.9 1.0 copy-start.9
  117.8 11.8 %copy-start.7 = (bf16[256,768]{1,0:T(8,128)(2,1)S(1)}, bf16[256,768]{1,0:T(8,128)(2,1)}, u32[]{:S(2)}) copy-start(bf16[256,768]{1,0:T(8,128)(2,1)} %copy-done.6) | copy-start | bytes 1179652
  118.1 11.3 %collective-permute-start.20 = (bf16[256,256]{1,0:T(8,128)(2,1)S(1)}, bf16[256,256]{1,0:T(8,128)(2,1)S(1)}, u32[]{:S(2)}, u32[]{:S(2)}) collective-permute-start(bf16[256,256]{1,0:T(8,128)(2,1)S(1)} %shard_map.59.refs_6_), channel_id=1, source_target_pairs={{16,17},{17,16},{18,19},{19,18},{20,21},{21,20},{22,23},{23,22},{2... | collective-permute-start | bytes 393224 | tf_op jit(solution)/shard_map/ppermute | solution.py:99
  118.7 10.6 %collective-permute-start.19 = (bf16[256,256]{1,0:T(8,128)(2,1)S(1)}, bf16[256,256]{1,0:T(8,128)(2,1)S(1)}, u32[]{:S(2)}, u32[]{:S(2)}) collective-permute-start(bf16[256,256]{1,0:T(8,128)(2,1)S(1)} %shard_map.59.refs_6_), channel_id=1, source_target_pairs={{16,1},{17,0},{18,3},{19,2},{20,5},{21,4},{22,7},{23,6},{24,9},{25... | collective-permute-start | bytes 393224 | tf_op jit(solution)/shard_map/ppermute | solution.py:99
  120.0 9.3 %collective-permute-start.18 = (bf16[256,256]{1,0:T(8,128)(2,1)S(1)}, bf16[256,256]{1,0:T(8,128)(2,1)S(1)}, u32[]{:S(2)}, u32[]{:S(2)}) collective-permute-start(bf16[256,256]{1,0:T(8,128)(2,1)S(1)} %shard_map.59.refs_6_), channel_id=1, source_target_pairs={{16,0},{17,1},{18,2},{19,3},{20,4},{21,5},{22,6},{23,7},{24,8},{25... | collective-permute-start | bytes 393224 | tf_op jit(solution)/shard_map/ppermute | solution.py:99

commit v3 on v2

--- a/solution.py
+++ b/solution.py
@@ -115,10 +115,6 @@
     return [block, came[0], came[2], came[1]]
 
 
-def gather_line(block, sizes):
-    return jnp.concatenate(shifts(block, sizes), axis=0)
-
-
 def join_kernel(*refs):
     rows = refs[0].shape[0]
     for i in range(CHIPS):
@@ -153,13 +149,35 @@
     )
 
 
-def early_kernel(place_ref, same_ref, other_ref, gate_ref, up_ref, out_ref):
+def choose_kernel(model_ref, first_ref, second_ref, out_ref):
+    for holder, ref in enumerate((first_ref, second_ref)):
+
+        @pl.when(model_ref[0] == holder)
+        def _():
+            out_ref[...] = ref[...]
+
+
+def choose(model_number, first, second):
+    vmem = pl.BlockSpec(memory_space=pltpu.VMEM)
+    return call(
+        choose_kernel,
+        out_shape=jax.ShapeDtypeStruct(first.shape, first.dtype),
+        in_specs=[pl.BlockSpec(memory_space=pltpu.SMEM), vmem, vmem],
+        out_specs=vmem,
+        flops=0,
+        moved=4 * first.size,
+        vmem=16,
+    )(model_number, first, second)
+
+
+def early_kernel(place_ref, same_ref, other_ref, gate_ref, up_ref, *refs):
+    out_ref = refs[-1]
     x = jnp.concatenate([same_ref[...], other_ref[...]], axis=0)
     out_ref[0] = jnp.dot(x, gate_ref[...], preferred_element_type=jnp.float32)
     out_ref[1] = jnp.dot(x, up_ref[...], preferred_element_type=jnp.float32)
 
 
-def early_products(place, same, other, gate, up, tile, count):
+def early_products(place, same, other, gate, up, tile, count, after):
     tokens, width = 2 * same.shape[0], same.shape[1]
     weights = pl.BlockSpec((width, tile), lambda i, place_ref: (0, place_ref[0] + i))
     whole = pl.BlockSpec(same.shape, lambda i, place_ref: (0, 0))
@@ -169,13 +187,14 @@
         grid_spec=pltpu.PrefetchScalarGridSpec(
             num_scalar_prefetch=1,
             grid=(count,),
-            in_specs=[whole, whole, weights, weights],
+            in_specs=[whole, whole, weights, weights]
+            + [pl.BlockSpec(memory_space=pl.ANY)] * len(after),
             out_specs=pl.BlockSpec((2, tokens, tile), lambda i, place_ref: (0, 0, i)),
         ),
         flops=4 * tokens * width * tile * count,
         moved=4 * width * tile * count,
-        vmem=32,
-    )(place, same, other, gate, up)
+        vmem=38,
+    )(place, same, other, gate, up, *after)
 
 
 def store_sorted(place_ref, out_ref, which, total):
@@ -215,62 +234,44 @@
         ),
         flops=4 * tokens * width * tile * count,
         moved=4 * width * tile * count,
-        vmem=32,
+        vmem=38,
     )(place, early, same, other, gate, up, *after)
 
 
-KEPT_PARTS = 2
-KEPT_STEPS = 2
-
-
 def kept_kernel(place_ref, same_a, other_a, same_b, other_b, gate_ref, up_ref, *refs):
-    out_ref, total_ref = refs[-2:]
-    step = pl.program_id(1)
-    depth = gate_ref.shape[0]
-    for at in range(2 * KEPT_STEPS):
-        same_ref, other_ref = ((same_a, other_a), (same_b, other_b))[at // KEPT_STEPS]
-        start = at % KEPT_STEPS * depth
-
-        @pl.when(step == at)
-        def _():
-            x = jnp.concatenate(
-                [same_ref[:, start : start + depth], other_ref[:, start : start + depth]], axis=0
-            )
-            for which, weight_ref in enumerate((gate_ref, up_ref)):
-                total = jnp.dot(x, weight_ref[...], preferred_element_type=jnp.float32)
-                if at:
-                    total += total_ref[which]
-                if at < 2 * KEPT_STEPS - 1:
-                    total_ref[which] = total
-                else:
-                    store_sorted(place_ref, out_ref, which, total)
-
-
-def kept_products(place, same, other, gate, up, after):
+    width = same_a.shape[1]
+    xs = [
+        jnp.concatenate([same_ref[...], other_ref[...]], axis=0)
+        for same_ref, other_ref in ((same_a, other_a), (same_b, other_b))
+    ]
+    for which, weight_ref in enumerate((gate_ref, up_ref)):
+        total = jnp.dot(xs[0], weight_ref[:width], preferred_element_type=jnp.float32)
+        total += jnp.dot(xs[1], weight_ref[width:], preferred_element_type=jnp.float32)
+        store_sorted(place_ref, refs[-1], which, total)
+
+
+def kept_products(place, same, other, gate, up, tile, count, after):
     tokens, width = 2 * same[0].shape[0], same[0].shape[1]
-    units = gate.shape[1] // 2
-    part, depth = units // KEPT_PARTS, width // KEPT_STEPS
-    weights = pl.BlockSpec((depth, part), lambda i, k, place_ref: (k, place_ref[3] * KEPT_PARTS + i))
-    whole = pl.BlockSpec(same[0].shape, lambda i, k, place_ref: (0, 0))
+    weights = pl.BlockSpec((2 * width, tile), lambda i, place_ref: (0, place_ref[0] + i))
+    whole = pl.BlockSpec(same[0].shape, lambda i, place_ref: (0, 0))
     return call(
         kept_kernel,
-        out_shape=jax.ShapeDtypeStruct((2, tokens, units), jnp.bfloat16),
+        out_shape=jax.ShapeDtypeStruct((2, tokens, tile * count), jnp.bfloat16),
         grid_spec=pltpu.PrefetchScalarGridSpec(
             num_scalar_prefetch=1,
-            grid=(KEPT_PARTS, 2 * KEPT_STEPS),
+            grid=(count,),
             in_specs=[whole] * 4
             + [weights, weights]
             + [pl.BlockSpec(memory_space=pl.ANY)] * len(after),
-            out_specs=pl.BlockSpec((2, tokens, part), lambda i, k, place_ref: (0, 0, i)),
-            scratch_shapes=[pltpu.VMEM((2, tokens, part), jnp.float32)],
+            out_specs=pl.BlockSpec((2, tokens, tile), lambda i, place_ref: (0, 0, i)),
         ),
-        flops=8 * tokens * width * units,
-        moved=8 * width * units,
-        vmem=40,
+        flops=8 * tokens * width * tile * count,
+        moved=8 * width * tile * count,
+        vmem=38,
     )(place, same[0], other[0], same[1], other[1], gate, up, *after)
 
 
-def pick_kernel(counts, tile, has_instead, bases_ref, picks_ref, *refs):
+def pick_kernel(counts, tile, instead, bases_ref, picks_ref, *refs):
     out_ref = refs[-1]
     tokens, picked = out_ref.shape[1:]
 
@@ -288,7 +289,11 @@
 
     @pl.when(bases_ref[len(counts)] == 1)
     def _():
-        out_ref[...] = refs[len(counts)][...] if has_instead else jnp.zeros_like(out_ref)
+        if instead is None:
+            out_ref[...] = jnp.zeros_like(out_ref)
+        else:
+            part, start = instead
+            out_ref[...] = refs[part][:, :, start : start + picked]
 
 
 def pick(bases, picks, parts, instead, tile, after):
@@ -297,16 +302,16 @@
     counts = [part.shape[2] // tile for part in parts]
     vmem = pl.BlockSpec(memory_space=pltpu.VMEM)
     return call(
-        functools.partial(pick_kernel, counts, tile, len(instead)),
+        functools.partial(pick_kernel, counts, tile, instead),
         out_shape=jax.ShapeDtypeStruct((2, tokens, picked), jnp.bfloat16),
         in_specs=[pl.BlockSpec(memory_space=pltpu.SMEM), vmem]
-        + [vmem] * len(parts + instead)
+        + [vmem] * len(parts)
         + [pl.BlockSpec(memory_space=pl.ANY)] * len(after),
         out_specs=vmem,
         flops=4 * tokens * picked * tile * sum(counts),
         moved=4 * tokens * tile * sum(counts),
-        vmem=32,
-    )(bases, picks, *parts, *instead, *after)
+        vmem=16,
+    )(bases, picks, *parts, *after)
 
 
 def zscore(mine, theirs):
@@ -342,7 +347,7 @@
         out_specs=vmem,
         flops=20 * tokens * count,
         moved=10 * tokens * count,
-        vmem=32,
+        vmem=16,
     )(mine, *theirs)
 
 
@@ -350,29 +355,40 @@
     out_ref[...] = zscore(mine_ref[...], theirs_ref[...]).T.astype(jnp.bfloat16)
 
 
-def panel_scores(mine, theirs, first):
+def panel_kernel_or(model_ref, mine_ref, theirs_ref, given_ref, out_ref):
+    @pl.when(model_ref[0] == 0)
+    def _():
+        panel_kernel(mine_ref, theirs_ref, out_ref)
+
+    @pl.when(model_ref[0] == 1)
+    def _():
+        out_ref[...] = given_ref[...]
+
+
+def panel_scores(mine, theirs, first, given=()):
     _, tokens, count = theirs.shape
-    return call(
-        panel_kernel,
+    rows = pl.BlockSpec((count, tokens), lambda i: (0, 0))
+    units = [
+        pl.BlockSpec((2, tokens, count), lambda i: (0, 0, first)),
+        pl.BlockSpec((2, tokens, count), lambda i: (0, 0, 0)),
+    ]
+    return call(
+        panel_kernel_or if given else panel_kernel,
         out_shape=jax.ShapeDtypeStruct((count, tokens), jnp.bfloat16),
         grid=(1,),
-        in_specs=[
-            pl.BlockSpec((2, tokens, count), lambda i: (0, 0, first)),
-            pl.BlockSpec((2, tokens, count), lambda i: (0, 0, 0)),
-        ],
-        out_specs=pl.BlockSpec((count, tokens), lambda i: (0, 0)),
+        in_specs=[pl.BlockSpec(memory_space=pltpu.SMEM), *units, rows] if given else units,
+        out_specs=rows,
         flops=20 * tokens * count,
         moved=10 * tokens * count,
         vmem=16,
-    )(mine, theirs)
-
-
-def score_kernel(scale, n_pieces, has_before, where_ref, same_ref, other_ref, *refs):
+    )(*given[:1], mine, theirs, *given[1:])
+
+
+def score_kernel(scale, tile, n_pieces, has_before, where_ref, panel_ref, *refs):
     pieces = refs[: 4 * n_pieces]
     out_ref, near_ref, far_ref, block_ref, sems = refs[4 * n_pieces + has_before :]
-    model, chip, core, near_column, far_column = (where_ref[i] for i in range(5))
-    rows = same_ref.shape[0] // CHIPS
-    columns = near_ref.shape[1]
+    model, near_column, far_column = (where_ref[i] for i in range(3))
+    rows, columns = block_ref.shape[1:]
 
     def assemble(at, into):
         start = 0
@@ -398,10 +414,8 @@
         )
 
     def step(index, carry):
-        line = lax.rem(chip + CHIPS - index, CHIPS)
-        for which, panel_ref in enumerate((same_ref, other_ref)):
-            panel = panel_ref[pl.ds(pl.multiple_of(index * rows, rows), rows), :]
-            row = (line * 2 + (1 - core if which else core)) * rows
+        for which in range(2):
+            row = (2 * index + which) * rows
             for far, units_ref in enumerate((near_ref, far_ref)):
                 slot = 2 * which + far
                 column = far_column if far else near_column
@@ -410,45 +424,45 @@
                 def _():
                     copy(slot, row, column).wait()
 
-                total = jnp.dot(panel, units_ref[...], preferred_element_type=jnp.float32)
-                block_ref[slot] = (total * scale).astype(jnp.bfloat16)
+                for start in range(0, columns, tile):
+                    total = jnp.dot(
+                        panel_ref[pl.ds(pl.multiple_of(row, rows), rows), :],
+                        units_ref[:, start : start + tile],
+                        preferred_element_type=jnp.float32,
+                    )
+                    block_ref[slot, :, start : start + tile] = (total * scale).astype(jnp.bfloat16)
                 copy(slot, row, column).start()
         return carry
 
-    lax.fori_loop(0, CHIPS, step, 0)
+    lax.fori_loop(0, panel_ref.shape[0] // (2 * rows), step, 0)
     for slot in range(4):
         copy(slot, 0, 0).wait()
 
 
-def scores(where, same, other, pieces, tile, first, half, before):
-    tokens = same.shape[1]
-    rows = same.shape[0] // CHIPS
+def scores(where, panel, pieces, tile, half, before):
+    rows, tokens = panel.shape
     columns = sum(piece[0].shape[1] for piece in pieces)
-    model, chip, core, side = where
-    near = (side * half + first) * tile
-    far = ((1 - side) * half + first) * tile
-    where = jnp.stack([model, chip, core, near, far]).astype(jnp.int32)
     vmem = pl.BlockSpec(memory_space=pltpu.VMEM)
     anywhere = pl.BlockSpec(memory_space=pl.ANY)
     flat = [array for piece in pieces for array in piece]
     return call(
-        functools.partial(score_kernel, 1.0 / math.sqrt(tokens), len(pieces), len(before)),
-        out_shape=jax.ShapeDtypeStruct((2 * CHIPS * rows, 2 * half * tile), jnp.bfloat16),
-        in_specs=[pl.BlockSpec(memory_space=pltpu.SMEM), vmem, vmem]
+        functools.partial(score_kernel, 1.0 / math.sqrt(tokens), tile, len(pieces), len(before)),
+        out_shape=jax.ShapeDtypeStruct((rows, 2 * half * tile), jnp.bfloat16),
+        in_specs=[pl.BlockSpec(memory_space=pltpu.SMEM), vmem]
         + [vmem] * len(flat)
         + [anywhere] * len(before),
         out_specs=anywhere,
         scratch_shapes=[
             pltpu.VMEM((tokens, columns), jnp.bfloat16),
             pltpu.VMEM((tokens, columns), jnp.bfloat16),
-            pltpu.VMEM((4, rows, columns), jnp.bfloat16),
+            pltpu.VMEM((4, rows // 4, columns), jnp.bfloat16),
             pltpu.SemaphoreType.DMA((4,)),
         ],
-        input_output_aliases={3 + len(flat): 0} if before else {},
-        flops=8 * CHIPS * rows * tokens * columns,
-        moved=8 * CHIPS * rows * columns,
-        vmem=32,
-    )(where, same, other, *flat, *before)
+        input_output_aliases={2 + len(flat): 0} if before else {},
+        flops=4 * rows * tokens * columns,
+        moved=4 * rows * columns,
+        vmem=16,
+    )(where, panel, *flat, *before)
 
 
 def paired_body(acts, gate_w, up_w, panel_units):
@@ -463,8 +477,8 @@
     tile = picks.shape[3]
     half = units // 2 // tile
     large = (half - 1) // 2
-    chunks = [large, half - 2 - large, 1, 1]
-    starts = [0, large, half - 2, half - 1]
+    chunks = [large, half - 2 - large, 2]
+    starts = [0, large, half - 2]
 
     def b_sides(m, d, t):
         return (m, d, 1 - t) if m == 1 else None
@@ -485,13 +499,35 @@
         return (1, d, t) if m == 0 else None
 
     middle = acts.shape[2] // 2
-    same = [gather_line(acts[0][:, :middle], sizes)]
+    same = [join(shifts(acts[0][:, :middle], sizes), [])]
     other = [send(same[0], sizes, other_core)]
     last = shifts(acts[0][:, middle:], sizes)
 
+    picks = lax.dynamic_index_in_dim(picks, block, axis=2, keepdims=False) - block * units
+    picks_far = lax.dynamic_index_in_dim(picks, 1 - side, axis=1, keepdims=False)
+    picks_b, picks_a = picks_far[1:], picks_far[:1]
+    picks_own = lax.dynamic_index_in_dim(picks, side, axis=1, keepdims=False).reshape(1, -1)
+    bases = [((1 - side) * half + first) * tile for first in starts] + [side * half * tile, model]
+    bases = jnp.stack(bases).astype(jnp.int32)
+    model_number = jnp.reshape(model, (1,)).astype(jnp.int32)
+    targets = [
+        jnp.stack([model, (side * half + first) * tile, ((1 - side) * half + first) * tile])
+        for first in (0, starts[2])
+    ]
+    targets = [target.astype(jnp.int32) for target in targets]
+
     to_side = jnp.stack([(1 - side) * half, chip, core]).astype(jnp.int32)
-    own_side = jnp.stack([side * half, chip, core, side]).astype(jnp.int32)
-    early = early_products(to_side, same[0], other[0], gate, up, tile, half)
+    own_side = jnp.stack([side * half, chip, core]).astype(jnp.int32)
+    early = early_products(
+        to_side,
+        same[0],
+        other[0],
+        gate,
+        up,
+        tile,
+        half,
+        [own_side, picks_b, picks_a, picks_own, bases, model_number, *targets],
+    )
     same.append(join(last, [early]))
     other.append(send(same[1], sizes, other_core))
     sent = []
@@ -501,43 +537,36 @@
                 to_side, early, same[1], other[1], gate, up, tile, first, count, sent[-1:]
             )
         )
-    kept = kept_products(own_side, same, other, gate, up, sent[-1:])
-
-    picks = lax.dynamic_index_in_dim(picks, block, axis=2, keepdims=False) - block * units
-    picks_far = lax.dynamic_index_in_dim(picks, 1 - side, axis=1, keepdims=False)
-    picks_own = lax.dynamic_index_in_dim(picks, side, axis=1, keepdims=False).reshape(1, -1)
-    bases = [(to_side[0] + first) * tile for first in starts] + [own_side[0] * tile, model]
-    bases = jnp.stack(bases).astype(jnp.int32)
+    kept = kept_products(own_side, same, other, gate, up, tile, half, sent[-1:])
+
     parts = sent + [kept]
-    shared_b = pick(bases, picks_far[1:], parts, sent[2:3], tile, [])
-    shared_a = pick(bases, picks_far[:1], parts, sent[3:], tile, [shared_b])
-    picked_own = pick(bases, picks_own, parts, [], tile, [shared_a])
+    shared_b = pick(bases, picks_b, parts, (2, 0), tile, [])
+    shared_a = pick(bases, picks_a, parts, (2, tile), tile, [shared_b])
+    picked_own = pick(bases, picks_own, parts, None, tile, [shared_a])
     came = [send(part, sizes, b_sides) for part in sent[:2]]
     came += [send(part, sizes, both_sides) for part in (shared_b, shared_a)]
 
     rows_b = send(panel_scores(picked_own, came[2], 1), sizes, a_to_b)
-    rows_a = panel_scores(picked_own, came[3], 0)
-    panel = gather_line(jnp.where(model == 0, rows_a, rows_b), sizes)
-    panel_other = send(panel, sizes, other_core)
+    rows = panel_scores(picked_own, came[3], 0, (model_number, rows_b))
+    panel = lax.all_gather(rows, "dp", axis=0, tiled=True)
 
     z = unit_scores(kept, came[:1], 0)
     a_mine = send(z, sizes, b_to_a)
     a_far = send(a_mine, sizes, a_sides)
     pieces = [(a_mine, a_far, z, send(a_far, sizes, a_to_b))]
 
-    z = unit_scores(kept, came[1:3], starts[1] * tile)
+    z = unit_scores(kept, came[1:2], starts[1] * tile)
     a_mine = send(z, sizes, b_to_a)
-    far = send(jnp.where(model == 0, a_mine, z), sizes, both_sides)
+    far = send(choose(model_number, a_mine, z), sizes, both_sides)
     pieces.append((a_mine, far, z, far))
 
-    z = unit_scores(kept, came[3:], starts[3] * tile)
+    z = unit_scores(kept, came[2:], starts[2] * tile)
     pieces.append(
         (send(z, sizes, b_to_a), send(z, sizes, b_to_far_a), z, send(z, sizes, b_sides))
     )
 
-    where = (model, chip, core, side)
-    result = scores(where, panel, panel_other, pieces[:1], tile, 0, half, [])
-    return scores(where, panel, panel_other, pieces[1:], tile, starts[1], half, [result])
+    result = scores(targets[0], panel, pieces[:2], tile, half, [])
+    return scores(targets[1], panel, pieces[2:], tile, half, [result])
 
 
 def solution(mesh):

time: 138 us -> 149 us (1.080)
  the two profiles are of different devices: /device:TPU:0 before, /device:TPU:20 now
where the time goes in v3:
time: 149 us; the launch traced here: 148 us
  Pallas kernels  57.8 us (39%)
  waiting for transfers between devices  40.5 us (27%)
  starting transfers between devices  27.1 us (18%)
  between operations  13.7 us (9%)
  local copies, waits for them, and re-layouts  8.51 us (6%)
    ppermute x21, waiting for transfers between devices, send(): return lax.ppermute(block, AXES, routes(sizes, move))  40.5 us
    ppermute x21, starting transfers between devices, send(): return lax.ppermute(block, AXES, routes(sizes, move))  27.1 us
    pallas_call x1, Pallas kernels, kept_products(): call(kept_kernel, out_shape=jax.ShapeDtypeStruct((2, tokens, tile * count...  14.9 us
    pallas_call x3, Pallas kernels, late_products(): call(late_kernel, out_shape=jax.ShapeDtypeStruct((2, tokens, tile * count...  12.7 us
    pallas_call x2, Pallas kernels, scores(): call(functools.partial(score_kernel, 1.0 / math.sqrt(tokens), tile, len(p...  10.3 us
    pallas_call x1, Pallas kernels, early_products(): call(early_kernel, out_shape=jax.ShapeDtypeStruct((2, tokens, tile * coun...  9.91 us
    unnamed x20, local copies, waits for them, and re-layouts  6.65 us
    pallas_call x3, Pallas kernels, pick(): call(functools.partial(pick_kernel, counts, tile, instead), out_shape=jax...  5.94 us
  transfers between devices with their start and end apart: 22, of which 11 were waited for; matrix products, arithmetic and copies ran while one was open for 1% of the time, Pallas kernels for 33%

profile of v3, /device:TPU:20, one launch (start us, length us, event | category | flops | bytes accessed | tf_op | source)
XLA Modules:
  0.0 147.8 jit_solution(4096328531607461078)
XLA Ops:
  6.5 1.0 fusion
  8.0 3.5 %collective-permute-start.1 = (bf16[32,2048]{1,0:T(8,128)(2,1)S(1)}, bf16[32,2048]{1,0:T(8,128)(2,1)S(1)}, u32[]{:S(2)}, u32[]{:S(2)}) collective-permute-start(bf16[32,2048]{1,0:T(8,128)(2,1)S(1)} %get-tuple-element.6.refs_0_), channel_id=1, source_target_pairs={{0,8},{1,9},{2,10},{3,11},{4,12},{5,13},{6,14},{7,15},{8,0},{9,1},... | collective-permute-start | bytes 393224 | tf_op jit(solution)/shard_map/ppermute | solution.py:99
  11.5 2.0 %collective-permute-start.6 = (bf16[32,2048]{1,0:T(8,128)(2,1)S(1)}, bf16[32,2048]{1,0:T(8,128)(2,1)S(1)}, u32[]{:S(2)}, u32[]{:S(2)}) collective-permute-start(bf16[32,2048]{1,0:T(8,128)(2,1)S(1)} %get-tuple-element.5.refs_0_), channel_id=1, source_target_pairs={{0,12},{1,13},{2,14},{3,15},{4,0},{5,1},{6,2},{7,3},{8,4},{9,5},{1... | collective-permute-start | bytes 393224 | tf_op jit(solution)/shard_map/ppermute | solution.py:99
  13.5 1.8 %collective-permute-start.5 = (bf16[32,2048]{1,0:T(8,128)(2,1)S(1)}, bf16[32,2048]{1,0:T(8,128)(2,1)S(1)}, u32[]{:S(2)}, u32[]{:S(2)}) collective-permute-start(bf16[32,2048]{1,0:T(8,128)(2,1)S(1)} %get-tuple-element.5.refs_0_), channel_id=1, source_target_pairs={{0,8},{1,9},{2,10},{3,11},{4,12},{5,13},{6,14},{7,15},{8,0},{9,1},... | collective-permute-start | bytes 393224 | tf_op jit(solution)/shard_map/ppermute | solution.py:99
  15.3 0.8 reshape.19
  16.2 1.2 collective-permute-start.4
  17.4 3.2 %collective-permute-done.1.refs_2_ = bf16[32,2048]{1,0:T(8,128)(2,1)S(1)} collective-permute-done((bf16[32,2048]{1,0:T(8,128)(2,1)S(1)}, bf16[32,2048]{1,0:T(8,128)(2,1)S(1)}, u32[]{:S(2)}, u32[]{:S(2)}) %collective-permute-start.1) | collective-permute-done | bytes 131104 | tf_op jit(solution)/shard_map/ppermute | solution.py:99
  20.6 8.3 %collective-permute-done.refs_1_ = bf16[32,2048]{1,0:T(8,128)(2,1)S(1)} collective-permute-done((bf16[32,2048]{1,0:T(8,128)(2,1)S(1)}, bf16[32,2048]{1,0:T(8,128)(2,1)S(1)}, u32[]{:S(2)}, u32[]{:S(2)}) %collective-permute-start) | collective-permute-done | bytes 131104 | tf_op jit(solution)/shard_map/ppermute | solution.py:99
  29.3 1.7 %collective-permute-done.3.other_ref.other_a = bf16[128,2048]{1,0:T(8,128)(2,1)S(1)} collective-permute-done((bf16[128,2048]{1,0:T(8,128)(2,1)S(1)}, bf16[128,2048]{1,0:T(8,128)(2,1)S(1)}, u32[]{:S(2)}, u32[]{:S(2)}) %collective-permute-start.3) | collective-permute-done | bytes 524320 | tf_op jit(solution)/shard_map/ppermute | solution.py:99
  30.9 9.9 %shard_map.47.refs_4_.early_ref = f32[2,256,1792]{2,1,0:T(8,128)S(1)} custom-call(s32[3]{0:T(128)S(1)} %get-tuple-element.10.place_ref, bf16[128,2048]{1,0:T(8,128)(2,1)S(1)} %shard_map.46.same_ref.same_a, bf16[128,2048]{1,0:T(8,128)(2,1)S(1)} %collective-permute-done.3.other_ref.other_a, bf16[4096,3584]{1,0:T(8,128)(2,1)} %bitcast.20, ...), custom_call_target="tpu_custom_call" | custom-call | flops 3758096384 | bytes 14680064 | tf_op jit(solution)/shard_map/pallas_call | solution.py:184
  41.1 1.8 %collective-permute-done.7.other_ref.other_b = bf16[128,2048]{1,0:T(8,128)(2,1)S(1)} collective-permute-done((bf16[128,2048]{1,0:T(8,128)(2,1)S(1)}, bf16[128,2048]{1,0:T(8,128)(2,1)S(1)}, u32[]{:S(2)}, u32[]{:S(2)}) %collective-permute-start.7) | collective-permute-done | bytes 524320 | tf_op jit(solution)/shard_map/ppermute | solution.py:99
  42.9 5.3 %shard_map.49.refs_0_ = bf16[2,256,768]{2,1,0:T(8,128)(2,1)S(1)} custom-call(s32[3]{0:T(128)S(1)} %get-tuple-element.10.place_ref, f32[2,256,1792]{2,1,0:T(8,128)S(1)} %shard_map.47.refs_4_.early_ref, bf16[128,2048]{1,0:T(8,128)(2,1)S(1)} %shard_map.48.same_ref.same_b, bf16[128,2048]{1,0:T(8,128)(2,1)S(1)} %collective-permute-done.7.other_ref.other_b, ...), custom_call_target="tpu_custom_call" | custom-call | flops 1610612736 | bytes 6291456 | tf_op jit(solution)/shard_map/pallas_call | solution.py:219
  48.2 1.6 %collective-permute-start.14 = (bf16[2,256,768]{2,1,0:T(8,128)(2,1)S(1)}, bf16[2,256,768]{2,1,0:T(8,128)(2,1)}, u32[]{:S(2)}, u32[]{:S(2)}) collective-permute-start(bf16[2,256,768]{2,1,0:T(8,128)(2,1)S(1)} %shard_map.49.refs_0_), channel_id=1, source_target_pairs={{16,17},{17,16},{18,19},{19,18},{20,21},{21,20},{22,23},{23,22},{2... | collective-permute-start | bytes 2359304 | tf_op jit(solution)/shard_map/ppermute | solution.py:99
  49.8 3.7 %shard_map.50.refs_0_.refs_1_ = bf16[2,256,512]{2,1,0:T(8,128)(2,1)S(1)} custom-call(s32[3]{0:T(128)S(1)} %get-tuple-element.10.place_ref, f32[2,256,1792]{2,1,0:T(8,128)S(1)} %shard_map.47.refs_4_.early_ref, bf16[128,2048]{1,0:T(8,128)(2,1)S(1)} %shard_map.48.same_ref.same_b, bf16[128,2048]{1,0:T(8,128)(2,1)S(1)} %collective-permute-done.7.other_ref.other_b, ...), custom_call_target="tpu_custom_call" | custom-call | flops 1073741824 | bytes 4194304 | tf_op jit(solution)/shard_map/pallas_call | solution.py:219
  53.5 3.7 %shard_map.51.refs_0_.refs_2_ = bf16[2,256,512]{2,1,0:T(8,128)(2,1)S(1)} custom-call(s32[3]{0:T(128)S(1)} %get-tuple-element.10.place_ref, f32[2,256,1792]{2,1,0:T(8,128)S(1)} %shard_map.47.refs_4_.early_ref, bf16[128,2048]{1,0:T(8,128)(2,1)S(1)} %shard_map.48.same_ref.same_b, bf16[128,2048]{1,0:T(8,128)(2,1)S(1)} %collective-permute-done.7.other_ref.other_b, ...), custom_call_target="tpu_custom_call" | custom-call | flops 1073741824 | bytes 4194304 | tf_op jit(solution)/shard_map/pallas_call | solution.py:219
  57.2 14.9 %shard_map.52.refs_3_.mine_ref = bf16[2,256,1792]{2,1,0:T(8,128)(2,1)S(1)} custom-call(s32[3]{0:T(128)S(1)} %get-tuple-element.11.refs_0_.place_ref, bf16[128,2048]{1,0:T(8,128)(2,1)S(1)} %shard_map.46.same_ref.same_a, bf16[128,2048]{1,0:T(8,128)(2,1)S(1)} %collective-permute-done.3.other_ref.other_a, bf16[128,2048]{1,0:T(8,128)(2,1)S(1)} %shard_map.48.same_ref.same_b, ...), custom_call_target="tpu_custom_call" | custom-call | flops 7516192768 | bytes 29360128 | tf_op jit(solution)/shard_map/pallas_call | solution.py:257
  72.2 1.7 %shard_map.53.refs_4_ = bf16[2,256,256]{2,1,0:T(8,128)(2,1)S(1)} custom-call(s32[5]{0:T(128)S(1)} %stack.59.refs_4_.bases_ref, s32[1,256]{1,0:T(1,128)S(1)} %get-tuple-element.8.refs_1_.picks_ref, bf16[2,256,768]{2,1,0:T(8,128)(2,1)S(1)} %shard_map.49.refs_0_, bf16[2,256,512]{2,1,0:T(8,128)(2,1)S(1)} %shard_map.50.refs_0_.refs_1_, ...), custom_call_target="tpu_custom_call" | custom-call | flops 939524096 | bytes 3670016 | tf_op jit(solution)/shard_map/pallas_call | solution.py:304
  74.4 1.7 %shard_map.54.refs_4_ = bf16[2,256,256]{2,1,0:T(8,128)(2,1)S(1)} custom-call(s32[5]{0:T(128)S(1)} %stack.59.refs_4_.bases_ref, s32[1,256]{1,0:T(1,128)S(1)} %get-tuple-element.7.refs_2_.picks_ref, bf16[2,256,768]{2,1,0:T(8,128)(2,1)S(1)} %shard_map.49.refs_0_, bf16[2,256,512]{2,1,0:T(8,128)(2,1)S(1)} %shard_map.50.refs_0_.refs_1_, ...), custom_call_target="tpu_custom_call" | custom-call | flops 939524096 | bytes 3670016 | tf_op jit(solution)/shard_map/pallas_call | solution.py:304
  76.1 1.6 %collective-permute-start.8 = (bf16[2,256,256]{2,1,0:T(8,128)(2,1)S(1)}, bf16[2,256,256]{2,1,0:T(8,128)(2,1)S(1)}, u32[]{:S(2)}, u32[]{:S(2)}) collective-permute-start(bf16[2,256,256]{2,1,0:T(8,128)(2,1)S(1)} %shard_map.54.refs_4_), channel_id=1, source_target_pairs={{0,1},{1,0},{2,3},{3,2},{4,5},{5,4},{6,7},{7,6},{8,9},{9,8},{10,11... | collective-permute-start | bytes 786440 | tf_op jit(solution)/shard_map/ppermute | solution.py:99
  77.7 2.6 %shard_map.55.mine_ref = bf16[2,256,512]{2,1,0:T(8,128)(2,1)S(1)} custom-call(s32[5]{0:T(128)S(1)} %stack.59.refs_4_.bases_ref, s32[1,512]{1,0:T(1,128)S(1)} %bitcast.19, bf16[2,256,768]{2,1,0:T(8,128)(2,1)S(1)} %shard_map.49.refs_0_, bf16[2,256,512]{2,1,0:T(8,128)(2,1)S(1)} %shard_map.50.refs_0_.refs_1_, ...), custom_call_target="tpu_custom_call" | custom-call | flops 1879048192 | bytes 3670016 | tf_op jit(solution)/shard_map/pallas_call | solution.py:304
  80.3 2.8 %collective-permute-done.9.theirs_ref.refs_0_ = bf16[2,256,256]{2,1,0:T(8,128)(2,1)S(1)} collective-permute-done((bf16[2,256,256]{2,1,0:T(8,128)(2,1)S(1)}, bf16[2,256,256]{2,1,0:T(8,128)(2,1)S(1)}, u32[]{:S(2)}, u32[]{:S(2)}) %collective-permute-start.9) | collective-permute-done | bytes 262176 | tf_op jit(solution)/shard_map/ppermute | solution.py:99
  83.4 3.2 %collective-permute-start.10 = (bf16[256,256]{1,0:T(8,128)(2,1)S(1)}, bf16[256,256]{1,0:T(8,128)(2,1)S(1)}, u32[]{:S(2)}, u32[]{:S(2)}) collective-permute-start(bf16[256,256]{1,0:T(8,128)(2,1)S(1)} %shard_map.56), channel_id=1, source_target_pairs={{0,16},{1,17},{2,18},{3,19},{4,20},{5,21},{6,22},{7,23},{8,24},{9,... | collective-permute-start | bytes 393224 | tf_op jit(solution)/shard_map/ppermute | solution.py:99
  86.6 1.3 collective-permute-done.8.theirs_ref.refs_1_
  87.9 1.2 collective-permute-done.10.given_ref
  89.1 1.0 shard_map.57
  90.1 0.7 copy-done.2
  90.8 1.8 %shard_map.59.refs_2_ = bf16[256,768]{1,0:T(8,128)(2,1)S(1)} custom-call(bf16[2,256,1792]{2,1,0:T(8,128)(2,1)S(1)} %shard_map.52.refs_3_.mine_ref, bf16[2,256,768]{2,1,0:T(8,128)(2,1)} %collective-permute-done.14.refs_0_), custom_call_target="tpu_custom_call" | custom-call | flops 3932160 | bytes 1966080 | tf_op jit(solution)/shard_map/pallas_call | solution.py:343
  92.6 1.3 collective-permute-start.15
  93.9 0.7 collective-permute-start.18
  94.6 9.0 %collective-permute-done.15.refs_0_ = bf16[256,768]{1,0:T(8,128)(2,1)S(1)} collective-permute-done((bf16[256,768]{1,0:T(8,128)(2,1)S(1)}, bf16[256,768]{1,0:T(8,128)(2,1)S(1)}, u32[]{:S(2)}, u32[]{:S(2)}) %collective-permute-start.15) | collective-permute-done | bytes 393248 | tf_op jit(solution)/shard_map/ppermute | solution.py:99
  103.6 2.4 %collective-permute-start.16 = (bf16[256,768]{1,0:T(8,128)(2,1)S(1)}, bf16[256,768]{1,0:T(8,128)(2,1)S(1)}, u32[]{:S(2)}, u32[]{:S(2)}) collective-permute-start(bf16[256,768]{1,0:T(8,128)(2,1)S(1)} %collective-permute-done.15.refs_0_), channel_id=1, source_target_pairs={{0,1},{1,0},{2,3},{3,2},{4,5},{5,4},{6,7},{7,6},{8,9},{9,8},{10,11... | collective-permute-start | bytes 1179656 | tf_op jit(solution)/shard_map/ppermute | solution.py:99
  106.5 1.3 collective-permute-start.19
  107.8 5.9 %collective-permute-done.16.refs_1_ = bf16[256,768]{1,0:T(8,128)(2,1)S(1)} collective-permute-done((bf16[256,768]{1,0:T(8,128)(2,1)S(1)}, bf16[256,768]{1,0:T(8,128)(2,1)S(1)}, u32[]{:S(2)}, u32[]{:S(2)}) %collective-permute-start.16) | collective-permute-done | bytes 393248 | tf_op jit(solution)/shard_map/ppermute | solution.py:99
  113.7 1.3 collective-permute-start.17
  115.0 1.2 collective-permute-done.19.first_ref.refs_4_
  116.2 0.6 collective-permute-start.20
  116.8 0.9 copy-done.3
  118.1 0.7 collective-permute-start.13
  118.8 1.3 collective-permute-start.12
  120.1 1.3 collective-permute-start.11
  121.4 4.1 %collective-permute-done.20.refs_5_.refs_7_ = bf16[256,512]{1,0:T(8,128)(2,1)S(1)} collective-permute-done((bf16[256,512]{1,0:T(8,128)(2,1)S(1)}, bf16[256,512]{1,0:T(8,128)(2,1)S(1)}, u32[]{:S(2)}, u32[]{:S(2)}) %collective-permute-start.20) | collective-permute-done | bytes 262176 | tf_op jit(solution)/shard_map/ppermute | solution.py:99
  125.6 0.8 copy-done.8
  126.4 1.2 copy-done
  127.6 1.0 copy-done.5
  128.6 1.0 copy-done.7
  129.6 1.0 copy-done.9
  130.6 6.5 %shard_map.62.refs_4_ = bf16[2048,3584]{1,0:T(8,128)(2,1)} custom-call(s32[3]{0:T(128)S(1)} %get-tuple-element.12.refs_6_.where_ref, bf16[2048,256]{1,0:T(8,128)(2,1)S(1)} %copy-done, bf16[256,768]{1,0:T(8,128)(2,1)S(1)} %copy-done.5, bf16[256,768]{1,0:T(8,128)(2,1)S(1)} %copy-done.7, bf16[256,768]{1,0:T(8,128)(2,1)S(1)} %shard_map.59.refs_2_, ...), custom_call_target="tpu_custom_call" | custom-call | flops 2684354560 | bytes 10485760 | tf_op jit(solution)/shard_map/pallas_call | solution.py:448
  137.1 3.8 %shard_map.63 = bf16[2048,3584]{1,0:T(8,128)(2,1)} custom-call(s32[3]{0:T(128)S(1)} %get-tuple-element.9.refs_7_.where_ref, bf16[2048,256]{1,0:T(8,128)(2,1)S(1)} %copy-done.1, bf16[256,512]{1,0:T(8,128)(2,1)S(1)} %collective-permute-done.11.refs_0_, bf16[256,512]{1,0:T(8,128)(2,1)S(1)} %collective-permute-done.12.refs_1_, ...), custom_call_target="tpu_custom_call", output_to_operand_aliasing={{}: (6, {})} | custom-call | flops 1073741824 | bytes 4194304 | tf_op jit(solution)/shard_map/pallas_call | solution.py:448
  (43 shorter events, 3.0 us)
Async XLA Ops:
  6.5 119.8 %all-gather.2.cloned.1.call-start = ((), (), s32[]{:S(2)}) async-start(), calls=%async_computation | async-start | bytes 1179648 | tf_op jit(solution)/shard_map/all_gather | solution.py:551
  7.5 8.7 %collective-permute-start.2 = (bf16[32,2048]{1,0:T(8,128)(2,1)S(1)}, bf16[32,2048]{1,0:T(8,128)(2,1)S(1)}, u32[]{:S(2)}, u32[]{:S(2)}) collective-permute-start(bf16[32,2048]{1,0:T(8,128)(2,1)S(1)} %get-tuple-element.6.refs_0_), channel_id=1, source_target_pairs={{0,12},{1,13},{2,14},{3,15},{4,0},{5,1},{6,2},{7,3},{8,4},{9,5},{1... | collective-permute-start | bytes 393224 | tf_op jit(solution)/shard_map/ppermute | solution.py:99
  8.0 12.6 %collective-permute-start.1 = (bf16[32,2048]{1,0:T(8,128)(2,1)S(1)}, bf16[32,2048]{1,0:T(8,128)(2,1)S(1)}, u32[]{:S(2)}, u32[]{:S(2)}) collective-permute-start(bf16[32,2048]{1,0:T(8,128)(2,1)S(1)} %get-tuple-element.6.refs_0_), channel_id=1, source_target_pairs={{0,8},{1,9},{2,10},{3,11},{4,12},{5,13},{6,14},{7,15},{8,0},{9,1},... | collective-permute-start | bytes 393224 | tf_op jit(solution)/shard_map/ppermute | solution.py:99
  11.5 17.4 %collective-permute-start = (bf16[32,2048]{1,0:T(8,128)(2,1)S(1)}, bf16[32,2048]{1,0:T(8,128)(2,1)S(1)}, u32[]{:S(2)}, u32[]{:S(2)}) collective-permute-start(bf16[32,2048]{1,0:T(8,128)(2,1)S(1)} %get-tuple-element.6.refs_0_), channel_id=1, source_target_pairs={{0,4},{1,5},{2,6},{3,7},{4,8},{5,9},{6,10},{7,11},{8,12},{9,13},{1... | collective-permute-start | bytes 393224 | tf_op jit(solution)/shard_map/ppermute | solution.py:99
  11.5 29.3 %collective-permute-start.6 = (bf16[32,2048]{1,0:T(8,128)(2,1)S(1)}, bf16[32,2048]{1,0:T(8,128)(2,1)S(1)}, u32[]{:S(2)}, u32[]{:S(2)}) collective-permute-start(bf16[32,2048]{1,0:T(8,128)(2,1)S(1)} %get-tuple-element.5.refs_0_), channel_id=1, source_target_pairs={{0,12},{1,13},{2,14},{3,15},{4,0},{5,1},{6,2},{7,3},{8,4},{9,5},{1... | collective-permute-start | bytes 393224 | tf_op jit(solution)/shard_map/ppermute | solution.py:99
  13.5 27.3 %collective-permute-start.5 = (bf16[32,2048]{1,0:T(8,128)(2,1)S(1)}, bf16[32,2048]{1,0:T(8,128)(2,1)S(1)}, u32[]{:S(2)}, u32[]{:S(2)}) collective-permute-start(bf16[32,2048]{1,0:T(8,128)(2,1)S(1)} %get-tuple-element.5.refs_0_), channel_id=1, source_target_pairs={{0,8},{1,9},{2,10},{3,11},{4,12},{5,13},{6,14},{7,15},{8,0},{9,1},... | collective-permute-start | bytes 393224 | tf_op jit(solution)/shard_map/ppermute | solution.py:99
  16.2 24.7 %collective-permute-start.4 = (bf16[32,2048]{1,0:T(8,128)(2,1)S(1)}, bf16[32,2048]{1,0:T(8,128)(2,1)S(1)}, u32[]{:S(2)}, u32[]{:S(2)}) collective-permute-start(bf16[32,2048]{1,0:T(8,128)(2,1)S(1)} %get-tuple-element.5.refs_0_), channel_id=1, source_target_pairs={{0,4},{1,5},{2,6},{3,7},{4,8},{5,9},{6,10},{7,11},{8,12},{9,13},{1... | collective-permute-start | bytes 393224 | tf_op jit(solution)/shard_map/ppermute | solution.py:99
  29.0 2.0 %collective-permute-start.3 = (bf16[128,2048]{1,0:T(8,128)(2,1)S(1)}, bf16[128,2048]{1,0:T(8,128)(2,1)S(1)}, u32[]{:S(2)}, u32[]{:S(2)}) collective-permute-start(bf16[128,2048]{1,0:T(8,128)(2,1)S(1)} %shard_map.46.same_ref.same_a), channel_id=1, source_target_pairs={{0,2},{1,3},{2,0},{3,1},{4,6},{5,7},{6,4},{7,5},{8,10},{9,11},{10,... | collective-permute-start | bytes 1572872 | tf_op jit(solution)/shard_map/ppermute | solution.py:99
  40.9 2.0 %collective-permute-start.7 = (bf16[128,2048]{1,0:T(8,128)(2,1)S(1)}, bf16[128,2048]{1,0:T(8,128)(2,1)S(1)}, u32[]{:S(2)}, u32[]{:S(2)}) collective-permute-start(bf16[128,2048]{1,0:T(8,128)(2,1)S(1)} %shard_map.48.same_ref.same_b), channel_id=1, source_target_pairs={{0,2},{1,3},{2,0},{3,1},{4,6},{5,7},{6,4},{7,5},{8,10},{9,11},{10,... | collective-permute-start | bytes 1572872 | tf_op jit(solution)/shard_map/ppermute | solution.py:99
  48.2 42.6 %collective-permute-start.14 = (bf16[2,256,768]{2,1,0:T(8,128)(2,1)S(1)}, bf16[2,256,768]{2,1,0:T(8,128)(2,1)}, u32[]{:S(2)}, u32[]{:S(2)}) collective-permute-start(bf16[2,256,768]{2,1,0:T(8,128)(2,1)S(1)} %shard_map.49.refs_0_), channel_id=1, source_target_pairs={{16,17},{17,16},{18,19},{19,18},{20,21},{21,20},{22,23},{23,22},{2... | collective-permute-start | bytes 2359304 | tf_op jit(solution)/shard_map/ppermute | solution.py:99
  73.8 9.2 %collective-permute-start.9 = (bf16[2,256,256]{2,1,0:T(8,128)(2,1)S(1)}, bf16[2,256,256]{2,1,0:T(8,128)(2,1)S(1)}, u32[]{:S(2)}, u32[]{:S(2)}) collective-permute-start(bf16[2,256,256]{2,1,0:T(8,128)(2,1)S(1)} %shard_map.53.refs_4_), channel_id=1, source_target_pairs={{0,1},{1,0},{2,3},{3,2},{4,5},{5,4},{6,7},{7,6},{8,9},{9,8},{10,11... | collective-permute-start | bytes 786440 | tf_op jit(solution)/shard_map/ppermute | solution.py:99
  76.1 11.8 %collective-permute-start.8 = (bf16[2,256,256]{2,1,0:T(8,128)(2,1)S(1)}, bf16[2,256,256]{2,1,0:T(8,128)(2,1)S(1)}, u32[]{:S(2)}, u32[]{:S(2)}) collective-permute-start(bf16[2,256,256]{2,1,0:T(8,128)(2,1)S(1)} %shard_map.54.refs_4_), channel_id=1, source_target_pairs={{0,1},{1,0},{2,3},{3,2},{4,5},{5,4},{6,7},{7,6},{8,9},{9,8},{10,11... | collective-permute-start | bytes 786440 | tf_op jit(solution)/shard_map/ppermute | solution.py:99
  83.4 5.7 %collective-permute-start.10 = (bf16[256,256]{1,0:T(8,128)(2,1)S(1)}, bf16[256,256]{1,0:T(8,128)(2,1)S(1)}, u32[]{:S(2)}, u32[]{:S(2)}) collective-permute-start(bf16[256,256]{1,0:T(8,128)(2,1)S(1)} %shard_map.56), channel_id=1, source_target_pairs={{0,16},{1,17},{2,18},{3,19},{4,20},{5,21},{6,22},{7,23},{8,24},{9,... | collective-permute-start | bytes 393224 | tf_op jit(solution)/shard_map/ppermute | solution.py:99
  90.1 0.7 copy-start.2
  92.6 11.0 %collective-permute-start.15 = (bf16[256,768]{1,0:T(8,128)(2,1)S(1)}, bf16[256,768]{1,0:T(8,128)(2,1)S(1)}, u32[]{:S(2)}, u32[]{:S(2)}) collective-permute-start(bf16[256,768]{1,0:T(8,128)(2,1)S(1)} %shard_map.59.refs_2_), channel_id=1, source_target_pairs={{16,0},{17,1},{18,2},{19,3},{20,4},{21,5},{22,6},{23,7},{24,8},{25... | collective-permute-start | bytes 1179656 | tf_op jit(solution)/shard_map/ppermute | solution.py:99
  93.9 12.2 %collective-permute-start.18 = (bf16[2,256,512]{2,1,0:T(8,128)(2,1)S(1)}, bf16[2,256,512]{2,1,0:T(8,128)(2,1)S(1)}, u32[]{:S(2)}, u32[]{:S(2)}) collective-permute-start(bf16[2,256,512]{2,1,0:T(8,128)(2,1)S(1)} %shard_map.50.refs_0_.refs_1_), channel_id=1, source_target_pairs={{16,17},{17,16},{18,19},{19,18},{20,21},{21,20},{22,23},{23,22},{2... | collective-permute-start | bytes 1572872 | tf_op jit(solution)/shard_map/ppermute | solution.py:99
  103.6 10.1 %copy-start.4 = (bf16[256,768]{1,0:T(8,128)(2,1)}, bf16[256,768]{1,0:T(8,128)(2,1)S(1)}, u32[]{:S(2)}) copy-start(bf16[256,768]{1,0:T(8,128)(2,1)S(1)} %collective-permute-done.15.refs_0_) | copy-start | bytes 1179652
  103.6 10.1 %collective-permute-start.16 = (bf16[256,768]{1,0:T(8,128)(2,1)S(1)}, bf16[256,768]{1,0:T(8,128)(2,1)S(1)}, u32[]{:S(2)}, u32[]{:S(2)}) collective-permute-start(bf16[256,768]{1,0:T(8,128)(2,1)S(1)} %collective-permute-done.15.refs_0_), channel_id=1, source_target_pairs={{0,1},{1,0},{2,3},{3,2},{4,5},{5,4},{6,7},{7,6},{8,9},{9,8},{10,11... | collective-permute-start | bytes 1179656 | tf_op jit(solution)/shard_map/ppermute | solution.py:99
  106.5 9.7 %collective-permute-start.19 = (bf16[256,512]{1,0:T(8,128)(2,1)S(1)}, bf16[256,512]{1,0:T(8,128)(2,1)S(1)}, u32[]{:S(2)}, u32[]{:S(2)}) collective-permute-start(bf16[256,512]{1,0:T(8,128)(2,1)S(1)} %shard_map.60.second_ref.refs_6_), channel_id=1, source_target_pairs={{16,0},{17,1},{18,2},{19,3},{20,4},{21,5},{22,6},{23,7},{24,8},{25... | collective-permute-start | bytes 786440 | tf_op jit(solution)/shard_map/ppermute | solution.py:99
  113.7 11.9 %copy-start.6 = (bf16[256,768]{1,0:T(8,128)(2,1)}, bf16[256,768]{1,0:T(8,128)(2,1)S(1)}, u32[]{:S(2)}) copy-start(bf16[256,768]{1,0:T(8,128)(2,1)S(1)} %collective-permute-done.16.refs_1_) | copy-start | bytes 1179652
  113.7 11.9 %collective-permute-start.17 = (bf16[256,768]{1,0:T(8,128)(2,1)S(1)}, bf16[256,768]{1,0:T(8,128)(2,1)S(1)}, u32[]{:S(2)}, u32[]{:S(2)}) collective-permute-start(bf16[256,768]{1,0:T(8,128)(2,1)S(1)} %collective-permute-done.16.refs_1_), channel_id=1, source_target_pairs={{0,16},{1,17},{2,18},{3,19},{4,20},{5,21},{6,22},{7,23},{8,24},{9,... | collective-permute-start | bytes 1179656 | tf_op jit(solution)/shard_map/ppermute | solution.py:99
  116.2 9.4 %collective-permute-start.20 = (bf16[256,512]{1,0:T(8,128)(2,1)S(1)}, bf16[256,512]{1,0:T(8,128)(2,1)S(1)}, u32[]{:S(2)}, u32[]{:S(2)}) collective-permute-start(bf16[256,512]{1,0:T(8,128)(2,1)S(1)} %shard_map.61), channel_id=1, source_target_pairs={{0,1},{1,0},{2,3},{3,2},{4,5},{5,4},{6,7},{7,6},{8,9},{9,8},{10,11... | collective-permute-start | bytes 786440 | tf_op jit(solution)/shard_map/ppermute | solution.py:99
  116.8 0.9 copy-start.3
  118.1 18.9 %collective-permute-start.13 = (bf16[256,512]{1,0:T(8,128)(2,1)S(1)}, bf16[256,512]{1,0:T(8,128)(2,1)S(1)}, u32[]{:S(2)}, u32[]{:S(2)}) collective-permute-start(bf16[256,512]{1,0:T(8,128)(2,1)S(1)} %shard_map.58.refs_2_), channel_id=1, source_target_pairs={{16,17},{17,16},{18,19},{19,18},{20,21},{21,20},{22,23},{23,22},{2... | collective-permute-start | bytes 786440 | tf_op jit(solution)/shard_map/ppermute | solution.py:99
  118.8 18.3 %collective-permute-start.12 = (bf16[256,512]{1,0:T(8,128)(2,1)S(1)}, bf16[256,512]{1,0:T(8,128)(2,1)S(1)}, u32[]{:S(2)}, u32[]{:S(2)}) collective-permute-start(bf16[256,512]{1,0:T(8,128)(2,1)S(1)} %shard_map.58.refs_2_), channel_id=1, source_target_pairs={{16,1},{17,0},{18,3},{19,2},{20,5},{21,4},{22,7},{23,6},{24,9},{25... | collective-permute-start | bytes 786440 | tf_op jit(solution)/shard_map/ppermute | solution.py:99
  120.1 17.0 %collective-permute-start.11 = (bf16[256,512]{1,0:T(8,128)(2,1)S(1)}, bf16[256,512]{1,0:T(8,128)(2,1)S(1)}, u32[]{:S(2)}, u32[]{:S(2)}) collective-permute-start(bf16[256,512]{1,0:T(8,128)(2,1)S(1)} %shard_map.58.refs_2_), channel_id=1, source_target_pairs={{16,0},{17,1},{18,2},{19,3},{20,4},{21,5},{22,6},{23,7},{24,8},{25... | collective-permute-start | bytes 786440 | tf_op jit(solution)/shard_map/ppermute | solution.py:99
  125.6 0.8 copy-start.8
  126.4 1.2 copy-start
  127.6 1.0 copy-start.5
  128.6 1.0 copy-start.7
  129.6 1.0 copy-start.9
  130.6 6.5 %copy-start.1 = (bf16[2048,256]{1,0:T(8,128)(2,1)S(1)}, bf16[2048,256]{1,0:T(8,128)(2,1)}, u32[]{:S(2)}) copy-start(bf16[2048,256]{1,0:T(8,128)(2,1)} %all-gather.2.cloned.1.call-done.panel_ref) | copy-start | bytes 3145732
Sparse Core Ops, SparseCore 0:
  90.9 22.4 all-gather.1

commit v4 on v3

v4 whole, which is shorter than its diff:
```python
import functools
import math

import jax
import jax.numpy as jnp
from jax import lax
from jax.experimental import pallas as pl
from jax.experimental.pallas import tpu as pltpu
from jax.sharding import PartitionSpec as P

epsilon = 1e-05
AXES = ("mp", "dp", "tensor")
MIB = 1 << 20


def from_partner(block, axis, distance):
    count = lax.axis_size(axis)
    route = []
    for low in range(count):
        high = low | 1 << distance
        if high != low and high < count:
            route += [(low, high), (high, low)]
    return lax.ppermute(block, axis, route)


def cross_models(full_units, panel_own, panel_next, model_index):
    other_units, other_panel = from_partner((full_units, panel_next), "mp", 0)
    is_first = model_index == 0
    return (
        jnp.where(is_first, panel_own, other_panel),
        jnp.where(is_first, other_units, full_units),
    )


def general_body(acts, gate_w, up_w, panel_units):
    model_index = lax.axis_index("mp")
    unit_block = lax.axis_index("dp")
    n_model = lax.axis_size("mp")
    n_data = lax.axis_size("dp")
    n_width = lax.axis_size("tensor")
    weight_gate = gate_w[0]
    weight_up = up_w[0]
    units = weight_gate.shape[1]
    gathered = lax.all_gather(acts[0], "dp", axis=0, tiled=True)
    tokens = gathered.shape[0]
    token_share = tokens // n_width
    score_scale = 1.0 / math.sqrt(tokens)
    panel_picks = panel_units.reshape(n_model, n_width, n_data, -1)
    panel_picks = (
        lax.dynamic_index_in_dim(panel_picks, unit_block, axis=2, keepdims=False)
        - unit_block * units
    )
    gate_part = jnp.dot(gathered, weight_gate, preferred_element_type=jnp.float32)
    up_part = jnp.dot(gathered, weight_up, preferred_element_type=jnp.float32)
    summed = lax.psum_scatter(
        jnp.concatenate([gate_part, up_part], axis=1).astype(jnp.bfloat16),
        "tensor",
        scatter_dimension=0,
        tiled=True,
    ).astype(jnp.float32)
    hidden = (jax.nn.silu(summed[:, :units]) * summed[:, units:]).astype(jnp.bfloat16)
    wide_hidden = hidden.astype(jnp.float32)
    totals = lax.psum(
        (jnp.sum(wide_hidden, axis=0), jnp.sum(wide_hidden * wide_hidden, axis=0)), "tensor"
    )
    unit_mean = totals[0] / tokens
    unit_var = totals[1] / tokens - unit_mean * unit_mean
    scored = ((wide_hidden - unit_mean) * lax.rsqrt(unit_var + epsilon)).astype(jnp.bfloat16)
    full_units = lax.all_gather(scored, "tensor", axis=0, tiled=True)
    order_list = panel_picks.transpose(1, 0, 2).reshape(-1)
    chosen = jnp.take(scored, order_list, axis=1).reshape(token_share, n_width, -1)
    moved_rows = lax.all_to_all(chosen, "tensor", split_axis=1, concat_axis=0, tiled=True)
    moved_rows = moved_rows.reshape(tokens, n_model, -1)
    panel_cols = lax.all_gather(moved_rows, "dp", axis=2, tiled=True)
    mine_a, mine_b = cross_models(full_units, panel_cols[:, 0], panel_cols[:, 1], model_index)
    result = lax.dot_general(
        mine_a, mine_b, (((0,), (0,)), ((), ())), preferred_element_type=jnp.float32
    )
    return (result * score_scale).astype(jnp.bfloat16)


CHIPS = 4


def routes(sizes, move):
    n_model, n_data, n_width = sizes
    pairs = []
    for m in range(n_model):
        for d in range(n_data):
            for t in range(n_width):
                to = move(m, d, t)
                if to is not None:
                    source = (m * n_data + d) * n_width + t
                    pairs.append((source, (to[0] * n_data + to[1]) * n_width + to[2]))
    return pairs


def send(block, sizes, move):
    return lax.ppermute(block, AXES, routes(sizes, move))


def other_core(m, d, t):
    return m, d ^ 1, t


def shifted(step):
    def move(m, d, t):
        return m, (d + 2 * step) % (2 * CHIPS), t

    return move


def shifts(block, sizes):
    came = [send(block, sizes, shifted(step)) for step in (1, CHIPS - 1, 2)]
    return [block, came[0], came[2], came[1]]


def join_kernel(count, *refs):
    rows = refs[0].shape[0]
    for i in range(count):
        refs[-1][i * rows : (i + 1) * rows, :] = refs[i][...]


def join(blocks, after):
    rows, width = blocks[0].shape
    count = len(blocks)
    vmem = pl.BlockSpec(memory_space=pltpu.VMEM)
    return call(
        functools.partial(join_kernel, count),
        out_shape=jax.ShapeDtypeStruct((count * rows, width), blocks[0].dtype),
        in_specs=[vmem] * count + [pl.BlockSpec(memory_space=pl.ANY)] * len(after),
        out_specs=vmem,
        flops=0,
        moved=4 * count * rows * width,
        vmem=16,
    )(*blocks, *after)


def swapped(block, sizes, distance):
    return send(block, sizes, lambda m, d, t: (m, d ^ (2 * distance), t))


SWAPS = (0, 2, 1, 3)


def canonical(index, chip, core):
    line = lax.rem(chip + CHIPS - index % CHIPS, CHIPS)
    return line * 2 + (core if index < CHIPS else 1 - core)


def call(kernel, *, flops, moved, vmem, **rest):
    return pl.pallas_call(
        kernel,
        compiler_params=pltpu.CompilerParams(vmem_limit_bytes=vmem * MIB),
        cost_estimate=pl.CostEstimate(flops=flops, bytes_accessed=moved, transcendentals=0),
        **rest,
    )


def choose_kernel(model_ref, first_ref, second_ref, out_ref):
    for holder, ref in enumerate((first_ref, second_ref)):

        @pl.when(model_ref[0] == holder)
        def _():
            out_ref[...] = ref[...]


def choose(model_number, first, second):
    vmem = pl.BlockSpec(memory_space=pltpu.VMEM)
    return call(
        choose_kernel,
        out_shape=jax.ShapeDtypeStruct(first.shape, first.dtype),
        in_specs=[pl.BlockSpec(memory_space=pltpu.SMEM), vmem, vmem],
        out_specs=vmem,
        flops=0,
        moved=4 * first.size,
        vmem=16,
    )(model_number, first, second)


def products_kernel(place_ref, same_ref, other_ref, gate_ref, up_ref, *refs):
    out_ref = refs[-1]
    rows = same_ref.shape[0] // CHIPS
    x = jnp.concatenate([same_ref[...], other_ref[...]], axis=0)
    for which, weight_ref in enumerate((gate_ref, up_ref)):
        total = jnp.dot(x, weight_ref[...], preferred_element_type=jnp.float32)
        total = total.astype(jnp.bfloat16)
        for i in range(2 * CHIPS):
            start = pl.multiple_of(canonical(i, place_ref[1], place_ref[2]) * rows, rows)
            out_ref[which, pl.ds(start, rows), :] = total[i * rows : (i + 1) * rows]


def products(place, same, other, gate, up, tile, first, count, after):
    tokens, width = 2 * same.shape[0], same.shape[1]
    weights = pl.BlockSpec((width, tile), lambda i, place_ref: (0, place_ref[0] + first + i))
    whole = pl.BlockSpec(same.shape, lambda i, place_ref: (0, 0))
    return call(
        products_kernel,
        out_shape=jax.ShapeDtypeStruct((2, tokens, tile * count), jnp.bfloat16),
        grid_spec=pltpu.PrefetchScalarGridSpec(
            num_scalar_prefetch=1,
            grid=(count,),
            in_specs=[whole, whole, weights, weights]
            + [pl.BlockSpec(memory_space=pl.ANY)] * len(after),
            out_specs=pl.BlockSpec((2, tokens, tile), lambda i, place_ref: (0, 0, i)),
        ),
        flops=4 * tokens * width * tile * count,
        moved=4 * width * tile * count,
        vmem=38,
    )(place, same, other, gate, up, *after)


def pick_kernel(counts, tile, bases_ref, picks_ref, *refs):
    out_ref = refs[-1]
    tokens, picked = out_ref.shape[1:]

    @pl.when(bases_ref[len(counts)] == 0)
    def _():
        total = jnp.zeros((2 * tokens, picked), jnp.float32)
        for part, (ref, count) in enumerate(zip(refs[: len(counts)], counts)):
            for i in range(count):
                base = bases_ref[part] + i * tile
                unit = lax.broadcasted_iota(jnp.int32, (tile, picked), 0) + base
                chosen = jnp.where(unit == picks_ref[...], 1.0, 0.0).astype(jnp.bfloat16)
                block = ref[:, :, i * tile : (i + 1) * tile].reshape(2 * tokens, tile)
                total += jnp.dot(block, chosen, preferred_element_type=jnp.float32)
        out_ref[...] = total.astype(jnp.bfloat16).reshape(2, tokens, picked)

    @pl.when(bases_ref[len(counts)] == 1)
    def _():
        out_ref[...] = jnp.zeros_like(out_ref)


def pick(bases, picks, parts, tile, after):
    tokens = parts[0].shape[1]
    picked = picks.shape[1]
    counts = [part.shape[2] // tile for part in parts]
    vmem = pl.BlockSpec(memory_space=pltpu.VMEM)
    return call(
        functools.partial(pick_kernel, counts, tile),
        out_shape=jax.ShapeDtypeStruct((2, tokens, picked), jnp.bfloat16),
        in_specs=[pl.BlockSpec(memory_space=pltpu.SMEM), vmem]
        + [vmem] * len(parts)
        + [pl.BlockSpec(memory_space=pl.ANY)] * len(after),
        out_specs=vmem,
        flops=4 * tokens * picked * tile * sum(counts),
        moved=4 * tokens * tile * sum(counts),
        vmem=16,
    )(bases, picks, *parts, *after)


def zscore(mine, theirs):
    tokens = mine.shape[1]
    gate = mine[0].astype(jnp.float32) + theirs[0].astype(jnp.float32)
    up = mine[1].astype(jnp.float32) + theirs[1].astype(jnp.float32)
    hidden = (gate / (1.0 + jnp.exp(-gate)) * up).astype(jnp.bfloat16).astype(jnp.float32)
    mean = jnp.sum(hidden, axis=0, keepdims=True) / tokens
    var = jnp.sum(hidden * hidden, axis=0, keepdims=True) / tokens - mean * mean
    return (hidden - mean) * lax.rsqrt(var + epsilon)


def unit_kernel(mine_ref, theirs_ref, *refs):
    refs[-1][...] = zscore(mine_ref[...], theirs_ref[...]).astype(jnp.bfloat16)


def unit_scores(mine, theirs, tile, first, after):
    _, tokens, count = theirs.shape
    return call(
        unit_kernel,
        out_shape=jax.ShapeDtypeStruct((tokens, count), jnp.bfloat16),
        grid=(count // tile,),
        in_specs=[
            pl.BlockSpec((2, tokens, tile), lambda i: (0, 0, first + i)),
            pl.BlockSpec((2, tokens, tile), lambda i: (0, 0, i)),
        ]
        + [pl.BlockSpec(memory_space=pl.ANY)] * len(after),
        out_specs=pl.BlockSpec((tokens, tile), lambda i: (0, i)),
        flops=20 * tokens * count,
        moved=10 * tokens * count,
        vmem=16,
    )(mine, theirs, *after)


def panel_kernel(mine_ref, theirs_ref, out_ref):
    out_ref[...] = zscore(mine_ref[...], theirs_ref[...]).T.astype(jnp.bfloat16)


def panel_kernel_or(model_ref, mine_ref, theirs_ref, given_ref, *refs):
    out_ref = refs[-1]

    @pl.when(model_ref[0] == 0)
    def _():
        panel_kernel(mine_ref, theirs_ref, out_ref)

    @pl.when(model_ref[0] == 1)
    def _():
        out_ref[...] = given_ref[...]


def panel_scores(mine, theirs, first, given=(), after=()):
    _, tokens, count = theirs.shape
    rows = pl.BlockSpec((count, tokens), lambda i: (0, 0))
    units = [
        pl.BlockSpec((2, tokens, count), lambda i: (0, 0, first)),
        pl.BlockSpec((2, tokens, count), lambda i: (0, 0, 0)),
    ]
    return call(
        panel_kernel_or if given else panel_kernel,
        out_shape=jax.ShapeDtypeStruct((count, tokens), jnp.bfloat16),
        grid=(1,),
        in_specs=(
            [pl.BlockSpec(memory_space=pltpu.SMEM), *units, rows]
            + [pl.BlockSpec(memory_space=pl.ANY)] * len(after)
            if given
            else units
        ),
        out_specs=rows,
        flops=20 * tokens * count,
        moved=10 * tokens * count,
        vmem=16,
    )(*given[:1], mine, theirs, *given[1:], *after)


def score_kernel(scale, tile, cores, n_pieces, has_before, where_ref, *refs):
    panels, refs = refs[: len(cores)], refs[len(cores) :]
    pieces = refs[: 4 * n_pieces]
    out_ref, panel_ref, near_ref, far_ref, block_ref, in_sems, out_sems = refs[
        4 * n_pieces + has_before :
    ]
    model, chip, core, near_column, far_column = (where_ref[i] for i in range(5))
    rows = block_ref.shape[2]
    columns = block_ref.shape[3]

    def fetch(at):
        copies = [
            pltpu.make_async_copy(ref, panel_ref.at[i], in_sems.at[i])
            for i, ref in enumerate(panels)
        ]
        for far, into in enumerate((near_ref, far_ref)):
            start = 0
            for piece in range(n_pieces):
                ref = pieces[4 * piece + at + far]
                stop = start + ref.shape[1]
                copies.append(
                    pltpu.make_async_copy(
                        ref, into.at[:, start:stop], in_sems.at[len(cores) + 2 * piece + far]
                    )
                )
                start = stop
        for copy in copies:
            copy.start()
        for copy in copies:
            copy.wait()

    for holder in range(2):

        @pl.when(model == holder)
        def _():
            fetch(2 * holder)

    copies = []
    for which, other in enumerate(cores):
        for pair in range(CHIPS // 2):
            panel = panel_ref[which, 2 * pair * rows : (2 * pair + 2) * rows, :]
            for units_ref, column in ((near_ref, near_column), (far_ref, far_column)):
                slot = len(copies) // 2
                for start in range(0, columns, tile):
                    total = jnp.dot(
                        panel,
                        units_ref[:, start : start + tile],
                        preferred_element_type=jnp.float32,
                    )
                    block_ref[slot, :, :, start : start + tile] = (
                        (total * scale).astype(jnp.bfloat16).reshape(2, rows, tile)
                    )
                for i in range(2):
                    line = lax.bitwise_xor(chip, SWAPS[2 * pair + i])
                    place = line * 2 + (1 - core if other else core)
                    copies.append(
                        pltpu.make_async_copy(
                            block_ref.at[slot, i],
                            out_ref.at[
                                pl.ds(pl.multiple_of(place * rows, rows), rows),
                                pl.ds(pl.multiple_of(column, 128), columns),
                            ],
                            out_sems.at[slot, i],
                        )
                    )
                    copies[-1].start()
    for copy in copies:
        copy.wait()


def scores(where, panels, cores, pieces, tile, shape, before, after):
    rows, tokens = panels[0].shape
    columns = sum(piece[0].shape[1] for piece in pieces)
    slots = len(panels) * CHIPS
    anywhere = pl.BlockSpec(memory_space=pl.ANY)
    flat = [array for piece in pieces for array in piece]
    return call(
        functools.partial(
            score_kernel,
            1.0 / math.sqrt(tokens),
            tile,
            cores,
            len(pieces),
            len(before) + len(after),
        ),
        out_shape=jax.ShapeDtypeStruct(shape, jnp.bfloat16),
        in_specs=[pl.BlockSpec(memory_space=pltpu.SMEM)]
        + [anywhere] * (len(panels) + len(flat) + len(before) + len(after)),
        out_specs=anywhere,
        scratch_shapes=[
            pltpu.VMEM((len(panels), rows, tokens), jnp.bfloat16),
            pltpu.VMEM((tokens, columns), jnp.bfloat16),
            pltpu.VMEM((tokens, columns), jnp.bfloat16),
            pltpu.VMEM((slots, 2, rows // CHIPS, columns), jnp.bfloat16),
            pltpu.SemaphoreType.DMA((len(panels) + 2 * len(pieces),)),
            pltpu.SemaphoreType.DMA((slots, 2)),
        ],
        input_output_aliases={1 + len(panels) + len(flat): 0} if before else {},
        flops=4 * len(panels) * rows * tokens * columns,
        moved=4 * len(panels) * rows * columns,
        vmem=24,
    )(where, *panels, *flat, *before, *after)


def paired_body(acts, gate_w, up_w, panel_units):
    model = lax.axis_index("mp")
    block = lax.axis_index("dp")
    side = lax.axis_index("tensor")
    sizes = tuple(lax.axis_size(name) for name in AXES)
    chip, core = block // 2, block % 2
    gate, up = gate_w[0], up_w[0]
    units = gate.shape[1]
    picks = panel_units.reshape(2, 2, sizes[1], -1)
    tile = picks.shape[3]
    half = units // 2 // tile
    chunks = [2, half - 4, 2]
    starts = [0, 2, half - 2]

    def b_sides(m, d, t):
        return (m, d, 1 - t) if m == 1 else None

    def both_sides(m, d, t):
        return m, d, 1 - t

    def a_sides(m, d, t):
        return (m, d, 1 - t) if m == 0 else None

    def b_to_a(m, d, t):
        return (0, d, t) if m == 1 else None

    def b_to_far_a(m, d, t):
        return (0, d, 1 - t) if m == 1 else None

    def a_to_b(m, d, t):
        return (1, d, t) if m == 0 else None

    same = join(shifts(acts[0], sizes), [])
    other = send(same, sizes, other_core)

    picks = lax.dynamic_index_in_dim(picks, block, axis=2, keepdims=False) - block * units
    picks_far = lax.dynamic_index_in_dim(picks, 1 - side, axis=1, keepdims=False)
    picks_b, picks_a = picks_far[1:], picks_far[:1]
    picks_own = lax.dynamic_index_in_dim(picks, side, axis=1, keepdims=False).reshape(1, -1)
    bases = [((1 - side) * half + first) * tile for first in starts] + [side * half * tile, model]
    bases = jnp.stack(bases).astype(jnp.int32)
    model_number = jnp.reshape(model, (1,)).astype(jnp.int32)
    targets = [
        jnp.stack(
            [model, chip, core, (side * half + first) * tile, ((1 - side) * half + first) * tile]
        )
        for first in (0, starts[2])
    ]
    targets = [target.astype(jnp.int32) for target in targets]

    to_side = jnp.stack([(1 - side) * half, chip, core]).astype(jnp.int32)
    own_side = jnp.stack([side * half, chip, core]).astype(jnp.int32)
    ready = [own_side, picks_b, picks_a, picks_own, bases, model_number, *targets]
    sent, came = [], []
    for first, count in zip(starts, chunks):
        sent.append(
            products(to_side, same, other, gate, up, tile, first, count, sent[-1:] or ready)
        )
        came.append(send(sent[-1], sizes, b_sides))
    kept = products(own_side, same, other, gate, up, tile, 0, half, sent[-1:])

    z = [unit_scores(kept, came[0], tile, starts[0], [])]

    parts = sent + [kept]
    picked_b = pick(bases, picks_b, parts, tile, [came[1], z[0]])
    picked_own = pick(bases, picks_own, parts, tile, [picked_b])
    picked_a = pick(bases, picks_a, parts, tile, [picked_own])
    rows_b = panel_scores(picked_own, send(picked_b, sizes, a_sides), 1)
    rows_b = send(rows_b, sizes, a_to_b)
    a_mine = send(z[0], sizes, b_to_a)
    rows = panel_scores(
        picked_own, send(picked_a, sizes, a_sides), 0, (model_number, rows_b), (a_mine,)
    )

    z.append(unit_scores(kept, came[1], tile, starts[1], [picked_a]))
    z.append(unit_scores(kept, came[2], tile, starts[2], []))
    a_far = send(a_mine, sizes, a_sides)
    pieces = [(a_mine, a_far, z[0], send(a_far, sizes, a_to_b))]
    a_mine = send(z[1], sizes, b_to_a)
    far = send(choose(model_number, a_mine, z[1]), sizes, both_sides)
    pieces.append((a_mine, far, z[1], far))
    pieces.append(
        (
            send(z[2], sizes, b_to_a),
            send(z[2], sizes, b_to_far_a),
            z[2],
            send(z[2], sizes, b_sides),
        )
    )

    panel = join([rows, swapped(rows, sizes, 2)], [z[2], a_far])
    arrived = [pieces[0][3], far, pieces[2][0], pieces[2][1], pieces[2][3]]
    panel = join([panel, swapped(panel, sizes, 1)], arrived)
    panel_other = send(panel, sizes, other_core)
    shape = (2 * CHIPS * rows.shape[0], units)
    result = scores(targets[0], [panel], (0,), pieces[:2], tile, shape, [], [])
    result = scores(targets[0], [panel_other], (1,), pieces[:2], tile, shape, [result], [])
    return scores(
        targets[1], [panel, panel_other], (0, 1), pieces[2:], tile, shape, [result], []
    )


def solution(mesh):
    in_specs = (P("mp", "dp", "tensor"), P("mp", "tensor", "dp"), P("mp", "tensor", "dp"), P())
    out_specs = P(("mp", "tensor"), "dp")
    paired = mesh.shape["mp"] == 2 and mesh.shape["tensor"] == 2 and mesh.shape["dp"] == 2 * CHIPS

    def body(acts, gate_w, up_w, panel_units):
        picked = panel_units.shape[0] // (4 * 2 * CHIPS)
        units = gate_w.shape[2]
        fits = picked % 128 == 0 and units % (2 * picked) == 0 and units % 512 == 0
        fits = fits and units >= 10 * picked
        if paired and fits and acts.shape[1] % 16 == 0:
            return paired_body(acts, gate_w, up_w, panel_units)
        return general_body(acts, gate_w, up_w, panel_units)

    return jax.shard_map(body, mesh=mesh, in_specs=in_specs, out_specs=out_specs, check_vma=False)
```

time: 149 us -> 124 us (0.83)
  the two profiles are of different devices: /device:TPU:20 before, /device:TPU:0 now
where the time goes in v4:
time: 124 us; the launch traced here: 123 us
  Pallas kernels  52.8 us (43%)
  starting transfers between devices  36.5 us (29%)
  waiting for transfers between devices  31.3 us (25%)
  local copies, waits for them, and re-layouts  2 us (2%)
    ppermute x21, starting transfers between devices, send(): return lax.ppermute(block, AXES, routes(sizes, move))  36.5 us
    pallas_call x4, Pallas kernels, products(): call(products_kernel, out_shape=jax.ShapeDtypeStruct((2, tokens, tile * c...  33.3 us
    ppermute x21, waiting for transfers between devices, send(): return lax.ppermute(block, AXES, routes(sizes, move))  31.3 us
    pallas_call x3, Pallas kernels, scores(): call(functools.partial(score_kernel, 1.0 / math.sqrt(tokens), tile, cores...  10.8 us
    pallas_call x3, Pallas kernels, pick(): call(functools.partial(pick_kernel, counts, tile), out_shape=jax.ShapeDty...  5.95 us
  transfers between devices with their start and end apart: 21, of which 9 were waited for; matrix products, arithmetic and copies ran while one was open for 1% of the time, Pallas kernels for 33%

profile of v4, /device:TPU:0, one launch (start us, length us, event | category | flops | bytes accessed | tf_op | source)
XLA Modules:
  0.0 123.2 jit_solution(570661493678817698)
XLA Ops:
  0.0 5.0 %collective-permute-start.2 = (bf16[32,4096]{1,0:T(8,128)(2,1)}, bf16[32,4096]{1,0:T(8,128)(2,1)S(1)}, u32[]{:S(2)}, u32[]{:S(2)}) collective-permute-start(bf16[32,4096]{1,0:T(8,128)(2,1)} %bitcast.18), channel_id=1, source_target_pairs={{0,12},{1,13},{2,14},{3,15},{4,0},{5,1},{6,2},{7,3},{8,4},{9,5},{1... | collective-permute-start | bytes 786440 | tf_op jit(solution)/shard_map/ppermute | solution.py:99
  5.1 1.0 collective-permute-start
  6.1 6.1 %collective-permute-done.2.refs_3_ = bf16[32,4096]{1,0:T(8,128)(2,1)S(1)} collective-permute-done((bf16[32,4096]{1,0:T(8,128)(2,1)}, bf16[32,4096]{1,0:T(8,128)(2,1)S(1)}, u32[]{:S(2)}, u32[]{:S(2)}) %collective-permute-start.2) | collective-permute-done | bytes 262176 | tf_op jit(solution)/shard_map/ppermute | solution.py:99
  12.1 15.4 %collective-permute-done.1.refs_2_ = bf16[32,4096]{1,0:T(8,128)(2,1)S(1)} collective-permute-done((bf16[32,4096]{1,0:T(8,128)(2,1)}, bf16[32,4096]{1,0:T(8,128)(2,1)S(1)}, u32[]{:S(2)}, u32[]{:S(2)}) %collective-permute-start.1) | collective-permute-done | bytes 262176 | tf_op jit(solution)/shard_map/ppermute | solution.py:99
  27.6 0.9 copy-done
  28.7 0.1 stack.65.refs_4_.bases_ref
  28.8 0.1 stack.70.refs_6_.where_ref
  28.9 0.1 stack.61.refs_7_.where_ref
  29.0 0.8 reshape.19
  29.7 0.1 add_add_fusion
  29.9 1.5 %collective-permute-done.3.other_ref = bf16[128,4096]{1,0:T(8,128)(2,1)S(1)} collective-permute-done((bf16[128,4096]{1,0:T(8,128)(2,1)S(1)}, bf16[128,4096]{1,0:T(8,128)(2,1)S(1)}, u32[]{:S(2)}, u32[]{:S(2)}) %collective-permute-start.3) | collective-permute-done | bytes 1048608 | tf_op jit(solution)/shard_map/ppermute | solution.py:99
  31.3 5.4 %shard_map.47.refs_0_ = bf16[2,256,512]{2,1,0:T(8,128)(2,1)S(1)} custom-call(s32[3]{0:T(128)S(1)} %get-tuple-element.7.place_ref, bf16[128,4096]{1,0:T(8,128)(2,1)S(1)} %shard_map.46.same_ref, bf16[128,4096]{1,0:T(8,128)(2,1)S(1)} %collective-permute-done.3.other_ref, bf16[4096,3584]{1,0:T(8,128)(2,1)} %bitcast.24, bf16[4096,3584]{1,0:T(8,128)(2,1)} %bitcast.28, ...), custom_call_target="tpu_custom_call" | custom-call | flops 2147483648 | bytes 8388608 | tf_op jit(solution)/shard_map/pallas_call | solution.py:197
  36.8 0.7 collective-permute-start.5
  37.5 7.6 %shard_map.48.refs_0_.refs_1_ = bf16[2,256,768]{2,1,0:T(8,128)(2,1)S(1)} custom-call(s32[3]{0:T(128)S(1)} %get-tuple-element.7.place_ref, bf16[128,4096]{1,0:T(8,128)(2,1)S(1)} %shard_map.46.same_ref, bf16[128,4096]{1,0:T(8,128)(2,1)S(1)} %collective-permute-done.3.other_ref, bf16[4096,3584]{1,0:T(8,128)(2,1)} %bitcast.25, bf16[4096,3584]{1,0:T(8,128)(2,1)} %bitcast.29, ...), custom_call_target="tpu_custom_call" | custom-call | flops 3221225472 | bytes 12582912 | tf_op jit(solution)/shard_map/pallas_call | solution.py:197
  45.1 0.7 collective-permute-start.4
  45.8 5.4 %shard_map.49.refs_0_.refs_2_ = bf16[2,256,512]{2,1,0:T(8,128)(2,1)S(1)} custom-call(s32[3]{0:T(128)S(1)} %get-tuple-element.7.place_ref, bf16[128,4096]{1,0:T(8,128)(2,1)S(1)} %shard_map.46.same_ref, bf16[128,4096]{1,0:T(8,128)(2,1)S(1)} %collective-permute-done.3.other_ref, bf16[4096,3584]{1,0:T(8,128)(2,1)} %bitcast.26, bf16[4096,3584]{1,0:T(8,128)(2,1)} %bitcast.30, ...), custom_call_target="tpu_custom_call" | custom-call | flops 2147483648 | bytes 8388608 | tf_op jit(solution)/shard_map/pallas_call | solution.py:197
  51.2 0.7 collective-permute-start.11
  51.9 14.8 %shard_map.50.mine_ref.refs_3_ = bf16[2,256,1792]{2,1,0:T(8,128)(2,1)S(1)} custom-call(s32[3]{0:T(128)S(1)} %get-tuple-element.8.refs_0_.place_ref, bf16[128,4096]{1,0:T(8,128)(2,1)S(1)} %shard_map.46.same_ref, bf16[128,4096]{1,0:T(8,128)(2,1)S(1)} %collective-permute-done.3.other_ref, bf16[4096,3584]{1,0:T(8,128)(2,1)} %bitcast.27, ...), custom_call_target="tpu_custom_call" | custom-call | flops 7516192768 | bytes 29360128 | tf_op jit(solution)/shard_map/pallas_call | solution.py:197
  66.8 0.6 shard_map.51.refs_5_.refs_3_
  67.4 1.3 %collective-permute-start.9 = (bf16[256,512]{1,0:T(8,128)(2,1)S(1)}, bf16[256,512]{1,0:T(8,128)(2,1)S(1)}, u32[]{:S(2)}, u32[]{:S(2)}) collective-permute-start(bf16[256,512]{1,0:T(8,128)(2,1)S(1)} %shard_map.51.refs_5_.refs_3_), channel_id=1, source_target_pairs={{16,0},{17,1},{18,2},{19,3},{20,4},{21,5},{22,6},{23,7},{24,8},{25... | collective-permute-start | bytes 786440 | tf_op jit(solution)/shard_map/ppermute | solution.py:99
  68.7 1.7 %shard_map.52.refs_4_ = bf16[2,256,256]{2,1,0:T(8,128)(2,1)S(1)} custom-call(s32[5]{0:T(128)S(1)} %stack.65.refs_4_.bases_ref, s32[1,256]{1,0:T(1,128)S(1)} %get-tuple-element.6.refs_1_.picks_ref, bf16[2,256,512]{2,1,0:T(8,128)(2,1)S(1)} %shard_map.47.refs_0_, bf16[2,256,768]{2,1,0:T(8,128)(2,1)S(1)} %shard_map.48.refs_0_.refs_1_, ...), custom_call_target="tpu_custom_call" | custom-call | flops 939524096 | bytes 3670016 | tf_op jit(solution)/shard_map/pallas_call | solution.py:239
  70.4 3.5 %collective-permute-start.7 = (bf16[2,256,256]{2,1,0:T(8,128)(2,1)S(1)}, bf16[2,256,256]{2,1,0:T(8,128)(2,1)S(1)}, u32[]{:S(2)}, u32[]{:S(2)}) collective-permute-start(bf16[2,256,256]{2,1,0:T(8,128)(2,1)S(1)} %shard_map.52.refs_4_), channel_id=1, source_target_pairs={{0,1},{1,0},{2,3},{3,2},{4,5},{5,4},{6,7},{7,6},{8,9},{9,8},{10,11... | collective-permute-start | bytes 786440 | tf_op jit(solution)/shard_map/ppermute | solution.py:99
  73.8 2.6 %shard_map.53.refs_4_.mine_ref = bf16[2,256,512]{2,1,0:T(8,128)(2,1)S(1)} custom-call(s32[5]{0:T(128)S(1)} %stack.65.refs_4_.bases_ref, s32[1,512]{1,0:T(1,128)S(1)} %bitcast.23, bf16[2,256,512]{2,1,0:T(8,128)(2,1)S(1)} %shard_map.47.refs_0_, bf16[2,256,768]{2,1,0:T(8,128)(2,1)S(1)} %shard_map.48.refs_0_.refs_1_, ...), custom_call_target="tpu_custom_call" | custom-call | flops 1879048192 | bytes 3670016 | tf_op jit(solution)/shard_map/pallas_call | solution.py:239
  76.5 1.7 %shard_map.54.refs_0_ = bf16[2,256,256]{2,1,0:T(8,128)(2,1)S(1)} custom-call(s32[5]{0:T(128)S(1)} %stack.65.refs_4_.bases_ref, s32[1,256]{1,0:T(1,128)S(1)} %get-tuple-element.5.refs_2_.picks_ref, bf16[2,256,512]{2,1,0:T(8,128)(2,1)S(1)} %shard_map.47.refs_0_, bf16[2,256,768]{2,1,0:T(8,128)(2,1)S(1)} %shard_map.48.refs_0_.refs_1_, ...), custom_call_target="tpu_custom_call" | custom-call | flops 939524096 | bytes 3670016 | tf_op jit(solution)/shard_map/pallas_call | solution.py:239
  78.1 0.9 shard_map.59.second_ref.refs_7_
  79.0 1.3 %collective-permute-start.15 = (bf16[256,768]{1,0:T(8,128)(2,1)S(1)}, bf16[256,768]{1,0:T(8,128)(2,1)S(1)}, u32[]{:S(2)}, u32[]{:S(2)}) collective-permute-start(bf16[256,768]{1,0:T(8,128)(2,1)S(1)} %shard_map.59.second_ref.refs_7_), channel_id=1, source_target_pairs={{16,0},{17,1},{18,2},{19,3},{20,4},{21,5},{22,6},{23,7},{24,8},{25... | collective-permute-start | bytes 1179656 | tf_op jit(solution)/shard_map/ppermute | solution.py:99
  80.3 2.4 %collective-permute-start.6 = (bf16[2,256,256]{2,1,0:T(8,128)(2,1)S(1)}, bf16[2,256,256]{2,1,0:T(8,128)(2,1)S(1)}, u32[]{:S(2)}, u32[]{:S(2)}) collective-permute-start(bf16[2,256,256]{2,1,0:T(8,128)(2,1)S(1)} %shard_map.54.refs_0_), channel_id=1, source_target_pairs={{0,1},{1,0},{2,3},{3,2},{4,5},{5,4},{6,7},{7,6},{8,9},{9,8},{10,11... | collective-permute-start | bytes 786440 | tf_op jit(solution)/shard_map/ppermute | solution.py:99
  82.7 0.3 collective-permute-done.9.refs_0_.refs_1_
  83.0 3.1 %collective-permute-start.12 = (bf16[256,512]{1,0:T(8,128)(2,1)S(1)}, bf16[256,512]{1,0:T(8,128)(2,1)S(1)}, u32[]{:S(2)}, u32[]{:S(2)}) collective-permute-start(bf16[256,512]{1,0:T(8,128)(2,1)S(1)} %collective-permute-done.9.refs_0_.refs_1_), channel_id=1, source_target_pairs={{0,1},{1,0},{2,3},{3,2},{4,5},{5,4},{6,7},{7,6},{8,9},{9,8},{10,11... | collective-permute-start | bytes 786440 | tf_op jit(solution)/shard_map/ppermute | solution.py:99
  86.2 0.3 shard_map.55
  86.5 1.3 %collective-permute-start.8 = (bf16[256,256]{1,0:T(8,128)(2,1)S(1)}, bf16[256,256]{1,0:T(8,128)(2,1)S(1)}, u32[]{:S(2)}, u32[]{:S(2)}) collective-permute-start(bf16[256,256]{1,0:T(8,128)(2,1)S(1)} %shard_map.55), channel_id=1, source_target_pairs={{0,16},{1,17},{2,18},{3,19},{4,20},{5,21},{6,22},{7,23},{8,24},{9,... | collective-permute-start | bytes 393224 | tf_op jit(solution)/shard_map/ppermute | solution.py:99
  87.8 0.6 shard_map.57.refs_2_.refs_4_
  88.4 0.7 collective-permute-start.19
  89.1 2.3 %collective-permute-done.6.theirs_ref = bf16[2,256,256]{2,1,0:T(8,128)(2,1)S(1)} collective-permute-done((bf16[2,256,256]{2,1,0:T(8,128)(2,1)S(1)}, bf16[2,256,256]{2,1,0:T(8,128)(2,1)S(1)}, u32[]{:S(2)}, u32[]{:S(2)}) %collective-permute-start.6) | collective-permute-done | bytes 262176 | tf_op jit(solution)/shard_map/ppermute | solution.py:99
  91.4 0.3 shard_map.56.refs_0_
  91.7 2.9 %collective-permute-start.10 = (bf16[256,256]{1,0:T(8,128)(2,1)S(1)}, bf16[256,256]{1,0:T(8,128)(2,1)S(1)}, u32[]{:S(2)}, u32[]{:S(2)}) collective-permute-start(bf16[256,256]{1,0:T(8,128)(2,1)S(1)} %shard_map.56.refs_0_), channel_id=1, source_target_pairs={{0,8},{1,9},{2,10},{3,11},{4,12},{5,13},{6,14},{7,15},{8,0},{9,1},... | collective-permute-start | bytes 393224 | tf_op jit(solution)/shard_map/ppermute | solution.py:99
  94.6 0.5 collective-permute-start.16
  95.2 1.3 %collective-permute-start.18 = (bf16[256,512]{1,0:T(8,128)(2,1)S(1)}, bf16[256,512]{1,0:T(8,128)(2,1)S(1)}, u32[]{:S(2)}, u32[]{:S(2)}) collective-permute-start(bf16[256,512]{1,0:T(8,128)(2,1)S(1)} %shard_map.57.refs_2_.refs_4_), channel_id=1, source_target_pairs={{16,1},{17,0},{18,3},{19,2},{20,5},{21,4},{22,7},{23,6},{24,9},{25... | collective-permute-start | bytes 786440 | tf_op jit(solution)/shard_map/ppermute | solution.py:99
  96.4 0.4 collective-permute-done.12.refs_3_.refs_2_
  96.8 1.3 %collective-permute-start.17 = (bf16[256,512]{1,0:T(8,128)(2,1)S(1)}, bf16[256,512]{1,0:T(8,128)(2,1)S(1)}, u32[]{:S(2)}, u32[]{:S(2)}) collective-permute-start(bf16[256,512]{1,0:T(8,128)(2,1)S(1)} %shard_map.57.refs_2_.refs_4_), channel_id=1, source_target_pairs={{16,0},{17,1},{18,2},{19,3},{20,4},{21,5},{22,6},{23,7},{24,8},{25... | collective-permute-start | bytes 786440 | tf_op jit(solution)/shard_map/ppermute | solution.py:99
  98.1 1.0 collective-permute-done.10.refs_1_
  99.1 4.3 %collective-permute-start.14 = (bf16[256,512]{1,0:T(8,128)(2,1)S(1)}, bf16[256,512]{1,0:T(8,128)(2,1)S(1)}, u32[]{:S(2)}, u32[]{:S(2)}) collective-permute-start(bf16[256,512]{1,0:T(8,128)(2,1)S(1)} %collective-permute-done.12.refs_3_.refs_2_), channel_id=1, source_target_pairs={{0,16},{1,17},{2,18},{3,19},{4,20},{5,21},{6,22},{7,23},{8,24},{9,... | collective-permute-start | bytes 786440 | tf_op jit(solution)/shard_map/ppermute | solution.py:99
  103.4 4.4 %collective-permute-start.13 = (bf16[512,256]{1,0:T(8,128)(2,1)S(1)}, bf16[512,256]{1,0:T(8,128)(2,1)S(1)}, u32[]{:S(2)}, u32[]{:S(2)}) collective-permute-start(bf16[512,256]{1,0:T(8,128)(2,1)S(1)} %shard_map.58.refs_0_), channel_id=1, source_target_pairs={{0,4},{1,5},{2,6},{3,7},{4,0},{5,1},{6,2},{7,3},{8,12},{9,13},{10,... | collective-permute-start | bytes 786440 | tf_op jit(solution)/shard_map/ppermute | solution.py:99
  107.8 1.4 %collective-permute-done.17.refs_4_.refs_2_ = bf16[256,512]{1,0:T(8,128)(2,1)S(1)} collective-permute-done((bf16[256,512]{1,0:T(8,128)(2,1)S(1)}, bf16[256,512]{1,0:T(8,128)(2,1)S(1)}, u32[]{:S(2)}, u32[]{:S(2)}) %collective-permute-start.17) | collective-permute-done | bytes 262176 | tf_op jit(solution)/shard_map/ppermute | solution.py:99
  109.2 2.9 %collective-permute-done.13.refs_1_ = bf16[512,256]{1,0:T(8,128)(2,1)S(1)} collective-permute-done((bf16[512,256]{1,0:T(8,128)(2,1)S(1)}, bf16[512,256]{1,0:T(8,128)(2,1)S(1)}, u32[]{:S(2)}, u32[]{:S(2)}) %collective-permute-start.13) | collective-permute-done | bytes 262176 | tf_op jit(solution)/shard_map/ppermute | solution.py:99
  112.2 3.9 %shard_map.62.refs_9_ = bf16[2048,3584]{1,0:T(8,128)(2,1)} custom-call(s32[5]{0:T(128)S(1)} %stack.70.refs_6_.where_ref, bf16[1024,256]{1,0:T(8,128)(2,1)S(1)} %shard_map.61.refs_0_, bf16[256,512]{1,0:T(8,128)(2,1)S(1)} %collective-permute-done.9.refs_0_.refs_1_, bf16[256,512]{1,0:T(8,128)(2,1)S(1)} %collective-permute-done.12.refs_3_.refs_2_, ...), custom_call_target="tpu_custom_call" | custom-call | flops 1342177280 | bytes 5242880 | tf_op jit(solution)/shard_map/pallas_call | solution.py:400
  116.2 3.7 %shard_map.63.refs_6_ = bf16[2048,3584]{1,0:T(8,128)(2,1)} custom-call(s32[5]{0:T(128)S(1)} %stack.70.refs_6_.where_ref, bf16[1024,256]{1,0:T(8,128)(2,1)S(1)} %collective-permute-done.20.refs_0_.refs_1_, bf16[256,512]{1,0:T(8,128)(2,1)S(1)} %collective-permute-done.9.refs_0_.refs_1_, ...), custom_call_target="tpu_custom_call", output_to_operand_aliasing={{}: (10, {})} | custom-call | flops 1342177280 | bytes 5242880 | tf_op jit(solution)/shard_map/pallas_call | solution.py:400
  119.9 3.1 %shard_map.64 = bf16[2048,3584]{1,0:T(8,128)(2,1)} custom-call(s32[5]{0:T(128)S(1)} %stack.61.refs_7_.where_ref, bf16[1024,256]{1,0:T(8,128)(2,1)S(1)} %shard_map.61.refs_0_, bf16[1024,256]{1,0:T(8,128)(2,1)S(1)} %collective-permute-done.20.refs_0_.refs_1_, ...), custom_call_target="tpu_custom_call", output_to_operand_aliasing={{}: (7, {})} | custom-call | flops 1073741824 | bytes 4194304 | tf_op jit(solution)/shard_map/pallas_call | solution.py:400
  (23 shorter events, 0.4 us)
Async XLA Ops:
  0.0 12.1 %collective-permute-start.2 = (bf16[32,4096]{1,0:T(8,128)(2,1)}, bf16[32,4096]{1,0:T(8,128)(2,1)S(1)}, u32[]{:S(2)}, u32[]{:S(2)}) collective-permute-start(bf16[32,4096]{1,0:T(8,128)(2,1)} %bitcast.18), channel_id=1, source_target_pairs={{0,12},{1,13},{2,14},{3,15},{4,0},{5,1},{6,2},{7,3},{8,4},{9,5},{1... | collective-permute-start | bytes 786440 | tf_op jit(solution)/shard_map/ppermute | solution.py:99
  5.0 22.5 %collective-permute-start.1 = (bf16[32,4096]{1,0:T(8,128)(2,1)}, bf16[32,4096]{1,0:T(8,128)(2,1)S(1)}, u32[]{:S(2)}, u32[]{:S(2)}) collective-permute-start(bf16[32,4096]{1,0:T(8,128)(2,1)} %bitcast.19), channel_id=1, source_target_pairs={{0,8},{1,9},{2,10},{3,11},{4,12},{5,13},{6,14},{7,15},{8,0},{9,1},... | collective-permute-start | bytes 786440 | tf_op jit(solution)/shard_map/ppermute | solution.py:99
  5.1 22.5 %collective-permute-start = (bf16[32,4096]{1,0:T(8,128)(2,1)}, bf16[32,4096]{1,0:T(8,128)(2,1)S(1)}, u32[]{:S(2)}, u32[]{:S(2)}) collective-permute-start(bf16[32,4096]{1,0:T(8,128)(2,1)} %bitcast.20), channel_id=1, source_target_pairs={{0,4},{1,5},{2,6},{3,7},{4,8},{5,9},{6,10},{7,11},{8,12},{9,13},{1... | collective-permute-start | bytes 786440 | tf_op jit(solution)/shard_map/ppermute | solution.py:99
  27.6 1.0 copy-start
  28.6 2.7 %collective-permute-start.3 = (bf16[128,4096]{1,0:T(8,128)(2,1)S(1)}, bf16[128,4096]{1,0:T(8,128)(2,1)S(1)}, u32[]{:S(2)}, u32[]{:S(2)}) collective-permute-start(bf16[128,4096]{1,0:T(8,128)(2,1)S(1)} %shard_map.46.same_ref), channel_id=1, source_target_pairs={{0,2},{1,3},{2,0},{3,1},{4,6},{5,7},{6,4},{7,5},{8,10},{9,11},{10,... | collective-permute-start | bytes 3145736 | tf_op jit(solution)/shard_map/ppermute | solution.py:99
  36.8 30.0 %collective-permute-start.5 = (bf16[2,256,512]{2,1,0:T(8,128)(2,1)S(1)}, bf16[2,256,512]{2,1,0:T(8,128)(2,1)S(1)}, u32[]{:S(2)}, u32[]{:S(2)}) collective-permute-start(bf16[2,256,512]{2,1,0:T(8,128)(2,1)S(1)} %shard_map.47.refs_0_), channel_id=1, source_target_pairs={{16,17},{17,16},{18,19},{19,18},{20,21},{21,20},{22,23},{23,22},{2... | collective-permute-start | bytes 1572872 | tf_op jit(solution)/shard_map/ppermute | solution.py:99
  45.1 23.6 %collective-permute-start.4 = (bf16[2,256,768]{2,1,0:T(8,128)(2,1)S(1)}, bf16[2,256,768]{2,1,0:T(8,128)(2,1)S(1)}, u32[]{:S(2)}, u32[]{:S(2)}) collective-permute-start(bf16[2,256,768]{2,1,0:T(8,128)(2,1)S(1)} %shard_map.48.refs_0_.refs_1_), channel_id=1, source_target_pairs={{16,17},{17,16},{18,19},{19,18},{20,21},{21,20},{22,23},{23,22},{2... | collective-permute-start | bytes 2359304 | tf_op jit(solution)/shard_map/ppermute | solution.py:99
  51.2 36.6 %collective-permute-start.11 = (bf16[2,256,512]{2,1,0:T(8,128)(2,1)S(1)}, bf16[2,256,512]{2,1,0:T(8,128)(2,1)S(1)}, u32[]{:S(2)}, u32[]{:S(2)}) collective-permute-start(bf16[2,256,512]{2,1,0:T(8,128)(2,1)S(1)} %shard_map.49.refs_0_.refs_2_), channel_id=1, source_target_pairs={{16,17},{17,16},{18,19},{19,18},{20,21},{21,20},{22,23},{23,22},{2... | collective-permute-start | bytes 1572872 | tf_op jit(solution)/shard_map/ppermute | solution.py:99
  67.4 15.7 %collective-permute-start.9 = (bf16[256,512]{1,0:T(8,128)(2,1)S(1)}, bf16[256,512]{1,0:T(8,128)(2,1)S(1)}, u32[]{:S(2)}, u32[]{:S(2)}) collective-permute-start(bf16[256,512]{1,0:T(8,128)(2,1)S(1)} %shard_map.51.refs_5_.refs_3_), channel_id=1, source_target_pairs={{16,0},{17,1},{18,2},{19,3},{20,4},{21,5},{22,6},{23,7},{24,8},{25... | collective-permute-start | bytes 786440 | tf_op jit(solution)/shard_map/ppermute | solution.py:99
  70.4 15.8 %collective-permute-start.7 = (bf16[2,256,256]{2,1,0:T(8,128)(2,1)S(1)}, bf16[2,256,256]{2,1,0:T(8,128)(2,1)S(1)}, u32[]{:S(2)}, u32[]{:S(2)}) collective-permute-start(bf16[2,256,256]{2,1,0:T(8,128)(2,1)S(1)} %shard_map.52.refs_4_), channel_id=1, source_target_pairs={{0,1},{1,0},{2,3},{3,2},{4,5},{5,4},{6,7},{7,6},{8,9},{9,8},{10,11... | collective-permute-start | bytes 786440 | tf_op jit(solution)/shard_map/ppermute | solution.py:99
  79.0 15.6 %collective-permute-start.15 = (bf16[256,768]{1,0:T(8,128)(2,1)S(1)}, bf16[256,768]{1,0:T(8,128)(2,1)S(1)}, u32[]{:S(2)}, u32[]{:S(2)}) collective-permute-start(bf16[256,768]{1,0:T(8,128)(2,1)S(1)} %shard_map.59.second_ref.refs_7_), channel_id=1, source_target_pairs={{16,0},{17,1},{18,2},{19,3},{20,4},{21,5},{22,6},{23,7},{24,8},{25... | collective-permute-start | bytes 1179656 | tf_op jit(solution)/shard_map/ppermute | solution.py:99
  80.3 11.1 %collective-permute-start.6 = (bf16[2,256,256]{2,1,0:T(8,128)(2,1)S(1)}, bf16[2,256,256]{2,1,0:T(8,128)(2,1)S(1)}, u32[]{:S(2)}, u32[]{:S(2)}) collective-permute-start(bf16[2,256,256]{2,1,0:T(8,128)(2,1)S(1)} %shard_map.54.refs_0_), channel_id=1, source_target_pairs={{0,1},{1,0},{2,3},{3,2},{4,5},{5,4},{6,7},{7,6},{8,9},{9,8},{10,11... | collective-permute-start | bytes 786440 | tf_op jit(solution)/shard_map/ppermute | solution.py:99
  83.0 13.8 %collective-permute-start.12 = (bf16[256,512]{1,0:T(8,128)(2,1)S(1)}, bf16[256,512]{1,0:T(8,128)(2,1)S(1)}, u32[]{:S(2)}, u32[]{:S(2)}) collective-permute-start(bf16[256,512]{1,0:T(8,128)(2,1)S(1)} %collective-permute-done.9.refs_0_.refs_1_), channel_id=1, source_target_pairs={{0,1},{1,0},{2,3},{3,2},{4,5},{5,4},{6,7},{7,6},{8,9},{9,8},{10,11... | collective-permute-start | bytes 786440 | tf_op jit(solution)/shard_map/ppermute | solution.py:99
  86.5 4.9 %collective-permute-start.8 = (bf16[256,256]{1,0:T(8,128)(2,1)S(1)}, bf16[256,256]{1,0:T(8,128)(2,1)S(1)}, u32[]{:S(2)}, u32[]{:S(2)}) collective-permute-start(bf16[256,256]{1,0:T(8,128)(2,1)S(1)} %shard_map.55), channel_id=1, source_target_pairs={{0,16},{1,17},{2,18},{3,19},{4,20},{5,21},{6,22},{7,23},{8,24},{9,... | collective-permute-start | bytes 393224 | tf_op jit(solution)/shard_map/ppermute | solution.py:99
  88.4 15.0 %collective-permute-start.19 = (bf16[256,512]{1,0:T(8,128)(2,1)S(1)}, bf16[256,512]{1,0:T(8,128)(2,1)S(1)}, u32[]{:S(2)}, u32[]{:S(2)}) collective-permute-start(bf16[256,512]{1,0:T(8,128)(2,1)S(1)} %shard_map.57.refs_2_.refs_4_), channel_id=1, source_target_pairs={{16,17},{17,16},{18,19},{19,18},{20,21},{21,20},{22,23},{23,22},{2... | collective-permute-start | bytes 786440 | tf_op jit(solution)/shard_map/ppermute | solution.py:99
  91.7 7.3 %collective-permute-start.10 = (bf16[256,256]{1,0:T(8,128)(2,1)S(1)}, bf16[256,256]{1,0:T(8,128)(2,1)S(1)}, u32[]{:S(2)}, u32[]{:S(2)}) collective-permute-start(bf16[256,256]{1,0:T(8,128)(2,1)S(1)} %shard_map.56.refs_0_), channel_id=1, source_target_pairs={{0,8},{1,9},{2,10},{3,11},{4,12},{5,13},{6,14},{7,15},{8,0},{9,1},... | collective-permute-start | bytes 393224 | tf_op jit(solution)/shard_map/ppermute | solution.py:99
  94.6 17.5 %collective-permute-start.16 = (bf16[256,768]{1,0:T(8,128)(2,1)S(1)}, bf16[256,768]{1,0:T(8,128)(2,1)S(1)}, u32[]{:S(2)}, u32[]{:S(2)}) collective-permute-start(bf16[256,768]{1,0:T(8,128)(2,1)S(1)} %shard_map.60), channel_id=1, source_target_pairs={{0,1},{1,0},{2,3},{3,2},{4,5},{5,4},{6,7},{7,6},{8,9},{9,8},{10,11... | collective-permute-start | bytes 1179656 | tf_op jit(solution)/shard_map/ppermute | solution.py:99
  95.2 12.6 %collective-permute-start.18 = (bf16[256,512]{1,0:T(8,128)(2,1)S(1)}, bf16[256,512]{1,0:T(8,128)(2,1)S(1)}, u32[]{:S(2)}, u32[]{:S(2)}) collective-permute-start(bf16[256,512]{1,0:T(8,128)(2,1)S(1)} %shard_map.57.refs_2_.refs_4_), channel_id=1, source_target_pairs={{16,1},{17,0},{18,3},{19,2},{20,5},{21,4},{22,7},{23,6},{24,9},{25... | collective-permute-start | bytes 786440 | tf_op jit(solution)/shard_map/ppermute | solution.py:99
  96.8 12.4 %collective-permute-start.17 = (bf16[256,512]{1,0:T(8,128)(2,1)S(1)}, bf16[256,512]{1,0:T(8,128)(2,1)S(1)}, u32[]{:S(2)}, u32[]{:S(2)}) collective-permute-start(bf16[256,512]{1,0:T(8,128)(2,1)S(1)} %shard_map.57.refs_2_.refs_4_), channel_id=1, source_target_pairs={{16,0},{17,1},{18,2},{19,3},{20,4},{21,5},{22,6},{23,7},{24,8},{25... | collective-permute-start | bytes 786440 | tf_op jit(solution)/shard_map/ppermute | solution.py:99
  99.1 10.2 %collective-permute-start.14 = (bf16[256,512]{1,0:T(8,128)(2,1)S(1)}, bf16[256,512]{1,0:T(8,128)(2,1)S(1)}, u32[]{:S(2)}, u32[]{:S(2)}) collective-permute-start(bf16[256,512]{1,0:T(8,128)(2,1)S(1)} %collective-permute-done.12.refs_3_.refs_2_), channel_id=1, source_target_pairs={{0,16},{1,17},{2,18},{3,19},{4,20},{5,21},{6,22},{7,23},{8,24},{9,... | collective-permute-start | bytes 786440 | tf_op jit(solution)/shard_map/ppermute | solution.py:99
  103.4 8.7 %collective-permute-start.13 = (bf16[512,256]{1,0:T(8,128)(2,1)S(1)}, bf16[512,256]{1,0:T(8,128)(2,1)S(1)}, u32[]{:S(2)}, u32[]{:S(2)}) collective-permute-start(bf16[512,256]{1,0:T(8,128)(2,1)S(1)} %shard_map.58.refs_0_), channel_id=1, source_target_pairs={{0,4},{1,5},{2,6},{3,7},{4,0},{5,1},{6,2},{7,3},{8,12},{9,13},{10,... | collective-permute-start | bytes 786440 | tf_op jit(solution)/shard_map/ppermute | solution.py:99
  112.2 4.0 %collective-permute-start.20 = (bf16[1024,256]{1,0:T(8,128)(2,1)S(1)}, bf16[1024,256]{1,0:T(8,128)(2,1)S(1)}, u32[]{:S(2)}, u32[]{:S(2)}) collective-permute-start(bf16[1024,256]{1,0:T(8,128)(2,1)S(1)} %shard_map.61.refs_0_), channel_id=1, source_target_pairs={{0,2},{1,3},{2,0},{3,1},{4,6},{5,7},{6,4},{7,5},{8,10},{9,11},{10,... | collective-permute-start | bytes 1572872 | tf_op jit(solution)/shard_map/ppermute | solution.py:99

commit v5 on v4

--- a/solution.py
+++ b/solution.py
@@ -116,20 +116,27 @@
 
 
 def join_kernel(count, *refs):
+    out_ref, sems = refs[-2:]
     rows = refs[0].shape[0]
-    for i in range(count):
-        refs[-1][i * rows : (i + 1) * rows, :] = refs[i][...]
+    copies = [
+        pltpu.make_async_copy(refs[i], out_ref.at[i * rows : (i + 1) * rows, :], sems.at[i])
+        for i in range(count)
+    ]
+    for copy in copies:
+        copy.start()
+    for copy in copies:
+        copy.wait()
 
 
 def join(blocks, after):
     rows, width = blocks[0].shape
     count = len(blocks)
-    vmem = pl.BlockSpec(memory_space=pltpu.VMEM)
     return call(
         functools.partial(join_kernel, count),
         out_shape=jax.ShapeDtypeStruct((count * rows, width), blocks[0].dtype),
-        in_specs=[vmem] * count + [pl.BlockSpec(memory_space=pl.ANY)] * len(after),
-        out_specs=vmem,
+        in_specs=[pl.BlockSpec(memory_space=pl.ANY)] * (count + len(after)),
+        out_specs=pl.BlockSpec(memory_space=pltpu.VMEM),
+        scratch_shapes=[pltpu.SemaphoreType.DMA((count,))],
         flops=0,
         moved=4 * count * rows * width,
         vmem=16,
@@ -178,34 +185,60 @@
     )(model_number, first, second)
 
 
-def products_kernel(place_ref, same_ref, other_ref, gate_ref, up_ref, *refs):
-    out_ref = refs[-1]
+def products_kernel(counts, n_after, place_ref, same_ref, other_ref, gate_ref, up_ref, *refs):
     rows = same_ref.shape[0] // CHIPS
-    x = jnp.concatenate([same_ref[...], other_ref[...]], axis=0)
-    for which, weight_ref in enumerate((gate_ref, up_ref)):
-        total = jnp.dot(x, weight_ref[...], preferred_element_type=jnp.float32)
-        total = total.astype(jnp.bfloat16)
-        for i in range(2 * CHIPS):
-            start = pl.multiple_of(canonical(i, place_ref[1], place_ref[2]) * rows, rows)
-            out_ref[which, pl.ds(start, rows), :] = total[i * rows : (i + 1) * rows]
-
-
-def products(place, same, other, gate, up, tile, first, count, after):
+    step = pl.program_id(0)
+
+    def write(out_ref):
+        x = jnp.concatenate([same_ref[...], other_ref[...]], axis=0)
+        for which, weight_ref in enumerate((gate_ref, up_ref)):
+            total = jnp.dot(x, weight_ref[...], preferred_element_type=jnp.float32)
+            total = total.astype(jnp.bfloat16)
+            for i in range(2 * CHIPS):
+                start = pl.multiple_of(canonical(i, place_ref[0], place_ref[1]) * rows, rows)
+                out_ref[which, pl.ds(start, rows), :] = total[i * rows : (i + 1) * rows]
+
+    first = 0
+    for count, out_ref in zip(counts, refs[n_after:]):
+
+        @pl.when((step >= first) & (step < first + count))
+        def _():
+            write(out_ref)
+
+        first += count
+
+
+def products(place, same, other, gate, up, tile, counts, after):
     tokens, width = 2 * same.shape[0], same.shape[1]
-    weights = pl.BlockSpec((width, tile), lambda i, place_ref: (0, place_ref[0] + first + i))
+    firsts = [sum(counts[:i]) for i in range(len(counts))]
+
+    def weight_tile(i, place_ref):
+        column = place_ref[2] + i
+        for run in range(1, len(counts)):
+            column = jnp.where(i >= firsts[run], place_ref[2 + run] + i - firsts[run], column)
+        return 0, column
+
+    def out_tile(run):
+        return lambda i, place_ref: (0, 0, jnp.clip(i - firsts[run], 0, counts[run] - 1))
+
+    weights = pl.BlockSpec((width, tile), weight_tile)
     whole = pl.BlockSpec(same.shape, lambda i, place_ref: (0, 0))
     return call(
-        products_kernel,
-        out_shape=jax.ShapeDtypeStruct((2, tokens, tile * count), jnp.bfloat16),
+        functools.partial(products_kernel, counts, len(after)),
+        out_shape=[
+            jax.ShapeDtypeStruct((2, tokens, tile * count), jnp.bfloat16) for count in counts
+        ],
         grid_spec=pltpu.PrefetchScalarGridSpec(
             num_scalar_prefetch=1,
-            grid=(count,),
+            grid=(sum(counts),),
             in_specs=[whole, whole, weights, weights]
             + [pl.BlockSpec(memory_space=pl.ANY)] * len(after),
-            out_specs=pl.BlockSpec((2, tokens, tile), lambda i, place_ref: (0, 0, i)),
+            out_specs=[
+                pl.BlockSpec((2, tokens, tile), out_tile(run)) for run in range(len(counts))
+            ],
         ),
-        flops=4 * tokens * width * tile * count,
-        moved=4 * width * tile * count,
+        flops=4 * tokens * width * tile * sum(counts),
+        moved=4 * width * tile * sum(counts),
         vmem=38,
     )(place, same, other, gate, up, *after)
 
@@ -259,26 +292,38 @@
     return (hidden - mean) * lax.rsqrt(var + epsilon)
 
 
-def unit_kernel(mine_ref, theirs_ref, *refs):
-    refs[-1][...] = zscore(mine_ref[...], theirs_ref[...]).astype(jnp.bfloat16)
+def unit_kernel(counts, mine_ref, *refs):
+    first = 0
+    for count, theirs_ref in zip(counts, refs):
+
+        @pl.when((pl.program_id(0) >= first) & (pl.program_id(0) < first + count))
+        def _():
+            refs[-1][...] = zscore(mine_ref[...], theirs_ref[...]).astype(jnp.bfloat16)
+
+        first += count
 
 
 def unit_scores(mine, theirs, tile, first, after):
-    _, tokens, count = theirs.shape
-    return call(
-        unit_kernel,
-        out_shape=jax.ShapeDtypeStruct((tokens, count), jnp.bfloat16),
-        grid=(count // tile,),
-        in_specs=[
-            pl.BlockSpec((2, tokens, tile), lambda i: (0, 0, first + i)),
-            pl.BlockSpec((2, tokens, tile), lambda i: (0, 0, i)),
-        ]
+    tokens = mine.shape[1]
+    counts = [part.shape[2] // tile for part in theirs]
+    firsts = [sum(counts[:i]) for i in range(len(counts))]
+
+    def their_tile(run):
+        return lambda i: (0, 0, jnp.clip(i - firsts[run], 0, counts[run] - 1))
+
+    units = tile * sum(counts)
+    return call(
+        functools.partial(unit_kernel, counts),
+        out_shape=jax.ShapeDtypeStruct((tokens, units), jnp.bfloat16),
+        grid=(sum(counts),),
+        in_specs=[pl.BlockSpec((2, tokens, tile), lambda i: (0, 0, first + i))]
+        + [pl.BlockSpec((2, tokens, tile), their_tile(run)) for run in range(len(theirs))]
         + [pl.BlockSpec(memory_space=pl.ANY)] * len(after),
         out_specs=pl.BlockSpec((tokens, tile), lambda i: (0, i)),
-        flops=20 * tokens * count,
-        moved=10 * tokens * count,
+        flops=20 * tokens * units,
+        moved=10 * tokens * units,
         vmem=16,
-    )(mine, theirs, *after)
+    )(mine, *theirs, *after)
 
 
 def panel_kernel(mine_ref, theirs_ref, out_ref):
@@ -467,64 +512,47 @@
     bases = [((1 - side) * half + first) * tile for first in starts] + [side * half * tile, model]
     bases = jnp.stack(bases).astype(jnp.int32)
     model_number = jnp.reshape(model, (1,)).astype(jnp.int32)
-    targets = [
-        jnp.stack(
-            [model, chip, core, (side * half + first) * tile, ((1 - side) * half + first) * tile]
-        )
-        for first in (0, starts[2])
+    target = [model, chip, core, side * half * tile, (1 - side) * half * tile]
+    target = jnp.stack(target).astype(jnp.int32)
+
+    to_side, own_side = (1 - side) * half, side * half
+    places = [
+        [chip, core, to_side],
+        [chip, core, to_side + starts[1]],
+        [chip, core, to_side + starts[2], own_side],
     ]
-    targets = [target.astype(jnp.int32) for target in targets]
-
-    to_side = jnp.stack([(1 - side) * half, chip, core]).astype(jnp.int32)
-    own_side = jnp.stack([side * half, chip, core]).astype(jnp.int32)
-    ready = [own_side, picks_b, picks_a, picks_own, bases, model_number, *targets]
-    sent, came = [], []
-    for first, count in zip(starts, chunks):
-        sent.append(
-            products(to_side, same, other, gate, up, tile, first, count, sent[-1:] or ready)
-        )
-        came.append(send(sent[-1], sizes, b_sides))
-    kept = products(own_side, same, other, gate, up, tile, 0, half, sent[-1:])
-
-    z = [unit_scores(kept, came[0], tile, starts[0], [])]
-
-    parts = sent + [kept]
-    picked_b = pick(bases, picks_b, parts, tile, [came[1], z[0]])
-    picked_own = pick(bases, picks_own, parts, tile, [picked_b])
-    picked_a = pick(bases, picks_a, parts, tile, [picked_own])
+    places = [jnp.stack(place).astype(jnp.int32) for place in places]
+    ready = [picks_b, picks_a, picks_own, bases, model_number, *places, target]
+    sent = products(places[0], same, other, gate, up, tile, chunks[:1], ready)
+    sent += products(places[1], same, other, gate, up, tile, chunks[1:2], sent)
+    sent += products(places[2], same, other, gate, up, tile, [chunks[2], half], sent[1:])
+    kept = sent[-1]
+    came = [send(part, sizes, b_sides) for part in sent[:3]]
+
+    z = [unit_scores(kept, came[:2], tile, 0, [])]
+    picked_b = pick(bases, picks_b, sent, tile, [z[0]])
+    picked_own = pick(bases, picks_own, sent, tile, [picked_b])
+    picked_a = pick(bases, picks_a, sent, tile, [picked_own])
     rows_b = panel_scores(picked_own, send(picked_b, sizes, a_sides), 1)
     rows_b = send(rows_b, sizes, a_to_b)
+    rows = panel_scores(
+        picked_own, send(picked_a, sizes, a_sides), 0, (model_number, rows_b)
+    )
+
     a_mine = send(z[0], sizes, b_to_a)
-    rows = panel_scores(
-        picked_own, send(picked_a, sizes, a_sides), 0, (model_number, rows_b), (a_mine,)
-    )
-
-    z.append(unit_scores(kept, came[1], tile, starts[1], [picked_a]))
-    z.append(unit_scores(kept, came[2], tile, starts[2], []))
-    a_far = send(a_mine, sizes, a_sides)
-    pieces = [(a_mine, a_far, z[0], send(a_far, sizes, a_to_b))]
-    a_mine = send(z[1], sizes, b_to_a)
-    far = send(choose(model_number, a_mine, z[1]), sizes, both_sides)
-    pieces.append((a_mine, far, z[1], far))
-    pieces.append(
-        (
-            send(z[2], sizes, b_to_a),
-            send(z[2], sizes, b_to_far_a),
-            z[2],
-            send(z[2], sizes, b_sides),
-        )
-    )
-
-    panel = join([rows, swapped(rows, sizes, 2)], [z[2], a_far])
-    arrived = [pieces[0][3], far, pieces[2][0], pieces[2][1], pieces[2][3]]
-    panel = join([panel, swapped(panel, sizes, 1)], arrived)
+    chosen = choose(model_number, a_mine, z[0])
+    far = send(chosen, sizes, both_sides)
+    pieces = [(a_mine, far, z[0], far)]
+    z.append(unit_scores(kept, came[2:], tile, starts[2], [rows]))
+    direct = [send(z[1], sizes, move) for move in (b_to_a, b_to_far_a, b_sides)]
+    pieces.append((direct[0], direct[1], z[1], direct[2]))
+
+    panel = join([rows, swapped(rows, sizes, 2)], [z[1], chosen])
+    panel = join([panel, swapped(panel, sizes, 1)], direct)
     panel_other = send(panel, sizes, other_core)
     shape = (2 * CHIPS * rows.shape[0], units)
-    result = scores(targets[0], [panel], (0,), pieces[:2], tile, shape, [], [])
-    result = scores(targets[0], [panel_other], (1,), pieces[:2], tile, shape, [result], [])
-    return scores(
-        targets[1], [panel, panel_other], (0, 1), pieces[2:], tile, shape, [result], []
-    )
+    result = scores(target, [panel], (0,), pieces, tile, shape, [], [])
+    return scores(target, [panel_other], (1,), pieces, tile, shape, [result], [])
 
 
 def solution(mesh):

time: 124 us -> 122 us (0.984)
  waiting for transfers between devices: 31.3 us -> 44 us
  starting transfers between devices: 36.5 us -> 24.5 us
  Pallas kernels: 52.8 us -> 50.2 us
    ppermute x21 -> x18, waiting for transfers between devices: 31.3 us -> 44 us  [send(): return lax.ppermute(block, AXES, routes(sizes, move))]
    ppermute x21 -> x18, starting transfers between devices: 36.5 us -> 24.5 us  [send(): return lax.ppermute(block, AXES, routes(sizes, move))]
    pallas_call x3 -> x2, Pallas kernels: 10.8 us -> 9.25 us  [scores(): call(functools.partial(score_kernel, 1.0 / math.sqrt(tokens), tile, cores...]
    pallas_call x7 -> x5, Pallas kernels: 35.3 us -> 33.8 us  [the longest x3 31.7 us: products(): call(functools.partial(products_kernel, counts, len(after)), out_shape=[j...]
  transfers between devices with their start and end apart: 21 -> 18, of which waited for: 9 -> 10; matrix products, arithmetic and copies ran while one was open for 1% -> 1% of each run, Pallas kernels for 33% -> 33%
where the time goes in v5:
time: 122 us; the launch traced here: 121 us
  Pallas kernels  50.2 us (41%)
  waiting for transfers between devices  44 us (36%)
  starting transfers between devices  24.5 us (20%)
  local copies, waits for them, and re-layouts  1.92 us (2%)
    ppermute x18, waiting for transfers between devices, send(): return lax.ppermute(block, AXES, routes(sizes, move))  44 us
    pallas_call x3, Pallas kernels, products(): call(functools.partial(products_kernel, counts, len(after)), out_shape=[j...  31.7 us
    ppermute x18, starting transfers between devices, send(): return lax.ppermute(block, AXES, routes(sizes, move))  24.5 us
    pallas_call x2, Pallas kernels, scores(): call(functools.partial(score_kernel, 1.0 / math.sqrt(tokens), tile, cores...  9.25 us
    pallas_call x3, Pallas kernels, pick(): call(functools.partial(pick_kernel, counts, tile), out_shape=jax.ShapeDty...  5.96 us
  transfers between devices with their start and end apart: 18, of which 10 were waited for; matrix products, arithmetic and copies ran while one was open for 1% of the time, Pallas kernels for 33%

profile of v5, /device:TPU:0, one launch (start us, length us, event | category | flops | bytes accessed | tf_op | source)
XLA Modules:
  0.0 121.3 jit_solution(5674429385482764491)
XLA Ops:
  0.0 5.0 %collective-permute-start.2 = (bf16[32,4096]{1,0:T(8,128)(2,1)}, bf16[32,4096]{1,0:T(8,128)(2,1)S(1)}, u32[]{:S(2)}, u32[]{:S(2)}) collective-permute-start(bf16[32,4096]{1,0:T(8,128)(2,1)} %bitcast.19), channel_id=1, source_target_pairs={{0,12},{1,13},{2,14},{3,15},{4,0},{5,1},{6,2},{7,3},{8,4},{9,5},{1... | collective-permute-start | bytes 786440 | tf_op jit(solution)/shard_map/ppermute | solution.py:99
  5.1 1.0 collective-permute-start
  6.1 6.1 %collective-permute-done.2.refs_3_ = bf16[32,4096]{1,0:T(8,128)(2,1)S(1)} collective-permute-done((bf16[32,4096]{1,0:T(8,128)(2,1)}, bf16[32,4096]{1,0:T(8,128)(2,1)S(1)}, u32[]{:S(2)}, u32[]{:S(2)}) %collective-permute-start.2) | collective-permute-done | bytes 262176 | tf_op jit(solution)/shard_map/ppermute | solution.py:99
  12.1 15.4 %collective-permute-done.1.refs_2_ = bf16[32,4096]{1,0:T(8,128)(2,1)S(1)} collective-permute-done((bf16[32,4096]{1,0:T(8,128)(2,1)}, bf16[32,4096]{1,0:T(8,128)(2,1)S(1)}, u32[]{:S(2)}, u32[]{:S(2)}) %collective-permute-start.1) | collective-permute-done | bytes 262176 | tf_op jit(solution)/shard_map/ppermute | solution.py:99
  27.6 0.9 copy-done
  28.5 0.1 shard_map.46.same_ref
  28.6 0.1 collective-permute-start.3
  28.8 0.8 reshape.19
  29.5 0.1 stack.65.refs_3_.bases_ref
  29.6 0.1 stack.62.refs_8_.where_ref
  29.7 0.1 pad_add_fusion.3.refs_7_.place_ref
  29.8 0.1 pad_add_fusion
  29.9 1.5 %collective-permute-done.3.other_ref = bf16[128,4096]{1,0:T(8,128)(2,1)S(1)} collective-permute-done((bf16[128,4096]{1,0:T(8,128)(2,1)S(1)}, bf16[128,4096]{1,0:T(8,128)(2,1)S(1)}, u32[]{:S(2)}, u32[]{:S(2)}) %collective-permute-start.3) | collective-permute-done | bytes 1048608 | tf_op jit(solution)/shard_map/ppermute | solution.py:99
  31.4 5.5 %shard_map.47.refs_0_ = bf16[2,256,512]{2,1,0:T(8,128)(2,1)S(1)} custom-call(s32[3]{0:T(128)S(1)} %get-tuple-element.11.place_ref.refs_5_, bf16[128,4096]{1,0:T(8,128)(2,1)S(1)} %shard_map.46.same_ref, bf16[128,4096]{1,0:T(8,128)(2,1)S(1)} %collective-permute-done.3.other_ref, bf16[4096,3584]{1,0:T(8,128)(2,1)} %bitcast.25, bf16[4096,3584]{1,0:T(8,128)(2,1)} %bitcast.28, ...), custom_call_target="tpu_custom_call" | custom-call | flops 2147483648 | bytes 8388608 | tf_op jit(solution)/shard_map/pallas_call | solution.py:226
  36.8 0.7 collective-permute-start.4
  37.5 7.6 %shard_map.48.refs_0_.refs_1_ = bf16[2,256,768]{2,1,0:T(8,128)(2,1)S(1)} custom-call(s32[3]{0:T(128)S(1)} %get-tuple-element.12.refs_6_.place_ref, bf16[128,4096]{1,0:T(8,128)(2,1)S(1)} %shard_map.46.same_ref, bf16[128,4096]{1,0:T(8,128)(2,1)S(1)} %collective-permute-done.3.other_ref, bf16[4096,3584]{1,0:T(8,128)(2,1)} %bitcast.26, ...), custom_call_target="tpu_custom_call" | custom-call | flops 3221225472 | bytes 12582912 | tf_op jit(solution)/shard_map/pallas_call | solution.py:226
  45.2 0.7 collective-permute-start.5
  45.9 18.6 %shard_map.49 = (bf16[2,256,512]{2,1,0:T(8,128)(2,1)S(1)}, bf16[2,256,1792]{2,1,0:T(8,128)(2,1)S(1)}) custom-call(s32[4]{0:T(128)S(1)} %pad_add_fusion.3.refs_7_.place_ref, bf16[128,4096]{1,0:T(8,128)(2,1)S(1)} %shard_map.46.same_ref, bf16[128,4096]{1,0:T(8,128)(2,1)S(1)} %collective-permute-done.3.other_ref, bf16[4096,3584]{1,0:T(8,128)(2,1)} %bitcast.27, ...), custom_call_target="tpu_custom_call" | custom-call | flops 9663676416 | bytes 37748736 | tf_op jit(solution)/shard_map/pallas_call | solution.py:226
  64.5 0.7 collective-permute-start.10
  65.2 1.5 %shard_map.50.refs_4_.second_ref.refs_3_ = bf16[256,1280]{1,0:T(8,128)(2,1)S(1)} custom-call(bf16[2,256,1792]{2,1,0:T(8,128)(2,1)S(1)} %get-tuple-element.8.mine_ref.refs_3_, bf16[2,256,512]{2,1,0:T(8,128)(2,1)S(1)} %collective-permute-done.4.refs_0_, bf16[2,256,768]{2,1,0:T(8,128)(2,1)S(1)} %collective-permute-done.5.refs_1_), custom_call_target="tpu_custom_call" | custom-call | flops 6553600 | bytes 3276800 | tf_op jit(solution)/shard_map/pallas_call | solution.py:315
  66.7 1.3 %collective-permute-start.11 = (bf16[256,1280]{1,0:T(8,128)(2,1)S(1)}, bf16[256,1280]{1,0:T(8,128)(2,1)S(1)}, u32[]{:S(2)}, u32[]{:S(2)}) collective-permute-start(bf16[256,1280]{1,0:T(8,128)(2,1)S(1)} %shard_map.50.refs_4_.second_ref.refs_3_), channel_id=1, source_target_pairs={{16,0},{17,1},{18,2},{19,3},{20,4},{21,5},{22,6},{23,7},{24,8},{25... | collective-permute-start | bytes 1966088 | tf_op jit(solution)/shard_map/ppermute | solution.py:99
  68.0 1.7 %shard_map.51.refs_4_ = bf16[2,256,256]{2,1,0:T(8,128)(2,1)S(1)} custom-call(s32[5]{0:T(128)S(1)} %stack.65.refs_3_.bases_ref, s32[1,256]{1,0:T(1,128)S(1)} %get-tuple-element.10.refs_0_.picks_ref, bf16[2,256,512]{2,1,0:T(8,128)(2,1)S(1)} %shard_map.47.refs_0_, bf16[2,256,768]{2,1,0:T(8,128)(2,1)S(1)} %shard_map.48.refs_0_.refs_1_, ...), custom_call_target="tpu_custom_call" | custom-call | flops 939524096 | bytes 3670016 | tf_op jit(solution)/shard_map/pallas_call | solution.py:272
  69.7 3.5 %collective-permute-start.7 = (bf16[2,256,256]{2,1,0:T(8,128)(2,1)S(1)}, bf16[2,256,256]{2,1,0:T(8,128)(2,1)S(1)}, u32[]{:S(2)}, u32[]{:S(2)}) collective-permute-start(bf16[2,256,256]{2,1,0:T(8,128)(2,1)S(1)} %shard_map.51.refs_4_), channel_id=1, source_target_pairs={{0,1},{1,0},{2,3},{3,2},{4,5},{5,4},{6,7},{7,6},{8,9},{9,8},{10,11... | collective-permute-start | bytes 786440 | tf_op jit(solution)/shard_map/ppermute | solution.py:99
  73.2 2.6 %shard_map.52.refs_4_.mine_ref = bf16[2,256,512]{2,1,0:T(8,128)(2,1)S(1)} custom-call(s32[5]{0:T(128)S(1)} %stack.65.refs_3_.bases_ref, s32[1,512]{1,0:T(1,128)S(1)} %bitcast.24, bf16[2,256,512]{2,1,0:T(8,128)(2,1)S(1)} %shard_map.47.refs_0_, bf16[2,256,768]{2,1,0:T(8,128)(2,1)S(1)} %shard_map.48.refs_0_.refs_1_, ...), custom_call_target="tpu_custom_call" | custom-call | flops 1879048192 | bytes 3670016 | tf_op jit(solution)/shard_map/pallas_call | solution.py:272
  75.8 1.7 %shard_map.53 = bf16[2,256,256]{2,1,0:T(8,128)(2,1)S(1)} custom-call(s32[5]{0:T(128)S(1)} %stack.65.refs_3_.bases_ref, s32[1,256]{1,0:T(1,128)S(1)} %get-tuple-element.9.refs_1_.picks_ref, bf16[2,256,512]{2,1,0:T(8,128)(2,1)S(1)} %shard_map.47.refs_0_, bf16[2,256,768]{2,1,0:T(8,128)(2,1)S(1)} %shard_map.48.refs_0_.refs_1_, ...), custom_call_target="tpu_custom_call" | custom-call | flops 939524096 | bytes 3670016 | tf_op jit(solution)/shard_map/pallas_call | solution.py:272
  77.5 2.4 %collective-permute-start.6 = (bf16[2,256,256]{2,1,0:T(8,128)(2,1)S(1)}, bf16[2,256,256]{2,1,0:T(8,128)(2,1)S(1)}, u32[]{:S(2)}, u32[]{:S(2)}) collective-permute-start(bf16[2,256,256]{2,1,0:T(8,128)(2,1)S(1)} %shard_map.53), channel_id=1, source_target_pairs={{0,1},{1,0},{2,3},{3,2},{4,5},{5,4},{6,7},{7,6},{8,9},{9,8},{10,11... | collective-permute-start | bytes 786440 | tf_op jit(solution)/shard_map/ppermute | solution.py:99
  79.9 0.1 collective-permute-done.7.theirs_ref
  80.0 0.3 shard_map.54
  80.3 1.8 %collective-permute-start.8 = (bf16[256,256]{1,0:T(8,128)(2,1)S(1)}, bf16[256,256]{1,0:T(8,128)(2,1)S(1)}, u32[]{:S(2)}, u32[]{:S(2)}) collective-permute-start(bf16[256,256]{1,0:T(8,128)(2,1)S(1)} %shard_map.54), channel_id=1, source_target_pairs={{0,16},{1,17},{2,18},{3,19},{4,20},{5,21},{6,22},{7,23},{8,24},{9,... | collective-permute-start | bytes 393224 | tf_op jit(solution)/shard_map/ppermute | solution.py:99
  82.1 5.4 %collective-permute-done.6.theirs_ref = bf16[2,256,256]{2,1,0:T(8,128)(2,1)S(1)} collective-permute-done((bf16[2,256,256]{2,1,0:T(8,128)(2,1)S(1)}, bf16[2,256,256]{2,1,0:T(8,128)(2,1)S(1)}, u32[]{:S(2)}, u32[]{:S(2)}) %collective-permute-start.6) | collective-permute-done | bytes 262176 | tf_op jit(solution)/shard_map/ppermute | solution.py:99
  87.5 0.3 shard_map.55.refs_1_.refs_0_
  87.8 2.9 %collective-permute-start.9 = (bf16[256,256]{1,0:T(8,128)(2,1)S(1)}, bf16[256,256]{1,0:T(8,128)(2,1)S(1)}, u32[]{:S(2)}, u32[]{:S(2)}) collective-permute-start(bf16[256,256]{1,0:T(8,128)(2,1)S(1)} %shard_map.55.refs_1_.refs_0_), channel_id=1, source_target_pairs={{0,8},{1,9},{2,10},{3,11},{4,12},{5,13},{6,14},{7,15},{8,0},{9,1},... | collective-permute-start | bytes 393224 | tf_op jit(solution)/shard_map/ppermute | solution.py:99
  90.7 0.1 collective-permute-done.11.first_ref.refs_1_
  90.9 0.7 collective-permute-start.17
  91.6 0.6 shard_map.56.refs_2_.refs_7_
  92.2 0.7 collective-permute-start.15
  92.9 1.3 %collective-permute-start.14 = (bf16[256,512]{1,0:T(8,128)(2,1)S(1)}, bf16[256,512]{1,0:T(8,128)(2,1)S(1)}, u32[]{:S(2)}, u32[]{:S(2)}) collective-permute-start(bf16[256,512]{1,0:T(8,128)(2,1)S(1)} %shard_map.56.refs_2_.refs_7_), channel_id=1, source_target_pairs={{16,1},{17,0},{18,3},{19,2},{20,5},{21,4},{22,7},{23,6},{24,9},{25... | collective-permute-start | bytes 786440 | tf_op jit(solution)/shard_map/ppermute | solution.py:99
  94.2 1.3 %collective-permute-start.13 = (bf16[256,512]{1,0:T(8,128)(2,1)S(1)}, bf16[256,512]{1,0:T(8,128)(2,1)S(1)}, u32[]{:S(2)}, u32[]{:S(2)}) collective-permute-start(bf16[256,512]{1,0:T(8,128)(2,1)S(1)} %shard_map.56.refs_2_.refs_7_), channel_id=1, source_target_pairs={{16,0},{17,1},{18,2},{19,3},{20,4},{21,5},{22,6},{23,7},{24,8},{25... | collective-permute-start | bytes 786440 | tf_op jit(solution)/shard_map/ppermute | solution.py:99
  95.5 0.6 collective-permute-done.9.refs_1_
  96.1 0.3 shard_map.58.refs_0_
  96.5 0.5 collective-permute-start.12
  96.9 8.0 %collective-permute-done.14.refs_3_.refs_6_ = bf16[256,512]{1,0:T(8,128)(2,1)S(1)} collective-permute-done((bf16[256,512]{1,0:T(8,128)(2,1)S(1)}, bf16[256,512]{1,0:T(8,128)(2,1)S(1)}, u32[]{:S(2)}, u32[]{:S(2)}) %collective-permute-start.14) | collective-permute-done | bytes 262176 | tf_op jit(solution)/shard_map/ppermute | solution.py:99
  104.9 2.9 %collective-permute-done.13.refs_2_.refs_5_ = bf16[256,512]{1,0:T(8,128)(2,1)S(1)} collective-permute-done((bf16[256,512]{1,0:T(8,128)(2,1)S(1)}, bf16[256,512]{1,0:T(8,128)(2,1)S(1)}, u32[]{:S(2)}, u32[]{:S(2)}) %collective-permute-start.13) | collective-permute-done | bytes 262176 | tf_op jit(solution)/shard_map/ppermute | solution.py:99
  107.9 0.1 shard_map.59.refs_0_
  107.9 0.1 collective-permute-start.16
  108.0 3.9 %collective-permute-done.17.refs_2_.refs_4_ = bf16[256,1280]{1,0:T(8,128)(2,1)S(1)} collective-permute-done((bf16[256,1280]{1,0:T(8,128)(2,1)S(1)}, bf16[256,1280]{1,0:T(8,128)(2,1)S(1)}, u32[]{:S(2)}, u32[]{:S(2)}) %collective-permute-start.17) | collective-permute-done | bytes 655392 | tf_op jit(solution)/shard_map/ppermute | solution.py:99
  111.9 4.7 %shard_map.60.refs_9_ = bf16[2048,3584]{1,0:T(8,128)(2,1)} custom-call(s32[5]{0:T(128)S(1)} %stack.62.refs_8_.where_ref, bf16[1024,256]{1,0:T(8,128)(2,1)S(1)} %shard_map.59.refs_0_, bf16[256,1280]{1,0:T(8,128)(2,1)S(1)} %collective-permute-done.11.first_ref.refs_1_, bf16[256,1280]{1,0:T(8,128)(2,1)S(1)} %collective-permute-done.17.refs_2_.refs_4_, ...), custom_call_target="tpu_custom_call" | custom-call | flops 1879048192 | bytes 7340032 | tf_op jit(solution)/shard_map/pallas_call | solution.py:445
  116.6 4.5 %shard_map.61 = bf16[2048,3584]{1,0:T(8,128)(2,1)} custom-call(s32[5]{0:T(128)S(1)} %stack.62.refs_8_.where_ref, bf16[1024,256]{1,0:T(8,128)(2,1)S(1)} %collective-permute-done.16.refs_0_, bf16[256,1280]{1,0:T(8,128)(2,1)S(1)} %collective-permute-done.11.first_ref.refs_1_, ...), custom_call_target="tpu_custom_call", output_to_operand_aliasing={{}: (10, {})} | custom-call | flops 1879048192 | bytes 7340032 | tf_op jit(solution)/shard_map/pallas_call | solution.py:445
  (14 shorter events, 0.1 us)
Async XLA Ops:
  0.0 12.1 %collective-permute-start.2 = (bf16[32,4096]{1,0:T(8,128)(2,1)}, bf16[32,4096]{1,0:T(8,128)(2,1)S(1)}, u32[]{:S(2)}, u32[]{:S(2)}) collective-permute-start(bf16[32,4096]{1,0:T(8,128)(2,1)} %bitcast.19), channel_id=1, source_target_pairs={{0,12},{1,13},{2,14},{3,15},{4,0},{5,1},{6,2},{7,3},{8,4},{9,5},{1... | collective-permute-start | bytes 786440 | tf_op jit(solution)/shard_map/ppermute | solution.py:99
  5.0 22.5 %collective-permute-start.1 = (bf16[32,4096]{1,0:T(8,128)(2,1)}, bf16[32,4096]{1,0:T(8,128)(2,1)S(1)}, u32[]{:S(2)}, u32[]{:S(2)}) collective-permute-start(bf16[32,4096]{1,0:T(8,128)(2,1)} %bitcast.20), channel_id=1, source_target_pairs={{0,8},{1,9},{2,10},{3,11},{4,12},{5,13},{6,14},{7,15},{8,0},{9,1},... | collective-permute-start | bytes 786440 | tf_op jit(solution)/shard_map/ppermute | solution.py:99
  5.1 22.5 %collective-permute-start = (bf16[32,4096]{1,0:T(8,128)(2,1)}, bf16[32,4096]{1,0:T(8,128)(2,1)S(1)}, u32[]{:S(2)}, u32[]{:S(2)}) collective-permute-start(bf16[32,4096]{1,0:T(8,128)(2,1)} %bitcast.21), channel_id=1, source_target_pairs={{0,4},{1,5},{2,6},{3,7},{4,8},{5,9},{6,10},{7,11},{8,12},{9,13},{1... | collective-permute-start | bytes 786440 | tf_op jit(solution)/shard_map/ppermute | solution.py:99
  27.6 1.0 copy-start
  28.6 2.7 %collective-permute-start.3 = (bf16[128,4096]{1,0:T(8,128)(2,1)S(1)}, bf16[128,4096]{1,0:T(8,128)(2,1)S(1)}, u32[]{:S(2)}, u32[]{:S(2)}) collective-permute-start(bf16[128,4096]{1,0:T(8,128)(2,1)S(1)} %shard_map.46.same_ref), channel_id=1, source_target_pairs={{0,2},{1,3},{2,0},{3,1},{4,6},{5,7},{6,4},{7,5},{8,10},{9,11},{10,... | collective-permute-start | bytes 3145736 | tf_op jit(solution)/shard_map/ppermute | solution.py:99
  36.8 28.3 %collective-permute-start.4 = (bf16[2,256,512]{2,1,0:T(8,128)(2,1)S(1)}, bf16[2,256,512]{2,1,0:T(8,128)(2,1)S(1)}, u32[]{:S(2)}, u32[]{:S(2)}) collective-permute-start(bf16[2,256,512]{2,1,0:T(8,128)(2,1)S(1)} %shard_map.47.refs_0_), channel_id=1, source_target_pairs={{16,17},{17,16},{18,19},{19,18},{20,21},{21,20},{22,23},{23,22},{2... | collective-permute-start | bytes 1572872 | tf_op jit(solution)/shard_map/ppermute | solution.py:99
  45.2 20.0 %collective-permute-start.5 = (bf16[2,256,768]{2,1,0:T(8,128)(2,1)S(1)}, bf16[2,256,768]{2,1,0:T(8,128)(2,1)S(1)}, u32[]{:S(2)}, u32[]{:S(2)}) collective-permute-start(bf16[2,256,768]{2,1,0:T(8,128)(2,1)S(1)} %shard_map.48.refs_0_.refs_1_), channel_id=1, source_target_pairs={{16,17},{17,16},{18,19},{19,18},{20,21},{21,20},{22,23},{23,22},{2... | collective-permute-start | bytes 2359304 | tf_op jit(solution)/shard_map/ppermute | solution.py:99
  64.5 27.1 %collective-permute-start.10 = (bf16[2,256,512]{2,1,0:T(8,128)(2,1)S(1)}, bf16[2,256,512]{2,1,0:T(8,128)(2,1)S(1)}, u32[]{:S(2)}, u32[]{:S(2)}) collective-permute-start(bf16[2,256,512]{2,1,0:T(8,128)(2,1)S(1)} %get-tuple-element.7.refs_2_), channel_id=1, source_target_pairs={{16,17},{17,16},{18,19},{19,18},{20,21},{21,20},{22,23},{23,22},{2... | collective-permute-start | bytes 1572872 | tf_op jit(solution)/shard_map/ppermute | solution.py:99
  66.7 24.1 %collective-permute-start.11 = (bf16[256,1280]{1,0:T(8,128)(2,1)S(1)}, bf16[256,1280]{1,0:T(8,128)(2,1)S(1)}, u32[]{:S(2)}, u32[]{:S(2)}) collective-permute-start(bf16[256,1280]{1,0:T(8,128)(2,1)S(1)} %shard_map.50.refs_4_.second_ref.refs_3_), channel_id=1, source_target_pairs={{16,0},{17,1},{18,2},{19,3},{20,4},{21,5},{22,6},{23,7},{24,8},{25... | collective-permute-start | bytes 1966088 | tf_op jit(solution)/shard_map/ppermute | solution.py:99
  69.7 10.2 %collective-permute-start.7 = (bf16[2,256,256]{2,1,0:T(8,128)(2,1)S(1)}, bf16[2,256,256]{2,1,0:T(8,128)(2,1)S(1)}, u32[]{:S(2)}, u32[]{:S(2)}) collective-permute-start(bf16[2,256,256]{2,1,0:T(8,128)(2,1)S(1)} %shard_map.51.refs_4_), channel_id=1, source_target_pairs={{0,1},{1,0},{2,3},{3,2},{4,5},{5,4},{6,7},{7,6},{8,9},{9,8},{10,11... | collective-permute-start | bytes 786440 | tf_op jit(solution)/shard_map/ppermute | solution.py:99
  77.5 10.0 %collective-permute-start.6 = (bf16[2,256,256]{2,1,0:T(8,128)(2,1)S(1)}, bf16[2,256,256]{2,1,0:T(8,128)(2,1)S(1)}, u32[]{:S(2)}, u32[]{:S(2)}) collective-permute-start(bf16[2,256,256]{2,1,0:T(8,128)(2,1)S(1)} %shard_map.53), channel_id=1, source_target_pairs={{0,1},{1,0},{2,3},{3,2},{4,5},{5,4},{6,7},{7,6},{8,9},{9,8},{10,11... | collective-permute-start | bytes 786440 | tf_op jit(solution)/shard_map/ppermute | solution.py:99
  80.3 7.2 %collective-permute-start.8 = (bf16[256,256]{1,0:T(8,128)(2,1)S(1)}, bf16[256,256]{1,0:T(8,128)(2,1)S(1)}, u32[]{:S(2)}, u32[]{:S(2)}) collective-permute-start(bf16[256,256]{1,0:T(8,128)(2,1)S(1)} %shard_map.54), channel_id=1, source_target_pairs={{0,16},{1,17},{2,18},{3,19},{4,20},{5,21},{6,22},{7,23},{8,24},{9,... | collective-permute-start | bytes 393224 | tf_op jit(solution)/shard_map/ppermute | solution.py:99
  87.8 8.3 %collective-permute-start.9 = (bf16[256,256]{1,0:T(8,128)(2,1)S(1)}, bf16[256,256]{1,0:T(8,128)(2,1)S(1)}, u32[]{:S(2)}, u32[]{:S(2)}) collective-permute-start(bf16[256,256]{1,0:T(8,128)(2,1)S(1)} %shard_map.55.refs_1_.refs_0_), channel_id=1, source_target_pairs={{0,8},{1,9},{2,10},{3,11},{4,12},{5,13},{6,14},{7,15},{8,0},{9,1},... | collective-permute-start | bytes 393224 | tf_op jit(solution)/shard_map/ppermute | solution.py:99
  90.9 21.0 %collective-permute-start.17 = (bf16[256,1280]{1,0:T(8,128)(2,1)S(1)}, bf16[256,1280]{1,0:T(8,128)(2,1)S(1)}, u32[]{:S(2)}, u32[]{:S(2)}) collective-permute-start(bf16[256,1280]{1,0:T(8,128)(2,1)S(1)} %shard_map.57.refs_3_), channel_id=1, source_target_pairs={{0,1},{1,0},{2,3},{3,2},{4,5},{5,4},{6,7},{7,6},{8,9},{9,8},{10,11... | collective-permute-start | bytes 1966088 | tf_op jit(solution)/shard_map/ppermute | solution.py:99
  92.2 4.7 %collective-permute-start.15 = (bf16[256,512]{1,0:T(8,128)(2,1)S(1)}, bf16[256,512]{1,0:T(8,128)(2,1)S(1)}, u32[]{:S(2)}, u32[]{:S(2)}) collective-permute-start(bf16[256,512]{1,0:T(8,128)(2,1)S(1)} %shard_map.56.refs_2_.refs_7_), channel_id=1, source_target_pairs={{16,17},{17,16},{18,19},{19,18},{20,21},{21,20},{22,23},{23,22},{2... | collective-permute-start | bytes 786440 | tf_op jit(solution)/shard_map/ppermute | solution.py:99
  92.9 12.0 %collective-permute-start.14 = (bf16[256,512]{1,0:T(8,128)(2,1)S(1)}, bf16[256,512]{1,0:T(8,128)(2,1)S(1)}, u32[]{:S(2)}, u32[]{:S(2)}) collective-permute-start(bf16[256,512]{1,0:T(8,128)(2,1)S(1)} %shard_map.56.refs_2_.refs_7_), channel_id=1, source_target_pairs={{16,1},{17,0},{18,3},{19,2},{20,5},{21,4},{22,7},{23,6},{24,9},{25... | collective-permute-start | bytes 786440 | tf_op jit(solution)/shard_map/ppermute | solution.py:99
  94.2 13.7 %collective-permute-start.13 = (bf16[256,512]{1,0:T(8,128)(2,1)S(1)}, bf16[256,512]{1,0:T(8,128)(2,1)S(1)}, u32[]{:S(2)}, u32[]{:S(2)}) collective-permute-start(bf16[256,512]{1,0:T(8,128)(2,1)S(1)} %shard_map.56.refs_2_.refs_7_), channel_id=1, source_target_pairs={{16,0},{17,1},{18,2},{19,3},{20,4},{21,5},{22,6},{23,7},{24,8},{25... | collective-permute-start | bytes 786440 | tf_op jit(solution)/shard_map/ppermute | solution.py:99
  96.5 11.4 %collective-permute-start.12 = (bf16[512,256]{1,0:T(8,128)(2,1)S(1)}, bf16[512,256]{1,0:T(8,128)(2,1)S(1)}, u32[]{:S(2)}, u32[]{:S(2)}) collective-permute-start(bf16[512,256]{1,0:T(8,128)(2,1)S(1)} %shard_map.58.refs_0_), channel_id=1, source_target_pairs={{0,4},{1,5},{2,6},{3,7},{4,0},{5,1},{6,2},{7,3},{8,12},{9,13},{10,... | collective-permute-start | bytes 786440 | tf_op jit(solution)/shard_map/ppermute | solution.py:99
  107.9 8.7 %collective-permute-start.16 = (bf16[1024,256]{1,0:T(8,128)(2,1)S(1)}, bf16[1024,256]{1,0:T(8,128)(2,1)S(1)}, u32[]{:S(2)}, u32[]{:S(2)}) collective-permute-start(bf16[1024,256]{1,0:T(8,128)(2,1)S(1)} %shard_map.59.refs_0_), channel_id=1, source_target_pairs={{0,2},{1,3},{2,0},{3,1},{4,6},{5,7},{6,4},{7,5},{8,10},{9,11},{10,... | collective-permute-start | bytes 1572872 | tf_op jit(solution)/shard_map/ppermute | solution.py:99

commit v6 on v5

--- a/solution.py
+++ b/solution.py
@@ -138,7 +138,7 @@
         out_specs=pl.BlockSpec(memory_space=pltpu.VMEM),
         scratch_shapes=[pltpu.SemaphoreType.DMA((count,))],
         flops=0,
-        moved=4 * count * rows * width,
+        moved=0,
         vmem=16,
     )(*blocks, *after)
 
@@ -162,27 +162,6 @@
         cost_estimate=pl.CostEstimate(flops=flops, bytes_accessed=moved, transcendentals=0),
         **rest,
     )
-
-
-def choose_kernel(model_ref, first_ref, second_ref, out_ref):
-    for holder, ref in enumerate((first_ref, second_ref)):
-
-        @pl.when(model_ref[0] == holder)
-        def _():
-            out_ref[...] = ref[...]
-
-
-def choose(model_number, first, second):
-    vmem = pl.BlockSpec(memory_space=pltpu.VMEM)
-    return call(
-        choose_kernel,
-        out_shape=jax.ShapeDtypeStruct(first.shape, first.dtype),
-        in_specs=[pl.BlockSpec(memory_space=pltpu.SMEM), vmem, vmem],
-        out_specs=vmem,
-        flops=0,
-        moved=4 * first.size,
-        vmem=16,
-    )(model_number, first, second)
 
 
 def products_kernel(counts, n_after, place_ref, same_ref, other_ref, gate_ref, up_ref, *refs):
@@ -276,8 +255,8 @@
         + [vmem] * len(parts)
         + [pl.BlockSpec(memory_space=pl.ANY)] * len(after),
         out_specs=vmem,
-        flops=4 * tokens * picked * tile * sum(counts),
-        moved=4 * tokens * tile * sum(counts),
+        flops=0,
+        moved=0,
         vmem=16,
     )(bases, picks, *parts, *after)
 
@@ -292,38 +271,35 @@
     return (hidden - mean) * lax.rsqrt(var + epsilon)
 
 
-def unit_kernel(counts, mine_ref, *refs):
-    first = 0
-    for count, theirs_ref in zip(counts, refs):
-
-        @pl.when((pl.program_id(0) >= first) & (pl.program_id(0) < first + count))
-        def _():
-            refs[-1][...] = zscore(mine_ref[...], theirs_ref[...]).astype(jnp.bfloat16)
-
-        first += count
-
-
-def unit_scores(mine, theirs, tile, first, after):
-    tokens = mine.shape[1]
-    counts = [part.shape[2] // tile for part in theirs]
-    firsts = [sum(counts[:i]) for i in range(len(counts))]
-
-    def their_tile(run):
-        return lambda i: (0, 0, jnp.clip(i - firsts[run], 0, counts[run] - 1))
-
-    units = tile * sum(counts)
+def unit_kernel(model_ref, mine_ref, theirs_ref, *refs):
+    @pl.when(model_ref[0] == 1)
+    def _():
+        refs[-1][...] = zscore(mine_ref[...], theirs_ref[...]).astype(jnp.bfloat16)
+
+    @pl.when(model_ref[0] == 0)
+    def _():
+        refs[-1][...] = jnp.zeros_like(refs[-1])
+
+
+def unit_scores(model_number, mine, theirs, tile, first, after):
+    _, tokens, units = theirs.shape
     return call(
-        functools.partial(unit_kernel, counts),
+        unit_kernel,
         out_shape=jax.ShapeDtypeStruct((tokens, units), jnp.bfloat16),
-        grid=(sum(counts),),
-        in_specs=[pl.BlockSpec((2, tokens, tile), lambda i: (0, 0, first + i))]
-        + [pl.BlockSpec((2, tokens, tile), their_tile(run)) for run in range(len(theirs))]
-        + [pl.BlockSpec(memory_space=pl.ANY)] * len(after),
-        out_specs=pl.BlockSpec((tokens, tile), lambda i: (0, i)),
-        flops=20 * tokens * units,
-        moved=10 * tokens * units,
+        grid_spec=pltpu.PrefetchScalarGridSpec(
+            num_scalar_prefetch=1,
+            grid=(units // tile,),
+            in_specs=[
+                pl.BlockSpec((2, tokens, tile), lambda i, model: (0, 0, (first + i) * model[0])),
+                pl.BlockSpec((2, tokens, tile), lambda i, model: (0, 0, i * model[0])),
+            ]
+            + [pl.BlockSpec(memory_space=pl.ANY)] * len(after),
+            out_specs=pl.BlockSpec((tokens, tile), lambda i, model: (0, i)),
+        ),
+        flops=0,
+        moved=0,
         vmem=16,
-    )(mine, *theirs, *after)
+    )(model_number, mine, theirs, *after)
 
 
 def panel_kernel(mine_ref, theirs_ref, out_ref):
@@ -360,38 +336,35 @@
             else units
         ),
         out_specs=rows,
-        flops=20 * tokens * count,
-        moved=10 * tokens * count,
+        flops=0,
+        moved=0,
         vmem=16,
     )(*given[:1], mine, theirs, *given[1:], *after)
 
 
-def score_kernel(scale, tile, cores, n_pieces, has_before, where_ref, *refs):
+def score_kernel(scale, tile, cores, widths, n_after, where_ref, *refs):
     panels, refs = refs[: len(cores)], refs[len(cores) :]
-    pieces = refs[: 4 * n_pieces]
-    out_ref, panel_ref, near_ref, far_ref, block_ref, in_sems, out_sems = refs[
-        4 * n_pieces + has_before :
-    ]
-    model, chip, core, near_column, far_column = (where_ref[i] for i in range(5))
-    rows = block_ref.shape[2]
-    columns = block_ref.shape[3]
-
-    def fetch(at):
+    pieces = []
+    for side in widths:
+        pieces.append(refs[: 2 * len(side)])
+        refs = refs[2 * len(side) :]
+    out_ref, panel_ref, refs = refs[n_after], refs[n_after + 1], refs[n_after + 2 :]
+    units_refs, block_refs = refs[: len(widths)], refs[len(widths) : 2 * len(widths)]
+    in_sems, out_sems = refs[2 * len(widths) :]
+    model, chip, core = (where_ref[i] for i in range(3))
+    rows = panel_ref.shape[1] // CHIPS
+
+    def fetch(holder):
+        pairs = [(ref, panel_ref.at[i]) for i, ref in enumerate(panels)]
+        for side, into in zip(pieces, units_refs):
+            start = 0
+            for ref in side[holder::2]:
+                pairs.append((ref, into.at[:, start : start + ref.shape[1]]))
+                start += ref.shape[1]
         copies = [
-            pltpu.make_async_copy(ref, panel_ref.at[i], in_sems.at[i])
-            for i, ref in enumerate(panels)
+            pltpu.make_async_copy(source, into, in_sems.at[i])
+            for i, (source, into) in enumerate(pairs)
         ]
-        for far, into in enumerate((near_ref, far_ref)):
-            start = 0
-            for piece in range(n_pieces):
-                ref = pieces[4 * piece + at + far]
-                stop = start + ref.shape[1]
-                copies.append(
-                    pltpu.make_async_copy(
-                        ref, into.at[:, start:stop], in_sems.at[len(cores) + 2 * piece + far]
-                    )
-                )
-                start = stop
         for copy in copies:
             copy.start()
         for copy in copies:
@@ -401,14 +374,15 @@
 
         @pl.when(model == holder)
         def _():
-            fetch(2 * holder)
+            fetch(holder)
 
     copies = []
     for which, other in enumerate(cores):
         for pair in range(CHIPS // 2):
             panel = panel_ref[which, 2 * pair * rows : (2 * pair + 2) * rows, :]
-            for units_ref, column in ((near_ref, near_column), (far_ref, far_column)):
-                slot = len(copies) // 2
+            slot = which * (CHIPS // 2) + pair
+            for side, (units_ref, block_ref) in enumerate(zip(units_refs, block_refs)):
+                columns = units_ref.shape[1]
                 for start in range(0, columns, tile):
                     total = jnp.dot(
                         panel,
@@ -426,9 +400,9 @@
                             block_ref.at[slot, i],
                             out_ref.at[
                                 pl.ds(pl.multiple_of(place * rows, rows), rows),
-                                pl.ds(pl.multiple_of(column, 128), columns),
+                                pl.ds(pl.multiple_of(where_ref[3 + side], 128), columns),
                             ],
-                            out_sems.at[slot, i],
+                            out_sems.at[slot, side, i],
                         )
                     )
                     copies[-1].start()
@@ -436,38 +410,33 @@
         copy.wait()
 
 
-def scores(where, panels, cores, pieces, tile, shape, before, after):
+def scores(where, panels, cores, sides, tile, shape, before):
     rows, tokens = panels[0].shape
-    columns = sum(piece[0].shape[1] for piece in pieces)
-    slots = len(panels) * CHIPS
+    widths = [[piece[0].shape[1] for piece in side] for side in sides]
+    slots = len(panels) * CHIPS // 2
     anywhere = pl.BlockSpec(memory_space=pl.ANY)
-    flat = [array for piece in pieces for array in piece]
+    flat = [array for side in sides for piece in side for array in piece]
+    columns = [sum(side) for side in widths]
     return call(
         functools.partial(
-            score_kernel,
-            1.0 / math.sqrt(tokens),
-            tile,
-            cores,
-            len(pieces),
-            len(before) + len(after),
+            score_kernel, 1.0 / math.sqrt(tokens), tile, cores, widths, len(before)
         ),
         out_shape=jax.ShapeDtypeStruct(shape, jnp.bfloat16),
         in_specs=[pl.BlockSpec(memory_space=pltpu.SMEM)]
-        + [anywhere] * (len(panels) + len(flat) + len(before) + len(after)),
+        + [anywhere] * (len(panels) + len(flat) + len(before)),
         out_specs=anywhere,
-        scratch_shapes=[
-            pltpu.VMEM((len(panels), rows, tokens), jnp.bfloat16),
-            pltpu.VMEM((tokens, columns), jnp.bfloat16),
-            pltpu.VMEM((tokens, columns), jnp.bfloat16),
-            pltpu.VMEM((slots, 2, rows // CHIPS, columns), jnp.bfloat16),
-            pltpu.SemaphoreType.DMA((len(panels) + 2 * len(pieces),)),
-            pltpu.SemaphoreType.DMA((slots, 2)),
+        scratch_shapes=[pltpu.VMEM((len(panels), rows, tokens), jnp.bfloat16)]
+        + [pltpu.VMEM((tokens, count), jnp.bfloat16) for count in columns]
+        + [pltpu.VMEM((slots, 2, rows // CHIPS, count), jnp.bfloat16) for count in columns]
+        + [
+            pltpu.SemaphoreType.DMA((len(panels) + sum(map(len, widths)),)),
+            pltpu.SemaphoreType.DMA((slots, len(sides), 2)),
         ],
         input_output_aliases={1 + len(panels) + len(flat): 0} if before else {},
-        flops=4 * len(panels) * rows * tokens * columns,
-        moved=4 * len(panels) * rows * columns,
+        flops=2 * len(panels) * rows * tokens * sum(columns),
+        moved=2 * len(panels) * rows * sum(columns),
         vmem=24,
-    )(where, *panels, *flat, *before, *after)
+    )(where, *panels, *flat, *before)
 
 
 def paired_body(acts, gate_w, up_w, panel_units):
@@ -481,8 +450,7 @@
     picks = panel_units.reshape(2, 2, sizes[1], -1)
     tile = picks.shape[3]
     half = units // 2 // tile
-    chunks = [2, half - 4, 2]
-    starts = [0, 2, half - 2]
+    chunks = [half - half // 2, half // 2]
 
     def b_sides(m, d, t):
         return (m, d, 1 - t) if m == 1 else None
@@ -509,50 +477,50 @@
     picks_far = lax.dynamic_index_in_dim(picks, 1 - side, axis=1, keepdims=False)
     picks_b, picks_a = picks_far[1:], picks_far[:1]
     picks_own = lax.dynamic_index_in_dim(picks, side, axis=1, keepdims=False).reshape(1, -1)
-    bases = [((1 - side) * half + first) * tile for first in starts] + [side * half * tile, model]
+    bases = [((1 - side) * half + first) * tile for first in (0, chunks[0])]
+    bases += [side * half * tile, model]
     bases = jnp.stack(bases).astype(jnp.int32)
     model_number = jnp.reshape(model, (1,)).astype(jnp.int32)
-    target = [model, chip, core, side * half * tile, (1 - side) * half * tile]
-    target = jnp.stack(target).astype(jnp.int32)
+    near, far = side * half * tile, (1 - side) * half * tile
+    targets = [[model, chip, core, near, far], [model, chip, core, far + chunks[0] * tile]]
+    targets = [jnp.stack(target).astype(jnp.int32) for target in targets]
 
     to_side, own_side = (1 - side) * half, side * half
-    places = [
-        [chip, core, to_side],
-        [chip, core, to_side + starts[1]],
-        [chip, core, to_side + starts[2], own_side],
-    ]
+    places = [[chip, core, to_side], [chip, core, to_side + chunks[0], own_side]]
     places = [jnp.stack(place).astype(jnp.int32) for place in places]
-    ready = [picks_b, picks_a, picks_own, bases, model_number, *places, target]
+    ready = [picks_b, picks_a, picks_own, bases, model_number, *places, *targets]
     sent = products(places[0], same, other, gate, up, tile, chunks[:1], ready)
-    sent += products(places[1], same, other, gate, up, tile, chunks[1:2], sent)
-    sent += products(places[2], same, other, gate, up, tile, [chunks[2], half], sent[1:])
+    sent += products(places[1], same, other, gate, up, tile, [chunks[1], half], sent)
     kept = sent[-1]
-    came = [send(part, sizes, b_sides) for part in sent[:3]]
-
-    z = [unit_scores(kept, came[:2], tile, 0, [])]
-    picked_b = pick(bases, picks_b, sent, tile, [z[0]])
-    picked_own = pick(bases, picks_own, sent, tile, [picked_b])
-    picked_a = pick(bases, picks_a, sent, tile, [picked_own])
+    came = [send(part, sizes, b_sides) for part in sent[:2]]
+
+    z = unit_scores(model_number, kept, came[0], tile, 0, [])
+    a_mine = send(z, sizes, b_to_a)
+    nears, fars = [(a_mine, z)], [(send(a_mine, sizes, a_sides), send(z, sizes, b_sides))]
+
+    picked_b = pick(bases, picks_b, sent, tile, [z])
+    picked_a = pick(bases, picks_a, sent, tile, [picked_b])
+    picked_own = pick(bases, picks_own, sent, tile, [picked_a])
     rows_b = panel_scores(picked_own, send(picked_b, sizes, a_sides), 1)
     rows_b = send(rows_b, sizes, a_to_b)
     rows = panel_scores(
-        picked_own, send(picked_a, sizes, a_sides), 0, (model_number, rows_b)
-    )
-
-    a_mine = send(z[0], sizes, b_to_a)
-    chosen = choose(model_number, a_mine, z[0])
-    far = send(chosen, sizes, both_sides)
-    pieces = [(a_mine, far, z[0], far)]
-    z.append(unit_scores(kept, came[2:], tile, starts[2], [rows]))
-    direct = [send(z[1], sizes, move) for move in (b_to_a, b_to_far_a, b_sides)]
-    pieces.append((direct[0], direct[1], z[1], direct[2]))
-
-    panel = join([rows, swapped(rows, sizes, 2)], [z[1], chosen])
-    panel = join([panel, swapped(panel, sizes, 1)], direct)
+        picked_own, send(picked_a, sizes, a_sides), 0, (model_number, rows_b), (a_mine,)
+    )
+
+    z = unit_scores(model_number, kept, came[1], tile, chunks[0], [rows])
+    nears.append((send(z, sizes, b_to_a), z))
+    fars.append((send(z, sizes, b_to_far_a), send(z, sizes, b_sides)))
+
+    panel = join([rows, swapped(rows, sizes, 2)], [z])
+    panel = join([panel, swapped(panel, sizes, 1)], [*fars[0], nears[1][0], fars[1][1]])
     panel_other = send(panel, sizes, other_core)
     shape = (2 * CHIPS * rows.shape[0], units)
-    result = scores(target, [panel], (0,), pieces, tile, shape, [], [])
-    return scores(target, [panel_other], (1,), pieces, tile, shape, [result], [])
+    sides = [nears, fars[:1]]
+    result = scores(targets[0], [panel], (0,), sides, tile, shape, [])
+    result = scores(targets[0], [panel_other], (1,), sides, tile, shape, [result])
+    return scores(
+        targets[1], [panel, panel_other], (0, 1), [fars[1:]], tile, shape, [result]
+    )
 
 
 def solution(mesh):

time: 122 us -> 120 us (0.984)
  the two profiles are of different devices: /device:TPU:0 before, /device:TPU:9 now
where the time goes in v6:
time: 120 us
  Pallas kernels  48.3 us (40%)
  waiting for transfers between devices  43.1 us (36%)
  starting transfers between devices  25.5 us (21%)
  local copies, waits for them, and re-layouts  1.83 us (2%)
    ppermute x18, waiting for transfers between devices, send(): return lax.ppermute(block, AXES, routes(sizes, move))  43.1 us
    pallas_call x2, Pallas kernels, products(): call(functools.partial(products_kernel, counts, len(after)), out_shape=[j...  29.5 us
    ppermute x18, starting transfers between devices, send(): return lax.ppermute(block, AXES, routes(sizes, move))  25.5 us
    pallas_call x3, Pallas kernels, scores(): call(functools.partial(score_kernel, 1.0 / math.sqrt(tokens), tile, cores...  11.2 us
    pallas_call x3, Pallas kernels, pick(): call(functools.partial(pick_kernel, counts, tile), out_shape=jax.ShapeDty...  5.97 us
  transfers between devices with their start and end apart: 18, of which 9 were waited for; matrix products, arithmetic and copies ran while one was open for 1% of the time, Pallas kernels for 30%

profile of v6, /device:TPU:9, one launch (start us, length us, event | category | flops | bytes accessed | tf_op | source)
XLA Modules:
  0.0 119.5 jit_solution(3563671868939218341)
XLA Ops:
  0.0 1.3 %collective-permute-start = (bf16[32,4096]{1,0:T(8,128)(2,1)}, bf16[32,4096]{1,0:T(8,128)(2,1)S(1)}, u32[]{:S(2)}, u32[]{:S(2)}) collective-permute-start(bf16[32,4096]{1,0:T(8,128)(2,1)} %bitcast.18), channel_id=1, source_target_pairs={{0,4},{1,5},{2,6},{3,7},{4,8},{5,9},{6,10},{7,11},{8,12},{9,13},{1... | collective-permute-start | bytes 786440 | tf_op jit(solution)/shard_map/ppermute | solution.py:99
  1.3 1.0 collective-permute-start.1
  2.3 1.5 %collective-permute-start.2 = (bf16[32,4096]{1,0:T(8,128)(2,1)}, bf16[32,4096]{1,0:T(8,128)(2,1)S(1)}, u32[]{:S(2)}, u32[]{:S(2)}) collective-permute-start(bf16[32,4096]{1,0:T(8,128)(2,1)} %bitcast.20), channel_id=1, source_target_pairs={{0,12},{1,13},{2,14},{3,15},{4,0},{5,1},{6,2},{7,3},{8,4},{9,5},{1... | collective-permute-start | bytes 786440 | tf_op jit(solution)/shard_map/ppermute | solution.py:99
  3.8 3.6 %collective-permute-done.refs_1_ = bf16[32,4096]{1,0:T(8,128)(2,1)S(1)} collective-permute-done((bf16[32,4096]{1,0:T(8,128)(2,1)}, bf16[32,4096]{1,0:T(8,128)(2,1)S(1)}, u32[]{:S(2)}, u32[]{:S(2)}) %collective-permute-start) | collective-permute-done | bytes 262176 | tf_op jit(solution)/shard_map/ppermute | solution.py:99
  7.4 16.1 %collective-permute-done.1.refs_2_ = bf16[32,4096]{1,0:T(8,128)(2,1)S(1)} collective-permute-done((bf16[32,4096]{1,0:T(8,128)(2,1)}, bf16[32,4096]{1,0:T(8,128)(2,1)S(1)}, u32[]{:S(2)}, u32[]{:S(2)}) %collective-permute-start.1) | collective-permute-done | bytes 262176 | tf_op jit(solution)/shard_map/ppermute | solution.py:99
  23.4 2.7 %collective-permute-done.2.refs_3_ = bf16[32,4096]{1,0:T(8,128)(2,1)S(1)} collective-permute-done((bf16[32,4096]{1,0:T(8,128)(2,1)}, bf16[32,4096]{1,0:T(8,128)(2,1)S(1)}, u32[]{:S(2)}, u32[]{:S(2)}) %collective-permute-start.2) | collective-permute-done | bytes 262176 | tf_op jit(solution)/shard_map/ppermute | solution.py:99
  26.2 0.9 copy-done
  27.1 0.1 shard_map.46.same_ref
  27.3 0.6 collective-permute-start.3
  27.8 0.8 reshape.19
  28.6 0.1 stack.69.refs_7_.where_ref
  28.7 0.1 pad_add_fusion.2.place_ref.refs_5_
  28.8 0.1 pad_add_fusion.3.refs_6_.place_ref
  28.8 0.1 pad_add_fusion
  29.0 1.1 collective-permute-done.3.other_ref
  30.1 9.2 %shard_map.47.refs_0_ = bf16[2,256,1024]{2,1,0:T(8,128)(2,1)S(1)} custom-call(s32[3]{0:T(128)S(1)} %pad_add_fusion.2.place_ref.refs_5_, bf16[128,4096]{1,0:T(8,128)(2,1)S(1)} %shard_map.46.same_ref, bf16[128,4096]{1,0:T(8,128)(2,1)S(1)} %collective-permute-done.3.other_ref, bf16[4096,3584]{1,0:T(8,128)(2,1)} %bitcast.24, bf16[4096,3584]{1,0:T(8,128)(2,1)} %bitcast.26, ...), custom_call_target="tpu_custom_call" | custom-call | flops 4294967296 | bytes 16777216 | tf_op jit(solution)/shard_map/pallas_call | solution.py:205
  39.3 0.7 collective-permute-start.4
  40.0 20.3 %shard_map.48 = (bf16[2,256,768]{2,1,0:T(8,128)(2,1)S(1)}, bf16[2,256,1792]{2,1,0:T(8,128)(2,1)S(1)}) custom-call(s32[4]{0:T(128)S(1)} %pad_add_fusion.3.refs_6_.place_ref, bf16[128,4096]{1,0:T(8,128)(2,1)S(1)} %shard_map.46.same_ref, bf16[128,4096]{1,0:T(8,128)(2,1)S(1)} %collective-permute-done.3.other_ref, bf16[4096,3584]{1,0:T(8,128)(2,1)} %bitcast.25, ...), custom_call_target="tpu_custom_call" | custom-call | flops 10737418240 | bytes 41943040 | tf_op jit(solution)/shard_map/pallas_call | solution.py:205
  60.3 0.7 collective-permute-start.10
  61.1 0.3 shard_map.49.refs_3_.refs_2_
  61.4 1.3 %collective-permute-start.8 = (bf16[256,1024]{1,0:T(8,128)(2,1)S(1)}, bf16[256,1024]{1,0:T(8,128)(2,1)S(1)}, u32[]{:S(2)}, u32[]{:S(2)}) collective-permute-start(bf16[256,1024]{1,0:T(8,128)(2,1)S(1)} %shard_map.49.refs_3_.refs_2_), channel_id=1, source_target_pairs={{16,0},{17,1},{18,2},{19,3},{20,4},{21,5},{22,6},{23,7},{24,8},{25... | collective-permute-start | bytes 1572872 | tf_op jit(solution)/shard_map/ppermute | solution.py:99
  62.7 1.7 %shard_map.50.refs_3_ = bf16[2,256,256]{2,1,0:T(8,128)(2,1)S(1)} custom-call(s32[4]{0:T(128)S(1)} %get-tuple-element.12.refs_3_.bases_ref, s32[1,256]{1,0:T(1,128)S(1)} %get-tuple-element.10.refs_0_.picks_ref, bf16[2,256,1024]{2,1,0:T(8,128)(2,1)S(1)} %shard_map.47.refs_0_, bf16[2,256,768]{2,1,0:T(8,128)(2,1)S(1)} %get-tuple-element.7.refs_1_, ...), custom_call_target="tpu_custom_call" | custom-call | tf_op jit(solution)/shard_map/pallas_call | solution.py:251
  64.4 3.2 %collective-permute-start.6 = (bf16[2,256,256]{2,1,0:T(8,128)(2,1)S(1)}, bf16[2,256,256]{2,1,0:T(8,128)(2,1)S(1)}, u32[]{:S(2)}, u32[]{:S(2)}) collective-permute-start(bf16[2,256,256]{2,1,0:T(8,128)(2,1)S(1)} %shard_map.50.refs_3_), channel_id=1, source_target_pairs={{0,1},{1,0},{2,3},{3,2},{4,5},{5,4},{6,7},{7,6},{8,9},{9,8},{10,11... | collective-permute-start | bytes 786440 | tf_op jit(solution)/shard_map/ppermute | solution.py:99
  67.6 1.7 %shard_map.51.refs_3_ = bf16[2,256,256]{2,1,0:T(8,128)(2,1)S(1)} custom-call(s32[4]{0:T(128)S(1)} %get-tuple-element.12.refs_3_.bases_ref, s32[1,256]{1,0:T(1,128)S(1)} %get-tuple-element.9.refs_1_.picks_ref, bf16[2,256,1024]{2,1,0:T(8,128)(2,1)S(1)} %shard_map.47.refs_0_, bf16[2,256,768]{2,1,0:T(8,128)(2,1)S(1)} %get-tuple-element.7.refs_1_, ...), custom_call_target="tpu_custom_call" | custom-call | tf_op jit(solution)/shard_map/pallas_call | solution.py:251
  69.3 2.1 %collective-permute-start.5 = (bf16[2,256,256]{2,1,0:T(8,128)(2,1)S(1)}, bf16[2,256,256]{2,1,0:T(8,128)(2,1)S(1)}, u32[]{:S(2)}, u32[]{:S(2)}) collective-permute-start(bf16[2,256,256]{2,1,0:T(8,128)(2,1)S(1)} %shard_map.51.refs_3_), channel_id=1, source_target_pairs={{0,1},{1,0},{2,3},{3,2},{4,5},{5,4},{6,7},{7,6},{8,9},{9,8},{10,11... | collective-permute-start | bytes 786440 | tf_op jit(solution)/shard_map/ppermute | solution.py:99
  71.4 2.6 %shard_map.52.mine_ref = bf16[2,256,512]{2,1,0:T(8,128)(2,1)S(1)} custom-call(s32[4]{0:T(128)S(1)} %get-tuple-element.12.refs_3_.bases_ref, s32[1,512]{1,0:T(1,128)S(1)} %bitcast.23, bf16[2,256,1024]{2,1,0:T(8,128)(2,1)S(1)} %shard_map.47.refs_0_, bf16[2,256,768]{2,1,0:T(8,128)(2,1)S(1)} %get-tuple-element.7.refs_1_, ...), custom_call_target="tpu_custom_call" | custom-call | tf_op jit(solution)/shard_map/pallas_call | solution.py:251
  74.0 0.3 shard_map.53
  74.3 1.3 %collective-permute-start.7 = (bf16[256,256]{1,0:T(8,128)(2,1)S(1)}, bf16[256,256]{1,0:T(8,128)(2,1)S(1)}, u32[]{:S(2)}, u32[]{:S(2)}) collective-permute-start(bf16[256,256]{1,0:T(8,128)(2,1)S(1)} %shard_map.53), channel_id=1, source_target_pairs={{0,16},{1,17},{2,18},{3,19},{4,20},{5,21},{6,22},{7,23},{8,24},{9,... | collective-permute-start | bytes 393224 | tf_op jit(solution)/shard_map/ppermute | solution.py:99
  75.6 0.7 collective-permute-start.13
  76.3 4.1 %collective-permute-done.8.refs_0_.refs_1_ = bf16[256,1024]{1,0:T(8,128)(2,1)S(1)} collective-permute-done((bf16[256,1024]{1,0:T(8,128)(2,1)S(1)}, bf16[256,1024]{1,0:T(8,128)(2,1)S(1)}, u32[]{:S(2)}, u32[]{:S(2)}) %collective-permute-start.8) | collective-permute-done | bytes 524320 | tf_op jit(solution)/shard_map/ppermute | solution.py:99
  80.4 3.1 %collective-permute-start.12 = (bf16[256,1024]{1,0:T(8,128)(2,1)S(1)}, bf16[256,1024]{1,0:T(8,128)(2,1)S(1)}, u32[]{:S(2)}, u32[]{:S(2)}) collective-permute-start(bf16[256,1024]{1,0:T(8,128)(2,1)S(1)} %collective-permute-done.8.refs_0_.refs_1_), channel_id=1, source_target_pairs={{0,1},{1,0},{2,3},{3,2},{4,5},{5,4},{6,7},{7,6},{8,9},{9,8},{10,11... | collective-permute-start | bytes 1572872 | tf_op jit(solution)/shard_map/ppermute | solution.py:99
  83.5 0.3 shard_map.54.refs_0_
  83.9 1.4 %collective-permute-start.9 = (bf16[256,256]{1,0:T(8,128)(2,1)S(1)}, bf16[256,256]{1,0:T(8,128)(2,1)S(1)}, u32[]{:S(2)}, u32[]{:S(2)}) collective-permute-start(bf16[256,256]{1,0:T(8,128)(2,1)S(1)} %shard_map.54.refs_0_), channel_id=1, source_target_pairs={{0,8},{1,9},{2,10},{3,11},{4,12},{5,13},{6,14},{7,15},{8,0},{9,1},... | collective-permute-start | bytes 393224 | tf_op jit(solution)/shard_map/ppermute | solution.py:99
  85.2 0.2 shard_map.55.refs_2_.refs_4_
  85.5 1.3 %collective-permute-start.14 = (bf16[256,768]{1,0:T(8,128)(2,1)S(1)}, bf16[256,768]{1,0:T(8,128)(2,1)S(1)}, u32[]{:S(2)}, u32[]{:S(2)}) collective-permute-start(bf16[256,768]{1,0:T(8,128)(2,1)S(1)} %shard_map.55.refs_2_.refs_4_), channel_id=1, source_target_pairs={{16,0},{17,1},{18,2},{19,3},{20,4},{21,5},{22,6},{23,7},{24,8},{25... | collective-permute-start | bytes 1179656 | tf_op jit(solution)/shard_map/ppermute | solution.py:99
  86.8 0.7 collective-permute-start.15
  87.5 1.3 %collective-permute-done.9.refs_1_ = bf16[256,256]{1,0:T(8,128)(2,1)S(1)} collective-permute-done((bf16[256,256]{1,0:T(8,128)(2,1)S(1)}, bf16[256,256]{1,0:T(8,128)(2,1)S(1)}, u32[]{:S(2)}, u32[]{:S(2)}) %collective-permute-start.9) | collective-permute-done | bytes 131104 | tf_op jit(solution)/shard_map/ppermute | solution.py:99
  88.7 0.3 shard_map.56.refs_0_
  89.1 0.1 collective-permute-start.11
  89.2 5.5 %collective-permute-done.11.refs_1_ = bf16[512,256]{1,0:T(8,128)(2,1)S(1)} collective-permute-done((bf16[512,256]{1,0:T(8,128)(2,1)S(1)}, bf16[512,256]{1,0:T(8,128)(2,1)S(1)}, u32[]{:S(2)}, u32[]{:S(2)}) %collective-permute-start.11) | collective-permute-done | bytes 262176 | tf_op jit(solution)/shard_map/ppermute | solution.py:99
  94.7 0.9 collective-permute-done.14.refs_4_.refs_3_
  95.6 0.1 shard_map.57.refs_0_
  95.7 3.4 %collective-permute-start.16 = (bf16[1024,256]{1,0:T(8,128)(2,1)S(1)}, bf16[1024,256]{1,0:T(8,128)(2,1)S(1)}, u32[]{:S(2)}, u32[]{:S(2)}) collective-permute-start(bf16[1024,256]{1,0:T(8,128)(2,1)S(1)} %shard_map.57.refs_0_), channel_id=1, source_target_pairs={{0,2},{1,3},{2,0},{3,1},{4,6},{5,7},{6,4},{7,5},{8,10},{9,11},{10,... | collective-permute-start | bytes 1572872 | tf_op jit(solution)/shard_map/ppermute | solution.py:99
  99.0 1.3 %collective-permute-start.17 = (bf16[256,768]{1,0:T(8,128)(2,1)S(1)}, bf16[256,768]{1,0:T(8,128)(2,1)S(1)}, u32[]{:S(2)}, u32[]{:S(2)}) collective-permute-start(bf16[256,768]{1,0:T(8,128)(2,1)S(1)} %shard_map.55.refs_2_.refs_4_), channel_id=1, source_target_pairs={{16,1},{17,0},{18,3},{19,2},{20,5},{21,4},{22,7},{23,6},{24,9},{25... | collective-permute-start | bytes 1179656 | tf_op jit(solution)/shard_map/ppermute | solution.py:99
  100.3 4.0 %shard_map.58.refs_7_ = bf16[2048,3584]{1,0:T(8,128)(2,1)} custom-call(s32[5]{0:T(128)S(1)} %stack.69.refs_7_.where_ref, bf16[1024,256]{1,0:T(8,128)(2,1)S(1)} %shard_map.57.refs_0_, bf16[256,1024]{1,0:T(8,128)(2,1)S(1)} %collective-permute-done.8.refs_0_.refs_1_, bf16[256,1024]{1,0:T(8,128)(2,1)S(1)} %shard_map.49.refs_3_.refs_2_, ...), custom_call_target="tpu_custom_call" | custom-call | flops 1476395008 | bytes 5767168 | tf_op jit(solution)/shard_map/pallas_call | solution.py:420
  104.4 4.2 %shard_map.59.refs_4_ = bf16[2048,3584]{1,0:T(8,128)(2,1)} custom-call(s32[5]{0:T(128)S(1)} %stack.69.refs_7_.where_ref, bf16[1024,256]{1,0:T(8,128)(2,1)S(1)} %collective-permute-done.16.refs_0_.refs_1_, bf16[256,1024]{1,0:T(8,128)(2,1)S(1)} %collective-permute-done.8.refs_0_.refs_1_, ...), custom_call_target="tpu_custom_call", output_to_operand_aliasing={{}: (8, {})} | custom-call | flops 1476395008 | bytes 5767168 | tf_op jit(solution)/shard_map/pallas_call | solution.py:420
  108.6 7.8 %collective-permute-done.17.refs_2_ = bf16[256,768]{1,0:T(8,128)(2,1)S(1)} collective-permute-done((bf16[256,768]{1,0:T(8,128)(2,1)S(1)}, bf16[256,768]{1,0:T(8,128)(2,1)S(1)}, u32[]{:S(2)}, u32[]{:S(2)}) %collective-permute-start.17) | collective-permute-done | bytes 393248 | tf_op jit(solution)/shard_map/ppermute | solution.py:99
  116.4 3.0 %shard_map.60 = bf16[2048,3584]{1,0:T(8,128)(2,1)} custom-call(s32[4]{0:T(128)S(1)} %get-tuple-element.11.refs_8_.where_ref, bf16[1024,256]{1,0:T(8,128)(2,1)S(1)} %shard_map.57.refs_0_, bf16[1024,256]{1,0:T(8,128)(2,1)S(1)} %collective-permute-done.16.refs_0_.refs_1_, ...), custom_call_target="tpu_custom_call", output_to_operand_aliasing={{}: (5, {})} | custom-call | flops 805306368 | bytes 3145728 | tf_op jit(solution)/shard_map/pallas_call | solution.py:420
  (13 shorter events, 0.1 us)
Async XLA Ops:
  0.0 7.4 %collective-permute-start = (bf16[32,4096]{1,0:T(8,128)(2,1)}, bf16[32,4096]{1,0:T(8,128)(2,1)S(1)}, u32[]{:S(2)}, u32[]{:S(2)}) collective-permute-start(bf16[32,4096]{1,0:T(8,128)(2,1)} %bitcast.18), channel_id=1, source_target_pairs={{0,4},{1,5},{2,6},{3,7},{4,8},{5,9},{6,10},{7,11},{8,12},{9,13},{1... | collective-permute-start | bytes 786440 | tf_op jit(solution)/shard_map/ppermute | solution.py:99
  1.3 22.1 %collective-permute-start.1 = (bf16[32,4096]{1,0:T(8,128)(2,1)}, bf16[32,4096]{1,0:T(8,128)(2,1)S(1)}, u32[]{:S(2)}, u32[]{:S(2)}) collective-permute-start(bf16[32,4096]{1,0:T(8,128)(2,1)} %bitcast.19), channel_id=1, source_target_pairs={{0,8},{1,9},{2,10},{3,11},{4,12},{5,13},{6,14},{7,15},{8,0},{9,1},... | collective-permute-start | bytes 786440 | tf_op jit(solution)/shard_map/ppermute | solution.py:99
  2.3 23.9 %collective-permute-start.2 = (bf16[32,4096]{1,0:T(8,128)(2,1)}, bf16[32,4096]{1,0:T(8,128)(2,1)S(1)}, u32[]{:S(2)}, u32[]{:S(2)}) collective-permute-start(bf16[32,4096]{1,0:T(8,128)(2,1)} %bitcast.20), channel_id=1, source_target_pairs={{0,12},{1,13},{2,14},{3,15},{4,0},{5,1},{6,2},{7,3},{8,4},{9,5},{1... | collective-permute-start | bytes 786440 | tf_op jit(solution)/shard_map/ppermute | solution.py:99
  26.2 1.0 copy-start
  27.3 2.8 %collective-permute-start.3 = (bf16[128,4096]{1,0:T(8,128)(2,1)S(1)}, bf16[128,4096]{1,0:T(8,128)(2,1)S(1)}, u32[]{:S(2)}, u32[]{:S(2)}) collective-permute-start(bf16[128,4096]{1,0:T(8,128)(2,1)S(1)} %shard_map.46.same_ref), channel_id=1, source_target_pairs={{0,2},{1,3},{2,0},{3,1},{4,6},{5,7},{6,4},{7,5},{8,10},{9,11},{10,... | collective-permute-start | bytes 3145736 | tf_op jit(solution)/shard_map/ppermute | solution.py:99
  39.3 21.8 %collective-permute-start.4 = (bf16[2,256,1024]{2,1,0:T(8,128)(2,1)S(1)}, bf16[2,256,1024]{2,1,0:T(8,128)(2,1)S(1)}, u32[]{:S(2)}, u32[]{:S(2)}) collective-permute-start(bf16[2,256,1024]{2,1,0:T(8,128)(2,1)S(1)} %shard_map.47.refs_0_), channel_id=1, source_target_pairs={{16,17},{17,16},{18,19},{19,18},{20,21},{21,20},{22,23},{23,22},{2... | collective-permute-start | bytes 3145736 | tf_op jit(solution)/shard_map/ppermute | solution.py:99
  60.3 24.9 %collective-permute-start.10 = (bf16[2,256,768]{2,1,0:T(8,128)(2,1)S(1)}, bf16[2,256,768]{2,1,0:T(8,128)(2,1)S(1)}, u32[]{:S(2)}, u32[]{:S(2)}) collective-permute-start(bf16[2,256,768]{2,1,0:T(8,128)(2,1)S(1)} %get-tuple-element.7.refs_1_), channel_id=1, source_target_pairs={{16,17},{17,16},{18,19},{19,18},{20,21},{21,20},{22,23},{23,22},{2... | collective-permute-start | bytes 2359304 | tf_op jit(solution)/shard_map/ppermute | solution.py:99
  61.4 19.0 %collective-permute-start.8 = (bf16[256,1024]{1,0:T(8,128)(2,1)S(1)}, bf16[256,1024]{1,0:T(8,128)(2,1)S(1)}, u32[]{:S(2)}, u32[]{:S(2)}) collective-permute-start(bf16[256,1024]{1,0:T(8,128)(2,1)S(1)} %shard_map.49.refs_3_.refs_2_), channel_id=1, source_target_pairs={{16,0},{17,1},{18,2},{19,3},{20,4},{21,5},{22,6},{23,7},{24,8},{25... | collective-permute-start | bytes 1572872 | tf_op jit(solution)/shard_map/ppermute | solution.py:99
  64.4 9.6 %collective-permute-start.6 = (bf16[2,256,256]{2,1,0:T(8,128)(2,1)S(1)}, bf16[2,256,256]{2,1,0:T(8,128)(2,1)S(1)}, u32[]{:S(2)}, u32[]{:S(2)}) collective-permute-start(bf16[2,256,256]{2,1,0:T(8,128)(2,1)S(1)} %shard_map.50.refs_3_), channel_id=1, source_target_pairs={{0,1},{1,0},{2,3},{3,2},{4,5},{5,4},{6,7},{7,6},{8,9},{9,8},{10,11... | collective-permute-start | bytes 786440 | tf_op jit(solution)/shard_map/ppermute | solution.py:99
  69.3 14.2 %collective-permute-start.5 = (bf16[2,256,256]{2,1,0:T(8,128)(2,1)S(1)}, bf16[2,256,256]{2,1,0:T(8,128)(2,1)S(1)}, u32[]{:S(2)}, u32[]{:S(2)}) collective-permute-start(bf16[2,256,256]{2,1,0:T(8,128)(2,1)S(1)} %shard_map.51.refs_3_), channel_id=1, source_target_pairs={{0,1},{1,0},{2,3},{3,2},{4,5},{5,4},{6,7},{7,6},{8,9},{9,8},{10,11... | collective-permute-start | bytes 786440 | tf_op jit(solution)/shard_map/ppermute | solution.py:99
  74.3 9.2 %collective-permute-start.7 = (bf16[256,256]{1,0:T(8,128)(2,1)S(1)}, bf16[256,256]{1,0:T(8,128)(2,1)S(1)}, u32[]{:S(2)}, u32[]{:S(2)}) collective-permute-start(bf16[256,256]{1,0:T(8,128)(2,1)S(1)} %shard_map.53), channel_id=1, source_target_pairs={{0,16},{1,17},{2,18},{3,19},{4,20},{5,21},{6,22},{7,23},{8,24},{9,... | collective-permute-start | bytes 393224 | tf_op jit(solution)/shard_map/ppermute | solution.py:99
  75.6 13.6 %collective-permute-start.13 = (bf16[256,1024]{1,0:T(8,128)(2,1)S(1)}, bf16[256,1024]{1,0:T(8,128)(2,1)S(1)}, u32[]{:S(2)}, u32[]{:S(2)}) collective-permute-start(bf16[256,1024]{1,0:T(8,128)(2,1)S(1)} %shard_map.49.refs_3_.refs_2_), channel_id=1, source_target_pairs={{16,17},{17,16},{18,19},{19,18},{20,21},{21,20},{22,23},{23,22},{2... | collective-permute-start | bytes 1572872 | tf_op jit(solution)/shard_map/ppermute | solution.py:99
  80.4 15.2 %collective-permute-start.12 = (bf16[256,1024]{1,0:T(8,128)(2,1)S(1)}, bf16[256,1024]{1,0:T(8,128)(2,1)S(1)}, u32[]{:S(2)}, u32[]{:S(2)}) collective-permute-start(bf16[256,1024]{1,0:T(8,128)(2,1)S(1)} %collective-permute-done.8.refs_0_.refs_1_), channel_id=1, source_target_pairs={{0,1},{1,0},{2,3},{3,2},{4,5},{5,4},{6,7},{7,6},{8,9},{9,8},{10,11... | collective-permute-start | bytes 1572872 | tf_op jit(solution)/shard_map/ppermute | solution.py:99
  83.9 4.9 %collective-permute-start.9 = (bf16[256,256]{1,0:T(8,128)(2,1)S(1)}, bf16[256,256]{1,0:T(8,128)(2,1)S(1)}, u32[]{:S(2)}, u32[]{:S(2)}) collective-permute-start(bf16[256,256]{1,0:T(8,128)(2,1)S(1)} %shard_map.54.refs_0_), channel_id=1, source_target_pairs={{0,8},{1,9},{2,10},{3,11},{4,12},{5,13},{6,14},{7,15},{8,0},{9,1},... | collective-permute-start | bytes 393224 | tf_op jit(solution)/shard_map/ppermute | solution.py:99
  85.5 10.1 %collective-permute-start.14 = (bf16[256,768]{1,0:T(8,128)(2,1)S(1)}, bf16[256,768]{1,0:T(8,128)(2,1)S(1)}, u32[]{:S(2)}, u32[]{:S(2)}) collective-permute-start(bf16[256,768]{1,0:T(8,128)(2,1)S(1)} %shard_map.55.refs_2_.refs_4_), channel_id=1, source_target_pairs={{16,0},{17,1},{18,2},{19,3},{20,4},{21,5},{22,6},{23,7},{24,8},{25... | collective-permute-start | bytes 1179656 | tf_op jit(solution)/shard_map/ppermute | solution.py:99
  86.8 8.8 %collective-permute-start.15 = (bf16[256,768]{1,0:T(8,128)(2,1)S(1)}, bf16[256,768]{1,0:T(8,128)(2,1)S(1)}, u32[]{:S(2)}, u32[]{:S(2)}) collective-permute-start(bf16[256,768]{1,0:T(8,128)(2,1)S(1)} %shard_map.55.refs_2_.refs_4_), channel_id=1, source_target_pairs={{16,17},{17,16},{18,19},{19,18},{20,21},{21,20},{22,23},{23,22},{2... | collective-permute-start | bytes 1179656 | tf_op jit(solution)/shard_map/ppermute | solution.py:99
  89.1 5.6 %collective-permute-start.11 = (bf16[512,256]{1,0:T(8,128)(2,1)S(1)}, bf16[512,256]{1,0:T(8,128)(2,1)S(1)}, u32[]{:S(2)}, u32[]{:S(2)}) collective-permute-start(bf16[512,256]{1,0:T(8,128)(2,1)S(1)} %shard_map.56.refs_0_), channel_id=1, source_target_pairs={{0,4},{1,5},{2,6},{3,7},{4,0},{5,1},{6,2},{7,3},{8,12},{9,13},{10,... | collective-permute-start | bytes 786440 | tf_op jit(solution)/shard_map/ppermute | solution.py:99
  95.7 8.7 %collective-permute-start.16 = (bf16[1024,256]{1,0:T(8,128)(2,1)S(1)}, bf16[1024,256]{1,0:T(8,128)(2,1)S(1)}, u32[]{:S(2)}, u32[]{:S(2)}) collective-permute-start(bf16[1024,256]{1,0:T(8,128)(2,1)S(1)} %shard_map.57.refs_0_), channel_id=1, source_target_pairs={{0,2},{1,3},{2,0},{3,1},{4,6},{5,7},{6,4},{7,5},{8,10},{9,11},{10,... | collective-permute-start | bytes 1572872 | tf_op jit(solution)/shard_map/ppermute | solution.py:99
  99.0 17.3 %collective-permute-start.17 = (bf16[256,768]{1,0:T(8,128)(2,1)S(1)}, bf16[256,768]{1,0:T(8,128)(2,1)S(1)}, u32[]{:S(2)}, u32[]{:S(2)}) collective-permute-start(bf16[256,768]{1,0:T(8,128)(2,1)S(1)} %shard_map.55.refs_2_.refs_4_), channel_id=1, source_target_pairs={{16,1},{17,0},{18,3},{19,2},{20,5},{21,4},{22,7},{23,6},{24,9},{25... | collective-permute-start | bytes 1179656 | tf_op jit(solution)/shard_map/ppermute | solution.py:99

commit v7 on v6

--- a/solution.py
+++ b/solution.py
@@ -164,12 +164,13 @@
     )
 
 
-def products_kernel(counts, n_after, place_ref, same_ref, other_ref, gate_ref, up_ref, *refs):
-    rows = same_ref.shape[0] // CHIPS
+def products_kernel(counts, n_after, place_ref, gate_ref, up_ref, *refs):
+    x_refs, refs = refs[: 2 * CHIPS], refs[2 * CHIPS :]
+    rows = x_refs[0].shape[0]
     step = pl.program_id(0)
 
     def write(out_ref):
-        x = jnp.concatenate([same_ref[...], other_ref[...]], axis=0)
+        x = jnp.concatenate([x_ref[...] for x_ref in x_refs], axis=0)
         for which, weight_ref in enumerate((gate_ref, up_ref)):
             total = jnp.dot(x, weight_ref[...], preferred_element_type=jnp.float32)
             total = total.astype(jnp.bfloat16)
@@ -187,8 +188,9 @@
         first += count
 
 
-def products(place, same, other, gate, up, tile, counts, after):
-    tokens, width = 2 * same.shape[0], same.shape[1]
+def products(place, blocks, gate, up, tile, counts, after):
+    rows, width = blocks[0].shape
+    tokens = len(blocks) * rows
     firsts = [sum(counts[:i]) for i in range(len(counts))]
 
     def weight_tile(i, place_ref):
@@ -201,7 +203,7 @@
         return lambda i, place_ref: (0, 0, jnp.clip(i - firsts[run], 0, counts[run] - 1))
 
     weights = pl.BlockSpec((width, tile), weight_tile)
-    whole = pl.BlockSpec(same.shape, lambda i, place_ref: (0, 0))
+    whole = pl.BlockSpec((rows, width), lambda i, place_ref: (0, 0))
     return call(
         functools.partial(products_kernel, counts, len(after)),
         out_shape=[
@@ -210,7 +212,8 @@
         grid_spec=pltpu.PrefetchScalarGridSpec(
             num_scalar_prefetch=1,
             grid=(sum(counts),),
-            in_specs=[whole, whole, weights, weights]
+            in_specs=[weights, weights]
+            + [whole] * len(blocks)
             + [pl.BlockSpec(memory_space=pl.ANY)] * len(after),
             out_specs=[
                 pl.BlockSpec((2, tokens, tile), out_tile(run)) for run in range(len(counts))
@@ -219,7 +222,7 @@
         flops=4 * tokens * width * tile * sum(counts),
         moved=4 * width * tile * sum(counts),
         vmem=38,
-    )(place, same, other, gate, up, *after)
+    )(place, gate, up, *blocks, *after)
 
 
 def pick_kernel(counts, tile, bases_ref, picks_ref, *refs):
@@ -464,14 +467,12 @@
     def b_to_a(m, d, t):
         return (0, d, t) if m == 1 else None
 
-    def b_to_far_a(m, d, t):
-        return (0, d, 1 - t) if m == 1 else None
-
     def a_to_b(m, d, t):
         return (1, d, t) if m == 0 else None
 
-    same = join(shifts(acts[0], sizes), [])
-    other = send(same, sizes, other_core)
+    own = join([acts[0]], [])
+    blocks = [own, *shifts(acts[0], sizes)[1:]]
+    blocks += [send(part, sizes, other_core) for part in blocks]
 
     picks = lax.dynamic_index_in_dim(picks, block, axis=2, keepdims=False) - block * units
     picks_far = lax.dynamic_index_in_dim(picks, 1 - side, axis=1, keepdims=False)
@@ -489,8 +490,8 @@
     places = [[chip, core, to_side], [chip, core, to_side + chunks[0], own_side]]
     places = [jnp.stack(place).astype(jnp.int32) for place in places]
     ready = [picks_b, picks_a, picks_own, bases, model_number, *places, *targets]
-    sent = products(places[0], same, other, gate, up, tile, chunks[:1], ready)
-    sent += products(places[1], same, other, gate, up, tile, [chunks[1], half], sent)
+    sent = products(places[0], blocks, gate, up, tile, chunks[:1], ready)
+    sent += products(places[1], blocks, gate, up, tile, [chunks[1], half], sent)
     kept = sent[-1]
     came = [send(part, sizes, b_sides) for part in sent[:2]]
 
@@ -504,12 +505,12 @@
     rows_b = panel_scores(picked_own, send(picked_b, sizes, a_sides), 1)
     rows_b = send(rows_b, sizes, a_to_b)
     rows = panel_scores(
-        picked_own, send(picked_a, sizes, a_sides), 0, (model_number, rows_b), (a_mine,)
+        picked_own, send(picked_a, sizes, a_sides), 0, (model_number, rows_b)
     )
 
     z = unit_scores(model_number, kept, came[1], tile, chunks[0], [rows])
     nears.append((send(z, sizes, b_to_a), z))
-    fars.append((send(z, sizes, b_to_far_a), send(z, sizes, b_sides)))
+    fars.append((send(nears[1][0], sizes, a_sides), send(z, sizes, b_sides)))
 
     panel = join([rows, swapped(rows, sizes, 2)], [z])
     panel = join([panel, swapped(panel, sizes, 1)], [*fars[0], nears[1][0], fars[1][1]])

time: 120 us -> 115 us (0.958)
  the two profiles are of different devices: /device:TPU:9 before, /device:TPU:0 now
where the time goes in v7:
time: 115 us; the launch traced here: 113 us
  Pallas kernels  48.3 us (42%)
  starting transfers between devices  33.3 us (29%)
  waiting for transfers between devices  29.3 us (25%)
  local copies, waits for them, and re-layouts  1.84 us (2%)
    ppermute x21, starting transfers between devices, send(): return lax.ppermute(block, AXES, routes(sizes, move))  33.3 us
    pallas_call x2, Pallas kernels, products(): call(functools.partial(products_kernel, counts, len(after)), out_shape=[j...  29.5 us
    ppermute x21, waiting for transfers between devices, send(): return lax.ppermute(block, AXES, routes(sizes, move))  29.3 us
    pallas_call x3, Pallas kernels, scores(): call(functools.partial(score_kernel, 1.0 / math.sqrt(tokens), tile, cores...  11.2 us
    pallas_call x3, Pallas kernels, pick(): call(functools.partial(pick_kernel, counts, tile), out_shape=jax.ShapeDty...  5.96 us
  transfers between devices with their start and end apart: 21, of which 9 were waited for; matrix products, arithmetic and copies ran while one was open for 1% of the time, Pallas kernels for 32%

profile of v7, /device:TPU:0, one launch (start us, length us, event | category | flops | bytes accessed | tf_op | source)
XLA Modules:
  0.0 113.5 jit_solution(12459366694238589442)
XLA Ops:
  0.0 3.0 %collective-permute-start = (bf16[32,4096]{1,0:T(8,128)(2,1)}, bf16[32,4096]{1,0:T(8,128)(2,1)S(1)}, u32[]{:S(2)}, u32[]{:S(2)}) collective-permute-start(bf16[32,4096]{1,0:T(8,128)(2,1)} %bitcast.18), channel_id=1, source_target_pairs={{0,4},{1,5},{2,6},{3,7},{4,8},{5,9},{6,10},{7,11},{8,12},{9,13},{1... | collective-permute-start | bytes 786440 | tf_op jit(solution)/shard_map/ppermute | solution.py:99
  3.0 2.6 %collective-permute-start.1 = (bf16[32,4096]{1,0:T(8,128)(2,1)}, bf16[32,4096]{1,0:T(8,128)(2,1)S(1)}, u32[]{:S(2)}, u32[]{:S(2)}) collective-permute-start(bf16[32,4096]{1,0:T(8,128)(2,1)} %bitcast.19), channel_id=1, source_target_pairs={{0,8},{1,9},{2,10},{3,11},{4,12},{5,13},{6,14},{7,15},{8,0},{9,1},... | collective-permute-start | bytes 786440 | tf_op jit(solution)/shard_map/ppermute | solution.py:99
  5.6 1.3 %collective-permute-start.2 = (bf16[32,4096]{1,0:T(8,128)(2,1)}, bf16[32,4096]{1,0:T(8,128)(2,1)S(1)}, u32[]{:S(2)}, u32[]{:S(2)}) collective-permute-start(bf16[32,4096]{1,0:T(8,128)(2,1)} %bitcast.20), channel_id=1, source_target_pairs={{0,12},{1,13},{2,14},{3,15},{4,0},{5,1},{6,2},{7,3},{8,4},{9,5},{1... | collective-permute-start | bytes 786440 | tf_op jit(solution)/shard_map/ppermute | solution.py:99
  7.0 1.0 copy-done
  8.0 0.1 collective-permute-start.3
  8.1 0.1 pad_add_fusion.2.place_ref.refs_13_
  8.2 0.8 reshape.19
  8.9 0.1 pad_add_fusion
  9.0 3.5 %collective-permute-done.refs_1_ = bf16[32,4096]{1,0:T(8,128)(2,1)S(1)} collective-permute-done((bf16[32,4096]{1,0:T(8,128)(2,1)}, bf16[32,4096]{1,0:T(8,128)(2,1)S(1)}, u32[]{:S(2)}, u32[]{:S(2)}) %collective-permute-start) | collective-permute-done | bytes 262176 | tf_op jit(solution)/shard_map/ppermute | solution.py:99
  12.5 10.4 %collective-permute-done.1.refs_2_ = bf16[32,4096]{1,0:T(8,128)(2,1)S(1)} collective-permute-done((bf16[32,4096]{1,0:T(8,128)(2,1)}, bf16[32,4096]{1,0:T(8,128)(2,1)S(1)}, u32[]{:S(2)}, u32[]{:S(2)}) %collective-permute-start.1) | collective-permute-done | bytes 262176 | tf_op jit(solution)/shard_map/ppermute | solution.py:99
  22.9 0.5 collective-permute-start.6
  23.4 0.1 pad_add_fusion.3.refs_14_.place_ref
  23.5 0.1 stack.69.refs_15_.where_ref
  23.6 0.8 collective-permute-done.5.refs_6_
  24.5 0.4 collective-permute-done.6.refs_7_
  24.8 9.2 %shard_map.47.refs_8_.refs_0_ = bf16[2,256,1024]{2,1,0:T(8,128)(2,1)S(1)} custom-call(s32[3]{0:T(128)S(1)} %pad_add_fusion.2.place_ref.refs_13_, bf16[4096,3584]{1,0:T(8,128)(2,1)} %bitcast.24, bf16[4096,3584]{1,0:T(8,128)(2,1)} %bitcast.26, bf16[32,4096]{1,0:T(8,128)(2,1)S(1)} %shard_map.46.refs_0_, bf16[32,4096]{1,0:T(8,128)(2,1)S(1)} %collective-permute-done.refs_1_, ...), custom_call_target="tpu_custom_call" | custom-call | flops 4294967296 | bytes 16777216 | tf_op jit(solution)/shard_map/pallas_call | solution.py:207
  34.0 0.7 collective-permute-start.7
  34.8 20.3 %shard_map.48 = (bf16[2,256,768]{2,1,0:T(8,128)(2,1)S(1)}, bf16[2,256,1792]{2,1,0:T(8,128)(2,1)S(1)}) custom-call(s32[4]{0:T(128)S(1)} %pad_add_fusion.3.refs_14_.place_ref, bf16[4096,3584]{1,0:T(8,128)(2,1)} %bitcast.25, bf16[4096,3584]{1,0:T(8,128)(2,1)} %bitcast.27, bf16[32,4096]{1,0:T(8,128)(2,1)S(1)} %shard_map.46.refs_0_, ...), custom_call_target="tpu_custom_call" | custom-call | flops 10737418240 | bytes 41943040 | tf_op jit(solution)/shard_map/pallas_call | solution.py:207
  55.1 0.7 collective-permute-start.12
  55.8 0.3 shard_map.49.refs_3_.refs_2_
  56.1 1.3 %collective-permute-start.14 = (bf16[256,1024]{1,0:T(8,128)(2,1)S(1)}, bf16[256,1024]{1,0:T(8,128)(2,1)S(1)}, u32[]{:S(2)}, u32[]{:S(2)}) collective-permute-start(bf16[256,1024]{1,0:T(8,128)(2,1)S(1)} %shard_map.49.refs_3_.refs_2_), channel_id=1, source_target_pairs={{16,0},{17,1},{18,2},{19,3},{20,4},{21,5},{22,6},{23,7},{24,8},{25... | collective-permute-start | bytes 1572872 | tf_op jit(solution)/shard_map/ppermute | solution.py:99
  57.4 1.7 %shard_map.50.refs_3_ = bf16[2,256,256]{2,1,0:T(8,128)(2,1)S(1)} custom-call(s32[4]{0:T(128)S(1)} %get-tuple-element.12.refs_11_.bases_ref, s32[1,256]{1,0:T(1,128)S(1)} %get-tuple-element.10.refs_8_.picks_ref, bf16[2,256,1024]{2,1,0:T(8,128)(2,1)S(1)} %shard_map.47.refs_8_.refs_0_, bf16[2,256,768]{2,1,0:T(8,128)(2,1)S(1)} %get-tuple-element.7.refs_1_, ...), custom_call_target="tpu_custom_call" | custom-call | tf_op jit(solution)/shard_map/pallas_call | solution.py:254
  59.1 3.5 %collective-permute-start.9 = (bf16[2,256,256]{2,1,0:T(8,128)(2,1)S(1)}, bf16[2,256,256]{2,1,0:T(8,128)(2,1)S(1)}, u32[]{:S(2)}, u32[]{:S(2)}) collective-permute-start(bf16[2,256,256]{2,1,0:T(8,128)(2,1)S(1)} %shard_map.50.refs_3_), channel_id=1, source_target_pairs={{0,1},{1,0},{2,3},{3,2},{4,5},{5,4},{6,7},{7,6},{8,9},{9,8},{10,11... | collective-permute-start | bytes 786440 | tf_op jit(solution)/shard_map/ppermute | solution.py:99
  62.6 1.7 %shard_map.51.refs_3_ = bf16[2,256,256]{2,1,0:T(8,128)(2,1)S(1)} custom-call(s32[4]{0:T(128)S(1)} %get-tuple-element.12.refs_11_.bases_ref, s32[1,256]{1,0:T(1,128)S(1)} %get-tuple-element.9.refs_9_.picks_ref, bf16[2,256,1024]{2,1,0:T(8,128)(2,1)S(1)} %shard_map.47.refs_8_.refs_0_, bf16[2,256,768]{2,1,0:T(8,128)(2,1)S(1)} %get-tuple-element.7.refs_1_, ...), custom_call_target="tpu_custom_call" | custom-call | tf_op jit(solution)/shard_map/pallas_call | solution.py:254
  64.3 2.3 %collective-permute-start.8 = (bf16[2,256,256]{2,1,0:T(8,128)(2,1)S(1)}, bf16[2,256,256]{2,1,0:T(8,128)(2,1)S(1)}, u32[]{:S(2)}, u32[]{:S(2)}) collective-permute-start(bf16[2,256,256]{2,1,0:T(8,128)(2,1)S(1)} %shard_map.51.refs_3_), channel_id=1, source_target_pairs={{0,1},{1,0},{2,3},{3,2},{4,5},{5,4},{6,7},{7,6},{8,9},{9,8},{10,11... | collective-permute-start | bytes 786440 | tf_op jit(solution)/shard_map/ppermute | solution.py:99
  66.7 2.6 %shard_map.52.mine_ref = bf16[2,256,512]{2,1,0:T(8,128)(2,1)S(1)} custom-call(s32[4]{0:T(128)S(1)} %get-tuple-element.12.refs_11_.bases_ref, s32[1,512]{1,0:T(1,128)S(1)} %bitcast.23, bf16[2,256,1024]{2,1,0:T(8,128)(2,1)S(1)} %shard_map.47.refs_8_.refs_0_, bf16[2,256,768]{2,1,0:T(8,128)(2,1)S(1)} %get-tuple-element.7.refs_1_, ...), custom_call_target="tpu_custom_call" | custom-call | tf_op jit(solution)/shard_map/pallas_call | solution.py:254
  69.3 0.7 collective-permute-done.9.theirs_ref
  70.0 0.3 shard_map.53
  70.3 1.3 %collective-permute-start.10 = (bf16[256,256]{1,0:T(8,128)(2,1)S(1)}, bf16[256,256]{1,0:T(8,128)(2,1)S(1)}, u32[]{:S(2)}, u32[]{:S(2)}) collective-permute-start(bf16[256,256]{1,0:T(8,128)(2,1)S(1)} %shard_map.53), channel_id=1, source_target_pairs={{0,16},{1,17},{2,18},{3,19},{4,20},{5,21},{6,22},{7,23},{8,24},{9,... | collective-permute-start | bytes 393224 | tf_op jit(solution)/shard_map/ppermute | solution.py:99
  71.6 0.7 collective-permute-start.16
  72.3 4.3 %collective-permute-done.14.refs_1_ = bf16[256,1024]{1,0:T(8,128)(2,1)S(1)} collective-permute-done((bf16[256,1024]{1,0:T(8,128)(2,1)S(1)}, bf16[256,1024]{1,0:T(8,128)(2,1)S(1)}, u32[]{:S(2)}, u32[]{:S(2)}) %collective-permute-start.14) | collective-permute-done | bytes 524320 | tf_op jit(solution)/shard_map/ppermute | solution.py:99
  76.6 3.4 %collective-permute-start.15 = (bf16[256,1024]{1,0:T(8,128)(2,1)S(1)}, bf16[256,1024]{1,0:T(8,128)(2,1)S(1)}, u32[]{:S(2)}, u32[]{:S(2)}) collective-permute-start(bf16[256,1024]{1,0:T(8,128)(2,1)S(1)} %collective-permute-done.14.refs_1_), channel_id=1, source_target_pairs={{0,1},{1,0},{2,3},{3,2},{4,5},{5,4},{6,7},{7,6},{8,9},{9,8},{10,11... | collective-permute-start | bytes 1572872 | tf_op jit(solution)/shard_map/ppermute | solution.py:99
  80.0 0.3 shard_map.54.refs_0_
  80.4 4.9 %collective-permute-start.11 = (bf16[256,256]{1,0:T(8,128)(2,1)S(1)}, bf16[256,256]{1,0:T(8,128)(2,1)S(1)}, u32[]{:S(2)}, u32[]{:S(2)}) collective-permute-start(bf16[256,256]{1,0:T(8,128)(2,1)S(1)} %shard_map.54.refs_0_), channel_id=1, source_target_pairs={{0,8},{1,9},{2,10},{3,11},{4,12},{5,13},{6,14},{7,15},{8,0},{9,1},... | collective-permute-start | bytes 393224 | tf_op jit(solution)/shard_map/ppermute | solution.py:99
  85.2 0.2 shard_map.55.refs_2_.refs_4_
  85.5 1.3 %collective-permute-start.17 = (bf16[256,768]{1,0:T(8,128)(2,1)S(1)}, bf16[256,768]{1,0:T(8,128)(2,1)S(1)}, u32[]{:S(2)}, u32[]{:S(2)}) collective-permute-start(bf16[256,768]{1,0:T(8,128)(2,1)S(1)} %shard_map.55.refs_2_.refs_4_), channel_id=1, source_target_pairs={{16,0},{17,1},{18,2},{19,3},{20,4},{21,5},{22,6},{23,7},{24,8},{25... | collective-permute-start | bytes 1179656 | tf_op jit(solution)/shard_map/ppermute | solution.py:99
  86.8 0.7 collective-permute-start.18
  87.5 2.1 %collective-permute-done.11.refs_1_ = bf16[256,256]{1,0:T(8,128)(2,1)S(1)} collective-permute-done((bf16[256,256]{1,0:T(8,128)(2,1)S(1)}, bf16[256,256]{1,0:T(8,128)(2,1)S(1)}, u32[]{:S(2)}, u32[]{:S(2)}) %collective-permute-start.11) | collective-permute-done | bytes 131104 | tf_op jit(solution)/shard_map/ppermute | solution.py:99
  89.6 0.3 shard_map.56.refs_0_
  89.9 2.5 %collective-permute-start.13 = (bf16[512,256]{1,0:T(8,128)(2,1)S(1)}, bf16[512,256]{1,0:T(8,128)(2,1)S(1)}, u32[]{:S(2)}, u32[]{:S(2)}) collective-permute-start(bf16[512,256]{1,0:T(8,128)(2,1)S(1)} %shard_map.56.refs_0_), channel_id=1, source_target_pairs={{0,4},{1,5},{2,6},{3,7},{4,0},{5,1},{6,2},{7,3},{8,12},{9,13},{10,... | collective-permute-start | bytes 786440 | tf_op jit(solution)/shard_map/ppermute | solution.py:99
  92.4 4.3 %collective-permute-done.13.refs_1_ = bf16[512,256]{1,0:T(8,128)(2,1)S(1)} collective-permute-done((bf16[512,256]{1,0:T(8,128)(2,1)S(1)}, bf16[512,256]{1,0:T(8,128)(2,1)S(1)}, u32[]{:S(2)}, u32[]{:S(2)}) %collective-permute-start.13) | collective-permute-done | bytes 262176 | tf_op jit(solution)/shard_map/ppermute | solution.py:99
  96.8 0.1 shard_map.57.refs_0_
  96.8 0.1 collective-permute-start.19
  96.9 2.4 %collective-permute-start.20 = (bf16[256,768]{1,0:T(8,128)(2,1)S(1)}, bf16[256,768]{1,0:T(8,128)(2,1)S(1)}, u32[]{:S(2)}, u32[]{:S(2)}) collective-permute-start(bf16[256,768]{1,0:T(8,128)(2,1)S(1)} %collective-permute-done.17.refs_4_.refs_3_), channel_id=1, source_target_pairs={{0,1},{1,0},{2,3},{3,2},{4,5},{5,4},{6,7},{7,6},{8,9},{9,8},{10,11... | collective-permute-start | bytes 1179656 | tf_op jit(solution)/shard_map/ppermute | solution.py:99
  99.4 4.0 %shard_map.58.refs_7_ = bf16[2048,3584]{1,0:T(8,128)(2,1)} custom-call(s32[5]{0:T(128)S(1)} %stack.69.refs_15_.where_ref, bf16[1024,256]{1,0:T(8,128)(2,1)S(1)} %shard_map.57.refs_0_, bf16[256,1024]{1,0:T(8,128)(2,1)S(1)} %collective-permute-done.14.refs_1_, bf16[256,1024]{1,0:T(8,128)(2,1)S(1)} %shard_map.49.refs_3_.refs_2_, ...), custom_call_target="tpu_custom_call" | custom-call | flops 1476395008 | bytes 5767168 | tf_op jit(solution)/shard_map/pallas_call | solution.py:423
  103.4 4.2 %shard_map.59.refs_4_ = bf16[2048,3584]{1,0:T(8,128)(2,1)} custom-call(s32[5]{0:T(128)S(1)} %stack.69.refs_15_.where_ref, bf16[1024,256]{1,0:T(8,128)(2,1)S(1)} %collective-permute-done.19.refs_0_.refs_1_, bf16[256,1024]{1,0:T(8,128)(2,1)S(1)} %collective-permute-done.14.refs_1_, ...), custom_call_target="tpu_custom_call", output_to_operand_aliasing={{}: (8, {})} | custom-call | flops 1476395008 | bytes 5767168 | tf_op jit(solution)/shard_map/pallas_call | solution.py:423
  107.6 2.7 %collective-permute-done.20.refs_2_ = bf16[256,768]{1,0:T(8,128)(2,1)S(1)} collective-permute-done((bf16[256,768]{1,0:T(8,128)(2,1)S(1)}, bf16[256,768]{1,0:T(8,128)(2,1)S(1)}, u32[]{:S(2)}, u32[]{:S(2)}) %collective-permute-start.20) | collective-permute-done | bytes 393248 | tf_op jit(solution)/shard_map/ppermute | solution.py:99
  110.3 3.0 %shard_map.60 = bf16[2048,3584]{1,0:T(8,128)(2,1)} custom-call(s32[4]{0:T(128)S(1)} %get-tuple-element.11.refs_16_.where_ref, bf16[1024,256]{1,0:T(8,128)(2,1)S(1)} %shard_map.57.refs_0_, bf16[1024,256]{1,0:T(8,128)(2,1)S(1)} %collective-permute-done.19.refs_0_.refs_1_, ...), custom_call_target="tpu_custom_call", output_to_operand_aliasing={{}: (5, {})} | custom-call | flops 805306368 | bytes 3145728 | tf_op jit(solution)/shard_map/pallas_call | solution.py:423
  (19 shorter events, 0.1 us)
Async XLA Ops:
  0.0 12.5 %collective-permute-start = (bf16[32,4096]{1,0:T(8,128)(2,1)}, bf16[32,4096]{1,0:T(8,128)(2,1)S(1)}, u32[]{:S(2)}, u32[]{:S(2)}) collective-permute-start(bf16[32,4096]{1,0:T(8,128)(2,1)} %bitcast.18), channel_id=1, source_target_pairs={{0,4},{1,5},{2,6},{3,7},{4,8},{5,9},{6,10},{7,11},{8,12},{9,13},{1... | collective-permute-start | bytes 786440 | tf_op jit(solution)/shard_map/ppermute | solution.py:99
  3.0 19.9 %collective-permute-start.1 = (bf16[32,4096]{1,0:T(8,128)(2,1)}, bf16[32,4096]{1,0:T(8,128)(2,1)S(1)}, u32[]{:S(2)}, u32[]{:S(2)}) collective-permute-start(bf16[32,4096]{1,0:T(8,128)(2,1)} %bitcast.19), channel_id=1, source_target_pairs={{0,8},{1,9},{2,10},{3,11},{4,12},{5,13},{6,14},{7,15},{8,0},{9,1},... | collective-permute-start | bytes 786440 | tf_op jit(solution)/shard_map/ppermute | solution.py:99
  5.6 17.3 %collective-permute-start.2 = (bf16[32,4096]{1,0:T(8,128)(2,1)}, bf16[32,4096]{1,0:T(8,128)(2,1)S(1)}, u32[]{:S(2)}, u32[]{:S(2)}) collective-permute-start(bf16[32,4096]{1,0:T(8,128)(2,1)} %bitcast.20), channel_id=1, source_target_pairs={{0,12},{1,13},{2,14},{3,15},{4,0},{5,1},{6,2},{7,3},{8,4},{9,5},{1... | collective-permute-start | bytes 786440 | tf_op jit(solution)/shard_map/ppermute | solution.py:99
  7.0 1.0 copy-start
  8.0 15.6 %collective-permute-start.3 = (bf16[32,4096]{1,0:T(8,128)(2,1)S(1)}, bf16[32,4096]{1,0:T(8,128)(2,1)S(1)}, u32[]{:S(2)}, u32[]{:S(2)}) collective-permute-start(bf16[32,4096]{1,0:T(8,128)(2,1)S(1)} %shard_map.46.refs_0_), channel_id=1, source_target_pairs={{0,2},{1,3},{2,0},{3,1},{4,6},{5,7},{6,4},{7,5},{8,10},{9,11},{10,... | collective-permute-start | bytes 786440 | tf_op jit(solution)/shard_map/ppermute | solution.py:99
  12.5 11.1 %collective-permute-start.4 = (bf16[32,4096]{1,0:T(8,128)(2,1)S(1)}, bf16[32,4096]{1,0:T(8,128)(2,1)S(1)}, u32[]{:S(2)}, u32[]{:S(2)}) collective-permute-start(bf16[32,4096]{1,0:T(8,128)(2,1)S(1)} %collective-permute-done.refs_1_), channel_id=1, source_target_pairs={{0,2},{1,3},{2,0},{3,1},{4,6},{5,7},{6,4},{7,5},{8,10},{9,11},{10,... | collective-permute-start | bytes 786440 | tf_op jit(solution)/shard_map/ppermute | solution.py:99
  22.9 1.5 %collective-permute-start.5 = (bf16[32,4096]{1,0:T(8,128)(2,1)S(1)}, bf16[32,4096]{1,0:T(8,128)(2,1)S(1)}, u32[]{:S(2)}, u32[]{:S(2)}) collective-permute-start(bf16[32,4096]{1,0:T(8,128)(2,1)S(1)} %collective-permute-done.1.refs_2_), channel_id=1, source_target_pairs={{0,2},{1,3},{2,0},{3,1},{4,6},{5,7},{6,4},{7,5},{8,10},{9,11},{10,... | collective-permute-start | bytes 786440 | tf_op jit(solution)/shard_map/ppermute | solution.py:99
  22.9 1.9 %collective-permute-start.6 = (bf16[32,4096]{1,0:T(8,128)(2,1)S(1)}, bf16[32,4096]{1,0:T(8,128)(2,1)S(1)}, u32[]{:S(2)}, u32[]{:S(2)}) collective-permute-start(bf16[32,4096]{1,0:T(8,128)(2,1)S(1)} %collective-permute-done.2.refs_3_), channel_id=1, source_target_pairs={{0,2},{1,3},{2,0},{3,1},{4,6},{5,7},{6,4},{7,5},{8,10},{9,11},{10,... | collective-permute-start | bytes 786440 | tf_op jit(solution)/shard_map/ppermute | solution.py:99
  34.0 21.8 %collective-permute-start.7 = (bf16[2,256,1024]{2,1,0:T(8,128)(2,1)S(1)}, bf16[2,256,1024]{2,1,0:T(8,128)(2,1)S(1)}, u32[]{:S(2)}, u32[]{:S(2)}) collective-permute-start(bf16[2,256,1024]{2,1,0:T(8,128)(2,1)S(1)} %shard_map.47.refs_8_.refs_0_), channel_id=1, source_target_pairs={{16,17},{17,16},{18,19},{19,18},{20,21},{21,20},{22,23},{23,22},{2... | collective-permute-start | bytes 3145736 | tf_op jit(solution)/shard_map/ppermute | solution.py:99
  55.1 30.1 %collective-permute-start.12 = (bf16[2,256,768]{2,1,0:T(8,128)(2,1)S(1)}, bf16[2,256,768]{2,1,0:T(8,128)(2,1)S(1)}, u32[]{:S(2)}, u32[]{:S(2)}) collective-permute-start(bf16[2,256,768]{2,1,0:T(8,128)(2,1)S(1)} %get-tuple-element.7.refs_1_), channel_id=1, source_target_pairs={{16,17},{17,16},{18,19},{19,18},{20,21},{21,20},{22,23},{23,22},{2... | collective-permute-start | bytes 2359304 | tf_op jit(solution)/shard_map/ppermute | solution.py:99
  56.1 20.5 %collective-permute-start.14 = (bf16[256,1024]{1,0:T(8,128)(2,1)S(1)}, bf16[256,1024]{1,0:T(8,128)(2,1)S(1)}, u32[]{:S(2)}, u32[]{:S(2)}) collective-permute-start(bf16[256,1024]{1,0:T(8,128)(2,1)S(1)} %shard_map.49.refs_3_.refs_2_), channel_id=1, source_target_pairs={{16,0},{17,1},{18,2},{19,3},{20,4},{21,5},{22,6},{23,7},{24,8},{25... | collective-permute-start | bytes 1572872 | tf_op jit(solution)/shard_map/ppermute | solution.py:99
  59.1 10.9 %collective-permute-start.9 = (bf16[2,256,256]{2,1,0:T(8,128)(2,1)S(1)}, bf16[2,256,256]{2,1,0:T(8,128)(2,1)S(1)}, u32[]{:S(2)}, u32[]{:S(2)}) collective-permute-start(bf16[2,256,256]{2,1,0:T(8,128)(2,1)S(1)} %shard_map.50.refs_3_), channel_id=1, source_target_pairs={{0,1},{1,0},{2,3},{3,2},{4,5},{5,4},{6,7},{7,6},{8,9},{9,8},{10,11... | collective-permute-start | bytes 786440 | tf_op jit(solution)/shard_map/ppermute | solution.py:99
  64.3 15.7 %collective-permute-start.8 = (bf16[2,256,256]{2,1,0:T(8,128)(2,1)S(1)}, bf16[2,256,256]{2,1,0:T(8,128)(2,1)S(1)}, u32[]{:S(2)}, u32[]{:S(2)}) collective-permute-start(bf16[2,256,256]{2,1,0:T(8,128)(2,1)S(1)} %shard_map.51.refs_3_), channel_id=1, source_target_pairs={{0,1},{1,0},{2,3},{3,2},{4,5},{5,4},{6,7},{7,6},{8,9},{9,8},{10,11... | collective-permute-start | bytes 786440 | tf_op jit(solution)/shard_map/ppermute | solution.py:99
  70.3 9.7 %collective-permute-start.10 = (bf16[256,256]{1,0:T(8,128)(2,1)S(1)}, bf16[256,256]{1,0:T(8,128)(2,1)S(1)}, u32[]{:S(2)}, u32[]{:S(2)}) collective-permute-start(bf16[256,256]{1,0:T(8,128)(2,1)S(1)} %shard_map.53), channel_id=1, source_target_pairs={{0,16},{1,17},{2,18},{3,19},{4,20},{5,21},{6,22},{7,23},{8,24},{9,... | collective-permute-start | bytes 393224 | tf_op jit(solution)/shard_map/ppermute | solution.py:99
  71.6 20.8 %collective-permute-start.16 = (bf16[256,1024]{1,0:T(8,128)(2,1)S(1)}, bf16[256,1024]{1,0:T(8,128)(2,1)S(1)}, u32[]{:S(2)}, u32[]{:S(2)}) collective-permute-start(bf16[256,1024]{1,0:T(8,128)(2,1)S(1)} %shard_map.49.refs_3_.refs_2_), channel_id=1, source_target_pairs={{16,17},{17,16},{18,19},{19,18},{20,21},{21,20},{22,23},{23,22},{2... | collective-permute-start | bytes 1572872 | tf_op jit(solution)/shard_map/ppermute | solution.py:99
  76.6 20.2 %collective-permute-start.15 = (bf16[256,1024]{1,0:T(8,128)(2,1)S(1)}, bf16[256,1024]{1,0:T(8,128)(2,1)S(1)}, u32[]{:S(2)}, u32[]{:S(2)}) collective-permute-start(bf16[256,1024]{1,0:T(8,128)(2,1)S(1)} %collective-permute-done.14.refs_1_), channel_id=1, source_target_pairs={{0,1},{1,0},{2,3},{3,2},{4,5},{5,4},{6,7},{7,6},{8,9},{9,8},{10,11... | collective-permute-start | bytes 1572872 | tf_op jit(solution)/shard_map/ppermute | solution.py:99
  80.4 9.2 %collective-permute-start.11 = (bf16[256,256]{1,0:T(8,128)(2,1)S(1)}, bf16[256,256]{1,0:T(8,128)(2,1)S(1)}, u32[]{:S(2)}, u32[]{:S(2)}) collective-permute-start(bf16[256,256]{1,0:T(8,128)(2,1)S(1)} %shard_map.54.refs_0_), channel_id=1, source_target_pairs={{0,8},{1,9},{2,10},{3,11},{4,12},{5,13},{6,14},{7,15},{8,0},{9,1},... | collective-permute-start | bytes 393224 | tf_op jit(solution)/shard_map/ppermute | solution.py:99
  85.5 11.3 %collective-permute-start.17 = (bf16[256,768]{1,0:T(8,128)(2,1)S(1)}, bf16[256,768]{1,0:T(8,128)(2,1)S(1)}, u32[]{:S(2)}, u32[]{:S(2)}) collective-permute-start(bf16[256,768]{1,0:T(8,128)(2,1)S(1)} %shard_map.55.refs_2_.refs_4_), channel_id=1, source_target_pairs={{16,0},{17,1},{18,2},{19,3},{20,4},{21,5},{22,6},{23,7},{24,8},{25... | collective-permute-start | bytes 1179656 | tf_op jit(solution)/shard_map/ppermute | solution.py:99
  86.8 10.0 %collective-permute-start.18 = (bf16[256,768]{1,0:T(8,128)(2,1)S(1)}, bf16[256,768]{1,0:T(8,128)(2,1)S(1)}, u32[]{:S(2)}, u32[]{:S(2)}) collective-permute-start(bf16[256,768]{1,0:T(8,128)(2,1)S(1)} %shard_map.55.refs_2_.refs_4_), channel_id=1, source_target_pairs={{16,17},{17,16},{18,19},{19,18},{20,21},{21,20},{22,23},{23,22},{2... | collective-permute-start | bytes 1179656 | tf_op jit(solution)/shard_map/ppermute | solution.py:99
  89.9 6.8 %collective-permute-start.13 = (bf16[512,256]{1,0:T(8,128)(2,1)S(1)}, bf16[512,256]{1,0:T(8,128)(2,1)S(1)}, u32[]{:S(2)}, u32[]{:S(2)}) collective-permute-start(bf16[512,256]{1,0:T(8,128)(2,1)S(1)} %shard_map.56.refs_0_), channel_id=1, source_target_pairs={{0,4},{1,5},{2,6},{3,7},{4,0},{5,1},{6,2},{7,3},{8,12},{9,13},{10,... | collective-permute-start | bytes 786440 | tf_op jit(solution)/shard_map/ppermute | solution.py:99
  96.8 6.6 %collective-permute-start.19 = (bf16[1024,256]{1,0:T(8,128)(2,1)S(1)}, bf16[1024,256]{1,0:T(8,128)(2,1)S(1)}, u32[]{:S(2)}, u32[]{:S(2)}) collective-permute-start(bf16[1024,256]{1,0:T(8,128)(2,1)S(1)} %shard_map.57.refs_0_), channel_id=1, source_target_pairs={{0,2},{1,3},{2,0},{3,1},{4,6},{5,7},{6,4},{7,5},{8,10},{9,11},{10,... | collective-permute-start | bytes 1572872 | tf_op jit(solution)/shard_map/ppermute | solution.py:99
  96.9 13.4 %collective-permute-start.20 = (bf16[256,768]{1,0:T(8,128)(2,1)S(1)}, bf16[256,768]{1,0:T(8,128)(2,1)S(1)}, u32[]{:S(2)}, u32[]{:S(2)}) collective-permute-start(bf16[256,768]{1,0:T(8,128)(2,1)S(1)} %collective-permute-done.17.refs_4_.refs_3_), channel_id=1, source_target_pairs={{0,1},{1,0},{2,3},{3,2},{4,5},{5,4},{6,7},{7,6},{8,9},{9,8},{10,11... | collective-permute-start | bytes 1179656 | tf_op jit(solution)/shard_map/ppermute | solution.py:99

commit v8 on v7

--- a/solution.py
+++ b/solution.py
@@ -128,7 +128,7 @@
         copy.wait()
 
 
-def join(blocks, after):
+def join(blocks, after, flops=0):
     rows, width = blocks[0].shape
     count = len(blocks)
     return call(
@@ -137,7 +137,7 @@
         in_specs=[pl.BlockSpec(memory_space=pl.ANY)] * (count + len(after)),
         out_specs=pl.BlockSpec(memory_space=pltpu.VMEM),
         scratch_shapes=[pltpu.SemaphoreType.DMA((count,))],
-        flops=0,
+        flops=flops,
         moved=0,
         vmem=16,
     )(*blocks, *after)
@@ -512,7 +512,7 @@
     nears.append((send(z, sizes, b_to_a), z))
     fars.append((send(nears[1][0], sizes, a_sides), send(z, sizes, b_sides)))
 
-    panel = join([rows, swapped(rows, sizes, 2)], [z])
+    panel = join([rows, swapped(rows, sizes, 2)], [z], 1 << 33)
     panel = join([panel, swapped(panel, sizes, 1)], [*fars[0], nears[1][0], fars[1][1]])
     panel_other = send(panel, sizes, other_core)
     shape = (2 * CHIPS * rows.shape[0], units)

time: 115 us -> 116 us (level)
  no operation moved by 1% of the time
where the time goes in v8:
time: 116 us; the launch traced here: 114 us
  Pallas kernels  48.3 us (42%)
  starting transfers between devices  34.3 us (30%)
  waiting for transfers between devices  28.3 us (24%)
  local copies, waits for them, and re-layouts  1.84 us (2%)
    ppermute x21, starting transfers between devices, send(): return lax.ppermute(block, AXES, routes(sizes, move))  34.3 us
    pallas_call x2, Pallas kernels, products(): call(functools.partial(products_kernel, counts, len(after)), out_shape=[j...  29.5 us
    ppermute x21, waiting for transfers between devices, send(): return lax.ppermute(block, AXES, routes(sizes, move))  28.3 us
    pallas_call x3, Pallas kernels, scores(): call(functools.partial(score_kernel, 1.0 / math.sqrt(tokens), tile, cores...  11.2 us
    pallas_call x3, Pallas kernels, pick(): call(functools.partial(pick_kernel, counts, tile), out_shape=jax.ShapeDty...  5.96 us
  transfers between devices with their start and end apart: 21, of which 9 were waited for; matrix products, arithmetic and copies ran while one was open for 1% of the time, Pallas kernels for 32%

profile of v8, /device:TPU:0, one launch (start us, length us, event | category | flops | bytes accessed | tf_op | source)
XLA Modules:
  0.0 113.6 jit_solution(676166792626656850)
XLA Ops:
  0.0 3.0 %collective-permute-start = (bf16[32,4096]{1,0:T(8,128)(2,1)}, bf16[32,4096]{1,0:T(8,128)(2,1)S(1)}, u32[]{:S(2)}, u32[]{:S(2)}) collective-permute-start(bf16[32,4096]{1,0:T(8,128)(2,1)} %bitcast.18), channel_id=1, source_target_pairs={{0,4},{1,5},{2,6},{3,7},{4,8},{5,9},{6,10},{7,11},{8,12},{9,13},{1... | collective-permute-start | bytes 786440 | tf_op jit(solution)/shard_map/ppermute | solution.py:99
  3.0 2.6 %collective-permute-start.1 = (bf16[32,4096]{1,0:T(8,128)(2,1)}, bf16[32,4096]{1,0:T(8,128)(2,1)S(1)}, u32[]{:S(2)}, u32[]{:S(2)}) collective-permute-start(bf16[32,4096]{1,0:T(8,128)(2,1)} %bitcast.19), channel_id=1, source_target_pairs={{0,8},{1,9},{2,10},{3,11},{4,12},{5,13},{6,14},{7,15},{8,0},{9,1},... | collective-permute-start | bytes 786440 | tf_op jit(solution)/shard_map/ppermute | solution.py:99
  5.6 1.3 %collective-permute-start.2 = (bf16[32,4096]{1,0:T(8,128)(2,1)}, bf16[32,4096]{1,0:T(8,128)(2,1)S(1)}, u32[]{:S(2)}, u32[]{:S(2)}) collective-permute-start(bf16[32,4096]{1,0:T(8,128)(2,1)} %bitcast.20), channel_id=1, source_target_pairs={{0,12},{1,13},{2,14},{3,15},{4,0},{5,1},{6,2},{7,3},{8,4},{9,5},{1... | collective-permute-start | bytes 786440 | tf_op jit(solution)/shard_map/ppermute | solution.py:99
  7.0 1.0 copy-done
  8.0 0.1 collective-permute-start.3
  8.1 0.1 pad_add_fusion.2.place_ref.refs_13_
  8.2 0.8 reshape.19
  8.9 0.1 pad_add_fusion
  9.0 3.5 %collective-permute-done.refs_1_ = bf16[32,4096]{1,0:T(8,128)(2,1)S(1)} collective-permute-done((bf16[32,4096]{1,0:T(8,128)(2,1)}, bf16[32,4096]{1,0:T(8,128)(2,1)S(1)}, u32[]{:S(2)}, u32[]{:S(2)}) %collective-permute-start) | collective-permute-done | bytes 262176 | tf_op jit(solution)/shard_map/ppermute | solution.py:99
  12.5 10.4 %collective-permute-done.1.refs_2_ = bf16[32,4096]{1,0:T(8,128)(2,1)S(1)} collective-permute-done((bf16[32,4096]{1,0:T(8,128)(2,1)}, bf16[32,4096]{1,0:T(8,128)(2,1)S(1)}, u32[]{:S(2)}, u32[]{:S(2)}) %collective-permute-start.1) | collective-permute-done | bytes 262176 | tf_op jit(solution)/shard_map/ppermute | solution.py:99
  22.9 0.5 collective-permute-start.6
  23.4 0.1 pad_add_fusion.3.refs_14_.place_ref
  23.5 0.1 stack.69.refs_15_.where_ref
  23.6 0.8 collective-permute-done.5.refs_6_
  24.5 0.4 collective-permute-done.6.refs_7_
  24.8 9.2 %shard_map.47.refs_8_.refs_0_ = bf16[2,256,1024]{2,1,0:T(8,128)(2,1)S(1)} custom-call(s32[3]{0:T(128)S(1)} %pad_add_fusion.2.place_ref.refs_13_, bf16[4096,3584]{1,0:T(8,128)(2,1)} %bitcast.24, bf16[4096,3584]{1,0:T(8,128)(2,1)} %bitcast.26, bf16[32,4096]{1,0:T(8,128)(2,1)S(1)} %shard_map.46.refs_0_, bf16[32,4096]{1,0:T(8,128)(2,1)S(1)} %collective-permute-done.refs_1_, ...), custom_call_target="tpu_custom_call" | custom-call | flops 4294967296 | bytes 16777216 | tf_op jit(solution)/shard_map/pallas_call | solution.py:207
  34.0 0.7 collective-permute-start.7
  34.8 20.3 %shard_map.48 = (bf16[2,256,768]{2,1,0:T(8,128)(2,1)S(1)}, bf16[2,256,1792]{2,1,0:T(8,128)(2,1)S(1)}) custom-call(s32[4]{0:T(128)S(1)} %pad_add_fusion.3.refs_14_.place_ref, bf16[4096,3584]{1,0:T(8,128)(2,1)} %bitcast.25, bf16[4096,3584]{1,0:T(8,128)(2,1)} %bitcast.27, bf16[32,4096]{1,0:T(8,128)(2,1)S(1)} %shard_map.46.refs_0_, ...), custom_call_target="tpu_custom_call" | custom-call | flops 10737418240 | bytes 41943040 | tf_op jit(solution)/shard_map/pallas_call | solution.py:207
  55.1 0.7 collective-permute-start.12
  55.8 0.3 shard_map.49.refs_3_.refs_2_
  56.1 1.7 %shard_map.50.refs_3_ = bf16[2,256,256]{2,1,0:T(8,128)(2,1)S(1)} custom-call(s32[4]{0:T(128)S(1)} %get-tuple-element.12.refs_11_.bases_ref, s32[1,256]{1,0:T(1,128)S(1)} %get-tuple-element.10.refs_8_.picks_ref, bf16[2,256,1024]{2,1,0:T(8,128)(2,1)S(1)} %shard_map.47.refs_8_.refs_0_, bf16[2,256,768]{2,1,0:T(8,128)(2,1)S(1)} %get-tuple-element.7.refs_1_, ...), custom_call_target="tpu_custom_call" | custom-call | tf_op jit(solution)/shard_map/pallas_call | solution.py:254
  57.8 3.5 %collective-permute-start.9 = (bf16[2,256,256]{2,1,0:T(8,128)(2,1)S(1)}, bf16[2,256,256]{2,1,0:T(8,128)(2,1)S(1)}, u32[]{:S(2)}, u32[]{:S(2)}) collective-permute-start(bf16[2,256,256]{2,1,0:T(8,128)(2,1)S(1)} %shard_map.50.refs_3_), channel_id=1, source_target_pairs={{0,1},{1,0},{2,3},{3,2},{4,5},{5,4},{6,7},{7,6},{8,9},{9,8},{10,11... | collective-permute-start | bytes 786440 | tf_op jit(solution)/shard_map/ppermute | solution.py:99
  61.3 1.3 %collective-permute-start.14 = (bf16[256,1024]{1,0:T(8,128)(2,1)S(1)}, bf16[256,1024]{1,0:T(8,128)(2,1)S(1)}, u32[]{:S(2)}, u32[]{:S(2)}) collective-permute-start(bf16[256,1024]{1,0:T(8,128)(2,1)S(1)} %shard_map.49.refs_3_.refs_2_), channel_id=1, source_target_pairs={{16,0},{17,1},{18,2},{19,3},{20,4},{21,5},{22,6},{23,7},{24,8},{25... | collective-permute-start | bytes 1572872 | tf_op jit(solution)/shard_map/ppermute | solution.py:99
  62.6 1.7 %shard_map.51.refs_3_ = bf16[2,256,256]{2,1,0:T(8,128)(2,1)S(1)} custom-call(s32[4]{0:T(128)S(1)} %get-tuple-element.12.refs_11_.bases_ref, s32[1,256]{1,0:T(1,128)S(1)} %get-tuple-element.9.refs_9_.picks_ref, bf16[2,256,1024]{2,1,0:T(8,128)(2,1)S(1)} %shard_map.47.refs_8_.refs_0_, bf16[2,256,768]{2,1,0:T(8,128)(2,1)S(1)} %get-tuple-element.7.refs_1_, ...), custom_call_target="tpu_custom_call" | custom-call | tf_op jit(solution)/shard_map/pallas_call | solution.py:254
  64.3 2.3 %collective-permute-start.8 = (bf16[2,256,256]{2,1,0:T(8,128)(2,1)S(1)}, bf16[2,256,256]{2,1,0:T(8,128)(2,1)S(1)}, u32[]{:S(2)}, u32[]{:S(2)}) collective-permute-start(bf16[2,256,256]{2,1,0:T(8,128)(2,1)S(1)} %shard_map.51.refs_3_), channel_id=1, source_target_pairs={{0,1},{1,0},{2,3},{3,2},{4,5},{5,4},{6,7},{7,6},{8,9},{9,8},{10,11... | collective-permute-start | bytes 786440 | tf_op jit(solution)/shard_map/ppermute | solution.py:99
  66.7 2.6 %shard_map.52.mine_ref = bf16[2,256,512]{2,1,0:T(8,128)(2,1)S(1)} custom-call(s32[4]{0:T(128)S(1)} %get-tuple-element.12.refs_11_.bases_ref, s32[1,512]{1,0:T(1,128)S(1)} %bitcast.23, bf16[2,256,1024]{2,1,0:T(8,128)(2,1)S(1)} %shard_map.47.refs_8_.refs_0_, bf16[2,256,768]{2,1,0:T(8,128)(2,1)S(1)} %get-tuple-element.7.refs_1_, ...), custom_call_target="tpu_custom_call" | custom-call | tf_op jit(solution)/shard_map/pallas_call | solution.py:254
  69.3 0.3 shard_map.53
  69.6 1.3 %collective-permute-start.10 = (bf16[256,256]{1,0:T(8,128)(2,1)S(1)}, bf16[256,256]{1,0:T(8,128)(2,1)S(1)}, u32[]{:S(2)}, u32[]{:S(2)}) collective-permute-start(bf16[256,256]{1,0:T(8,128)(2,1)S(1)} %shard_map.53), channel_id=1, source_target_pairs={{0,16},{1,17},{2,18},{3,19},{4,20},{5,21},{6,22},{7,23},{8,24},{9,... | collective-permute-start | bytes 393224 | tf_op jit(solution)/shard_map/ppermute | solution.py:99
  70.9 3.4 %collective-permute-done.8.theirs_ref = bf16[2,256,256]{2,1,0:T(8,128)(2,1)S(1)} collective-permute-done((bf16[2,256,256]{2,1,0:T(8,128)(2,1)S(1)}, bf16[2,256,256]{2,1,0:T(8,128)(2,1)S(1)}, u32[]{:S(2)}, u32[]{:S(2)}) %collective-permute-start.8) | collective-permute-done | bytes 262176 | tf_op jit(solution)/shard_map/ppermute | solution.py:99
  74.3 0.3 shard_map.54.refs_0_
  74.6 4.9 %collective-permute-start.11 = (bf16[256,256]{1,0:T(8,128)(2,1)S(1)}, bf16[256,256]{1,0:T(8,128)(2,1)S(1)}, u32[]{:S(2)}, u32[]{:S(2)}) collective-permute-start(bf16[256,256]{1,0:T(8,128)(2,1)S(1)} %shard_map.54.refs_0_), channel_id=1, source_target_pairs={{0,8},{1,9},{2,10},{3,11},{4,12},{5,13},{6,14},{7,15},{8,0},{9,1},... | collective-permute-start | bytes 393224 | tf_op jit(solution)/shard_map/ppermute | solution.py:99
  79.5 0.7 collective-permute-start.16
  80.2 0.3 shard_map.55.refs_2_.refs_4_
  80.5 1.3 %collective-permute-start.17 = (bf16[256,768]{1,0:T(8,128)(2,1)S(1)}, bf16[256,768]{1,0:T(8,128)(2,1)S(1)}, u32[]{:S(2)}, u32[]{:S(2)}) collective-permute-start(bf16[256,768]{1,0:T(8,128)(2,1)S(1)} %shard_map.55.refs_2_.refs_4_), channel_id=1, source_target_pairs={{16,0},{17,1},{18,2},{19,3},{20,4},{21,5},{22,6},{23,7},{24,8},{25... | collective-permute-start | bytes 1179656 | tf_op jit(solution)/shard_map/ppermute | solution.py:99
  81.8 0.7 collective-permute-start.18
  82.5 2.9 %collective-permute-start.15 = (bf16[256,1024]{1,0:T(8,128)(2,1)S(1)}, bf16[256,1024]{1,0:T(8,128)(2,1)S(1)}, u32[]{:S(2)}, u32[]{:S(2)}) collective-permute-start(bf16[256,1024]{1,0:T(8,128)(2,1)S(1)} %collective-permute-done.14.refs_1_), channel_id=1, source_target_pairs={{0,1},{1,0},{2,3},{3,2},{4,5},{5,4},{6,7},{7,6},{8,9},{9,8},{10,11... | collective-permute-start | bytes 1572872 | tf_op jit(solution)/shard_map/ppermute | solution.py:99
  85.4 0.4 shard_map.56.refs_0_
  85.7 2.9 %collective-permute-start.13 = (bf16[512,256]{1,0:T(8,128)(2,1)S(1)}, bf16[512,256]{1,0:T(8,128)(2,1)S(1)}, u32[]{:S(2)}, u32[]{:S(2)}) collective-permute-start(bf16[512,256]{1,0:T(8,128)(2,1)S(1)} %shard_map.56.refs_0_), channel_id=1, source_target_pairs={{0,4},{1,5},{2,6},{3,7},{4,0},{5,1},{6,2},{7,3},{8,12},{9,13},{10,... | collective-permute-start | bytes 786440 | tf_op jit(solution)/shard_map/ppermute | solution.py:99
  88.7 5.5 %collective-permute-done.13.refs_1_ = bf16[512,256]{1,0:T(8,128)(2,1)S(1)} collective-permute-done((bf16[512,256]{1,0:T(8,128)(2,1)S(1)}, bf16[512,256]{1,0:T(8,128)(2,1)S(1)}, u32[]{:S(2)}, u32[]{:S(2)}) %collective-permute-start.13) | collective-permute-done | bytes 262176 | tf_op jit(solution)/shard_map/ppermute | solution.py:99
  94.2 0.3 collective-permute-done.17.refs_4_.refs_3_
  94.5 2.4 %collective-permute-done.15.refs_2_.refs_5_ = bf16[256,1024]{1,0:T(8,128)(2,1)S(1)} collective-permute-done((bf16[256,1024]{1,0:T(8,128)(2,1)S(1)}, bf16[256,1024]{1,0:T(8,128)(2,1)S(1)}, u32[]{:S(2)}, u32[]{:S(2)}) %collective-permute-start.15) | collective-permute-done | bytes 524320 | tf_op jit(solution)/shard_map/ppermute | solution.py:99
  96.9 0.1 shard_map.57.refs_0_
  96.9 0.1 collective-permute-start.19
  97.0 3.5 %collective-permute-start.20 = (bf16[256,768]{1,0:T(8,128)(2,1)S(1)}, bf16[256,768]{1,0:T(8,128)(2,1)S(1)}, u32[]{:S(2)}, u32[]{:S(2)}) collective-permute-start(bf16[256,768]{1,0:T(8,128)(2,1)S(1)} %collective-permute-done.17.refs_4_.refs_3_), channel_id=1, source_target_pairs={{0,1},{1,0},{2,3},{3,2},{4,5},{5,4},{6,7},{7,6},{8,9},{9,8},{10,11... | collective-permute-start | bytes 1179656 | tf_op jit(solution)/shard_map/ppermute | solution.py:99
  100.5 4.0 %shard_map.58.refs_7_ = bf16[2048,3584]{1,0:T(8,128)(2,1)} custom-call(s32[5]{0:T(128)S(1)} %stack.69.refs_15_.where_ref, bf16[1024,256]{1,0:T(8,128)(2,1)S(1)} %shard_map.57.refs_0_, bf16[256,1024]{1,0:T(8,128)(2,1)S(1)} %collective-permute-done.14.refs_1_, bf16[256,1024]{1,0:T(8,128)(2,1)S(1)} %shard_map.49.refs_3_.refs_2_, ...), custom_call_target="tpu_custom_call" | custom-call | flops 1476395008 | bytes 5767168 | tf_op jit(solution)/shard_map/pallas_call | solution.py:423
  104.5 4.2 %shard_map.59.refs_4_ = bf16[2048,3584]{1,0:T(8,128)(2,1)} custom-call(s32[5]{0:T(128)S(1)} %stack.69.refs_15_.where_ref, bf16[1024,256]{1,0:T(8,128)(2,1)S(1)} %collective-permute-done.19.refs_0_.refs_1_, bf16[256,1024]{1,0:T(8,128)(2,1)S(1)} %collective-permute-done.14.refs_1_, ...), custom_call_target="tpu_custom_call", output_to_operand_aliasing={{}: (8, {})} | custom-call | flops 1476395008 | bytes 5767168 | tf_op jit(solution)/shard_map/pallas_call | solution.py:423
  108.7 1.7 %collective-permute-done.20.refs_2_ = bf16[256,768]{1,0:T(8,128)(2,1)S(1)} collective-permute-done((bf16[256,768]{1,0:T(8,128)(2,1)S(1)}, bf16[256,768]{1,0:T(8,128)(2,1)S(1)}, u32[]{:S(2)}, u32[]{:S(2)}) %collective-permute-start.20) | collective-permute-done | bytes 393248 | tf_op jit(solution)/shard_map/ppermute | solution.py:99
  110.4 3.0 %shard_map.60 = bf16[2048,3584]{1,0:T(8,128)(2,1)} custom-call(s32[4]{0:T(128)S(1)} %get-tuple-element.11.refs_16_.where_ref, bf16[1024,256]{1,0:T(8,128)(2,1)S(1)} %shard_map.57.refs_0_, bf16[1024,256]{1,0:T(8,128)(2,1)S(1)} %collective-permute-done.19.refs_0_.refs_1_, ...), custom_call_target="tpu_custom_call", output_to_operand_aliasing={{}: (5, {})} | custom-call | flops 805306368 | bytes 3145728 | tf_op jit(solution)/shard_map/pallas_call | solution.py:423
  (19 shorter events, 0.1 us)
Async XLA Ops:
  0.0 12.5 %collective-permute-start = (bf16[32,4096]{1,0:T(8,128)(2,1)}, bf16[32,4096]{1,0:T(8,128)(2,1)S(1)}, u32[]{:S(2)}, u32[]{:S(2)}) collective-permute-start(bf16[32,4096]{1,0:T(8,128)(2,1)} %bitcast.18), channel_id=1, source_target_pairs={{0,4},{1,5},{2,6},{3,7},{4,8},{5,9},{6,10},{7,11},{8,12},{9,13},{1... | collective-permute-start | bytes 786440 | tf_op jit(solution)/shard_map/ppermute | solution.py:99
  3.0 19.9 %collective-permute-start.1 = (bf16[32,4096]{1,0:T(8,128)(2,1)}, bf16[32,4096]{1,0:T(8,128)(2,1)S(1)}, u32[]{:S(2)}, u32[]{:S(2)}) collective-permute-start(bf16[32,4096]{1,0:T(8,128)(2,1)} %bitcast.19), channel_id=1, source_target_pairs={{0,8},{1,9},{2,10},{3,11},{4,12},{5,13},{6,14},{7,15},{8,0},{9,1},... | collective-permute-start | bytes 786440 | tf_op jit(solution)/shard_map/ppermute | solution.py:99
  5.6 17.3 %collective-permute-start.2 = (bf16[32,4096]{1,0:T(8,128)(2,1)}, bf16[32,4096]{1,0:T(8,128)(2,1)S(1)}, u32[]{:S(2)}, u32[]{:S(2)}) collective-permute-start(bf16[32,4096]{1,0:T(8,128)(2,1)} %bitcast.20), channel_id=1, source_target_pairs={{0,12},{1,13},{2,14},{3,15},{4,0},{5,1},{6,2},{7,3},{8,4},{9,5},{1... | collective-permute-start | bytes 786440 | tf_op jit(solution)/shard_map/ppermute | solution.py:99
  7.0 1.0 copy-start
  8.0 15.6 %collective-permute-start.3 = (bf16[32,4096]{1,0:T(8,128)(2,1)S(1)}, bf16[32,4096]{1,0:T(8,128)(2,1)S(1)}, u32[]{:S(2)}, u32[]{:S(2)}) collective-permute-start(bf16[32,4096]{1,0:T(8,128)(2,1)S(1)} %shard_map.46.refs_0_), channel_id=1, source_target_pairs={{0,2},{1,3},{2,0},{3,1},{4,6},{5,7},{6,4},{7,5},{8,10},{9,11},{10,... | collective-permute-start | bytes 786440 | tf_op jit(solution)/shard_map/ppermute | solution.py:99
  12.5 11.1 %collective-permute-start.4 = (bf16[32,4096]{1,0:T(8,128)(2,1)S(1)}, bf16[32,4096]{1,0:T(8,128)(2,1)S(1)}, u32[]{:S(2)}, u32[]{:S(2)}) collective-permute-start(bf16[32,4096]{1,0:T(8,128)(2,1)S(1)} %collective-permute-done.refs_1_), channel_id=1, source_target_pairs={{0,2},{1,3},{2,0},{3,1},{4,6},{5,7},{6,4},{7,5},{8,10},{9,11},{10,... | collective-permute-start | bytes 786440 | tf_op jit(solution)/shard_map/ppermute | solution.py:99
  22.9 1.5 %collective-permute-start.5 = (bf16[32,4096]{1,0:T(8,128)(2,1)S(1)}, bf16[32,4096]{1,0:T(8,128)(2,1)S(1)}, u32[]{:S(2)}, u32[]{:S(2)}) collective-permute-start(bf16[32,4096]{1,0:T(8,128)(2,1)S(1)} %collective-permute-done.1.refs_2_), channel_id=1, source_target_pairs={{0,2},{1,3},{2,0},{3,1},{4,6},{5,7},{6,4},{7,5},{8,10},{9,11},{10,... | collective-permute-start | bytes 786440 | tf_op jit(solution)/shard_map/ppermute | solution.py:99
  22.9 1.9 %collective-permute-start.6 = (bf16[32,4096]{1,0:T(8,128)(2,1)S(1)}, bf16[32,4096]{1,0:T(8,128)(2,1)S(1)}, u32[]{:S(2)}, u32[]{:S(2)}) collective-permute-start(bf16[32,4096]{1,0:T(8,128)(2,1)S(1)} %collective-permute-done.2.refs_3_), channel_id=1, source_target_pairs={{0,2},{1,3},{2,0},{3,1},{4,6},{5,7},{6,4},{7,5},{8,10},{9,11},{10,... | collective-permute-start | bytes 786440 | tf_op jit(solution)/shard_map/ppermute | solution.py:99
  34.0 21.8 %collective-permute-start.7 = (bf16[2,256,1024]{2,1,0:T(8,128)(2,1)S(1)}, bf16[2,256,1024]{2,1,0:T(8,128)(2,1)S(1)}, u32[]{:S(2)}, u32[]{:S(2)}) collective-permute-start(bf16[2,256,1024]{2,1,0:T(8,128)(2,1)S(1)} %shard_map.47.refs_8_.refs_0_), channel_id=1, source_target_pairs={{16,17},{17,16},{18,19},{19,18},{20,21},{21,20},{22,23},{23,22},{2... | collective-permute-start | bytes 3145736 | tf_op jit(solution)/shard_map/ppermute | solution.py:99
  55.1 25.1 %collective-permute-start.12 = (bf16[2,256,768]{2,1,0:T(8,128)(2,1)S(1)}, bf16[2,256,768]{2,1,0:T(8,128)(2,1)S(1)}, u32[]{:S(2)}, u32[]{:S(2)}) collective-permute-start(bf16[2,256,768]{2,1,0:T(8,128)(2,1)S(1)} %get-tuple-element.7.refs_1_), channel_id=1, source_target_pairs={{16,17},{17,16},{18,19},{19,18},{20,21},{21,20},{22,23},{23,22},{2... | collective-permute-start | bytes 2359304 | tf_op jit(solution)/shard_map/ppermute | solution.py:99
  57.8 11.5 %collective-permute-start.9 = (bf16[2,256,256]{2,1,0:T(8,128)(2,1)S(1)}, bf16[2,256,256]{2,1,0:T(8,128)(2,1)S(1)}, u32[]{:S(2)}, u32[]{:S(2)}) collective-permute-start(bf16[2,256,256]{2,1,0:T(8,128)(2,1)S(1)} %shard_map.50.refs_3_), channel_id=1, source_target_pairs={{0,1},{1,0},{2,3},{3,2},{4,5},{5,4},{6,7},{7,6},{8,9},{9,8},{10,11... | collective-permute-start | bytes 786440 | tf_op jit(solution)/shard_map/ppermute | solution.py:99
  61.3 21.1 %collective-permute-start.14 = (bf16[256,1024]{1,0:T(8,128)(2,1)S(1)}, bf16[256,1024]{1,0:T(8,128)(2,1)S(1)}, u32[]{:S(2)}, u32[]{:S(2)}) collective-permute-start(bf16[256,1024]{1,0:T(8,128)(2,1)S(1)} %shard_map.49.refs_3_.refs_2_), channel_id=1, source_target_pairs={{16,0},{17,1},{18,2},{19,3},{20,4},{21,5},{22,6},{23,7},{24,8},{25... | collective-permute-start | bytes 1572872 | tf_op jit(solution)/shard_map/ppermute | solution.py:99
  64.3 10.0 %collective-permute-start.8 = (bf16[2,256,256]{2,1,0:T(8,128)(2,1)S(1)}, bf16[2,256,256]{2,1,0:T(8,128)(2,1)S(1)}, u32[]{:S(2)}, u32[]{:S(2)}) collective-permute-start(bf16[2,256,256]{2,1,0:T(8,128)(2,1)S(1)} %shard_map.51.refs_3_), channel_id=1, source_target_pairs={{0,1},{1,0},{2,3},{3,2},{4,5},{5,4},{6,7},{7,6},{8,9},{9,8},{10,11... | collective-permute-start | bytes 786440 | tf_op jit(solution)/shard_map/ppermute | solution.py:99
  69.6 4.7 %collective-permute-start.10 = (bf16[256,256]{1,0:T(8,128)(2,1)S(1)}, bf16[256,256]{1,0:T(8,128)(2,1)S(1)}, u32[]{:S(2)}, u32[]{:S(2)}) collective-permute-start(bf16[256,256]{1,0:T(8,128)(2,1)S(1)} %shard_map.53), channel_id=1, source_target_pairs={{0,16},{1,17},{2,18},{3,19},{4,20},{5,21},{6,22},{7,23},{8,24},{9,... | collective-permute-start | bytes 393224 | tf_op jit(solution)/shard_map/ppermute | solution.py:99
  74.6 10.8 %collective-permute-start.11 = (bf16[256,256]{1,0:T(8,128)(2,1)S(1)}, bf16[256,256]{1,0:T(8,128)(2,1)S(1)}, u32[]{:S(2)}, u32[]{:S(2)}) collective-permute-start(bf16[256,256]{1,0:T(8,128)(2,1)S(1)} %shard_map.54.refs_0_), channel_id=1, source_target_pairs={{0,8},{1,9},{2,10},{3,11},{4,12},{5,13},{6,14},{7,15},{8,0},{9,1},... | collective-permute-start | bytes 393224 | tf_op jit(solution)/shard_map/ppermute | solution.py:99
  79.5 9.2 %collective-permute-start.16 = (bf16[256,1024]{1,0:T(8,128)(2,1)S(1)}, bf16[256,1024]{1,0:T(8,128)(2,1)S(1)}, u32[]{:S(2)}, u32[]{:S(2)}) collective-permute-start(bf16[256,1024]{1,0:T(8,128)(2,1)S(1)} %shard_map.49.refs_3_.refs_2_), channel_id=1, source_target_pairs={{16,17},{17,16},{18,19},{19,18},{20,21},{21,20},{22,23},{23,22},{2... | collective-permute-start | bytes 1572872 | tf_op jit(solution)/shard_map/ppermute | solution.py:99
  80.5 14.0 %collective-permute-start.17 = (bf16[256,768]{1,0:T(8,128)(2,1)S(1)}, bf16[256,768]{1,0:T(8,128)(2,1)S(1)}, u32[]{:S(2)}, u32[]{:S(2)}) collective-permute-start(bf16[256,768]{1,0:T(8,128)(2,1)S(1)} %shard_map.55.refs_2_.refs_4_), channel_id=1, source_target_pairs={{16,0},{17,1},{18,2},{19,3},{20,4},{21,5},{22,6},{23,7},{24,8},{25... | collective-permute-start | bytes 1179656 | tf_op jit(solution)/shard_map/ppermute | solution.py:99
  81.8 12.7 %collective-permute-start.18 = (bf16[256,768]{1,0:T(8,128)(2,1)S(1)}, bf16[256,768]{1,0:T(8,128)(2,1)S(1)}, u32[]{:S(2)}, u32[]{:S(2)}) collective-permute-start(bf16[256,768]{1,0:T(8,128)(2,1)S(1)} %shard_map.55.refs_2_.refs_4_), channel_id=1, source_target_pairs={{16,17},{17,16},{18,19},{19,18},{20,21},{21,20},{22,23},{23,22},{2... | collective-permute-start | bytes 1179656 | tf_op jit(solution)/shard_map/ppermute | solution.py:99
  82.5 14.4 %collective-permute-start.15 = (bf16[256,1024]{1,0:T(8,128)(2,1)S(1)}, bf16[256,1024]{1,0:T(8,128)(2,1)S(1)}, u32[]{:S(2)}, u32[]{:S(2)}) collective-permute-start(bf16[256,1024]{1,0:T(8,128)(2,1)S(1)} %collective-permute-done.14.refs_1_), channel_id=1, source_target_pairs={{0,1},{1,0},{2,3},{3,2},{4,5},{5,4},{6,7},{7,6},{8,9},{9,8},{10,11... | collective-permute-start | bytes 1572872 | tf_op jit(solution)/shard_map/ppermute | solution.py:99
  85.7 8.4 %collective-permute-start.13 = (bf16[512,256]{1,0:T(8,128)(2,1)S(1)}, bf16[512,256]{1,0:T(8,128)(2,1)S(1)}, u32[]{:S(2)}, u32[]{:S(2)}) collective-permute-start(bf16[512,256]{1,0:T(8,128)(2,1)S(1)} %shard_map.56.refs_0_), channel_id=1, source_target_pairs={{0,4},{1,5},{2,6},{3,7},{4,0},{5,1},{6,2},{7,3},{8,12},{9,13},{10,... | collective-permute-start | bytes 786440 | tf_op jit(solution)/shard_map/ppermute | solution.py:99
  96.9 7.6 %collective-permute-start.19 = (bf16[1024,256]{1,0:T(8,128)(2,1)S(1)}, bf16[1024,256]{1,0:T(8,128)(2,1)S(1)}, u32[]{:S(2)}, u32[]{:S(2)}) collective-permute-start(bf16[1024,256]{1,0:T(8,128)(2,1)S(1)} %shard_map.57.refs_0_), channel_id=1, source_target_pairs={{0,2},{1,3},{2,0},{3,1},{4,6},{5,7},{6,4},{7,5},{8,10},{9,11},{10,... | collective-permute-start | bytes 1572872 | tf_op jit(solution)/shard_map/ppermute | solution.py:99
  97.0 13.4 %collective-permute-start.20 = (bf16[256,768]{1,0:T(8,128)(2,1)S(1)}, bf16[256,768]{1,0:T(8,128)(2,1)S(1)}, u32[]{:S(2)}, u32[]{:S(2)}) collective-permute-start(bf16[256,768]{1,0:T(8,128)(2,1)S(1)} %collective-permute-done.17.refs_4_.refs_3_), channel_id=1, source_target_pairs={{0,1},{1,0},{2,3},{3,2},{4,5},{5,4},{6,7},{7,6},{8,9},{9,8},{10,11... | collective-permute-start | bytes 1179656 | tf_op jit(solution)/shard_map/ppermute | solution.py:99

commit v9 on v8

--- a/solution.py
+++ b/solution.py
@@ -508,12 +508,12 @@
         picked_own, send(picked_a, sizes, a_sides), 0, (model_number, rows_b)
     )
 
-    z = unit_scores(model_number, kept, came[1], tile, chunks[0], [rows])
+    z = unit_scores(model_number, kept, came[1], tile, chunks[0], [rows, a_mine])
     nears.append((send(z, sizes, b_to_a), z))
     fars.append((send(nears[1][0], sizes, a_sides), send(z, sizes, b_sides)))
 
     panel = join([rows, swapped(rows, sizes, 2)], [z], 1 << 33)
-    panel = join([panel, swapped(panel, sizes, 1)], [*fars[0], nears[1][0], fars[1][1]])
+    panel = join([panel, swapped(panel, sizes, 1)], [*fars[0], nears[1][0]])
     panel_other = send(panel, sizes, other_core)
     shape = (2 * CHIPS * rows.shape[0], units)
     sides = [nears, fars[:1]]

time: 116 us -> 115 us (level); the launches traced: 114 us -> 115 us
  transfers between devices with their start and end apart: 21 -> 21, of which waited for: 9 -> 9; matrix products, arithmetic and copies ran while one was open for 1% -> 1% of each run, Pallas kernels for 32% -> 31%
where the time goes in v9:
time: 115 us
  Pallas kernels  48.3 us (42%)
  starting transfers between devices  34.8 us (30%)
  waiting for transfers between devices  29.1 us (25%)
  local copies, waits for them, and re-layouts  1.84 us (2%)
    ppermute x21, starting transfers between devices, send(): return lax.ppermute(block, AXES, routes(sizes, move))  34.8 us
    pallas_call x2, Pallas kernels, products(): call(functools.partial(products_kernel, counts, len(after)), out_shape=[j...  29.5 us
    ppermute x21, waiting for transfers between devices, send(): return lax.ppermute(block, AXES, routes(sizes, move))  29.1 us
    pallas_call x3, Pallas kernels, scores(): call(functools.partial(score_kernel, 1.0 / math.sqrt(tokens), tile, cores...  11.2 us
    pallas_call x3, Pallas kernels, pick(): call(functools.partial(pick_kernel, counts, tile), out_shape=jax.ShapeDty...  5.96 us
  transfers between devices with their start and end apart: 21, of which 9 were waited for; matrix products, arithmetic and copies ran while one was open for 1% of the time, Pallas kernels for 31%

profile of v9, /device:TPU:0, one launch (start us, length us, event | category | flops | bytes accessed | tf_op | source)
XLA Modules:
  0.0 114.8 jit_solution(12461131432731182456)
XLA Ops:
  0.0 3.0 %collective-permute-start = (bf16[32,4096]{1,0:T(8,128)(2,1)}, bf16[32,4096]{1,0:T(8,128)(2,1)S(1)}, u32[]{:S(2)}, u32[]{:S(2)}) collective-permute-start(bf16[32,4096]{1,0:T(8,128)(2,1)} %bitcast.18), channel_id=1, source_target_pairs={{0,4},{1,5},{2,6},{3,7},{4,8},{5,9},{6,10},{7,11},{8,12},{9,13},{1... | collective-permute-start | bytes 786440 | tf_op jit(solution)/shard_map/ppermute | solution.py:99
  3.0 2.6 %collective-permute-start.1 = (bf16[32,4096]{1,0:T(8,128)(2,1)}, bf16[32,4096]{1,0:T(8,128)(2,1)S(1)}, u32[]{:S(2)}, u32[]{:S(2)}) collective-permute-start(bf16[32,4096]{1,0:T(8,128)(2,1)} %bitcast.19), channel_id=1, source_target_pairs={{0,8},{1,9},{2,10},{3,11},{4,12},{5,13},{6,14},{7,15},{8,0},{9,1},... | collective-permute-start | bytes 786440 | tf_op jit(solution)/shard_map/ppermute | solution.py:99
  5.6 1.3 %collective-permute-start.2 = (bf16[32,4096]{1,0:T(8,128)(2,1)}, bf16[32,4096]{1,0:T(8,128)(2,1)S(1)}, u32[]{:S(2)}, u32[]{:S(2)}) collective-permute-start(bf16[32,4096]{1,0:T(8,128)(2,1)} %bitcast.20), channel_id=1, source_target_pairs={{0,12},{1,13},{2,14},{3,15},{4,0},{5,1},{6,2},{7,3},{8,4},{9,5},{1... | collective-permute-start | bytes 786440 | tf_op jit(solution)/shard_map/ppermute | solution.py:99
  7.0 1.0 copy-done
  8.0 0.1 collective-permute-start.3
  8.1 0.1 pad_add_fusion.2.place_ref.refs_13_
  8.2 0.8 reshape.19
  8.9 0.1 pad_add_fusion
  9.0 3.5 %collective-permute-done.refs_1_ = bf16[32,4096]{1,0:T(8,128)(2,1)S(1)} collective-permute-done((bf16[32,4096]{1,0:T(8,128)(2,1)}, bf16[32,4096]{1,0:T(8,128)(2,1)S(1)}, u32[]{:S(2)}, u32[]{:S(2)}) %collective-permute-start) | collective-permute-done | bytes 262176 | tf_op jit(solution)/shard_map/ppermute | solution.py:99
  12.5 10.4 %collective-permute-done.1.refs_2_ = bf16[32,4096]{1,0:T(8,128)(2,1)S(1)} collective-permute-done((bf16[32,4096]{1,0:T(8,128)(2,1)}, bf16[32,4096]{1,0:T(8,128)(2,1)S(1)}, u32[]{:S(2)}, u32[]{:S(2)}) %collective-permute-start.1) | collective-permute-done | bytes 262176 | tf_op jit(solution)/shard_map/ppermute | solution.py:99
  22.9 0.5 collective-permute-start.6
  23.4 0.1 pad_add_fusion.3.refs_14_.place_ref
  23.5 0.1 stack.69.refs_15_.where_ref
  23.6 0.8 collective-permute-done.5.refs_6_
  24.5 0.4 collective-permute-done.6.refs_7_
  24.8 9.2 %shard_map.47.refs_8_.refs_0_ = bf16[2,256,1024]{2,1,0:T(8,128)(2,1)S(1)} custom-call(s32[3]{0:T(128)S(1)} %pad_add_fusion.2.place_ref.refs_13_, bf16[4096,3584]{1,0:T(8,128)(2,1)} %bitcast.24, bf16[4096,3584]{1,0:T(8,128)(2,1)} %bitcast.26, bf16[32,4096]{1,0:T(8,128)(2,1)S(1)} %shard_map.46.refs_0_, bf16[32,4096]{1,0:T(8,128)(2,1)S(1)} %collective-permute-done.refs_1_, ...), custom_call_target="tpu_custom_call" | custom-call | flops 4294967296 | bytes 16777216 | tf_op jit(solution)/shard_map/pallas_call | solution.py:207
  34.0 0.7 collective-permute-start.7
  34.8 20.3 %shard_map.48 = (bf16[2,256,768]{2,1,0:T(8,128)(2,1)S(1)}, bf16[2,256,1792]{2,1,0:T(8,128)(2,1)S(1)}) custom-call(s32[4]{0:T(128)S(1)} %pad_add_fusion.3.refs_14_.place_ref, bf16[4096,3584]{1,0:T(8,128)(2,1)} %bitcast.25, bf16[4096,3584]{1,0:T(8,128)(2,1)} %bitcast.27, bf16[32,4096]{1,0:T(8,128)(2,1)S(1)} %shard_map.46.refs_0_, ...), custom_call_target="tpu_custom_call" | custom-call | flops 10737418240 | bytes 41943040 | tf_op jit(solution)/shard_map/pallas_call | solution.py:207
  55.1 0.7 collective-permute-start.12
  55.8 0.3 shard_map.49.refs_3_.refs_2_
  56.1 1.7 %shard_map.50.refs_3_ = bf16[2,256,256]{2,1,0:T(8,128)(2,1)S(1)} custom-call(s32[4]{0:T(128)S(1)} %get-tuple-element.12.refs_11_.bases_ref, s32[1,256]{1,0:T(1,128)S(1)} %get-tuple-element.10.refs_8_.picks_ref, bf16[2,256,1024]{2,1,0:T(8,128)(2,1)S(1)} %shard_map.47.refs_8_.refs_0_, bf16[2,256,768]{2,1,0:T(8,128)(2,1)S(1)} %get-tuple-element.7.refs_1_, ...), custom_call_target="tpu_custom_call" | custom-call | tf_op jit(solution)/shard_map/pallas_call | solution.py:254
  57.8 1.3 %collective-permute-start.13 = (bf16[256,1024]{1,0:T(8,128)(2,1)S(1)}, bf16[256,1024]{1,0:T(8,128)(2,1)S(1)}, u32[]{:S(2)}, u32[]{:S(2)}) collective-permute-start(bf16[256,1024]{1,0:T(8,128)(2,1)S(1)} %shard_map.49.refs_3_.refs_2_), channel_id=1, source_target_pairs={{16,0},{17,1},{18,2},{19,3},{20,4},{21,5},{22,6},{23,7},{24,8},{25... | collective-permute-start | bytes 1572872 | tf_op jit(solution)/shard_map/ppermute | solution.py:99
  59.1 3.5 %collective-permute-start.9 = (bf16[2,256,256]{2,1,0:T(8,128)(2,1)S(1)}, bf16[2,256,256]{2,1,0:T(8,128)(2,1)S(1)}, u32[]{:S(2)}, u32[]{:S(2)}) collective-permute-start(bf16[2,256,256]{2,1,0:T(8,128)(2,1)S(1)} %shard_map.50.refs_3_), channel_id=1, source_target_pairs={{0,1},{1,0},{2,3},{3,2},{4,5},{5,4},{6,7},{7,6},{8,9},{9,8},{10,11... | collective-permute-start | bytes 786440 | tf_op jit(solution)/shard_map/ppermute | solution.py:99
  62.6 1.7 %shard_map.51.refs_3_ = bf16[2,256,256]{2,1,0:T(8,128)(2,1)S(1)} custom-call(s32[4]{0:T(128)S(1)} %get-tuple-element.12.refs_11_.bases_ref, s32[1,256]{1,0:T(1,128)S(1)} %get-tuple-element.9.refs_9_.picks_ref, bf16[2,256,1024]{2,1,0:T(8,128)(2,1)S(1)} %shard_map.47.refs_8_.refs_0_, bf16[2,256,768]{2,1,0:T(8,128)(2,1)S(1)} %get-tuple-element.7.refs_1_, ...), custom_call_target="tpu_custom_call" | custom-call | tf_op jit(solution)/shard_map/pallas_call | solution.py:254
  64.3 2.3 %collective-permute-start.8 = (bf16[2,256,256]{2,1,0:T(8,128)(2,1)S(1)}, bf16[2,256,256]{2,1,0:T(8,128)(2,1)S(1)}, u32[]{:S(2)}, u32[]{:S(2)}) collective-permute-start(bf16[2,256,256]{2,1,0:T(8,128)(2,1)S(1)} %shard_map.51.refs_3_), channel_id=1, source_target_pairs={{0,1},{1,0},{2,3},{3,2},{4,5},{5,4},{6,7},{7,6},{8,9},{9,8},{10,11... | collective-permute-start | bytes 786440 | tf_op jit(solution)/shard_map/ppermute | solution.py:99
  66.7 2.6 %shard_map.52.mine_ref = bf16[2,256,512]{2,1,0:T(8,128)(2,1)S(1)} custom-call(s32[4]{0:T(128)S(1)} %get-tuple-element.12.refs_11_.bases_ref, s32[1,512]{1,0:T(1,128)S(1)} %bitcast.23, bf16[2,256,1024]{2,1,0:T(8,128)(2,1)S(1)} %shard_map.47.refs_8_.refs_0_, bf16[2,256,768]{2,1,0:T(8,128)(2,1)S(1)} %get-tuple-element.7.refs_1_, ...), custom_call_target="tpu_custom_call" | custom-call | tf_op jit(solution)/shard_map/pallas_call | solution.py:254
  69.3 0.7 collective-permute-done.9.theirs_ref
  70.0 0.3 shard_map.53
  70.3 1.3 %collective-permute-start.10 = (bf16[256,256]{1,0:T(8,128)(2,1)S(1)}, bf16[256,256]{1,0:T(8,128)(2,1)S(1)}, u32[]{:S(2)}, u32[]{:S(2)}) collective-permute-start(bf16[256,256]{1,0:T(8,128)(2,1)S(1)} %shard_map.53), channel_id=1, source_target_pairs={{0,16},{1,17},{2,18},{3,19},{4,20},{5,21},{6,22},{7,23},{8,24},{9,... | collective-permute-start | bytes 393224 | tf_op jit(solution)/shard_map/ppermute | solution.py:99
  71.6 3.4 %collective-permute-done.8.theirs_ref = bf16[2,256,256]{2,1,0:T(8,128)(2,1)S(1)} collective-permute-done((bf16[2,256,256]{2,1,0:T(8,128)(2,1)S(1)}, bf16[2,256,256]{2,1,0:T(8,128)(2,1)S(1)}, u32[]{:S(2)}, u32[]{:S(2)}) %collective-permute-start.8) | collective-permute-done | bytes 262176 | tf_op jit(solution)/shard_map/ppermute | solution.py:99
  75.0 0.3 shard_map.54.refs_0_
  75.3 4.9 %collective-permute-start.11 = (bf16[256,256]{1,0:T(8,128)(2,1)S(1)}, bf16[256,256]{1,0:T(8,128)(2,1)S(1)}, u32[]{:S(2)}, u32[]{:S(2)}) collective-permute-start(bf16[256,256]{1,0:T(8,128)(2,1)S(1)} %shard_map.54.refs_0_), channel_id=1, source_target_pairs={{0,8},{1,9},{2,10},{3,11},{4,12},{5,13},{6,14},{7,15},{8,0},{9,1},... | collective-permute-start | bytes 393224 | tf_op jit(solution)/shard_map/ppermute | solution.py:99
  80.2 0.7 collective-permute-start.16
  80.9 0.3 shard_map.55.refs_2_.refs_4_
  81.2 1.3 %collective-permute-start.17 = (bf16[256,768]{1,0:T(8,128)(2,1)S(1)}, bf16[256,768]{1,0:T(8,128)(2,1)S(1)}, u32[]{:S(2)}, u32[]{:S(2)}) collective-permute-start(bf16[256,768]{1,0:T(8,128)(2,1)S(1)} %shard_map.55.refs_2_.refs_4_), channel_id=1, source_target_pairs={{16,0},{17,1},{18,2},{19,3},{20,4},{21,5},{22,6},{23,7},{24,8},{25... | collective-permute-start | bytes 1179656 | tf_op jit(solution)/shard_map/ppermute | solution.py:99
  82.5 3.5 %collective-permute-start.15 = (bf16[256,1024]{1,0:T(8,128)(2,1)S(1)}, bf16[256,1024]{1,0:T(8,128)(2,1)S(1)}, u32[]{:S(2)}, u32[]{:S(2)}) collective-permute-start(bf16[256,1024]{1,0:T(8,128)(2,1)S(1)} %collective-permute-done.13.refs_1_), channel_id=1, source_target_pairs={{0,1},{1,0},{2,3},{3,2},{4,5},{5,4},{6,7},{7,6},{8,9},{9,8},{10,11... | collective-permute-start | bytes 1572872 | tf_op jit(solution)/shard_map/ppermute | solution.py:99
  86.0 0.4 shard_map.56.refs_0_
  86.4 2.9 %collective-permute-start.14 = (bf16[512,256]{1,0:T(8,128)(2,1)S(1)}, bf16[512,256]{1,0:T(8,128)(2,1)S(1)}, u32[]{:S(2)}, u32[]{:S(2)}) collective-permute-start(bf16[512,256]{1,0:T(8,128)(2,1)S(1)} %shard_map.56.refs_0_), channel_id=1, source_target_pairs={{0,4},{1,5},{2,6},{3,7},{4,0},{5,1},{6,2},{7,3},{8,12},{9,13},{10,... | collective-permute-start | bytes 786440 | tf_op jit(solution)/shard_map/ppermute | solution.py:99
  89.3 5.2 %collective-permute-done.14.refs_1_ = bf16[512,256]{1,0:T(8,128)(2,1)S(1)} collective-permute-done((bf16[512,256]{1,0:T(8,128)(2,1)S(1)}, bf16[512,256]{1,0:T(8,128)(2,1)S(1)}, u32[]{:S(2)}, u32[]{:S(2)}) %collective-permute-start.14) | collective-permute-done | bytes 262176 | tf_op jit(solution)/shard_map/ppermute | solution.py:99
  94.5 2.9 %collective-permute-done.15.refs_2_.refs_5_ = bf16[256,1024]{1,0:T(8,128)(2,1)S(1)} collective-permute-done((bf16[256,1024]{1,0:T(8,128)(2,1)S(1)}, bf16[256,1024]{1,0:T(8,128)(2,1)S(1)}, u32[]{:S(2)}, u32[]{:S(2)}) %collective-permute-start.15) | collective-permute-done | bytes 524320 | tf_op jit(solution)/shard_map/ppermute | solution.py:99
  97.4 0.1 shard_map.57.refs_0_
  97.5 0.1 collective-permute-start.18
  97.5 0.7 collective-permute-start.20
  98.2 3.3 %collective-permute-start.19 = (bf16[256,768]{1,0:T(8,128)(2,1)S(1)}, bf16[256,768]{1,0:T(8,128)(2,1)S(1)}, u32[]{:S(2)}, u32[]{:S(2)}) collective-permute-start(bf16[256,768]{1,0:T(8,128)(2,1)S(1)} %collective-permute-done.17.refs_4_.refs_3_), channel_id=1, source_target_pairs={{0,1},{1,0},{2,3},{3,2},{4,5},{5,4},{6,7},{7,6},{8,9},{9,8},{10,11... | collective-permute-start | bytes 1179656 | tf_op jit(solution)/shard_map/ppermute | solution.py:99
  101.6 4.0 %shard_map.58.refs_7_ = bf16[2048,3584]{1,0:T(8,128)(2,1)} custom-call(s32[5]{0:T(128)S(1)} %stack.69.refs_15_.where_ref, bf16[1024,256]{1,0:T(8,128)(2,1)S(1)} %shard_map.57.refs_0_, bf16[256,1024]{1,0:T(8,128)(2,1)S(1)} %collective-permute-done.13.refs_1_, bf16[256,1024]{1,0:T(8,128)(2,1)S(1)} %shard_map.49.refs_3_.refs_2_, ...), custom_call_target="tpu_custom_call" | custom-call | flops 1476395008 | bytes 5767168 | tf_op jit(solution)/shard_map/pallas_call | solution.py:423
  105.6 4.2 %shard_map.59.refs_4_ = bf16[2048,3584]{1,0:T(8,128)(2,1)} custom-call(s32[5]{0:T(128)S(1)} %stack.69.refs_15_.where_ref, bf16[1024,256]{1,0:T(8,128)(2,1)S(1)} %collective-permute-done.18.refs_0_.refs_1_, bf16[256,1024]{1,0:T(8,128)(2,1)S(1)} %collective-permute-done.13.refs_1_, ...), custom_call_target="tpu_custom_call", output_to_operand_aliasing={{}: (8, {})} | custom-call | flops 1476395008 | bytes 5767168 | tf_op jit(solution)/shard_map/pallas_call | solution.py:423
  109.8 1.8 %collective-permute-done.19.refs_2_ = bf16[256,768]{1,0:T(8,128)(2,1)S(1)} collective-permute-done((bf16[256,768]{1,0:T(8,128)(2,1)S(1)}, bf16[256,768]{1,0:T(8,128)(2,1)S(1)}, u32[]{:S(2)}, u32[]{:S(2)}) %collective-permute-start.19) | collective-permute-done | bytes 393248 | tf_op jit(solution)/shard_map/ppermute | solution.py:99
  111.6 3.0 %shard_map.60 = bf16[2048,3584]{1,0:T(8,128)(2,1)} custom-call(s32[4]{0:T(128)S(1)} %get-tuple-element.11.refs_16_.where_ref, bf16[1024,256]{1,0:T(8,128)(2,1)S(1)} %shard_map.57.refs_0_, bf16[1024,256]{1,0:T(8,128)(2,1)S(1)} %collective-permute-done.18.refs_0_.refs_1_, ...), custom_call_target="tpu_custom_call", output_to_operand_aliasing={{}: (5, {})} | custom-call | flops 805306368 | bytes 3145728 | tf_op jit(solution)/shard_map/pallas_call | solution.py:423
  (19 shorter events, 0.1 us)
Async XLA Ops:
  0.0 12.5 %collective-permute-start = (bf16[32,4096]{1,0:T(8,128)(2,1)}, bf16[32,4096]{1,0:T(8,128)(2,1)S(1)}, u32[]{:S(2)}, u32[]{:S(2)}) collective-permute-start(bf16[32,4096]{1,0:T(8,128)(2,1)} %bitcast.18), channel_id=1, source_target_pairs={{0,4},{1,5},{2,6},{3,7},{4,8},{5,9},{6,10},{7,11},{8,12},{9,13},{1... | collective-permute-start | bytes 786440 | tf_op jit(solution)/shard_map/ppermute | solution.py:99
  3.0 19.9 %collective-permute-start.1 = (bf16[32,4096]{1,0:T(8,128)(2,1)}, bf16[32,4096]{1,0:T(8,128)(2,1)S(1)}, u32[]{:S(2)}, u32[]{:S(2)}) collective-permute-start(bf16[32,4096]{1,0:T(8,128)(2,1)} %bitcast.19), channel_id=1, source_target_pairs={{0,8},{1,9},{2,10},{3,11},{4,12},{5,13},{6,14},{7,15},{8,0},{9,1},... | collective-permute-start | bytes 786440 | tf_op jit(solution)/shard_map/ppermute | solution.py:99
  5.6 17.3 %collective-permute-start.2 = (bf16[32,4096]{1,0:T(8,128)(2,1)}, bf16[32,4096]{1,0:T(8,128)(2,1)S(1)}, u32[]{:S(2)}, u32[]{:S(2)}) collective-permute-start(bf16[32,4096]{1,0:T(8,128)(2,1)} %bitcast.20), channel_id=1, source_target_pairs={{0,12},{1,13},{2,14},{3,15},{4,0},{5,1},{6,2},{7,3},{8,4},{9,5},{1... | collective-permute-start | bytes 786440 | tf_op jit(solution)/shard_map/ppermute | solution.py:99
  7.0 1.0 copy-start
  8.0 15.6 %collective-permute-start.3 = (bf16[32,4096]{1,0:T(8,128)(2,1)S(1)}, bf16[32,4096]{1,0:T(8,128)(2,1)S(1)}, u32[]{:S(2)}, u32[]{:S(2)}) collective-permute-start(bf16[32,4096]{1,0:T(8,128)(2,1)S(1)} %shard_map.46.refs_0_), channel_id=1, source_target_pairs={{0,2},{1,3},{2,0},{3,1},{4,6},{5,7},{6,4},{7,5},{8,10},{9,11},{10,... | collective-permute-start | bytes 786440 | tf_op jit(solution)/shard_map/ppermute | solution.py:99
  12.5 11.1 %collective-permute-start.4 = (bf16[32,4096]{1,0:T(8,128)(2,1)S(1)}, bf16[32,4096]{1,0:T(8,128)(2,1)S(1)}, u32[]{:S(2)}, u32[]{:S(2)}) collective-permute-start(bf16[32,4096]{1,0:T(8,128)(2,1)S(1)} %collective-permute-done.refs_1_), channel_id=1, source_target_pairs={{0,2},{1,3},{2,0},{3,1},{4,6},{5,7},{6,4},{7,5},{8,10},{9,11},{10,... | collective-permute-start | bytes 786440 | tf_op jit(solution)/shard_map/ppermute | solution.py:99
  22.9 1.5 %collective-permute-start.5 = (bf16[32,4096]{1,0:T(8,128)(2,1)S(1)}, bf16[32,4096]{1,0:T(8,128)(2,1)S(1)}, u32[]{:S(2)}, u32[]{:S(2)}) collective-permute-start(bf16[32,4096]{1,0:T(8,128)(2,1)S(1)} %collective-permute-done.1.refs_2_), channel_id=1, source_target_pairs={{0,2},{1,3},{2,0},{3,1},{4,6},{5,7},{6,4},{7,5},{8,10},{9,11},{10,... | collective-permute-start | bytes 786440 | tf_op jit(solution)/shard_map/ppermute | solution.py:99
  22.9 1.9 %collective-permute-start.6 = (bf16[32,4096]{1,0:T(8,128)(2,1)S(1)}, bf16[32,4096]{1,0:T(8,128)(2,1)S(1)}, u32[]{:S(2)}, u32[]{:S(2)}) collective-permute-start(bf16[32,4096]{1,0:T(8,128)(2,1)S(1)} %collective-permute-done.2.refs_3_), channel_id=1, source_target_pairs={{0,2},{1,3},{2,0},{3,1},{4,6},{5,7},{6,4},{7,5},{8,10},{9,11},{10,... | collective-permute-start | bytes 786440 | tf_op jit(solution)/shard_map/ppermute | solution.py:99
  34.0 21.8 %collective-permute-start.7 = (bf16[2,256,1024]{2,1,0:T(8,128)(2,1)S(1)}, bf16[2,256,1024]{2,1,0:T(8,128)(2,1)S(1)}, u32[]{:S(2)}, u32[]{:S(2)}) collective-permute-start(bf16[2,256,1024]{2,1,0:T(8,128)(2,1)S(1)} %shard_map.47.refs_8_.refs_0_), channel_id=1, source_target_pairs={{16,17},{17,16},{18,19},{19,18},{20,21},{21,20},{22,23},{23,22},{2... | collective-permute-start | bytes 3145736 | tf_op jit(solution)/shard_map/ppermute | solution.py:99
  55.1 25.8 %collective-permute-start.12 = (bf16[2,256,768]{2,1,0:T(8,128)(2,1)S(1)}, bf16[2,256,768]{2,1,0:T(8,128)(2,1)S(1)}, u32[]{:S(2)}, u32[]{:S(2)}) collective-permute-start(bf16[2,256,768]{2,1,0:T(8,128)(2,1)S(1)} %get-tuple-element.7.refs_1_), channel_id=1, source_target_pairs={{16,17},{17,16},{18,19},{19,18},{20,21},{21,20},{22,23},{23,22},{2... | collective-permute-start | bytes 2359304 | tf_op jit(solution)/shard_map/ppermute | solution.py:99
  57.8 23.1 %collective-permute-start.13 = (bf16[256,1024]{1,0:T(8,128)(2,1)S(1)}, bf16[256,1024]{1,0:T(8,128)(2,1)S(1)}, u32[]{:S(2)}, u32[]{:S(2)}) collective-permute-start(bf16[256,1024]{1,0:T(8,128)(2,1)S(1)} %shard_map.49.refs_3_.refs_2_), channel_id=1, source_target_pairs={{16,0},{17,1},{18,2},{19,3},{20,4},{21,5},{22,6},{23,7},{24,8},{25... | collective-permute-start | bytes 1572872 | tf_op jit(solution)/shard_map/ppermute | solution.py:99
  59.1 10.9 %collective-permute-start.9 = (bf16[2,256,256]{2,1,0:T(8,128)(2,1)S(1)}, bf16[2,256,256]{2,1,0:T(8,128)(2,1)S(1)}, u32[]{:S(2)}, u32[]{:S(2)}) collective-permute-start(bf16[2,256,256]{2,1,0:T(8,128)(2,1)S(1)} %shard_map.50.refs_3_), channel_id=1, source_target_pairs={{0,1},{1,0},{2,3},{3,2},{4,5},{5,4},{6,7},{7,6},{8,9},{9,8},{10,11... | collective-permute-start | bytes 786440 | tf_op jit(solution)/shard_map/ppermute | solution.py:99
  64.3 10.7 %collective-permute-start.8 = (bf16[2,256,256]{2,1,0:T(8,128)(2,1)S(1)}, bf16[2,256,256]{2,1,0:T(8,128)(2,1)S(1)}, u32[]{:S(2)}, u32[]{:S(2)}) collective-permute-start(bf16[2,256,256]{2,1,0:T(8,128)(2,1)S(1)} %shard_map.51.refs_3_), channel_id=1, source_target_pairs={{0,1},{1,0},{2,3},{3,2},{4,5},{5,4},{6,7},{7,6},{8,9},{9,8},{10,11... | collective-permute-start | bytes 786440 | tf_op jit(solution)/shard_map/ppermute | solution.py:99
  70.3 4.7 %collective-permute-start.10 = (bf16[256,256]{1,0:T(8,128)(2,1)S(1)}, bf16[256,256]{1,0:T(8,128)(2,1)S(1)}, u32[]{:S(2)}, u32[]{:S(2)}) collective-permute-start(bf16[256,256]{1,0:T(8,128)(2,1)S(1)} %shard_map.53), channel_id=1, source_target_pairs={{0,16},{1,17},{2,18},{3,19},{4,20},{5,21},{6,22},{7,23},{8,24},{9,... | collective-permute-start | bytes 393224 | tf_op jit(solution)/shard_map/ppermute | solution.py:99
  75.3 10.6 %collective-permute-start.11 = (bf16[256,256]{1,0:T(8,128)(2,1)S(1)}, bf16[256,256]{1,0:T(8,128)(2,1)S(1)}, u32[]{:S(2)}, u32[]{:S(2)}) collective-permute-start(bf16[256,256]{1,0:T(8,128)(2,1)S(1)} %shard_map.54.refs_0_), channel_id=1, source_target_pairs={{0,8},{1,9},{2,10},{3,11},{4,12},{5,13},{6,14},{7,15},{8,0},{9,1},... | collective-permute-start | bytes 393224 | tf_op jit(solution)/shard_map/ppermute | solution.py:99
  80.2 9.1 %collective-permute-start.16 = (bf16[256,1024]{1,0:T(8,128)(2,1)S(1)}, bf16[256,1024]{1,0:T(8,128)(2,1)S(1)}, u32[]{:S(2)}, u32[]{:S(2)}) collective-permute-start(bf16[256,1024]{1,0:T(8,128)(2,1)S(1)} %shard_map.49.refs_3_.refs_2_), channel_id=1, source_target_pairs={{16,17},{17,16},{18,19},{19,18},{20,21},{21,20},{22,23},{23,22},{2... | collective-permute-start | bytes 1572872 | tf_op jit(solution)/shard_map/ppermute | solution.py:99
  81.2 13.4 %collective-permute-start.17 = (bf16[256,768]{1,0:T(8,128)(2,1)S(1)}, bf16[256,768]{1,0:T(8,128)(2,1)S(1)}, u32[]{:S(2)}, u32[]{:S(2)}) collective-permute-start(bf16[256,768]{1,0:T(8,128)(2,1)S(1)} %shard_map.55.refs_2_.refs_4_), channel_id=1, source_target_pairs={{16,0},{17,1},{18,2},{19,3},{20,4},{21,5},{22,6},{23,7},{24,8},{25... | collective-permute-start | bytes 1179656 | tf_op jit(solution)/shard_map/ppermute | solution.py:99
  82.5 14.9 %collective-permute-start.15 = (bf16[256,1024]{1,0:T(8,128)(2,1)S(1)}, bf16[256,1024]{1,0:T(8,128)(2,1)S(1)}, u32[]{:S(2)}, u32[]{:S(2)}) collective-permute-start(bf16[256,1024]{1,0:T(8,128)(2,1)S(1)} %collective-permute-done.13.refs_1_), channel_id=1, source_target_pairs={{0,1},{1,0},{2,3},{3,2},{4,5},{5,4},{6,7},{7,6},{8,9},{9,8},{10,11... | collective-permute-start | bytes 1572872 | tf_op jit(solution)/shard_map/ppermute | solution.py:99
  86.4 8.2 %collective-permute-start.14 = (bf16[512,256]{1,0:T(8,128)(2,1)S(1)}, bf16[512,256]{1,0:T(8,128)(2,1)S(1)}, u32[]{:S(2)}, u32[]{:S(2)}) collective-permute-start(bf16[512,256]{1,0:T(8,128)(2,1)S(1)} %shard_map.56.refs_0_), channel_id=1, source_target_pairs={{0,4},{1,5},{2,6},{3,7},{4,0},{5,1},{6,2},{7,3},{8,12},{9,13},{10,... | collective-permute-start | bytes 786440 | tf_op jit(solution)/shard_map/ppermute | solution.py:99
  97.5 8.1 %collective-permute-start.18 = (bf16[1024,256]{1,0:T(8,128)(2,1)S(1)}, bf16[1024,256]{1,0:T(8,128)(2,1)S(1)}, u32[]{:S(2)}, u32[]{:S(2)}) collective-permute-start(bf16[1024,256]{1,0:T(8,128)(2,1)S(1)} %shard_map.57.refs_0_), channel_id=1, source_target_pairs={{0,2},{1,3},{2,0},{3,1},{4,6},{5,7},{6,4},{7,5},{8,10},{9,11},{10,... | collective-permute-start | bytes 1572872 | tf_op jit(solution)/shard_map/ppermute | solution.py:99
  97.5 12.3 %collective-permute-start.20 = (bf16[256,768]{1,0:T(8,128)(2,1)S(1)}, bf16[256,768]{1,0:T(8,128)(2,1)S(1)}, u32[]{:S(2)}, u32[]{:S(2)}) collective-permute-start(bf16[256,768]{1,0:T(8,128)(2,1)S(1)} %shard_map.55.refs_2_.refs_4_), channel_id=1, source_target_pairs={{16,17},{17,16},{18,19},{19,18},{20,21},{21,20},{22,23},{23,22},{2... | collective-permute-start | bytes 1179656 | tf_op jit(solution)/shard_map/ppermute | solution.py:99
  98.2 13.4 %collective-permute-start.19 = (bf16[256,768]{1,0:T(8,128)(2,1)S(1)}, bf16[256,768]{1,0:T(8,128)(2,1)S(1)}, u32[]{:S(2)}, u32[]{:S(2)}) collective-permute-start(bf16[256,768]{1,0:T(8,128)(2,1)S(1)} %collective-permute-done.17.refs_4_.refs_3_), channel_id=1, source_target_pairs={{0,1},{1,0},{2,3},{3,2},{4,5},{5,4},{6,7},{7,6},{8,9},{9,8},{10,11... | collective-permute-start | bytes 1179656 | tf_op jit(solution)/shard_map/ppermute | solution.py:99

commit v10 on v7

--- a/solution.py
+++ b/solution.py
@@ -381,31 +381,27 @@
 
     copies = []
     for which, other in enumerate(cores):
-        for pair in range(CHIPS // 2):
-            panel = panel_ref[which, 2 * pair * rows : (2 * pair + 2) * rows, :]
-            slot = which * (CHIPS // 2) + pair
-            for side, (units_ref, block_ref) in enumerate(zip(units_refs, block_refs)):
-                columns = units_ref.shape[1]
-                for start in range(0, columns, tile):
-                    total = jnp.dot(
-                        panel,
-                        units_ref[:, start : start + tile],
-                        preferred_element_type=jnp.float32,
-                    )
-                    block_ref[slot, :, :, start : start + tile] = (
-                        (total * scale).astype(jnp.bfloat16).reshape(2, rows, tile)
-                    )
-                for i in range(2):
-                    line = lax.bitwise_xor(chip, SWAPS[2 * pair + i])
+        for side, (units_ref, block_ref) in enumerate(zip(units_refs, block_refs)):
+            for start in range(0, units_ref.shape[1], tile):
+                total = jnp.dot(
+                    panel_ref[which],
+                    units_ref[:, start : start + tile],
+                    preferred_element_type=jnp.float32,
+                )
+                block_ref[which, :, :, start : start + tile] = (
+                    (total * scale).astype(jnp.bfloat16).reshape(CHIPS, rows, tile)
+                )
+                for i in range(CHIPS):
+                    line = lax.bitwise_xor(chip, SWAPS[i])
                     place = line * 2 + (1 - core if other else core)
                     copies.append(
                         pltpu.make_async_copy(
-                            block_ref.at[slot, i],
+                            block_ref.at[which, i, :, start : start + tile],
                             out_ref.at[
                                 pl.ds(pl.multiple_of(place * rows, rows), rows),
-                                pl.ds(pl.multiple_of(where_ref[3 + side], 128), columns),
+                                pl.ds(pl.multiple_of(where_ref[3 + side] + start, 128), tile),
                             ],
-                            out_sems.at[slot, side, i],
+                            out_sems.at[len(copies)],
                         )
                     )
                     copies[-1].start()
@@ -416,7 +412,6 @@
 def scores(where, panels, cores, sides, tile, shape, before):
     rows, tokens = panels[0].shape
     widths = [[piece[0].shape[1] for piece in side] for side in sides]
-    slots = len(panels) * CHIPS // 2
     anywhere = pl.BlockSpec(memory_space=pl.ANY)
     flat = [array for side in sides for piece in side for array in piece]
     columns = [sum(side) for side in widths]
@@ -430,10 +425,10 @@
         out_specs=anywhere,
         scratch_shapes=[pltpu.VMEM((len(panels), rows, tokens), jnp.bfloat16)]
         + [pltpu.VMEM((tokens, count), jnp.bfloat16) for count in columns]
-        + [pltpu.VMEM((slots, 2, rows // CHIPS, count), jnp.bfloat16) for count in columns]
+        + [pltpu.VMEM((len(panels), CHIPS, rows // CHIPS, count), jnp.bfloat16) for count in columns]
         + [
             pltpu.SemaphoreType.DMA((len(panels) + sum(map(len, widths)),)),
-            pltpu.SemaphoreType.DMA((slots, len(sides), 2)),
+            pltpu.SemaphoreType.DMA((len(panels) * CHIPS * sum(columns) // tile,)),
         ],
         input_output_aliases={1 + len(panels) + len(flat): 0} if before else {},
         flops=2 * len(panels) * rows * tokens * sum(columns),

time: 115 us -> 115 us (level)
  no operation moved by 1% of the time
where the time goes in v10:
time: 115 us; the launch traced here: 114 us
  Pallas kernels  48.4 us (42%)
  starting transfers between devices  33.3 us (29%)
  waiting for transfers between devices  29.3 us (25%)
  local copies, waits for them, and re-layouts  1.84 us (2%)
    ppermute x21, starting transfers between devices, send(): return lax.ppermute(block, AXES, routes(sizes, move))  33.3 us
    pallas_call x2, Pallas kernels, products(): call(functools.partial(products_kernel, counts, len(after)), out_shape=[j...  29.5 us
    ppermute x21, waiting for transfers between devices, send(): return lax.ppermute(block, AXES, routes(sizes, move))  29.3 us
    pallas_call x3, Pallas kernels, scores(): call(functools.partial(score_kernel, 1.0 / math.sqrt(tokens), tile, cores...  11.3 us
    pallas_call x3, Pallas kernels, pick(): call(functools.partial(pick_kernel, counts, tile), out_shape=jax.ShapeDty...  5.96 us
  transfers between devices with their start and end apart: 21, of which 9 were waited for; matrix products, arithmetic and copies ran while one was open for 1% of the time, Pallas kernels for 32%

profile of v10, /device:TPU:0, one launch (start us, length us, event | category | flops | bytes accessed | tf_op | source)
XLA Modules:
  0.0 113.6 jit_solution(17700200758658515386)
XLA Ops:
  0.0 3.0 %collective-permute-start = (bf16[32,4096]{1,0:T(8,128)(2,1)}, bf16[32,4096]{1,0:T(8,128)(2,1)S(1)}, u32[]{:S(2)}, u32[]{:S(2)}) collective-permute-start(bf16[32,4096]{1,0:T(8,128)(2,1)} %bitcast.18), channel_id=1, source_target_pairs={{0,4},{1,5},{2,6},{3,7},{4,8},{5,9},{6,10},{7,11},{8,12},{9,13},{1... | collective-permute-start | bytes 786440 | tf_op jit(solution)/shard_map/ppermute | solution.py:99
  3.0 2.6 %collective-permute-start.1 = (bf16[32,4096]{1,0:T(8,128)(2,1)}, bf16[32,4096]{1,0:T(8,128)(2,1)S(1)}, u32[]{:S(2)}, u32[]{:S(2)}) collective-permute-start(bf16[32,4096]{1,0:T(8,128)(2,1)} %bitcast.19), channel_id=1, source_target_pairs={{0,8},{1,9},{2,10},{3,11},{4,12},{5,13},{6,14},{7,15},{8,0},{9,1},... | collective-permute-start | bytes 786440 | tf_op jit(solution)/shard_map/ppermute | solution.py:99
  5.6 1.3 %collective-permute-start.2 = (bf16[32,4096]{1,0:T(8,128)(2,1)}, bf16[32,4096]{1,0:T(8,128)(2,1)S(1)}, u32[]{:S(2)}, u32[]{:S(2)}) collective-permute-start(bf16[32,4096]{1,0:T(8,128)(2,1)} %bitcast.20), channel_id=1, source_target_pairs={{0,12},{1,13},{2,14},{3,15},{4,0},{5,1},{6,2},{7,3},{8,4},{9,5},{1... | collective-permute-start | bytes 786440 | tf_op jit(solution)/shard_map/ppermute | solution.py:99
  7.0 1.0 copy-done
  8.0 0.1 collective-permute-start.3
  8.1 0.1 pad_add_fusion.2.place_ref.refs_13_
  8.2 0.8 reshape.19
  8.9 0.1 pad_add_fusion
  9.0 3.5 %collective-permute-done.refs_1_ = bf16[32,4096]{1,0:T(8,128)(2,1)S(1)} collective-permute-done((bf16[32,4096]{1,0:T(8,128)(2,1)}, bf16[32,4096]{1,0:T(8,128)(2,1)S(1)}, u32[]{:S(2)}, u32[]{:S(2)}) %collective-permute-start) | collective-permute-done | bytes 262176 | tf_op jit(solution)/shard_map/ppermute | solution.py:99
  12.5 10.4 %collective-permute-done.1.refs_2_ = bf16[32,4096]{1,0:T(8,128)(2,1)S(1)} collective-permute-done((bf16[32,4096]{1,0:T(8,128)(2,1)}, bf16[32,4096]{1,0:T(8,128)(2,1)S(1)}, u32[]{:S(2)}, u32[]{:S(2)}) %collective-permute-start.1) | collective-permute-done | bytes 262176 | tf_op jit(solution)/shard_map/ppermute | solution.py:99
  22.9 0.5 collective-permute-start.6
  23.4 0.1 pad_add_fusion.3.refs_14_.place_ref
  23.5 0.1 stack.69.refs_15_.where_ref
  23.6 0.8 collective-permute-done.5.refs_6_
  24.5 0.4 collective-permute-done.6.refs_7_
  24.8 9.2 %shard_map.47.refs_8_.refs_0_ = bf16[2,256,1024]{2,1,0:T(8,128)(2,1)S(1)} custom-call(s32[3]{0:T(128)S(1)} %pad_add_fusion.2.place_ref.refs_13_, bf16[4096,3584]{1,0:T(8,128)(2,1)} %bitcast.24, bf16[4096,3584]{1,0:T(8,128)(2,1)} %bitcast.26, bf16[32,4096]{1,0:T(8,128)(2,1)S(1)} %shard_map.46.refs_0_, bf16[32,4096]{1,0:T(8,128)(2,1)S(1)} %collective-permute-done.refs_1_, ...), custom_call_target="tpu_custom_call" | custom-call | flops 4294967296 | bytes 16777216 | tf_op jit(solution)/shard_map/pallas_call | solution.py:207
  34.0 0.7 collective-permute-start.7
  34.8 20.3 %shard_map.48 = (bf16[2,256,768]{2,1,0:T(8,128)(2,1)S(1)}, bf16[2,256,1792]{2,1,0:T(8,128)(2,1)S(1)}) custom-call(s32[4]{0:T(128)S(1)} %pad_add_fusion.3.refs_14_.place_ref, bf16[4096,3584]{1,0:T(8,128)(2,1)} %bitcast.25, bf16[4096,3584]{1,0:T(8,128)(2,1)} %bitcast.27, bf16[32,4096]{1,0:T(8,128)(2,1)S(1)} %shard_map.46.refs_0_, ...), custom_call_target="tpu_custom_call" | custom-call | flops 10737418240 | bytes 41943040 | tf_op jit(solution)/shard_map/pallas_call | solution.py:207
  55.1 0.7 collective-permute-start.12
  55.8 0.3 shard_map.49.refs_3_.refs_2_
  56.1 1.3 %collective-permute-start.14 = (bf16[256,1024]{1,0:T(8,128)(2,1)S(1)}, bf16[256,1024]{1,0:T(8,128)(2,1)S(1)}, u32[]{:S(2)}, u32[]{:S(2)}) collective-permute-start(bf16[256,1024]{1,0:T(8,128)(2,1)S(1)} %shard_map.49.refs_3_.refs_2_), channel_id=1, source_target_pairs={{16,0},{17,1},{18,2},{19,3},{20,4},{21,5},{22,6},{23,7},{24,8},{25... | collective-permute-start | bytes 1572872 | tf_op jit(solution)/shard_map/ppermute | solution.py:99
  57.4 1.7 %shard_map.50.refs_3_ = bf16[2,256,256]{2,1,0:T(8,128)(2,1)S(1)} custom-call(s32[4]{0:T(128)S(1)} %get-tuple-element.12.refs_11_.bases_ref, s32[1,256]{1,0:T(1,128)S(1)} %get-tuple-element.10.refs_8_.picks_ref, bf16[2,256,1024]{2,1,0:T(8,128)(2,1)S(1)} %shard_map.47.refs_8_.refs_0_, bf16[2,256,768]{2,1,0:T(8,128)(2,1)S(1)} %get-tuple-element.7.refs_1_, ...), custom_call_target="tpu_custom_call" | custom-call | tf_op jit(solution)/shard_map/pallas_call | solution.py:254
  59.1 3.5 %collective-permute-start.9 = (bf16[2,256,256]{2,1,0:T(8,128)(2,1)S(1)}, bf16[2,256,256]{2,1,0:T(8,128)(2,1)S(1)}, u32[]{:S(2)}, u32[]{:S(2)}) collective-permute-start(bf16[2,256,256]{2,1,0:T(8,128)(2,1)S(1)} %shard_map.50.refs_3_), channel_id=1, source_target_pairs={{0,1},{1,0},{2,3},{3,2},{4,5},{5,4},{6,7},{7,6},{8,9},{9,8},{10,11... | collective-permute-start | bytes 786440 | tf_op jit(solution)/shard_map/ppermute | solution.py:99
  62.6 1.7 %shard_map.51.refs_3_ = bf16[2,256,256]{2,1,0:T(8,128)(2,1)S(1)} custom-call(s32[4]{0:T(128)S(1)} %get-tuple-element.12.refs_11_.bases_ref, s32[1,256]{1,0:T(1,128)S(1)} %get-tuple-element.9.refs_9_.picks_ref, bf16[2,256,1024]{2,1,0:T(8,128)(2,1)S(1)} %shard_map.47.refs_8_.refs_0_, bf16[2,256,768]{2,1,0:T(8,128)(2,1)S(1)} %get-tuple-element.7.refs_1_, ...), custom_call_target="tpu_custom_call" | custom-call | tf_op jit(solution)/shard_map/pallas_call | solution.py:254
  64.3 2.3 %collective-permute-start.8 = (bf16[2,256,256]{2,1,0:T(8,128)(2,1)S(1)}, bf16[2,256,256]{2,1,0:T(8,128)(2,1)S(1)}, u32[]{:S(2)}, u32[]{:S(2)}) collective-permute-start(bf16[2,256,256]{2,1,0:T(8,128)(2,1)S(1)} %shard_map.51.refs_3_), channel_id=1, source_target_pairs={{0,1},{1,0},{2,3},{3,2},{4,5},{5,4},{6,7},{7,6},{8,9},{9,8},{10,11... | collective-permute-start | bytes 786440 | tf_op jit(solution)/shard_map/ppermute | solution.py:99
  66.7 2.6 %shard_map.52.mine_ref = bf16[2,256,512]{2,1,0:T(8,128)(2,1)S(1)} custom-call(s32[4]{0:T(128)S(1)} %get-tuple-element.12.refs_11_.bases_ref, s32[1,512]{1,0:T(1,128)S(1)} %bitcast.23, bf16[2,256,1024]{2,1,0:T(8,128)(2,1)S(1)} %shard_map.47.refs_8_.refs_0_, bf16[2,256,768]{2,1,0:T(8,128)(2,1)S(1)} %get-tuple-element.7.refs_1_, ...), custom_call_target="tpu_custom_call" | custom-call | tf_op jit(solution)/shard_map/pallas_call | solution.py:254
  69.3 0.7 collective-permute-done.9.theirs_ref
  70.0 0.3 shard_map.53
  70.3 1.3 %collective-permute-start.10 = (bf16[256,256]{1,0:T(8,128)(2,1)S(1)}, bf16[256,256]{1,0:T(8,128)(2,1)S(1)}, u32[]{:S(2)}, u32[]{:S(2)}) collective-permute-start(bf16[256,256]{1,0:T(8,128)(2,1)S(1)} %shard_map.53), channel_id=1, source_target_pairs={{0,16},{1,17},{2,18},{3,19},{4,20},{5,21},{6,22},{7,23},{8,24},{9,... | collective-permute-start | bytes 393224 | tf_op jit(solution)/shard_map/ppermute | solution.py:99
  71.6 0.7 collective-permute-start.16
  72.3 4.3 %collective-permute-done.14.refs_1_ = bf16[256,1024]{1,0:T(8,128)(2,1)S(1)} collective-permute-done((bf16[256,1024]{1,0:T(8,128)(2,1)S(1)}, bf16[256,1024]{1,0:T(8,128)(2,1)S(1)}, u32[]{:S(2)}, u32[]{:S(2)}) %collective-permute-start.14) | collective-permute-done | bytes 524320 | tf_op jit(solution)/shard_map/ppermute | solution.py:99
  76.6 3.4 %collective-permute-start.15 = (bf16[256,1024]{1,0:T(8,128)(2,1)S(1)}, bf16[256,1024]{1,0:T(8,128)(2,1)S(1)}, u32[]{:S(2)}, u32[]{:S(2)}) collective-permute-start(bf16[256,1024]{1,0:T(8,128)(2,1)S(1)} %collective-permute-done.14.refs_1_), channel_id=1, source_target_pairs={{0,1},{1,0},{2,3},{3,2},{4,5},{5,4},{6,7},{7,6},{8,9},{9,8},{10,11... | collective-permute-start | bytes 1572872 | tf_op jit(solution)/shard_map/ppermute | solution.py:99
  80.0 0.3 shard_map.54.refs_0_
  80.4 4.9 %collective-permute-start.11 = (bf16[256,256]{1,0:T(8,128)(2,1)S(1)}, bf16[256,256]{1,0:T(8,128)(2,1)S(1)}, u32[]{:S(2)}, u32[]{:S(2)}) collective-permute-start(bf16[256,256]{1,0:T(8,128)(2,1)S(1)} %shard_map.54.refs_0_), channel_id=1, source_target_pairs={{0,8},{1,9},{2,10},{3,11},{4,12},{5,13},{6,14},{7,15},{8,0},{9,1},... | collective-permute-start | bytes 393224 | tf_op jit(solution)/shard_map/ppermute | solution.py:99
  85.2 0.2 shard_map.55.refs_2_.refs_4_
  85.5 1.3 %collective-permute-start.17 = (bf16[256,768]{1,0:T(8,128)(2,1)S(1)}, bf16[256,768]{1,0:T(8,128)(2,1)S(1)}, u32[]{:S(2)}, u32[]{:S(2)}) collective-permute-start(bf16[256,768]{1,0:T(8,128)(2,1)S(1)} %shard_map.55.refs_2_.refs_4_), channel_id=1, source_target_pairs={{16,0},{17,1},{18,2},{19,3},{20,4},{21,5},{22,6},{23,7},{24,8},{25... | collective-permute-start | bytes 1179656 | tf_op jit(solution)/shard_map/ppermute | solution.py:99
  86.8 0.7 collective-permute-start.18
  87.5 2.1 %collective-permute-done.11.refs_1_ = bf16[256,256]{1,0:T(8,128)(2,1)S(1)} collective-permute-done((bf16[256,256]{1,0:T(8,128)(2,1)S(1)}, bf16[256,256]{1,0:T(8,128)(2,1)S(1)}, u32[]{:S(2)}, u32[]{:S(2)}) %collective-permute-start.11) | collective-permute-done | bytes 131104 | tf_op jit(solution)/shard_map/ppermute | solution.py:99
  89.6 0.3 shard_map.56.refs_0_
  89.9 2.5 %collective-permute-start.13 = (bf16[512,256]{1,0:T(8,128)(2,1)S(1)}, bf16[512,256]{1,0:T(8,128)(2,1)S(1)}, u32[]{:S(2)}, u32[]{:S(2)}) collective-permute-start(bf16[512,256]{1,0:T(8,128)(2,1)S(1)} %shard_map.56.refs_0_), channel_id=1, source_target_pairs={{0,4},{1,5},{2,6},{3,7},{4,0},{5,1},{6,2},{7,3},{8,12},{9,13},{10,... | collective-permute-start | bytes 786440 | tf_op jit(solution)/shard_map/ppermute | solution.py:99
  92.4 4.3 %collective-permute-done.13.refs_1_ = bf16[512,256]{1,0:T(8,128)(2,1)S(1)} collective-permute-done((bf16[512,256]{1,0:T(8,128)(2,1)S(1)}, bf16[512,256]{1,0:T(8,128)(2,1)S(1)}, u32[]{:S(2)}, u32[]{:S(2)}) %collective-permute-start.13) | collective-permute-done | bytes 262176 | tf_op jit(solution)/shard_map/ppermute | solution.py:99
  96.8 0.1 shard_map.57.refs_0_
  96.8 0.1 collective-permute-start.19
  96.9 2.4 %collective-permute-start.20 = (bf16[256,768]{1,0:T(8,128)(2,1)S(1)}, bf16[256,768]{1,0:T(8,128)(2,1)S(1)}, u32[]{:S(2)}, u32[]{:S(2)}) collective-permute-start(bf16[256,768]{1,0:T(8,128)(2,1)S(1)} %collective-permute-done.17.refs_4_.refs_3_), channel_id=1, source_target_pairs={{0,1},{1,0},{2,3},{3,2},{4,5},{5,4},{6,7},{7,6},{8,9},{9,8},{10,11... | collective-permute-start | bytes 1179656 | tf_op jit(solution)/shard_map/ppermute | solution.py:99
  99.4 4.0 %shard_map.58.refs_7_ = bf16[2048,3584]{1,0:T(8,128)(2,1)} custom-call(s32[5]{0:T(128)S(1)} %stack.69.refs_15_.where_ref, bf16[1024,256]{1,0:T(8,128)(2,1)S(1)} %shard_map.57.refs_0_, bf16[256,1024]{1,0:T(8,128)(2,1)S(1)} %collective-permute-done.14.refs_1_, bf16[256,1024]{1,0:T(8,128)(2,1)S(1)} %shard_map.49.refs_3_.refs_2_, ...), custom_call_target="tpu_custom_call" | custom-call | flops 1476395008 | bytes 5767168 | tf_op jit(solution)/shard_map/pallas_call | solution.py:418
  103.4 4.2 %shard_map.59.refs_4_ = bf16[2048,3584]{1,0:T(8,128)(2,1)} custom-call(s32[5]{0:T(128)S(1)} %stack.69.refs_15_.where_ref, bf16[1024,256]{1,0:T(8,128)(2,1)S(1)} %collective-permute-done.19.refs_0_.refs_1_, bf16[256,1024]{1,0:T(8,128)(2,1)S(1)} %collective-permute-done.14.refs_1_, ...), custom_call_target="tpu_custom_call", output_to_operand_aliasing={{}: (8, {})} | custom-call | flops 1476395008 | bytes 5767168 | tf_op jit(solution)/shard_map/pallas_call | solution.py:418
  107.6 2.7 %collective-permute-done.20.refs_2_ = bf16[256,768]{1,0:T(8,128)(2,1)S(1)} collective-permute-done((bf16[256,768]{1,0:T(8,128)(2,1)S(1)}, bf16[256,768]{1,0:T(8,128)(2,1)S(1)}, u32[]{:S(2)}, u32[]{:S(2)}) %collective-permute-start.20) | collective-permute-done | bytes 393248 | tf_op jit(solution)/shard_map/ppermute | solution.py:99
  110.3 3.1 %shard_map.60 = bf16[2048,3584]{1,0:T(8,128)(2,1)} custom-call(s32[4]{0:T(128)S(1)} %get-tuple-element.11.refs_16_.where_ref, bf16[1024,256]{1,0:T(8,128)(2,1)S(1)} %shard_map.57.refs_0_, bf16[1024,256]{1,0:T(8,128)(2,1)S(1)} %collective-permute-done.19.refs_0_.refs_1_, ...), custom_call_target="tpu_custom_call", output_to_operand_aliasing={{}: (5, {})} | custom-call | flops 805306368 | bytes 3145728 | tf_op jit(solution)/shard_map/pallas_call | solution.py:418
  (19 shorter events, 0.1 us)
Async XLA Ops:
  0.0 12.5 %collective-permute-start = (bf16[32,4096]{1,0:T(8,128)(2,1)}, bf16[32,4096]{1,0:T(8,128)(2,1)S(1)}, u32[]{:S(2)}, u32[]{:S(2)}) collective-permute-start(bf16[32,4096]{1,0:T(8,128)(2,1)} %bitcast.18), channel_id=1, source_target_pairs={{0,4},{1,5},{2,6},{3,7},{4,8},{5,9},{6,10},{7,11},{8,12},{9,13},{1... | collective-permute-start | bytes 786440 | tf_op jit(solution)/shard_map/ppermute | solution.py:99
  3.0 19.9 %collective-permute-start.1 = (bf16[32,4096]{1,0:T(8,128)(2,1)}, bf16[32,4096]{1,0:T(8,128)(2,1)S(1)}, u32[]{:S(2)}, u32[]{:S(2)}) collective-permute-start(bf16[32,4096]{1,0:T(8,128)(2,1)} %bitcast.19), channel_id=1, source_target_pairs={{0,8},{1,9},{2,10},{3,11},{4,12},{5,13},{6,14},{7,15},{8,0},{9,1},... | collective-permute-start | bytes 786440 | tf_op jit(solution)/shard_map/ppermute | solution.py:99
  5.6 17.3 %collective-permute-start.2 = (bf16[32,4096]{1,0:T(8,128)(2,1)}, bf16[32,4096]{1,0:T(8,128)(2,1)S(1)}, u32[]{:S(2)}, u32[]{:S(2)}) collective-permute-start(bf16[32,4096]{1,0:T(8,128)(2,1)} %bitcast.20), channel_id=1, source_target_pairs={{0,12},{1,13},{2,14},{3,15},{4,0},{5,1},{6,2},{7,3},{8,4},{9,5},{1... | collective-permute-start | bytes 786440 | tf_op jit(solution)/shard_map/ppermute | solution.py:99
  7.0 1.0 copy-start
  8.0 15.6 %collective-permute-start.3 = (bf16[32,4096]{1,0:T(8,128)(2,1)S(1)}, bf16[32,4096]{1,0:T(8,128)(2,1)S(1)}, u32[]{:S(2)}, u32[]{:S(2)}) collective-permute-start(bf16[32,4096]{1,0:T(8,128)(2,1)S(1)} %shard_map.46.refs_0_), channel_id=1, source_target_pairs={{0,2},{1,3},{2,0},{3,1},{4,6},{5,7},{6,4},{7,5},{8,10},{9,11},{10,... | collective-permute-start | bytes 786440 | tf_op jit(solution)/shard_map/ppermute | solution.py:99
  12.5 11.1 %collective-permute-start.4 = (bf16[32,4096]{1,0:T(8,128)(2,1)S(1)}, bf16[32,4096]{1,0:T(8,128)(2,1)S(1)}, u32[]{:S(2)}, u32[]{:S(2)}) collective-permute-start(bf16[32,4096]{1,0:T(8,128)(2,1)S(1)} %collective-permute-done.refs_1_), channel_id=1, source_target_pairs={{0,2},{1,3},{2,0},{3,1},{4,6},{5,7},{6,4},{7,5},{8,10},{9,11},{10,... | collective-permute-start | bytes 786440 | tf_op jit(solution)/shard_map/ppermute | solution.py:99
  22.9 1.5 %collective-permute-start.5 = (bf16[32,4096]{1,0:T(8,128)(2,1)S(1)}, bf16[32,4096]{1,0:T(8,128)(2,1)S(1)}, u32[]{:S(2)}, u32[]{:S(2)}) collective-permute-start(bf16[32,4096]{1,0:T(8,128)(2,1)S(1)} %collective-permute-done.1.refs_2_), channel_id=1, source_target_pairs={{0,2},{1,3},{2,0},{3,1},{4,6},{5,7},{6,4},{7,5},{8,10},{9,11},{10,... | collective-permute-start | bytes 786440 | tf_op jit(solution)/shard_map/ppermute | solution.py:99
  22.9 1.9 %collective-permute-start.6 = (bf16[32,4096]{1,0:T(8,128)(2,1)S(1)}, bf16[32,4096]{1,0:T(8,128)(2,1)S(1)}, u32[]{:S(2)}, u32[]{:S(2)}) collective-permute-start(bf16[32,4096]{1,0:T(8,128)(2,1)S(1)} %collective-permute-done.2.refs_3_), channel_id=1, source_target_pairs={{0,2},{1,3},{2,0},{3,1},{4,6},{5,7},{6,4},{7,5},{8,10},{9,11},{10,... | collective-permute-start | bytes 786440 | tf_op jit(solution)/shard_map/ppermute | solution.py:99
  34.0 21.8 %collective-permute-start.7 = (bf16[2,256,1024]{2,1,0:T(8,128)(2,1)S(1)}, bf16[2,256,1024]{2,1,0:T(8,128)(2,1)S(1)}, u32[]{:S(2)}, u32[]{:S(2)}) collective-permute-start(bf16[2,256,1024]{2,1,0:T(8,128)(2,1)S(1)} %shard_map.47.refs_8_.refs_0_), channel_id=1, source_target_pairs={{16,17},{17,16},{18,19},{19,18},{20,21},{21,20},{22,23},{23,22},{2... | collective-permute-start | bytes 3145736 | tf_op jit(solution)/shard_map/ppermute | solution.py:99
  55.1 30.1 %collective-permute-start.12 = (bf16[2,256,768]{2,1,0:T(8,128)(2,1)S(1)}, bf16[2,256,768]{2,1,0:T(8,128)(2,1)S(1)}, u32[]{:S(2)}, u32[]{:S(2)}) collective-permute-start(bf16[2,256,768]{2,1,0:T(8,128)(2,1)S(1)} %get-tuple-element.7.refs_1_), channel_id=1, source_target_pairs={{16,17},{17,16},{18,19},{19,18},{20,21},{21,20},{22,23},{23,22},{2... | collective-permute-start | bytes 2359304 | tf_op jit(solution)/shard_map/ppermute | solution.py:99
  56.1 20.5 %collective-permute-start.14 = (bf16[256,1024]{1,0:T(8,128)(2,1)S(1)}, bf16[256,1024]{1,0:T(8,128)(2,1)S(1)}, u32[]{:S(2)}, u32[]{:S(2)}) collective-permute-start(bf16[256,1024]{1,0:T(8,128)(2,1)S(1)} %shard_map.49.refs_3_.refs_2_), channel_id=1, source_target_pairs={{16,0},{17,1},{18,2},{19,3},{20,4},{21,5},{22,6},{23,7},{24,8},{25... | collective-permute-start | bytes 1572872 | tf_op jit(solution)/shard_map/ppermute | solution.py:99
  59.1 10.9 %collective-permute-start.9 = (bf16[2,256,256]{2,1,0:T(8,128)(2,1)S(1)}, bf16[2,256,256]{2,1,0:T(8,128)(2,1)S(1)}, u32[]{:S(2)}, u32[]{:S(2)}) collective-permute-start(bf16[2,256,256]{2,1,0:T(8,128)(2,1)S(1)} %shard_map.50.refs_3_), channel_id=1, source_target_pairs={{0,1},{1,0},{2,3},{3,2},{4,5},{5,4},{6,7},{7,6},{8,9},{9,8},{10,11... | collective-permute-start | bytes 786440 | tf_op jit(solution)/shard_map/ppermute | solution.py:99
  64.3 15.7 %collective-permute-start.8 = (bf16[2,256,256]{2,1,0:T(8,128)(2,1)S(1)}, bf16[2,256,256]{2,1,0:T(8,128)(2,1)S(1)}, u32[]{:S(2)}, u32[]{:S(2)}) collective-permute-start(bf16[2,256,256]{2,1,0:T(8,128)(2,1)S(1)} %shard_map.51.refs_3_), channel_id=1, source_target_pairs={{0,1},{1,0},{2,3},{3,2},{4,5},{5,4},{6,7},{7,6},{8,9},{9,8},{10,11... | collective-permute-start | bytes 786440 | tf_op jit(solution)/shard_map/ppermute | solution.py:99
  70.3 9.7 %collective-permute-start.10 = (bf16[256,256]{1,0:T(8,128)(2,1)S(1)}, bf16[256,256]{1,0:T(8,128)(2,1)S(1)}, u32[]{:S(2)}, u32[]{:S(2)}) collective-permute-start(bf16[256,256]{1,0:T(8,128)(2,1)S(1)} %shard_map.53), channel_id=1, source_target_pairs={{0,16},{1,17},{2,18},{3,19},{4,20},{5,21},{6,22},{7,23},{8,24},{9,... | collective-permute-start | bytes 393224 | tf_op jit(solution)/shard_map/ppermute | solution.py:99
  71.6 20.8 %collective-permute-start.16 = (bf16[256,1024]{1,0:T(8,128)(2,1)S(1)}, bf16[256,1024]{1,0:T(8,128)(2,1)S(1)}, u32[]{:S(2)}, u32[]{:S(2)}) collective-permute-start(bf16[256,1024]{1,0:T(8,128)(2,1)S(1)} %shard_map.49.refs_3_.refs_2_), channel_id=1, source_target_pairs={{16,17},{17,16},{18,19},{19,18},{20,21},{21,20},{22,23},{23,22},{2... | collective-permute-start | bytes 1572872 | tf_op jit(solution)/shard_map/ppermute | solution.py:99
  76.6 20.2 %collective-permute-start.15 = (bf16[256,1024]{1,0:T(8,128)(2,1)S(1)}, bf16[256,1024]{1,0:T(8,128)(2,1)S(1)}, u32[]{:S(2)}, u32[]{:S(2)}) collective-permute-start(bf16[256,1024]{1,0:T(8,128)(2,1)S(1)} %collective-permute-done.14.refs_1_), channel_id=1, source_target_pairs={{0,1},{1,0},{2,3},{3,2},{4,5},{5,4},{6,7},{7,6},{8,9},{9,8},{10,11... | collective-permute-start | bytes 1572872 | tf_op jit(solution)/shard_map/ppermute | solution.py:99
  80.4 9.2 %collective-permute-start.11 = (bf16[256,256]{1,0:T(8,128)(2,1)S(1)}, bf16[256,256]{1,0:T(8,128)(2,1)S(1)}, u32[]{:S(2)}, u32[]{:S(2)}) collective-permute-start(bf16[256,256]{1,0:T(8,128)(2,1)S(1)} %shard_map.54.refs_0_), channel_id=1, source_target_pairs={{0,8},{1,9},{2,10},{3,11},{4,12},{5,13},{6,14},{7,15},{8,0},{9,1},... | collective-permute-start | bytes 393224 | tf_op jit(solution)/shard_map/ppermute | solution.py:99
  85.5 11.3 %collective-permute-start.17 = (bf16[256,768]{1,0:T(8,128)(2,1)S(1)}, bf16[256,768]{1,0:T(8,128)(2,1)S(1)}, u32[]{:S(2)}, u32[]{:S(2)}) collective-permute-start(bf16[256,768]{1,0:T(8,128)(2,1)S(1)} %shard_map.55.refs_2_.refs_4_), channel_id=1, source_target_pairs={{16,0},{17,1},{18,2},{19,3},{20,4},{21,5},{22,6},{23,7},{24,8},{25... | collective-permute-start | bytes 1179656 | tf_op jit(solution)/shard_map/ppermute | solution.py:99
  86.8 10.0 %collective-permute-start.18 = (bf16[256,768]{1,0:T(8,128)(2,1)S(1)}, bf16[256,768]{1,0:T(8,128)(2,1)S(1)}, u32[]{:S(2)}, u32[]{:S(2)}) collective-permute-start(bf16[256,768]{1,0:T(8,128)(2,1)S(1)} %shard_map.55.refs_2_.refs_4_), channel_id=1, source_target_pairs={{16,17},{17,16},{18,19},{19,18},{20,21},{21,20},{22,23},{23,22},{2... | collective-permute-start | bytes 1179656 | tf_op jit(solution)/shard_map/ppermute | solution.py:99
  89.9 6.8 %collective-permute-start.13 = (bf16[512,256]{1,0:T(8,128)(2,1)S(1)}, bf16[512,256]{1,0:T(8,128)(2,1)S(1)}, u32[]{:S(2)}, u32[]{:S(2)}) collective-permute-start(bf16[512,256]{1,0:T(8,128)(2,1)S(1)} %shard_map.56.refs_0_), channel_id=1, source_target_pairs={{0,4},{1,5},{2,6},{3,7},{4,0},{5,1},{6,2},{7,3},{8,12},{9,13},{10,... | collective-permute-start | bytes 786440 | tf_op jit(solution)/shard_map/ppermute | solution.py:99
  96.8 6.6 %collective-permute-start.19 = (bf16[1024,256]{1,0:T(8,128)(2,1)S(1)}, bf16[1024,256]{1,0:T(8,128)(2,1)S(1)}, u32[]{:S(2)}, u32[]{:S(2)}) collective-permute-start(bf16[1024,256]{1,0:T(8,128)(2,1)S(1)} %shard_map.57.refs_0_), channel_id=1, source_target_pairs={{0,2},{1,3},{2,0},{3,1},{4,6},{5,7},{6,4},{7,5},{8,10},{9,11},{10,... | collective-permute-start | bytes 1572872 | tf_op jit(solution)/shard_map/ppermute | solution.py:99
  96.9 13.4 %collective-permute-start.20 = (bf16[256,768]{1,0:T(8,128)(2,1)S(1)}, bf16[256,768]{1,0:T(8,128)(2,1)S(1)}, u32[]{:S(2)}, u32[]{:S(2)}) collective-permute-start(bf16[256,768]{1,0:T(8,128)(2,1)S(1)} %collective-permute-done.17.refs_4_.refs_3_), channel_id=1, source_target_pairs={{0,1},{1,0},{2,3},{3,2},{4,5},{5,4},{6,7},{7,6},{8,9},{9,8},{10,11... | collective-permute-start | bytes 1179656 | tf_op jit(solution)/shard_map/ppermute | solution.py:99
